TPU v7x, 32 devices: a whole 2x2x4 slice. The times are simulated.
32 devices in a mesh: cfg: 2 (over core), req: 8 (over z, x), seq: 2 (over y).
Axes of the slice: x: 2, y: 2, z: 4, core: 2. Of those that a mesh axis runs over, the one named last changes fastest.
Arguments:
- hidden: bfloat16 [2, 8, 576, 1536], P('cfg', 'req', 'seq'), may hold values from -6 to 6
- latent: float32 [8, 576, 64], P('req', 'seq', 'cfg'), may hold values from -6 to 6
- modulation: float32 [8, 5, 1536], P('req'), may hold values from -3 to 3
- w_qkv: bfloat16 [1536, 4608], P('req'), may hold values from -1 to 1
- w_out: bfloat16 [1536, 1536], P('req'), may hold values from -0.15625 to 0.15625
- q_gain: float32 [1536], replicated, may hold values from 0 to 2
- k_gain: float32 [1536], replicated, may hold values from 0 to 2
- w_head: bfloat16 [1536, 64], replicated, may hold values from -0.15625 to 0.15625
- lengths: int32 [8], P('req'), may hold values from 288 to 576, as said below
- guidance: float32 [8], P('req'), may hold values from 3 to 7
- step_size: float32 [8], P('req'), may hold values from 0.03 to 0.3
Outputs:
- new_latent: float32 [8, 576, 64], P('req', 'seq', 'cfg')
Inputs may be any that keep to these rules, and one draw needn't show every extreme that they name: `lengths`: some request has exactly 576 video tokens in every draw.
All inputs are finite; a program needn't handle non-finite values.
Results may differ from a plain program's by a relative error of at most 0.01.
Values may be sent and summed in bfloat16 or wider, within the bound.
No kernel may reach another device: no remote copies, remote signals or barrier semaphores. Data moves between devices by JAX's collectives and lax.ppermute only.
A program may use at most 128 MiB of HBM per device.

v0:
```python
import jax
import jax.numpy as jnp
from jax import lax
from jax.sharding import PartitionSpec as P

DH = 128


def passed_along(value, axis, steps):
    count = lax.axis_size(axis)
    pairs = [(source, (source + steps) % count) for source in range(count)]
    return lax.ppermute(value, axis, pairs)


def from_partner(value, axis, apart):
    mask = 2**apart
    pairs = [(source, source ^ mask) for source in range(lax.axis_size(axis))]
    return lax.ppermute(value, axis, pairs)


def layer_norm(values):
    centered = values - jnp.mean(values, axis=-1, keepdims=True)
    return centered / jnp.sqrt(jnp.mean(centered * centered, axis=-1, keepdims=True) + 1e-06)


def rms_gain(values, gain):
    return values / jnp.sqrt(jnp.mean(values * values, axis=-1, keepdims=True) + 1e-06) * gain


def add_rows(left, piece):
    return jnp.dot(left, piece, preferred_element_type=jnp.float32)


def attend(state, query, stacked, start, length):
    top, total, weighted = state
    keys = stacked[0]
    values = stacked[1]
    count = keys.shape[0]
    scores = jnp.einsum("qhd,khd->qhk", query, keys, preferred_element_type=jnp.float32) / jnp.sqrt(
        jnp.float32(query.shape[2])
    )
    valid = start + jnp.arange(count, dtype=jnp.int32) < length
    scores = jnp.where(valid[None, None, :], scores, jnp.float32(-1e30))
    new_top = jnp.maximum(top, jnp.max(scores, axis=-1))
    factor = jnp.exp(top - new_top)
    probs = jnp.where(valid[None, None, :], jnp.exp(scores - new_top[:, :, None]), jnp.float32(0.0))
    total = total * factor + jnp.sum(probs, axis=-1)
    weighted = weighted * factor[:, :, None] + jnp.einsum(
        "qhk,khd->qhd", probs.astype(jnp.bfloat16), values, preferred_element_type=jnp.float32
    )
    return (new_top, total, weighted)


def local(
    hidden, latent, modulation, w_qkv, w_out, q_gain, k_gain, w_head, lengths, guidance, step_size
):
    state = hidden[0, 0]
    modes = modulation[0]
    length = lengths[0]
    rows = state.shape[0]
    width = state.shape[1]
    heads = q_gain.shape[0] // DH
    wide = state.astype(jnp.float32)
    normed = (layer_norm(wide) * (1.0 + modes[1]) + modes[0]).astype(jnp.bfloat16)
    qkv = add_rows(normed, lax.all_gather(w_qkv, "req", axis=0, tiled=True))
    query = rms_gain(qkv[:, :width], q_gain).astype(jnp.bfloat16).reshape(rows, heads, DH)
    keys = rms_gain(qkv[:, width : 2 * width], k_gain).astype(jnp.bfloat16).reshape(rows, heads, DH)
    values = qkv[:, 2 * width :].astype(jnp.bfloat16).reshape(rows, heads, DH)
    stacked = jnp.stack([keys, values])
    position = lax.axis_index("seq")
    members = lax.axis_size("seq")
    start_state = (
        jnp.full((rows, heads), -1e30, jnp.float32),
        jnp.zeros((rows, heads), jnp.float32),
        jnp.zeros((rows, heads, DH), jnp.float32),
    )
    first = attend(start_state, query, stacked, position * rows, length)

    def cycle_step(turn, carry):
        moving, inner = carry
        moving = passed_along(moving, "seq", 1)
        source = (position - turn) % members
        return (moving, attend(inner, query, moving, source * rows, length))

    moved, result = lax.fori_loop(1, members, cycle_step, (stacked, first))
    top, total, weighted = result
    attended = (weighted / total[:, :, None]).reshape(rows, width).astype(jnp.bfloat16)
    projected = add_rows(attended, lax.all_gather(w_out, "req", axis=0, tiled=True))
    block_out = (wide + modes[2] * projected).astype(jnp.bfloat16)
    head_in = (layer_norm(block_out.astype(jnp.float32)) * (1.0 + modes[4]) + modes[3]).astype(
        jnp.bfloat16
    )
    velocity = jnp.dot(head_in, w_head, preferred_element_type=jnp.float32)
    branch = lax.axis_index("cfg")
    scale = guidance[0]
    channels = velocity.shape[1] // 2
    own = lax.dynamic_slice_in_dim(velocity, branch * channels, channels, 1)
    outgoing = lax.dynamic_slice_in_dim(velocity, (1 - branch) * channels, channels, 1)
    other = from_partner(outgoing.astype(jnp.bfloat16), "cfg", 0).astype(outgoing.dtype)
    cond = jnp.where(branch == 0, own, other)
    uncond = jnp.where(branch == 0, other, own)
    guided = uncond + scale * (cond - uncond)
    valid = position * rows + jnp.arange(rows, dtype=jnp.int32) < length
    current = latent[0]
    updated = jnp.where(valid[:, None], current - step_size[0] * guided, current)
    return updated[None]


def solution(mesh):
    return jax.shard_map(
        local,
        mesh=mesh,
        in_specs=(
            P("cfg", "req", "seq", None),
            P("req", "seq", "cfg"),
            P("req", None, None),
            P("req", None),
            P("req", None),
            P(),
            P(),
            P(),
            P("req"),
            P("req"),
            P("req"),
        ),
        out_specs=P("req", "seq", "cfg"),
        check_vma=False,
    )
```

profile of v0, /device:TPU:0, one launch (start us, length us, event | category | flops | bytes accessed | tf_op | source)
XLA Modules:
  0.0 302.0 jit_solution(3949994219796695452)
XLA Ops:
  6.5 0.0 copy-start
  6.5 0.0 copy-start.7
  6.5 0.0 copy-start.2
  6.5 0.0 all-gather.3.cloned.1.call-start
  6.5 0.7 all-gather.3.cloned.1.call-update
  7.3 0.0 all-gather.5.cloned.1.call-start
  7.3 0.7 all-gather.5.cloned.1.call-update
  8.0 0.0 copy-done.7
  8.0 0.1 add_reduce_fusion
  8.1 0.0 copy-done.2
  8.1 0.2 convert_reduce_fusion
  8.3 0.4 fusion.30
  8.7 199.1 %all-gather.3.cloned.1.call-done = bf16[1536,4608]{1,0:T(8,128)(2,1)} async-done(((bf16[192,4608]{1,0:T(8,128)(2,1)}), bf16[1536,4608]{1,0:T(8,128)(2,1)}) %all-gather.3.cloned.1.call-update) | async-done | bytes 14155792 | tf_op jit(solution)/shard_map/all_gather | solution.py:65
  207.9 7.9 %fusion.42 = f32[288,4608]{1,0:T(8,128)S(1)} fusion(bf16[1536,4608]{1,0:T(8,128)(2,1)} %all-gather.3.cloned.1.call-done, bf16[1,1,288,1536]{3,2,1,0:T(8,128)(2,1)S(1)} %copy-done.2, f32[1536]{0:T(1024)S(1)} %get-tuple-element.24, f32[1536]{0:T(1024)S(1)} %get-tuple-element.25, f32[288]{0:T(512)S(1)} %add_sqrt_fusion.3, f32[288]{0:T(512)S(1)} %broadcast_multiply_fusion.1), kind=kOutput, calls=%fused_computation.55 | convolution fusion | flops 4079517696 | bytes 20363520 | tf_op jit(solution)/shard_map/dot_general | solution.py:31
  215.8 0.0 copy-start.1
  215.8 1.1 slice.69
  217.0 0.0 copy-start.8
  217.0 0.0 copy-start.9
  217.0 0.3 multiply_reduce_fusion.1
  217.3 1.1 copy-done.1
  218.4 0.0 copy-done.8
  218.4 0.0 copy-done.9
  218.4 1.6 fusion.58
  220.0 0.0 copy-start.3
  220.0 0.9 copy-done.3
  220.9 0.6 stack_reshape.6
  221.5 0.2 copy.24
  221.8 1.9 stack_reshape.7
  223.6 0.2 copy.25
  223.9 0.0 copy-start.4
  223.9 1.4 pad_maximum_fusion
  225.3 1.5 collective-permute-start
  227.5 0.0 copy-done.4
  227.5 0.0 copy-start.5
  227.5 2.2 bitcast_reduce_fusion.1
  229.8 35.9 %collective-permute-done = bf16[2,288,12,128]{3,1,2,0:T(8,128)(2,1)} collective-permute-done((bf16[2,288,12,128]{3,1,2,0:T(8,128)(2,1)}, bf16[2,288,12,128]{3,1,2,0:T(8,128)(2,1)}, u32[]{:S(2)}, u32[]{:S(2)}) %collective-permute-start) | collective-permute-done | bytes 1769504 | tf_op jit(solution)/shard_map/while/body/eval_jaxpr/ppermute | solution.py:12
  265.6 0.0 copy-done.5
  265.6 2.1 bitcast_reduce_fusion
  267.8 1.5 fusion.4
  269.3 1.5 fusion.6
  270.8 3.4 %fusion.11 = f32[12,128,288]{1,2,0:T(8,128)S(1)} fusion(f32[12,288,288]{2,1,0:T(8,128)S(1)} %get-tuple-element.47, f32[288,12]{0,1:T(8,128)S(1)} %get-tuple-element.45, pred[288]{0:T(512)(128)(4,1)S(1)} %get-tuple-element.53, f32[288,4608]{1,0:T(8,128)} %copy-done.1), kind=kOutput, calls=%fused_computation.17 | convolution fusion | flops 259780608 | bytes 7988224 | tf_op jit(solution)/shard_map/qhk,khd->qhd/dot_general | solution.py:48
  274.1 4.3 %fusion.39 = bf16[12,36,8,128]{3,2,1,0:T(8,128)(2,1)S(1)} fusion(f32[12,288,288]{2,1,0:T(8,128)S(1)} %get-tuple-element.49, f32[288,12]{0,1:T(8,128)S(1)} %get-tuple-element.44, pred[288]{0:T(512)(128)(4,1)S(1)} %get-tuple-element.52, f32[12,128,288]{1,2,0:T(8,128)S(1)} %fusion.11, bf16[2,288,12,128]{3,1,2,0:T(8,128)(2,1)} %collective-permute-done, ...), kind=kOutput, calls=%fused_computation.54 | convolution fusion | flops 261992448 | bytes 8946688 | tf_op jit(solution)/shard_map/while/body/eval_jaxpr/qhk,khd->qhd/dot_general | solution.py:48
  278.4 9.7 %all-gather.5.cloned.1.call-done = bf16[1536,1536]{1,0:T(8,128)(2,1)} async-done(((bf16[192,1536]{1,0:T(8,128)(2,1)}), bf16[1536,1536]{1,0:T(8,128)(2,1)}) %all-gather.5.cloned.1.call-update) | async-done | bytes 4718608 | tf_op jit(solution)/shard_map/all_gather | solution.py:88
  288.2 4.0 %fusion.74 = (f32[288]{0:T(512)S(1)}, f32[288,1536]{1,0:T(8,128)S(1)}) fusion(bf16[1536,1536]{1,0:T(8,128)(2,1)} %all-gather.5.cloned.1.call-done, bf16[12,36,8,128]{3,2,1,0:T(8,128)(2,1)S(1)} %fusion.39, f32[1536]{0:T(1024)S(1)} %get-tuple-element.26, bf16[1,1,288,1536]{3,2,1,0:T(8,128)(2,1)S(1)} %copy-done.2), kind=kOutput, calls=%fused_computation.109 | convolution fusion | flops 1361608448 | bytes 8264832 | tf_op jit(solution)/shard_map/dot_general | solution.py:31
  292.2 0.3 multiply_reduce_fusion
  292.5 0.0 copy-done
  292.5 0.0 copy-start.6
  292.6 0.5 fusion.59
  293.1 0.1 collective-permute-start.1
  294.5 0.0 collective-permute-done.1
  294.5 0.0 copy-done.6
  294.5 0.6 fusion.66
  (9 shorter events, 0.1 us)
Async XLA Ops:
  6.5 286.0 %copy-start = (bf16[1536,64]{0,1:T(8,128)(2,1)S(1)}, bf16[1536,64]{0,1:T(8,128)(2,1)}, u32[]{:S(2)}) copy-start(bf16[1536,64]{0,1:T(8,128)(2,1)} %param.18) | copy-start | bytes 589828
  6.5 1.5 copy-start.7
  6.5 1.6 copy-start.2
  6.5 201.4 %all-gather.3.cloned.1.call-start = ((), (), s32[]{:S(2)}) async-start(), calls=%async_computation | async-start | bytes 15925248 | tf_op jit(solution)/shard_map/all_gather | solution.py:65
  7.3 280.9 %all-gather.5.cloned.1.call-start = ((), (), s32[]{:S(2)}) async-start(), calls=%async_computation.1 | async-start | bytes 5308416 | tf_op jit(solution)/shard_map/all_gather | solution.py:88
  215.8 2.6 copy-start.1
  217.0 1.4 copy-start.8
  217.0 1.4 copy-start.9
  220.0 0.9 copy-start.3
  223.9 3.6 %copy-start.4 = (bf16[288,1536]{1,0:T(8,128)(2,1)S(1)}, bf16[288,1536]{1,0:T(8,128)(2,1)}, u32[]{:S(2)}) copy-start(bf16[288,1536]{1,0:T(8,128)(2,1)} %copy-done.3) | copy-start | bytes 2654212
  225.3 40.3 %collective-permute-start = (bf16[2,288,12,128]{3,1,2,0:T(8,128)(2,1)}, bf16[2,288,12,128]{3,1,2,0:T(8,128)(2,1)}, u32[]{:S(2)}, u32[]{:S(2)}) collective-permute-start(bf16[2,288,12,128]{3,1,2,0:T(8,128)(2,1)} %pad_maximum_fusion), channel_id=1, source_target_pairs={{0,1},{1,0},{2,3},{3,2},{4,5},{5,4},{6,7},{7,6},{8,9},{9,8},{10,11... | collective-permute-start | bytes 5308424 | tf_op jit(solution)/shard_map/while/body/eval_jaxpr/ppermute | solution.py:12
  227.5 38.1 %copy-start.5 = (bf16[36,12,8,128]{3,2,1,0:T(8,128)(2,1)S(1)}, bf16[36,12,8,128]{3,2,1,0:T(8,128)(2,1)}, u32[]{:S(2)}) copy-start(bf16[36,12,8,128]{3,2,1,0:T(8,128)(2,1)} %get-tuple-element.41) | copy-start | bytes 2654212
  292.5 2.0 copy-start.6
  293.1 1.4 collective-permute-start.1
Sparse Core Ops, SparseCore 0:
  9.6 198.2 all-gather.2
  210.1 78.0 all-gather.4
where the time goes:
time: 302 us
  waiting for transfers between devices  246 us (81%)
  matrix products  24.5 us (8%)
  between operations  15.6 us (5%)
  other arithmetic  8.06 us (3%)
  local copies, waits for them, and re-layouts  6.14 us (2%)
    all_gather x1, waiting for transfers between devices, local(): qkv = add_rows(normed, lax.all_gather(w_qkv, 'req', axis=0, tiled=True))  199 us
    ppermute x1, waiting for transfers between devices, passed_along(): return lax.ppermute(value, axis, pairs)  35.9 us
    dot_general x2, matrix products, add_rows(): return jnp.dot(left, piece, preferred_element_type=jnp.float32)  11.9 us
    all_gather x1, waiting for transfers between devices, local(): lax.all_gather(w_out, 'req', axis=0, tiled=True)  9.74 us
    dot_general x2, matrix products, attend(): jnp.einsum('qhk,khd->qhd', probs.astype(jnp.bfloat16), values, preferred_...  7.67 us
  transfers between devices with their start and end apart: 4, of which 3 were waited for; matrix products, arithmetic and copies ran while one was open for 10% of the time, Pallas kernels for 0%

commit v1 on v0

--- a/solution.py
+++ b/solution.py
@@ -1,9 +1,26 @@
+import functools
+
 import jax
 import jax.numpy as jnp
 from jax import lax
+from jax.experimental import pallas as pl
+from jax.experimental.pallas import tpu as pltpu
 from jax.sharding import PartitionSpec as P
 
 DH = 128
+SWAP = [(0, 1), (1, 0)]
+VMEM = pl.BlockSpec(memory_space=pltpu.VMEM)
+SMEM = pl.BlockSpec(memory_space=pltpu.SMEM)
+BF16 = jnp.bfloat16
+F32 = jnp.float32
+
+
+def params(megabytes):
+    return pltpu.CompilerParams(vmem_limit_bytes=megabytes * 2**20)
+
+
+def cost(flops, moved, exps=0):
+    return pl.CostEstimate(flops=int(flops), bytes_accessed=int(moved), transcendentals=int(exps))
 
 
 def passed_along(value, axis, steps):
@@ -51,7 +68,7 @@
     return (new_top, total, weighted)
 
 
-def local(
+def ring_local(
     hidden, latent, modulation, w_qkv, w_out, q_gain, k_gain, w_head, lengths, guidance, step_size
 ):
     state = hidden[0, 0]
@@ -106,23 +123,343 @@
     return updated[None]
 
 
+def norm_kernel(state_ref, modes_ref, out_ref):
+    wide = state_ref[...].astype(F32)
+    scale = 1.0 + modes_ref[1:2, :]
+    out_ref[...] = (layer_norm(wide) * scale + modes_ref[0:1, :]).astype(BF16)
+
+
+def normalise(state, modes):
+    return pl.pallas_call(
+        norm_kernel,
+        out_shape=jax.ShapeDtypeStruct(state.shape, BF16),
+        in_specs=[VMEM, VMEM],
+        out_specs=VMEM,
+        compiler_params=params(24),
+        cost_estimate=cost(10 * state.size, 4 * state.size),
+    )(state, modes)
+
+
+def place_pair(pair_ref, first_ref, second_ref, side):
+    depth = first_ref.shape[0]
+    pair_ref[pl.ds(pl.multiple_of(side * depth, depth), depth), :] = first_ref[...]
+    pair_ref[pl.ds(pl.multiple_of((1 - side) * depth, depth), depth), :] = second_ref[...]
+
+
+def qkv_kernel(pairs, has_acc, sums, *refs):
+    where_ref = refs[0]
+    norm_refs = refs[1:5]
+    piece_refs = refs[5 : 5 + 2 * pairs]
+    refs = refs[5 + 2 * pairs :]
+    acc_ref = None
+    if has_acc:
+        acc_ref, refs = refs[0], refs[1:]
+    out_ref = refs[0]
+    pair_ref = refs[-1]
+    depth = piece_refs[0].shape[0]
+    side = where_ref[0]
+    for k in range(pairs):
+        place_pair(pair_ref.at[pl.ds(2 * depth * k, 2 * depth)], piece_refs[2 * k], piece_refs[2 * k + 1], side)
+    third = out_ref.shape[2] // 3
+    for block in range(4):
+        total = acc_ref[block] if has_acc else None
+        for k in range(pairs):
+            columns = pl.ds(pl.multiple_of(where_ref[1 + k] * 2 * depth, 2 * depth), 2 * depth)
+            part = jnp.dot(
+                norm_refs[block][:, columns],
+                pair_ref[2 * depth * k : 2 * depth * (k + 1), :],
+                preferred_element_type=F32,
+            )
+            total = part if total is None else total + part
+        out_ref[block] = total
+        if sums:
+            sums_ref = refs[1]
+            ones = jnp.ones((8, third), F32)
+            for j in range(2):
+                part = total[:, j * third : (j + 1) * third]
+                sums_ref[block, 8 * j : 8 * j + 8, :] = lax.dot_general(
+                    ones,
+                    part * part,
+                    (((1,), (1,)), ((), ())),
+                    precision=lax.Precision.HIGHEST,
+                    preferred_element_type=F32,
+                )
+
+
+def qkv_part(where, norms, pieces, acc, sums):
+    rows = norms[0].shape[0]
+    depth, columns = pieces[0].shape
+    pairs = len(pieces) // 2
+    out_shape = [jax.ShapeDtypeStruct((4, rows, columns), F32)]
+    if sums:
+        out_shape.append(jax.ShapeDtypeStruct((4, 16, rows), F32))
+    inputs = [where, *norms, *pieces] + ([] if acc is None else [acc])
+    return pl.pallas_call(
+        functools.partial(qkv_kernel, pairs, acc is not None, sums),
+        out_shape=out_shape,
+        in_specs=[SMEM] + [VMEM] * (len(inputs) - 1),
+        out_specs=[VMEM] * len(out_shape),
+        scratch_shapes=[pltpu.VMEM((2 * depth * pairs, columns), BF16)],
+        compiler_params=params(40),
+        cost_estimate=cost(2 * 4 * rows * 2 * depth * pairs * columns, 4 * rows * columns * 4),
+    )(*inputs)
+
+
+def heads_kernel(length_ref, qkv_ref, sums_ref, q_gain_ref, k_gain_ref, far1_ref, far3_ref, q_ref, k_ref, v_ref):
+    rows = qkv_ref.shape[1]
+    third = qkv_ref.shape[2] // 3
+    width = 4 * third
+    factor = 1.4426950408889634 / DH**0.5
+    row = lax.broadcasted_iota(jnp.int32, (16, DH), 0)
+    pick_q = (row == 0).astype(F32)
+    pick_k = (row == 8).astype(F32)
+
+    def inverse(block, pick):
+        total = lax.dot_general(
+            sums_ref[block],
+            pick,
+            (((0,), (0,)), ((), ())),
+            precision=lax.Precision.HIGHEST,
+            preferred_element_type=F32,
+        )
+        return lax.rsqrt(total * (1.0 / width) + 1e-06)
+
+    for block in range(4):
+        scale_q = inverse(block, pick_q) * factor
+        scale_k = inverse(block, pick_k)
+        for h in range(third // DH):
+            at = slice(h * DH, (h + 1) * DH)
+            q_ref[block, :, at] = (qkv_ref[block, :, at] * scale_q * q_gain_ref[:, at]).astype(BF16)
+            at_k = slice(third + h * DH, third + (h + 1) * DH)
+            k_ref[block, :, at] = (qkv_ref[block, :, at_k] * scale_k * k_gain_ref[:, at]).astype(BF16)
+        v_ref[block] = qkv_ref[block, :, 2 * third :].astype(BF16)
+    attend_block(length_ref, q_ref, k_ref, v_ref, 1, far1_ref)
+    attend_block(length_ref, q_ref, k_ref, v_ref, 3, far3_ref)
+
+
+def attend_block(length_ref, q_ref, k_ref, v_ref, block, out_ref):
+    rows = q_ref.shape[1]
+    first = block - block % 2
+    place = lax.broadcasted_iota(jnp.int32, (1, rows), 1)
+    masks = [place < length_ref[j] for j in range(2)]
+    for h in range(q_ref.shape[2] // DH):
+        at = slice(h * DH, (h + 1) * DH)
+        query = q_ref[block, :, at]
+        scores = []
+        for j in range(2):
+            part = lax.dot_general(
+                query, k_ref[first + j, :, at], (((1,), (1,)), ((), ())), preferred_element_type=F32
+            )
+            scores.append(jnp.where(masks[j], part, -1e30))
+        top = jnp.maximum(
+            jnp.max(scores[0], axis=-1, keepdims=True), jnp.max(scores[1], axis=-1, keepdims=True)
+        )
+        total = 0.0
+        weighted = 0.0
+        for j in range(2):
+            probs = jnp.exp2(scores[j] - top)
+            total += jnp.sum(probs, axis=-1, keepdims=True)
+            weighted += jnp.dot(probs.astype(BF16), v_ref[first + j, :, at], preferred_element_type=F32)
+        out_ref[:, at] = (weighted / total).astype(BF16)
+
+
+def near_kernel(length_ref, q_ref, k_ref, v_ref, near2_ref, near0_ref):
+    attend_block(length_ref, q_ref, k_ref, v_ref, 2, near2_ref)
+    attend_block(length_ref, q_ref, k_ref, v_ref, 0, near0_ref)
+
+
+def attention(lengths, qkv, sums, q_gain, k_gain):
+    rows = qkv.shape[1]
+    third = qkv.shape[2] // 3
+    block = jax.ShapeDtypeStruct((rows, third), BF16)
+    blocks = jax.ShapeDtypeStruct((4, rows, third), BF16)
+    flops = 2 * 2 * rows * 2 * 2 * rows * third
+    far1, far3, q, k, v = pl.pallas_call(
+        heads_kernel,
+        out_shape=[block, block, blocks, blocks, blocks],
+        in_specs=[SMEM] + [VMEM] * 4,
+        out_specs=[VMEM] * 5,
+        compiler_params=params(40),
+        cost_estimate=cost(flops, qkv.size * 6, flops // 512),
+    )(lengths, qkv, sums, q_gain, k_gain)
+    near2, near0 = pl.pallas_call(
+        near_kernel,
+        out_shape=[block, block],
+        in_specs=[SMEM] + [VMEM] * 3,
+        out_specs=[VMEM] * 2,
+        compiler_params=params(40),
+        cost_estimate=cost(flops, qkv.size * 2, flops // 512),
+    )(lengths, q, k, v)
+    return far1, far3, near2, near0
+
+
+def out_kernel(where_ref, state_ref, modes_ref, head_ref, *refs):
+    attended = refs[:4]
+    rest = refs[4:]
+    pieces = rest[:-4]
+    out_ref, group_ref, pair_ref, sum_ref = rest[-4:]
+    side, core, own = where_ref[0], where_ref[1], where_ref[2]
+    for j in range(4):
+        group_ref[j] = attended[j][...]
+    half = len(pieces) // 2
+    columns = pieces[0].shape[1]
+    pairs = half // 2
+    depth = pieces[0].shape[0]
+    for which in range(2):
+        total = None
+        for k in range(pairs):
+            base = which * half + 2 * k
+            place_pair(pair_ref.at[which * pairs + k], pieces[base], pieces[base + 1], side)
+            part = jnp.dot(
+                group_ref[where_ref[3 + k] ^ own],
+                pair_ref[which * pairs + k],
+                preferred_element_type=F32,
+            )
+            total = part if total is None else total + part
+        spot = (core if which == 0 else 1 - core) * columns
+        sum_ref[:, pl.ds(pl.multiple_of(spot, columns), columns)] = total
+    block_out = (state_ref[...].astype(F32) + modes_ref[2:3, :] * sum_ref[...]).astype(BF16)
+    head_in = layer_norm(block_out.astype(F32)) * (1.0 + modes_ref[4:5, :]) + modes_ref[3:4, :]
+    out_ref[...] = jnp.dot(head_in.astype(BF16), head_ref[...], preferred_element_type=F32)
+
+
+def project(where, state, modes, w_head, attended, pieces):
+    rows, width = state.shape
+    depth, columns = pieces[0].shape
+    inputs = [where, state, modes, w_head, *attended, *pieces]
+    return pl.pallas_call(
+        out_kernel,
+        out_shape=jax.ShapeDtypeStruct((rows, w_head.shape[1]), F32),
+        in_specs=[SMEM] + [VMEM] * (len(inputs) - 1),
+        out_specs=VMEM,
+        scratch_shapes=[
+            pltpu.VMEM((4, rows, width // 4), BF16),
+            pltpu.VMEM((len(pieces) // 2, 2 * depth, columns), BF16),
+            pltpu.VMEM((rows, width), F32),
+        ],
+        compiler_params=params(48),
+        cost_estimate=cost(2 * rows * width * width, 2 * width * width),
+    )(*inputs)
+
+
+def updated_latent(velocity, latent, guidance, step_size, length, position):
+    rows = velocity.shape[0]
+    branch = lax.axis_index("cfg")
+    scale = guidance[0]
+    channels = velocity.shape[1] // 2
+    own = lax.dynamic_slice_in_dim(velocity, branch * channels, channels, 1)
+    outgoing = lax.dynamic_slice_in_dim(velocity, (1 - branch) * channels, channels, 1)
+    other = lax.ppermute(outgoing.astype(BF16), "cfg", SWAP).astype(outgoing.dtype)
+    cond = jnp.where(branch == 0, own, other)
+    uncond = jnp.where(branch == 0, other, own)
+    guided = uncond + scale * (cond - uncond)
+    valid = position * rows + jnp.arange(rows, dtype=jnp.int32) < length
+    current = latent[0]
+    updated = jnp.where(valid[:, None], current - step_size[0] * guided, current)
+    return updated[None]
+
+
+def team_local(
+    hidden, latent, modulation, w_qkv, w_out, q_gain, k_gain, w_head, lengths, guidance, step_size
+):
+    state = hidden[0, 0]
+    modes = modulation[0]
+    rows, width = state.shape
+    depth = w_qkv.shape[0]
+    third = width // 4
+    core = lax.axis_index("cfg")
+    position = lax.axis_index("seq")
+    place = lax.axis_index("req")
+    parts = lax.axis_size("req")
+    side, pair = place % 2, place // 2
+    group = 2 * position + core
+    along = [(i, (i - 2) % parts) for i in range(parts)]
+    across = [(i, i ^ 1) for i in range(parts)]
+    steps = parts // 2
+    owners = [(pair + k) % steps for k in range(steps)]
+
+    def gathered(own):
+        mine = [own]
+        for _ in range(steps - 1):
+            mine.append(lax.ppermute(mine[-1], "req", along))
+        theirs = [lax.ppermute(piece, "req", across) for piece in mine]
+        return [piece for both in zip(mine, theirs) for piece in both]
+
+    normed = normalise(state, modes)
+    normed_y = lax.ppermute(normed, "seq", SWAP)
+    normed_c = lax.ppermute(normed, "cfg", SWAP)
+    normed_yc = lax.ppermute(normed_y, "cfg", SWAP)
+    norms = [normed, normed_y, normed_c, normed_yc]
+    columns = jnp.concatenate(
+        [lax.dynamic_slice_in_dim(w_qkv, j * width + group * third, third, 1) for j in range(3)], axis=1
+    )
+    pieces = gathered(columns)
+    half = width // 2
+    out_own = gathered(lax.dynamic_slice_in_dim(w_out, core * half, half, 1))
+    out_other = [lax.ppermute(piece, "cfg", SWAP) for piece in out_own]
+
+    first = jnp.stack([side] + owners[:-1]).astype(jnp.int32)
+    last = jnp.stack([side, owners[-1]]).astype(jnp.int32)
+    (acc,) = qkv_part(first, norms, pieces[:-2], None, False)
+    qkv, sums = qkv_part(last, norms, pieces[-2:], acc, True)
+    theirs = lax.ppermute(sums, "cfg", SWAP)
+    sums = sums + jnp.concatenate([theirs[2:], theirs[:2]])
+    theirs = lax.ppermute(sums, "seq", SWAP)
+    sums = sums + jnp.concatenate([theirs[1:2], theirs[0:1], theirs[3:4], theirs[2:3]])
+    length = lengths[0]
+    limits = jnp.stack([length - position * rows, length - (1 - position) * rows]).astype(jnp.int32)
+    gain_q = lax.dynamic_slice_in_dim(q_gain, group * third, third, 0)[None]
+    gain_k = lax.dynamic_slice_in_dim(k_gain, group * third, third, 0)[None]
+    far1, far3, near2, near0 = attention(limits, qkv, sums, gain_q, gain_k)
+    diagonal = [(i, 3 - i) for i in range(4)]
+    attended = [
+        near0,
+        lax.ppermute(near2, "cfg", SWAP),
+        lax.ppermute(far1, "seq", SWAP),
+        lax.ppermute(far3, ("cfg", "seq"), diagonal),
+    ]
+    where = jnp.stack([side, core, group] + owners).astype(jnp.int32)
+    velocity = project(where, state, modes, w_head, attended, out_own + out_other)
+    return updated_latent(velocity, latent, guidance, step_size, length, position)
+
+
+def by_team(mesh, arguments):
+    hidden, w_qkv = arguments[0], arguments[3]
+    sizes = mesh.shape
+    width = hidden.shape[3]
+    depth = w_qkv.shape[0] // sizes["req"]
+    return (
+        sizes["cfg"] == 2
+        and sizes["seq"] == 2
+        and sizes["req"] % 2 == 0
+        and width % (4 * DH) == 0
+        and 2 * depth == width // 4
+        and depth % 16 == 0
+        and hidden.shape[2] // sizes["seq"] % 16 == 0
+    )
+
+
 def solution(mesh):
-    return jax.shard_map(
-        local,
-        mesh=mesh,
-        in_specs=(
-            P("cfg", "req", "seq", None),
-            P("req", "seq", "cfg"),
-            P("req", None, None),
-            P("req", None),
-            P("req", None),
-            P(),
-            P(),
-            P(),
-            P("req"),
-            P("req"),
-            P("req"),
-        ),
-        out_specs=P("req", "seq", "cfg"),
-        check_vma=False,
-    )
+    def whole(*arguments):
+        body = team_local if by_team(mesh, arguments) else ring_local
+        return jax.shard_map(
+            body,
+            mesh=mesh,
+            in_specs=(
+                P("cfg", "req", "seq", None),
+                P("req", "seq", "cfg"),
+                P("req", None, None),
+                P("req", None),
+                P("req", None),
+                P(),
+                P(),
+                P(),
+                P("req"),
+                P("req"),
+                P("req"),
+            ),
+            out_specs=P("req", "seq", "cfg"),
+            check_vma=False,
+        )(*arguments)
+
+    return whole

time: 302 us -> 156 us (0.52)
  waiting for transfers between devices: 246 us -> 57.3 us
  starting transfers between devices: 1.59 us -> 41.6 us
  Pallas kernels: 0 us -> 30.4 us
  matrix products: 24.5 us -> 0 us
  local copies, waits for them, and re-layouts: 6.14 us -> 22.2 us
  between operations: 15.6 us -> 2.15 us
  other arithmetic: 8.06 us -> 2.12 us
    all_gather x2 -> x0, waiting for transfers between devices: 209 us -> none  [the longest x1 199 us: local(): qkv = add_rows(normed, lax.all_gather(w_qkv, 'req', axis=0, tiled=True))]
    ppermute x2 -> x31, starting transfers between devices: 1.54 us -> 41.6 us  [the longest x6 23.3 us: gathered(): mine.append(lax.ppermute(mine[-1], 'req', along))]
    pallas_call x0 -> x6, Pallas kernels: none -> 30.4 us  [the longest x2 15 us: qkv_part(): pl.pallas_call(functools.partial(qkv_kernel, pairs, acc is not None, sums...]
    dot_general x7 -> x0, matrix products: 24.5 us -> none  [the longest x2 11.9 us: add_rows(): return jnp.dot(left, piece, preferred_element_type=jnp.float32)]
    ppermute x2 -> x31, waiting for transfers between devices: 35.9 us -> 57.3 us  [the longest x6 27.9 us: gathered(): mine.append(lax.ppermute(mine[-1], 'req', along))]
    unnamed x20 -> x37, local copies, waits for them, and re-layouts: 2.05 us -> 18.6 us
    reduce_sum x6 -> x0, other arithmetic: 4.2 us -> none  [the longest x2 2.94 us: attend(): total = total * factor + jnp.sum(probs, axis=-1)]
  transfers between devices with their start and end apart: 4 -> 31, of which waited for: 3 -> 11; matrix products, arithmetic and copies ran while one was open for 10% -> 4% of each run, Pallas kernels for 0% -> 16%
where the time goes in v1:
time: 156 us
  waiting for transfers between devices  57.3 us (37%)
  starting transfers between devices  41.6 us (27%)
  Pallas kernels  30.4 us (19%)
  local copies, waits for them, and re-layouts  22.2 us (14%)
  between operations  2.15 us (1%)
  other arithmetic  2.12 us (1%)
    ppermute x6, waiting for transfers between devices, gathered(): mine.append(lax.ppermute(mine[-1], 'req', along))  27.9 us
    ppermute x6, starting transfers between devices, gathered(): mine.append(lax.ppermute(mine[-1], 'req', along))  23.3 us
    ppermute x8, waiting for transfers between devices, gathered(): theirs = [lax.ppermute(piece, 'req', across) for piece in mine]  21.2 us
    unnamed x37, local copies, waits for them, and re-layouts  18.6 us
    pallas_call x2, Pallas kernels, qkv_part(): pl.pallas_call(functools.partial(qkv_kernel, pairs, acc is not None, sums...  15 us
    ppermute x8, starting transfers between devices, gathered(): theirs = [lax.ppermute(piece, 'req', across) for piece in mine]  10.1 us
    pallas_call x1, Pallas kernels, project(): pl.pallas_call(out_kernel, out_shape=jax.ShapeDtypeStruct((rows, w_head.s...  5.56 us
    pallas_call x1, Pallas kernels, attention(): pl.pallas_call(heads_kernel, out_shape=[block, block, blocks, blocks, blo...  5.29 us
  transfers between devices with their start and end apart: 31, of which 11 were waited for; matrix products, arithmetic and copies ran while one was open for 4% of the time, Pallas kernels for 16%

profile of v1, /device:TPU:0, one launch (start us, length us, event | category | flops | bytes accessed | tf_op | source)
XLA Modules:
  0.0 155.7 jit_solution(4821121563002439332)
XLA Ops:
  0.0 0.8 copy.17
  0.8 1.2 copy-done.4
  2.0 0.7 shard_map.109.refs_1_
  2.7 3.0 %collective-permute-start = (bf16[288,1536]{1,0:T(8,128)(2,1)S(1)}, bf16[288,1536]{1,0:T(8,128)(2,1)S(1)}, u32[]{:S(2)}, u32[]{:S(2)}) collective-permute-start(bf16[288,1536]{1,0:T(8,128)(2,1)S(1)} %shard_map.109.refs_1_), channel_id=1, source_target_pairs={{0,1},{1,0},{2,3},{3,2},{4,5},{5,4},{6,7},{7,6},{8,9},{9,8},{10,11... | collective-permute-start | bytes 2654216 | tf_op jit(solution)/shard_map/ppermute | solution.py:389
  5.7 1.1 constant_dynamic-slice_fusion.3
  6.8 0.8 pad_maximum_fusion.refs_5_
  7.7 3.6 %collective-permute-start.3 = (bf16[192,1152]{1,0:T(8,128)(2,1)}, bf16[192,1152]{1,0:T(8,128)(2,1)}, u32[]{:S(2)}, u32[]{:S(2)}) collective-permute-start(bf16[192,1152]{1,0:T(8,128)(2,1)} %pad_maximum_fusion.refs_5_), channel_id=1, source_target_pairs={{0,12},{2,14},{4,0},{6,2},{8,4},{10,6},{12,8},{14,10},{1,13},{3,15... | collective-permute-start | bytes 1327112 | tf_op jit(solution)/shard_map/ppermute | solution.py:384
  11.3 9.5 %collective-permute-done.3.refs_7_ = bf16[192,1152]{1,0:T(8,128)(2,1)} collective-permute-done((bf16[192,1152]{1,0:T(8,128)(2,1)}, bf16[192,1152]{1,0:T(8,128)(2,1)}, u32[]{:S(2)}, u32[]{:S(2)}) %collective-permute-start.3) | collective-permute-done | bytes 442400 | tf_op jit(solution)/shard_map/ppermute | solution.py:384
  20.7 4.3 %collective-permute-start.4 = (bf16[192,1152]{1,0:T(8,128)(2,1)}, bf16[192,1152]{1,0:T(8,128)(2,1)}, u32[]{:S(2)}, u32[]{:S(2)}) collective-permute-start(bf16[192,1152]{1,0:T(8,128)(2,1)} %collective-permute-done.3.refs_7_), channel_id=1, source_target_pairs={{0,12},{2,14},{4,0},{6,2},{8,4},{10,6},{12,8},{14,10},{1,13},{3,15... | collective-permute-start | bytes 1327112 | tf_op jit(solution)/shard_map/ppermute | solution.py:384
  25.0 1.5 collective-permute-start.7
  26.5 0.2 collective-permute-start.2
  26.8 2.5 %collective-permute-start.16 = (bf16[192,768]{1,0:T(8,128)(2,1)S(1)}, bf16[192,768]{1,0:T(8,128)(2,1)S(1)}, u32[]{:S(2)}, u32[]{:S(2)}) collective-permute-start(bf16[192,768]{1,0:T(8,128)(2,1)S(1)} %constant_dynamic-slice_fusion.refs_4_), channel_id=1, source_target_pairs={{0,12},{2,14},{4,0},{6,2},{8,4},{10,6},{12,8},{14,10},{1,13},{3,15... | collective-permute-start | bytes 884744 | tf_op jit(solution)/shard_map/ppermute | solution.py:384
  29.3 6.6 %collective-permute-done.4.refs_9_ = bf16[192,1152]{1,0:T(8,128)(2,1)} collective-permute-done((bf16[192,1152]{1,0:T(8,128)(2,1)}, bf16[192,1152]{1,0:T(8,128)(2,1)}, u32[]{:S(2)}, u32[]{:S(2)}) %collective-permute-start.4) | collective-permute-done | bytes 442400 | tf_op jit(solution)/shard_map/ppermute | solution.py:384
  35.9 4.3 %collective-permute-start.5 = (bf16[192,1152]{1,0:T(8,128)(2,1)}, bf16[192,1152]{1,0:T(8,128)(2,1)}, u32[]{:S(2)}, u32[]{:S(2)}) collective-permute-start(bf16[192,1152]{1,0:T(8,128)(2,1)} %collective-permute-done.4.refs_9_), channel_id=1, source_target_pairs={{0,12},{2,14},{4,0},{6,2},{8,4},{10,6},{12,8},{14,10},{1,13},{3,15... | collective-permute-start | bytes 1327112 | tf_op jit(solution)/shard_map/ppermute | solution.py:384
  40.2 1.9 %collective-permute-done.16.refs_6_ = bf16[192,768]{1,0:T(8,128)(2,1)S(1)} collective-permute-done((bf16[192,768]{1,0:T(8,128)(2,1)S(1)}, bf16[192,768]{1,0:T(8,128)(2,1)S(1)}, u32[]{:S(2)}, u32[]{:S(2)}) %collective-permute-start.16) | collective-permute-done | bytes 294944 | tf_op jit(solution)/shard_map/ppermute | solution.py:384
  42.2 0.7 copy-done.7
  42.9 1.5 collective-permute-start.8
  44.4 0.5 collective-permute-start.9
  44.9 4.5 %collective-permute-done.5.refs_5_ = bf16[192,1152]{1,0:T(8,128)(2,1)} collective-permute-done((bf16[192,1152]{1,0:T(8,128)(2,1)}, bf16[192,1152]{1,0:T(8,128)(2,1)}, u32[]{:S(2)}, u32[]{:S(2)}) %collective-permute-start.5) | collective-permute-done | bytes 442400 | tf_op jit(solution)/shard_map/ppermute | solution.py:384
  49.4 1.5 collective-permute-start.6
  51.0 5.3 %collective-permute-done.8.refs_8_ = bf16[192,1152]{1,0:T(8,128)(2,1)} collective-permute-done((bf16[192,1152]{1,0:T(8,128)(2,1)}, bf16[192,1152]{1,0:T(8,128)(2,1)}, u32[]{:S(2)}, u32[]{:S(2)}) %collective-permute-start.8) | collective-permute-done | bytes 442400 | tf_op jit(solution)/shard_map/ppermute | solution.py:385
  56.3 1.5 collective-permute-start.15
  57.8 4.3 %collective-permute-start.18 = (bf16[192,768]{1,0:T(8,128)(2,1)}, bf16[192,768]{1,0:T(8,128)(2,1)}, u32[]{:S(2)}, u32[]{:S(2)}) collective-permute-start(bf16[192,768]{1,0:T(8,128)(2,1)} %copy-done.7), channel_id=1, source_target_pairs={{0,12},{2,14},{4,0},{6,2},{8,4},{10,6},{12,8},{14,10},{1,13},{3,15... | collective-permute-start | bytes 884744 | tf_op jit(solution)/shard_map/ppermute | solution.py:384
  62.1 3.7 %collective-permute-done.9.refs_10_ = bf16[192,1152]{1,0:T(8,128)(2,1)} collective-permute-done((bf16[192,1152]{1,0:T(8,128)(2,1)}, bf16[192,1152]{1,0:T(8,128)(2,1)}, u32[]{:S(2)}, u32[]{:S(2)}) %collective-permute-start.9) | collective-permute-done | bytes 442400 | tf_op jit(solution)/shard_map/ppermute | solution.py:385
  65.8 6.7 %shard_map.110.refs_7_ = f32[4,288,1152]{2,1,0:T(8,128)S(1)} custom-call(s32[4]{0:T(128)S(1)} %pad_add_fusion.2.refs_0_, bf16[288,1536]{1,0:T(8,128)(2,1)S(1)} %shard_map.109.refs_1_, bf16[288,1536]{1,0:T(8,128)(2,1)S(1)} %collective-permute-done.refs_2_, bf16[288,1536]{1,0:T(8,128)(2,1)S(1)} %collective-permute-done.1.refs_3_, ...), custom_call_target="tpu_custom_call" | custom-call | flops 3057647616 | bytes 5308416 | tf_op jit(solution)/shard_map/pallas_call | solution.py:197
  72.5 2.3 %copy-done.1 = f32[4,288,1152]{2,1,0:T(8,128)} copy-done((f32[4,288,1152]{2,1,0:T(8,128)}, f32[4,288,1152]{2,1,0:T(8,128)S(1)}, u32[]{:S(2)}) %copy-start.1) | copy-done | bytes 5308440
  74.8 8.3 %shard_map.111 = (f32[4,288,1152]{2,1,0:T(8,128)S(1)}, f32[4,16,288]{2,1,0:T(8,128)}) custom-call(s32[2]{0:T(128)S(1)} %pad_add_fusion.1.refs_0_, bf16[288,1536]{1,0:T(8,128)(2,1)S(1)} %shard_map.109.refs_1_, bf16[288,1536]{1,0:T(8,128)(2,1)S(1)} %collective-permute-done.refs_2_, bf16[288,1536]{1,0:T(8,128)(2,1)S(1)} %collective-permute-done.1.refs_3_, ...), custom_call_target="tpu_custom_call" | custom-call | flops 1019215872 | bytes 5308416 | tf_op jit(solution)/shard_map/pallas_call | solution.py:197
  83.1 2.3 %copy-done.2 = f32[4,288,1152]{2,1,0:T(8,128)} copy-done((f32[4,288,1152]{2,1,0:T(8,128)}, f32[4,288,1152]{2,1,0:T(8,128)S(1)}, u32[]{:S(2)}) %copy-start.2) | copy-done | bytes 5308440
  85.5 0.5 collective-permute-start.22
  86.0 0.8 dynamic_slice.27
  86.8 0.8 dynamic_slice.28
  88.2 1.6 %collective-permute-start.17 = (bf16[192,768]{1,0:T(8,128)(2,1)}, bf16[192,768]{1,0:T(8,128)(2,1)S(1)}, u32[]{:S(2)}, u32[]{:S(2)}) collective-permute-start(bf16[192,768]{1,0:T(8,128)(2,1)} %copy-done.7), channel_id=1, source_target_pairs={{0,2},{2,0},{4,6},{6,4},{8,10},{10,8},{12,14},{14,12},{1,3},{3,1},... | collective-permute-start | bytes 884744 | tf_op jit(solution)/shard_map/ppermute | solution.py:385
  89.8 0.5 collective-permute-start.23
  90.3 4.3 %collective-permute-start.20 = (bf16[192,768]{1,0:T(8,128)(2,1)}, bf16[192,768]{1,0:T(8,128)(2,1)S(1)}, u32[]{:S(2)}, u32[]{:S(2)}) collective-permute-start(bf16[192,768]{1,0:T(8,128)(2,1)} %collective-permute-done.18.refs_8_), channel_id=1, source_target_pairs={{0,12},{2,14},{4,0},{6,2},{8,4},{10,6},{12,8},{14,10},{1,13},{3,15... | collective-permute-start | bytes 884744 | tf_op jit(solution)/shard_map/ppermute | solution.py:384
  94.6 0.9 maximum_add_fusion
  95.5 0.6 collective-permute-start.11
  96.2 5.4 %collective-permute-done.20.refs_10_ = bf16[192,768]{1,0:T(8,128)(2,1)S(1)} collective-permute-done((bf16[192,768]{1,0:T(8,128)(2,1)}, bf16[192,768]{1,0:T(8,128)(2,1)S(1)}, u32[]{:S(2)}, u32[]{:S(2)}) %collective-permute-start.20) | collective-permute-done | bytes 294944 | tf_op jit(solution)/shard_map/ppermute | solution.py:384
  101.6 0.5 collective-permute-start.19
  102.1 1.5 collective-permute-start.21
  103.7 0.5 collective-permute-start.25
  104.3 7.4 %collective-permute-done.19.refs_9_ = bf16[192,768]{1,0:T(8,128)(2,1)S(1)} collective-permute-done((bf16[192,768]{1,0:T(8,128)(2,1)}, bf16[192,768]{1,0:T(8,128)(2,1)S(1)}, u32[]{:S(2)}, u32[]{:S(2)}) %collective-permute-start.19) | collective-permute-done | bytes 294944 | tf_op jit(solution)/shard_map/ppermute | solution.py:385
  111.8 4.8 %collective-permute-done.21.refs_11_ = bf16[192,768]{1,0:T(8,128)(2,1)} collective-permute-done((bf16[192,768]{1,0:T(8,128)(2,1)S(1)}, bf16[192,768]{1,0:T(8,128)(2,1)}, u32[]{:S(2)}, u32[]{:S(2)}) %collective-permute-start.21) | collective-permute-done | bytes 294944 | tf_op jit(solution)/shard_map/ppermute | solution.py:385
  116.6 2.5 %copy-done.3 = f32[4,288,1152]{2,1,0:T(8,128)S(1)} copy-done((f32[4,288,1152]{2,1,0:T(8,128)S(1)}, f32[4,288,1152]{2,1,0:T(8,128)}, u32[]{:S(2)}) %copy-start.3) | copy-done | bytes 5308440
  119.1 5.3 %shard_map.112 = (bf16[288,384]{1,0:T(8,128)(2,1)}, bf16[288,384]{1,0:T(8,128)(2,1)}, bf16[4,288,384]{2,1,0:T(8,128)(2,1)S(1)}, bf16[4,288,384]{2,1,0:T(8,128)(2,1)S(1)}, bf16[4,288,384]{2,1,0:T(8,128)(2,1)S(1)}) custom-call(s32[2]{0:T(128)S(1)} %pad_add_fusion.length_ref, f32[4,288,1152]{2,1,0:T(8,128)S(1)} %copy-done.3, ...), custom_call_target="tpu_custom_call" | custom-call | flops 509607936 | bytes 7962624 | tf_op jit(solution)/shard_map/pallas_call | solution.py:277
  124.4 3.8 %shard_map.113 = (bf16[288,384]{1,0:T(8,128)(2,1)}, bf16[288,384]{1,0:T(8,128)(2,1)S(1)}) custom-call(s32[2]{0:T(128)S(1)} %pad_add_fusion.length_ref, bf16[4,288,384]{2,1,0:T(8,128)(2,1)S(1)} %get-tuple-element.16.q_ref, bf16[4,288,384]{2,1,0:T(8,128)(2,1)S(1)} %get-tuple-element.17.k_ref, bf16[4,288,384]{2,1,0:T(8,128)(2,1)S(1)} %get-tuple-element.18.v_ref), custom_call_target="tpu_custom_call" | custom-call | flops 509607936 | bytes 2654208 | tf_op jit(solution)/shard_map/pallas_call | solution.py:285
  128.2 0.7 copy-done.15
  128.9 0.7 copy-done.9
  129.6 0.5 collective-permute-start.12
  130.1 0.7 copy-done.11
  130.8 0.5 collective-permute-start.13
  131.3 0.7 copy-done.13
  132.0 0.9 collective-permute-start.14
  132.9 1.1 copy.13.head_ref
  134.2 5.3 %collective-permute-done.13.refs_2_ = bf16[288,384]{1,0:T(8,128)(2,1)} collective-permute-done((bf16[288,384]{1,0:T(8,128)(2,1)}, bf16[288,384]{1,0:T(8,128)(2,1)}, u32[]{:S(2)}, u32[]{:S(2)}) %collective-permute-start.13) | collective-permute-done | bytes 221216 | tf_op jit(solution)/shard_map/ppermute | solution.py:418
  139.4 2.8 %collective-permute-done.14.refs_3_ = bf16[288,384]{1,0:T(8,128)(2,1)} collective-permute-done((bf16[288,384]{1,0:T(8,128)(2,1)}, bf16[288,384]{1,0:T(8,128)(2,1)}, u32[]{:S(2)}, u32[]{:S(2)}) %collective-permute-start.14) | collective-permute-done | bytes 221216 | tf_op jit(solution)/shard_map/ppermute | solution.py:419
  142.3 1.0 copy-done.10
  143.2 1.0 copy-done.12
  144.2 1.0 copy-done.14
  145.2 0.9 copy-done.16
  146.1 5.6 %shard_map.114 = f32[288,64]{1,0:T(8,128)S(1)} custom-call(s32[7]{0:T(128)S(1)} %stack.52.where_ref, bf16[288,1536]{1,0:T(8,128)(2,1)} %bitcast.25, f32[5,1536]{1,0:T(8,128)S(1)} %bitcast.28, bf16[1536,64]{1,0:T(8,128)(2,1)S(1)} %copy.13.head_ref, bf16[288,384]{1,0:T(8,128)(2,1)S(1)} %copy-done.16, bf16[288,384]{1,0:T(8,128)(2,1)} %collective-permute-done.12.refs_1_, ...), custom_call_target="tpu_custom_call" | custom-call | flops 1358954496 | bytes 4718592 | tf_op jit(solution)/shard_map/pallas_call | solution.py:330
  151.8 0.9 collective-permute-start.30
  152.6 0.9 copy.12
  154.9 0.1 fusion.4
  155.0 0.7 copy.14
  (60 shorter events, 0.7 us)
Async XLA Ops:
  0.0 26.7 %copy-start = (bf16[192,1536]{1,0:T(8,128)(2,1)S(1)}, bf16[192,1536]{1,0:T(8,128)(2,1)}, u32[]{:S(2)}) copy-start(bf16[192,1536]{1,0:T(8,128)(2,1)} %param.15) | copy-start | bytes 1769476
  0.8 1.9 %copy-start.5 = (f32[1,5,1536]{2,1,0:T(8,128)}, f32[1,5,1536]{2,1,0:T(8,128)S(1)}, u32[]{:S(2)}) copy-start(f32[1,5,1536]{2,1,0:T(8,128)S(1)} %copy.17) | copy-start | bytes 92164
  0.8 1.2 copy-start.4
  2.7 23.8 %collective-permute-start = (bf16[288,1536]{1,0:T(8,128)(2,1)S(1)}, bf16[288,1536]{1,0:T(8,128)(2,1)S(1)}, u32[]{:S(2)}, u32[]{:S(2)}) collective-permute-start(bf16[288,1536]{1,0:T(8,128)(2,1)S(1)} %shard_map.109.refs_1_), channel_id=1, source_target_pairs={{0,1},{1,0},{2,3},{3,2},{4,5},{5,4},{6,7},{7,6},{8,9},{9,8},{10,11... | collective-permute-start | bytes 2654216 | tf_op jit(solution)/shard_map/ppermute | solution.py:389
  7.7 13.1 %collective-permute-start.3 = (bf16[192,1152]{1,0:T(8,128)(2,1)}, bf16[192,1152]{1,0:T(8,128)(2,1)}, u32[]{:S(2)}, u32[]{:S(2)}) collective-permute-start(bf16[192,1152]{1,0:T(8,128)(2,1)} %pad_maximum_fusion.refs_5_), channel_id=1, source_target_pairs={{0,12},{2,14},{4,0},{6,2},{8,4},{10,6},{12,8},{14,10},{1,13},{3,15... | collective-permute-start | bytes 1327112 | tf_op jit(solution)/shard_map/ppermute | solution.py:384
  20.7 15.2 %collective-permute-start.4 = (bf16[192,1152]{1,0:T(8,128)(2,1)}, bf16[192,1152]{1,0:T(8,128)(2,1)}, u32[]{:S(2)}, u32[]{:S(2)}) collective-permute-start(bf16[192,1152]{1,0:T(8,128)(2,1)} %collective-permute-done.3.refs_7_), channel_id=1, source_target_pairs={{0,12},{2,14},{4,0},{6,2},{8,4},{10,6},{12,8},{14,10},{1,13},{3,15... | collective-permute-start | bytes 1327112 | tf_op jit(solution)/shard_map/ppermute | solution.py:384
  25.0 32.8 %collective-permute-start.1 = (bf16[288,1536]{1,0:T(8,128)(2,1)S(1)}, bf16[288,1536]{1,0:T(8,128)(2,1)S(1)}, u32[]{:S(2)}, u32[]{:S(2)}) collective-permute-start(bf16[288,1536]{1,0:T(8,128)(2,1)S(1)} %shard_map.109.refs_1_), channel_id=1, source_target_pairs={{0,16},{16,0},{1,17},{17,1},{2,18},{18,2},{3,19},{19,3},{4,20},{20... | collective-permute-start | bytes 2654216 | tf_op jit(solution)/shard_map/ppermute | solution.py:390
  25.0 19.4 %collective-permute-start.7 = (bf16[192,1152]{1,0:T(8,128)(2,1)}, bf16[192,1152]{1,0:T(8,128)(2,1)}, u32[]{:S(2)}, u32[]{:S(2)}) collective-permute-start(bf16[192,1152]{1,0:T(8,128)(2,1)} %pad_maximum_fusion.refs_5_), channel_id=1, source_target_pairs={{0,2},{2,0},{4,6},{6,4},{8,10},{10,8},{12,14},{14,12},{1,3},{3,1},... | collective-permute-start | bytes 1327112 | tf_op jit(solution)/shard_map/ppermute | solution.py:385
  26.5 39.3 %collective-permute-start.2 = (bf16[288,1536]{1,0:T(8,128)(2,1)S(1)}, bf16[288,1536]{1,0:T(8,128)(2,1)}, u32[]{:S(2)}, u32[]{:S(2)}) collective-permute-start(bf16[288,1536]{1,0:T(8,128)(2,1)S(1)} %collective-permute-done.refs_2_), channel_id=1, source_target_pairs={{0,16},{16,0},{1,17},{17,1},{2,18},{18,2},{3,19},{19,3},{4,20},{20... | collective-permute-start | bytes 2654216 | tf_op jit(solution)/shard_map/ppermute | solution.py:391
  26.8 15.4 %collective-permute-start.16 = (bf16[192,768]{1,0:T(8,128)(2,1)S(1)}, bf16[192,768]{1,0:T(8,128)(2,1)S(1)}, u32[]{:S(2)}, u32[]{:S(2)}) collective-permute-start(bf16[192,768]{1,0:T(8,128)(2,1)S(1)} %constant_dynamic-slice_fusion.refs_4_), channel_id=1, source_target_pairs={{0,12},{2,14},{4,0},{6,2},{8,4},{10,6},{12,8},{14,10},{1,13},{3,15... | collective-permute-start | bytes 884744 | tf_op jit(solution)/shard_map/ppermute | solution.py:384
  35.9 13.4 %collective-permute-start.5 = (bf16[192,1152]{1,0:T(8,128)(2,1)}, bf16[192,1152]{1,0:T(8,128)(2,1)}, u32[]{:S(2)}, u32[]{:S(2)}) collective-permute-start(bf16[192,1152]{1,0:T(8,128)(2,1)} %collective-permute-done.4.refs_9_), channel_id=1, source_target_pairs={{0,12},{2,14},{4,0},{6,2},{8,4},{10,6},{12,8},{14,10},{1,13},{3,15... | collective-permute-start | bytes 1327112 | tf_op jit(solution)/shard_map/ppermute | solution.py:384
  42.2 0.7 copy-start.7
  42.9 13.4 %collective-permute-start.8 = (bf16[192,1152]{1,0:T(8,128)(2,1)}, bf16[192,1152]{1,0:T(8,128)(2,1)}, u32[]{:S(2)}, u32[]{:S(2)}) collective-permute-start(bf16[192,1152]{1,0:T(8,128)(2,1)} %collective-permute-done.3.refs_7_), channel_id=1, source_target_pairs={{0,2},{2,0},{4,6},{6,4},{8,10},{10,8},{12,14},{14,12},{1,3},{3,1},... | collective-permute-start | bytes 1327112 | tf_op jit(solution)/shard_map/ppermute | solution.py:385
  44.4 21.4 %collective-permute-start.9 = (bf16[192,1152]{1,0:T(8,128)(2,1)}, bf16[192,1152]{1,0:T(8,128)(2,1)}, u32[]{:S(2)}, u32[]{:S(2)}) collective-permute-start(bf16[192,1152]{1,0:T(8,128)(2,1)} %collective-permute-done.4.refs_9_), channel_id=1, source_target_pairs={{0,2},{2,0},{4,6},{6,4},{8,10},{10,8},{12,14},{14,12},{1,3},{3,1},... | collective-permute-start | bytes 1327112 | tf_op jit(solution)/shard_map/ppermute | solution.py:385
  49.4 25.5 %collective-permute-start.6 = (bf16[192,1152]{1,0:T(8,128)(2,1)}, bf16[192,1152]{1,0:T(8,128)(2,1)}, u32[]{:S(2)}, u32[]{:S(2)}) collective-permute-start(bf16[192,1152]{1,0:T(8,128)(2,1)} %collective-permute-done.5.refs_5_), channel_id=1, source_target_pairs={{0,2},{2,0},{4,6},{6,4},{8,10},{10,8},{12,14},{14,12},{1,3},{3,1},... | collective-permute-start | bytes 1327112 | tf_op jit(solution)/shard_map/ppermute | solution.py:385
  56.3 33.5 %collective-permute-start.15 = (bf16[192,768]{1,0:T(8,128)(2,1)S(1)}, bf16[192,768]{1,0:T(8,128)(2,1)}, u32[]{:S(2)}, u32[]{:S(2)}) collective-permute-start(bf16[192,768]{1,0:T(8,128)(2,1)S(1)} %constant_dynamic-slice_fusion.refs_4_), channel_id=1, source_target_pairs={{0,2},{2,0},{4,6},{6,4},{8,10},{10,8},{12,14},{14,12},{1,3},{3,1},... | collective-permute-start | bytes 884744 | tf_op jit(solution)/shard_map/ppermute | solution.py:385
  57.8 32.0 %collective-permute-start.18 = (bf16[192,768]{1,0:T(8,128)(2,1)}, bf16[192,768]{1,0:T(8,128)(2,1)}, u32[]{:S(2)}, u32[]{:S(2)}) collective-permute-start(bf16[192,768]{1,0:T(8,128)(2,1)} %copy-done.7), channel_id=1, source_target_pairs={{0,12},{2,14},{4,0},{6,2},{8,4},{10,6},{12,8},{14,10},{1,13},{3,15... | collective-permute-start | bytes 884744 | tf_op jit(solution)/shard_map/ppermute | solution.py:384
  72.5 2.3 %copy-start.1 = (f32[4,288,1152]{2,1,0:T(8,128)}, f32[4,288,1152]{2,1,0:T(8,128)S(1)}, u32[]{:S(2)}) copy-start(f32[4,288,1152]{2,1,0:T(8,128)S(1)} %shard_map.110.refs_7_) | copy-start | bytes 15925252
  83.1 2.3 %copy-start.2 = (f32[4,288,1152]{2,1,0:T(8,128)}, f32[4,288,1152]{2,1,0:T(8,128)S(1)}, u32[]{:S(2)}) copy-start(f32[4,288,1152]{2,1,0:T(8,128)S(1)} %get-tuple-element.14.qkv_ref) | copy-start | bytes 15925252
  85.5 56.8 %copy-start.6 = (f32[1,5,1536]{2,1,0:T(8,128)S(1)}, f32[1,5,1536]{2,1,0:T(8,128)}, u32[]{:S(2)}) copy-start(f32[1,5,1536]{2,1,0:T(8,128)} %copy-done.5) | copy-start | bytes 92164
  85.5 56.8 %copy-start.8 = (bf16[192,768]{1,0:T(8,128)(2,1)S(1)}, bf16[192,768]{1,0:T(8,128)(2,1)}, u32[]{:S(2)}) copy-start(bf16[192,768]{1,0:T(8,128)(2,1)} %copy-done.7) | copy-start | bytes 884740
  85.5 4.8 %collective-permute-start.10 = (f32[4,16,288]{2,1,0:T(8,128)}, f32[4,16,288]{2,1,0:T(8,128)S(1)}, u32[]{:S(2)}, u32[]{:S(2)}) collective-permute-start(f32[4,16,288]{2,1,0:T(8,128)} %get-tuple-element.15), channel_id=1, source_target_pairs={{0,16},{16,0},{1,17},{17,1},{2,18},{18,2},{3,19},{19,3},{4,20},{20... | collective-permute-start | bytes 221192 | tf_op jit(solution)/shard_map/ppermute | solution.py:405
  85.5 10.0 %collective-permute-start.22 = (bf16[192,768]{1,0:T(8,128)(2,1)S(1)}, bf16[192,768]{1,0:T(8,128)(2,1)S(1)}, u32[]{:S(2)}, u32[]{:S(2)}) collective-permute-start(bf16[192,768]{1,0:T(8,128)(2,1)S(1)} %constant_dynamic-slice_fusion.refs_4_), channel_id=1, source_target_pairs={{0,16},{16,0},{1,17},{17,1},{2,18},{18,2},{3,19},{19,3},{4,20},{20... | collective-permute-start | bytes 884744 | tf_op jit(solution)/shard_map/ppermute | solution.py:399
  88.2 15.4 %collective-permute-start.17 = (bf16[192,768]{1,0:T(8,128)(2,1)}, bf16[192,768]{1,0:T(8,128)(2,1)S(1)}, u32[]{:S(2)}, u32[]{:S(2)}) collective-permute-start(bf16[192,768]{1,0:T(8,128)(2,1)} %copy-done.7), channel_id=1, source_target_pairs={{0,2},{2,0},{4,6},{6,4},{8,10},{10,8},{12,14},{14,12},{1,3},{3,1},... | collective-permute-start | bytes 884744 | tf_op jit(solution)/shard_map/ppermute | solution.py:385
  89.8 13.9 %collective-permute-start.24 = (bf16[192,768]{1,0:T(8,128)(2,1)}, bf16[192,768]{1,0:T(8,128)(2,1)S(1)}, u32[]{:S(2)}, u32[]{:S(2)}) collective-permute-start(bf16[192,768]{1,0:T(8,128)(2,1)} %copy-done.7), channel_id=1, source_target_pairs={{0,16},{16,0},{1,17},{17,1},{2,18},{18,2},{3,19},{19,3},{4,20},{20... | collective-permute-start | bytes 884744 | tf_op jit(solution)/shard_map/ppermute | solution.py:399
  89.8 14.4 %collective-permute-start.23 = (bf16[192,768]{1,0:T(8,128)(2,1)}, bf16[192,768]{1,0:T(8,128)(2,1)S(1)}, u32[]{:S(2)}, u32[]{:S(2)}) collective-permute-start(bf16[192,768]{1,0:T(8,128)(2,1)} %collective-permute-done.15.refs_5_), channel_id=1, source_target_pairs={{0,16},{16,0},{1,17},{17,1},{2,18},{18,2},{3,19},{19,3},{4,20},{20... | collective-permute-start | bytes 884744 | tf_op jit(solution)/shard_map/ppermute | solution.py:399
  90.3 11.3 %collective-permute-start.20 = (bf16[192,768]{1,0:T(8,128)(2,1)}, bf16[192,768]{1,0:T(8,128)(2,1)S(1)}, u32[]{:S(2)}, u32[]{:S(2)}) collective-permute-start(bf16[192,768]{1,0:T(8,128)(2,1)} %collective-permute-done.18.refs_8_), channel_id=1, source_target_pairs={{0,12},{2,14},{4,0},{6,2},{8,4},{10,6},{12,8},{14,10},{1,13},{3,15... | collective-permute-start | bytes 884744 | tf_op jit(solution)/shard_map/ppermute | solution.py:384
  95.5 6.6 %collective-permute-start.11 = (f32[4,16,288]{2,1,0:T(8,128)S(1)}, f32[4,16,288]{2,1,0:T(8,128)S(1)}, u32[]{:S(2)}, u32[]{:S(2)}) collective-permute-start(f32[4,16,288]{2,1,0:T(8,128)S(1)} %maximum_add_fusion), channel_id=1, source_target_pairs={{0,1},{1,0},{2,3},{3,2},{4,5},{5,4},{6,7},{7,6},{8,9},{9,8},{10,11... | collective-permute-start | bytes 221192 | tf_op jit(solution)/shard_map/ppermute | solution.py:407
  101.6 10.2 %collective-permute-start.19 = (bf16[192,768]{1,0:T(8,128)(2,1)}, bf16[192,768]{1,0:T(8,128)(2,1)S(1)}, u32[]{:S(2)}, u32[]{:S(2)}) collective-permute-start(bf16[192,768]{1,0:T(8,128)(2,1)} %collective-permute-done.18.refs_8_), channel_id=1, source_target_pairs={{0,2},{2,0},{4,6},{6,4},{8,10},{10,8},{12,14},{14,12},{1,3},{3,1},... | collective-permute-start | bytes 884744 | tf_op jit(solution)/shard_map/ppermute | solution.py:385
  102.1 14.4 %collective-permute-start.21 = (bf16[192,768]{1,0:T(8,128)(2,1)S(1)}, bf16[192,768]{1,0:T(8,128)(2,1)}, u32[]{:S(2)}, u32[]{:S(2)}) collective-permute-start(bf16[192,768]{1,0:T(8,128)(2,1)S(1)} %collective-permute-done.20.refs_10_), channel_id=1, source_target_pairs={{0,2},{2,0},{4,6},{6,4},{8,10},{10,8},{12,14},{14,12},{1,3},{3,1},... | collective-permute-start | bytes 884744 | tf_op jit(solution)/shard_map/ppermute | solution.py:385
  103.6 25.3 %collective-permute-start.26 = (bf16[192,768]{1,0:T(8,128)(2,1)}, bf16[192,768]{1,0:T(8,128)(2,1)S(1)}, u32[]{:S(2)}, u32[]{:S(2)}) collective-permute-start(bf16[192,768]{1,0:T(8,128)(2,1)} %collective-permute-done.18.refs_8_), channel_id=1, source_target_pairs={{0,16},{16,0},{1,17},{17,1},{2,18},{18,2},{3,19},{19,3},{4,20},{20... | collective-permute-start | bytes 884744 | tf_op jit(solution)/shard_map/ppermute | solution.py:399
  103.7 26.4 %collective-permute-start.25 = (bf16[192,768]{1,0:T(8,128)(2,1)S(1)}, bf16[192,768]{1,0:T(8,128)(2,1)S(1)}, u32[]{:S(2)}, u32[]{:S(2)}) collective-permute-start(bf16[192,768]{1,0:T(8,128)(2,1)S(1)} %collective-permute-done.17.refs_7_), channel_id=1, source_target_pairs={{0,16},{16,0},{1,17},{17,1},{2,18},{18,2},{3,19},{19,3},{4,20},{20... | collective-permute-start | bytes 884744 | tf_op jit(solution)/shard_map/ppermute | solution.py:399
  104.2 27.1 %collective-permute-start.28 = (bf16[192,768]{1,0:T(8,128)(2,1)S(1)}, bf16[192,768]{1,0:T(8,128)(2,1)S(1)}, u32[]{:S(2)}, u32[]{:S(2)}) collective-permute-start(bf16[192,768]{1,0:T(8,128)(2,1)S(1)} %collective-permute-done.20.refs_10_), channel_id=1, source_target_pairs={{0,16},{16,0},{1,17},{17,1},{2,18},{18,2},{3,19},{19,3},{4,20},{20... | collective-permute-start | bytes 884744 | tf_op jit(solution)/shard_map/ppermute | solution.py:399
  111.8 22.4 %collective-permute-start.27 = (bf16[192,768]{1,0:T(8,128)(2,1)S(1)}, bf16[192,768]{1,0:T(8,128)(2,1)}, u32[]{:S(2)}, u32[]{:S(2)}) collective-permute-start(bf16[192,768]{1,0:T(8,128)(2,1)S(1)} %collective-permute-done.19.refs_9_), channel_id=1, source_target_pairs={{0,16},{16,0},{1,17},{17,1},{2,18},{18,2},{3,19},{19,3},{4,20},{20... | collective-permute-start | bytes 884744 | tf_op jit(solution)/shard_map/ppermute | solution.py:399
  116.6 17.6 %collective-permute-start.29 = (bf16[192,768]{1,0:T(8,128)(2,1)}, bf16[192,768]{1,0:T(8,128)(2,1)}, u32[]{:S(2)}, u32[]{:S(2)}) collective-permute-start(bf16[192,768]{1,0:T(8,128)(2,1)} %collective-permute-done.21.refs_11_), channel_id=1, source_target_pairs={{0,16},{16,0},{1,17},{17,1},{2,18},{18,2},{3,19},{19,3},{4,20},{20... | collective-permute-start | bytes 884744 | tf_op jit(solution)/shard_map/ppermute | solution.py:399
  116.6 2.5 %copy-start.3 = (f32[4,288,1152]{2,1,0:T(8,128)S(1)}, f32[4,288,1152]{2,1,0:T(8,128)}, u32[]{:S(2)}) copy-start(f32[4,288,1152]{2,1,0:T(8,128)} %copy-done.2) | copy-start | bytes 15925252
  128.2 0.7 copy-start.15
  128.9 0.7 copy-start.9
  129.6 4.5 %collective-permute-start.12 = (bf16[288,384]{1,0:T(8,128)(2,1)}, bf16[288,384]{1,0:T(8,128)(2,1)}, u32[]{:S(2)}, u32[]{:S(2)}) collective-permute-start(bf16[288,384]{1,0:T(8,128)(2,1)} %get-tuple-element.20), channel_id=1, source_target_pairs={{0,16},{16,0},{1,17},{17,1},{2,18},{18,2},{3,19},{19,3},{4,20},{20... | collective-permute-start | bytes 663560 | tf_op jit(solution)/shard_map/ppermute | solution.py:417
  130.1 0.7 copy-start.11
  130.8 8.6 %collective-permute-start.13 = (bf16[288,384]{1,0:T(8,128)(2,1)}, bf16[288,384]{1,0:T(8,128)(2,1)}, u32[]{:S(2)}, u32[]{:S(2)}) collective-permute-start(bf16[288,384]{1,0:T(8,128)(2,1)} %get-tuple-element.21), channel_id=1, source_target_pairs={{0,1},{1,0},{2,3},{3,2},{4,5},{5,4},{6,7},{7,6},{8,9},{9,8},{10,11... | collective-permute-start | bytes 663560 | tf_op jit(solution)/shard_map/ppermute | solution.py:418
  131.3 0.7 copy-start.13
  132.0 10.2 %collective-permute-start.14 = (bf16[288,384]{1,0:T(8,128)(2,1)}, bf16[288,384]{1,0:T(8,128)(2,1)}, u32[]{:S(2)}, u32[]{:S(2)}) collective-permute-start(bf16[288,384]{1,0:T(8,128)(2,1)} %get-tuple-element.22), channel_id=1, source_target_pairs={{0,17},{1,16},{16,1},{17,0},{2,19},{3,18},{18,3},{19,2},{4,21},{5,... | collective-permute-start | bytes 663560 | tf_op jit(solution)/shard_map/ppermute | solution.py:419
  142.3 1.0 copy-start.10
  143.2 1.0 copy-start.12
  144.2 1.0 copy-start.14
  145.2 0.9 copy-start.16
  151.8 3.1 %collective-permute-start.30 = (bf16[288,32]{1,0:T(8,128)(2,1)S(1)}, bf16[288,32]{1,0:T(8,128)(2,1)S(1)}, u32[]{:S(2)}, u32[]{:S(2)}) collective-permute-start(bf16[288,32]{1,0:T(8,128)(2,1)S(1)} %dynamic-slice_convert_fusion), channel_id=1, source_target_pairs={{0,16},{16,0},{1,17},{17,1},{2,18},{18,2},{3,19},{19,3},{4,20},{20... | collective-permute-start | bytes 55304 | tf_op jit(solution)/shard_map/ppermute | solution.py:352

commit v2 on v0

--- a/solution.py
+++ b/solution.py
@@ -1,9 +1,45 @@
+import functools
+
 import jax
 import jax.numpy as jnp
 from jax import lax
+from jax.experimental import pallas as pl
+from jax.experimental.pallas import tpu as pltpu
 from jax.sharding import PartitionSpec as P
 
 DH = 128
+SWAP = [(0, 1), (1, 0)]
+SMEM = pl.BlockSpec(memory_space=pltpu.SMEM)
+ANY = pl.BlockSpec(memory_space=pl.ANY)
+BF16 = jnp.bfloat16
+F32 = jnp.float32
+
+
+def params():
+    return pltpu.CompilerParams(vmem_limit_bytes=60 * 2**20)
+
+
+def cost(flops, moved, exps=0):
+    return pl.CostEstimate(flops=int(flops), bytes_accessed=int(moved), transcendentals=int(exps))
+
+
+def shape_of(*dims, dtype=BF16):
+    return jax.ShapeDtypeStruct(dims, dtype)
+
+
+def times(left, right):
+    return jnp.dot(left, right, preferred_element_type=F32)
+
+
+def times_turned(left, right):
+    return lax.dot_general(left, right, (((1,), (1,)), ((), ())), preferred_element_type=F32)
+
+
+def load_all(pairs, sem):
+    copies = [pltpu.make_async_copy(source, target, sem.at[j]) for j, (source, target) in enumerate(pairs)]
+    for copy in copies:
+        copy.start()
+    return copies
 
 
 def passed_along(value, axis, steps):
@@ -51,7 +87,7 @@
     return (new_top, total, weighted)
 
 
-def local(
+def ring_local(
     hidden, latent, modulation, w_qkv, w_out, q_gain, k_gain, w_head, lengths, guidance, step_size
 ):
     state = hidden[0, 0]
@@ -106,23 +142,552 @@
     return updated[None]
 
 
+def norm_kernel(where_ref, state_ref, modes_ref, out_ref, state_in, modes_in, full_ref, out_buf, sem):
+    side, pair, steps = where_ref[0], where_ref[1], where_ref[2]
+    for copy in load_all([(state_ref, state_in), (modes_ref, modes_in)], sem):
+        copy.wait()
+    wide = state_in[...].astype(F32)
+    full_ref[...] = layer_norm(wide) * (1.0 + modes_in[1]) + modes_in[0]
+    count = 4
+    depth = out_ref.shape[1] // count
+    for k in range(count):
+        owner = lax.rem(pair + k, steps)
+        part = full_ref[:, pl.ds(pl.multiple_of(owner * depth, depth), depth)]
+        part = jnp.where(side == 0, part, pltpu.roll(part, depth // 2, 1))
+        out_buf[:, k * depth : (k + 1) * depth] = part.astype(BF16)
+    for copy in load_all([(out_buf, out_ref)], sem):
+        copy.wait()
+
+
+def normalise(where, state, modes):
+    return pl.pallas_call(
+        norm_kernel,
+        out_shape=shape_of(*state.shape),
+        in_specs=[SMEM, ANY, ANY],
+        out_specs=ANY,
+        scratch_shapes=[
+            pltpu.VMEM(state.shape, BF16),
+            pltpu.VMEM(modes.shape, F32),
+            pltpu.VMEM(state.shape, F32),
+            pltpu.VMEM(state.shape, BF16),
+            pltpu.SemaphoreType.DMA((2,)),
+        ],
+        compiler_params=params(),
+        cost_estimate=cost(4e9, 1e6),
+    )(where, state, modes)
+
+
+def cut_kernel(where_ref, qkv_ref, out_ref, cut_ref, buf, sem):
+    group = where_ref[0]
+    third = cut_ref.shape[1] // 4
+    width = qkv_ref.shape[1] // 3
+    pairs = []
+    for j in range(4):
+        source_ref, base = (qkv_ref, j * width) if j < 3 else (out_ref, 0)
+        source = source_ref.at[:, pl.ds(pl.multiple_of(base + group * third, third), third)]
+        pairs.append((source, buf.at[:, j * third : (j + 1) * third]))
+    for copy in load_all(pairs, sem):
+        copy.wait()
+    for copy in load_all([(buf, cut_ref)], sem):
+        copy.wait()
+
+
+def cut_columns(group, w_qkv, w_out):
+    depth, width = w_out.shape
+    return pl.pallas_call(
+        cut_kernel,
+        out_shape=shape_of(depth, width),
+        in_specs=[SMEM, ANY, ANY],
+        out_specs=ANY,
+        scratch_shapes=[pltpu.VMEM((depth, width), BF16), pltpu.SemaphoreType.DMA((4,))],
+        compiler_params=params(),
+        cost_estimate=cost(2e9, 1e6),
+    )(group, w_qkv, w_out)
+
+
+def pack_kernel(count, *refs):
+    pieces, packed_ref, held_ref, sem = refs[:count], refs[count], refs[count + 1], refs[count + 2]
+    depth = held_ref.shape[0] // count
+    columns = held_ref.shape[1]
+    pairs = []
+    for k, piece in enumerate(pieces):
+        pairs.append((piece.at[:, piece.shape[1] - columns :], held_ref.at[k * depth : (k + 1) * depth]))
+    for copy in load_all(pairs, sem):
+        copy.wait()
+    for copy in load_all([(held_ref, packed_ref)], sem):
+        copy.wait()
+
+
+def pack(pieces, columns):
+    depth = pieces[0].shape[0]
+    full = shape_of(depth * len(pieces), columns)
+    return pl.pallas_call(
+        functools.partial(pack_kernel, len(pieces)),
+        out_shape=full,
+        in_specs=[ANY] * len(pieces),
+        out_specs=ANY,
+        scratch_shapes=[pltpu.VMEM(full.shape, BF16), pltpu.SemaphoreType.DMA((len(pieces),))],
+        compiler_params=params(),
+        cost_estimate=cost(3e9, 1e6),
+    )(*pieces)
+
+
+def rows_of(piece_refs, held_ref, start=0):
+    found, at = [], 0
+    for piece in piece_refs:
+        rows = piece.shape[0]
+        source = piece.at[:, start : start + held_ref.shape[1]]
+        found.append((source, held_ref.at[at : at + rows]))
+        at += rows
+    return found
+
+
+def first_kernel(count, *refs):
+    norms, pieces = refs[:4], refs[4 : 4 + count]
+    qk_ref, v_ref = refs[4 + count : 6 + count]
+    left_ref, held_ref, qk_out, v_out, sem, out_sem = refs[6 + count :]
+    deep, columns = held_ref.shape
+    split = 2 * columns // 3
+    loads = load_all(
+        rows_of(pieces, held_ref) + [(norms[b].at[:, :deep], left_ref.at[b]) for b in range(4)], sem
+    )
+    for copy in loads:
+        copy.wait()
+    stores = []
+    for block in range(4):
+        qk_out[block] = times(left_ref[block], held_ref[:, :split])
+        v_out[block] = times(left_ref[block], held_ref[:, split:])
+        for j, (source, target) in enumerate(((qk_out, qk_ref), (v_out, v_ref))):
+            copy = pltpu.make_async_copy(source.at[block], target.at[block], out_sem.at[2 * block + j])
+            copy.start()
+            stores.append(copy)
+    for copy in stores:
+        copy.wait()
+
+
+def first_part(norms, pieces):
+    rows = norms[0].shape[0]
+    columns = 3 * norms[0].shape[1] // 4
+    deep = sum(piece.shape[0] for piece in pieces)
+    qk = shape_of(4, rows, 2 * columns // 3, dtype=F32)
+    v = shape_of(4, rows, columns // 3, dtype=F32)
+    return pl.pallas_call(
+        functools.partial(first_kernel, len(pieces)),
+        out_shape=[qk, v],
+        in_specs=[ANY] * (4 + len(pieces)),
+        out_specs=[ANY] * 2,
+        scratch_shapes=[
+            pltpu.VMEM((4, rows, deep), BF16),
+            pltpu.VMEM((deep, columns), BF16),
+            pltpu.VMEM(qk.shape, F32),
+            pltpu.VMEM(v.shape, F32),
+            pltpu.SemaphoreType.DMA((4 + len(pieces),)),
+            pltpu.SemaphoreType.DMA((8,)),
+        ],
+        compiler_params=params(),
+        cost_estimate=cost(6e9, 1e6),
+    )(*norms, *pieces)
+
+
+def scores_kernel(count, *refs):
+    norms, acc_ref, pieces = refs[:4], refs[4], refs[5 : 5 + count]
+    out_ref, sums_ref, left_ref, held_ref, acc_in, sums_buf, sem, out_sem = refs[5 + count :]
+    deep = held_ref.shape[0]
+    third = out_ref.shape[2] // 2
+    width = norms[0].shape[1]
+    loads = load_all(
+        rows_of(pieces, held_ref)
+        + [(norms[b].at[:, width - deep :], left_ref.at[b]) for b in range(4)]
+        + [(acc_ref.at[b], acc_in.at[b]) for b in range(4)],
+        sem,
+    )
+    for copy in loads[: count + 4]:
+        copy.wait()
+    row = lax.broadcasted_iota(jnp.int32, (8, 4 * DH), 0)
+    lane = lax.broadcasted_iota(jnp.int32, (8, 4 * DH), 1)
+    pick = (row == lane // (2 * DH)).astype(BF16)
+    stores = []
+    for block in range(4):
+        product = times(left_ref[block], held_ref[...])
+        loads[count + 4 + block].wait()
+        total = acc_in[block] + product
+        acc_in[block] = total
+        stores.append(pltpu.make_async_copy(acc_in.at[block], out_ref.at[block], out_sem.at[block]))
+        stores[-1].start()
+        squares = []
+        for j in range(2):
+            square = 0.0
+            for h in range(third // DH):
+                part = total[:, j * third + h * DH : j * third + (h + 1) * DH]
+                square += part * part
+            high = square.astype(BF16)
+            squares += [high, (square - high.astype(F32)).astype(BF16)]
+        sums_buf[block] = times_turned(pick, jnp.concatenate(squares, axis=1))
+    stores.append(pltpu.make_async_copy(sums_buf, sums_ref, out_sem.at[4]))
+    stores[-1].start()
+    for copy in stores:
+        copy.wait()
+
+
+def last_scores(norms, acc, pieces):
+    rows = norms[0].shape[0]
+    columns = acc.shape[2]
+    deep = sum(piece.shape[0] for piece in pieces)
+    return pl.pallas_call(
+        functools.partial(scores_kernel, len(pieces)),
+        out_shape=[shape_of(4, rows, columns, dtype=F32), shape_of(4, 8, rows, dtype=F32)],
+        in_specs=[ANY] * 5 + [ANY] * len(pieces),
+        out_specs=[ANY, ANY],
+        scratch_shapes=[
+            pltpu.VMEM((4, rows, deep), BF16),
+            pltpu.VMEM((deep, columns), BF16),
+            pltpu.VMEM(acc.shape, F32),
+            pltpu.VMEM((4, 8, rows), F32),
+            pltpu.SemaphoreType.DMA((8 + len(pieces),)),
+            pltpu.SemaphoreType.DMA((5,)),
+        ],
+        compiler_params=params(),
+        cost_estimate=cost(6e9, 1e6),
+    )(*norms, acc, *pieces)
+
+
+def values_kernel(count, *refs):
+    norms, acc_ref, pieces = refs[:4], refs[4], refs[5 : 5 + count]
+    out_ref, left_ref, held_ref, acc_in, out_buf, sem = refs[5 + count :]
+    deep, columns = held_ref.shape
+    width = norms[0].shape[1]
+    loads = load_all(
+        rows_of(pieces, held_ref, 2 * columns)
+        + [(norms[b].at[:, width - deep :], left_ref.at[b]) for b in range(4)]
+        + [(acc_ref.at[b], acc_in.at[b]) for b in range(4)],
+        sem,
+    )
+    for copy in loads:
+        copy.wait()
+    for block in range(4):
+        out_buf[block] = (acc_in[block] + times(left_ref[block], held_ref[...])).astype(BF16)
+    for copy in load_all([(out_buf, out_ref)], sem):
+        copy.wait()
+
+
+def last_values(norms, acc, pieces):
+    rows = norms[0].shape[0]
+    columns = acc.shape[2]
+    deep = sum(piece.shape[0] for piece in pieces)
+    return pl.pallas_call(
+        functools.partial(values_kernel, len(pieces)),
+        out_shape=shape_of(4, rows, columns),
+        in_specs=[ANY] * 5 + [ANY] * len(pieces),
+        out_specs=ANY,
+        scratch_shapes=[
+            pltpu.VMEM((4, rows, deep), BF16),
+            pltpu.VMEM((deep, columns), BF16),
+            pltpu.VMEM(acc.shape, F32),
+            pltpu.VMEM(acc.shape, BF16),
+            pltpu.SemaphoreType.DMA((8 + len(pieces),)),
+        ],
+        compiler_params=params(),
+        cost_estimate=cost(4e9, 1e6),
+    )(*norms, acc, *pieces)
+
+
+def heads_kernel(where_ref, qk_ref, v_ref, s0_ref, s1_ref, s2_ref, s3_ref, gains_ref, *refs):
+    outs = refs[:4]
+    qk_in, v_in, sums_in, gains_in, out_buf, q_buf, k_buf, sem, out_sem = refs[4:]
+    third = qk_ref.shape[2] // 2
+    width = 4 * third
+    factor = 1.4426950408889634 / DH**0.5
+    sum_refs = (s0_ref, s1_ref, s2_ref, s3_ref)
+    loads = load_all(
+        [(sum_refs[j], sums_in.at[j]) for j in range(4)]
+        + [(gains_ref, gains_in)]
+        + [(qk_ref.at[b], qk_in.at[b]) for b in range(4)]
+        + [(v_ref, v_in)],
+        sem,
+    )
+    row = lax.broadcasted_iota(jnp.int32, (24, 2 * DH), 0)
+    lane = lax.broadcasted_iota(jnp.int32, (24, 2 * DH), 1)
+    pick = (row % 8 == lane // DH).astype(BF16)
+    mine = pl.ds(pl.multiple_of(where_ref[3] * third, third), third)
+    for copy in loads[:5]:
+        copy.wait()
+    gains = [gains_in[0, :, mine] * factor, gains_in[1, :, mine]]
+    stores = []
+    for block in range(4):
+        sums = sums_in[0, block] + sums_in[1, block ^ 1] + sums_in[2, block ^ 2] + sums_in[3, block ^ 3]
+        inverse = lax.rsqrt(sums * (1.0 / width) + 1e-06)
+        high = inverse.astype(BF16).astype(F32)
+        middle = (inverse - high).astype(BF16).astype(F32)
+        stacked = jnp.concatenate([high, middle, inverse - high - middle], axis=0).astype(BF16)
+        scales = lax.dot_general(stacked, pick, (((0,), (0,)), ((), ())), preferred_element_type=F32)
+        loads[5 + block].wait()
+        for j, buf in enumerate((q_buf, k_buf)):
+            scale = scales[:, j * DH : (j + 1) * DH]
+            for h in range(third // DH):
+                at = slice(h * DH, (h + 1) * DH)
+                raw = qk_in[block, :, j * third + h * DH : j * third + (h + 1) * DH]
+                buf[block, :, at] = (raw * scale * gains[j][:, at]).astype(BF16)
+    loads[9].wait()
+    for block in (1, 3, 2, 0):
+        attend_heads(where_ref, q_buf, k_buf, v_in, block, out_buf.at[block])
+        stores.append(pltpu.make_async_copy(out_buf.at[block], outs[block], out_sem.at[block]))
+        stores[-1].start()
+    for copy in stores:
+        copy.wait()
+
+
+def attend_heads(where_ref, q_ref, k_ref, v_ref, block, out_ref):
+    rows = q_ref.shape[1]
+    first = block - block % 2
+    place = lax.broadcasted_iota(jnp.int32, (1, rows), 1)
+    masks = [place < where_ref[4 + j] for j in range(2)]
+    for h in range(q_ref.shape[2] // DH):
+        at = slice(h * DH, (h + 1) * DH)
+        query = q_ref[block, :, at]
+        scores = []
+        for j in range(2):
+            part = times_turned(query, k_ref[first + j, :, at])
+            scores.append(jnp.where(masks[j], part, -1e30))
+        top = jnp.maximum(
+            jnp.max(scores[0], axis=-1, keepdims=True), jnp.max(scores[1], axis=-1, keepdims=True)
+        )
+        total = 0.0
+        weighted = 0.0
+        for j in range(2):
+            probs = jnp.exp2(scores[j] - top)
+            total += jnp.sum(probs, axis=-1, keepdims=True)
+            weighted += times(probs.astype(BF16), v_ref[first + j, :, at])
+        out_ref[:, at] = (weighted / total).astype(BF16)
+
+
+def team_attention(where, qk, v, sums, gains):
+    rows = qk.shape[1]
+    third = qk.shape[2] // 2
+    return pl.pallas_call(
+        heads_kernel,
+        out_shape=[shape_of(rows, third)] * 4,
+        in_specs=[SMEM] + [ANY] * 7,
+        out_specs=[ANY] * 4,
+        scratch_shapes=[
+            pltpu.VMEM(qk.shape, F32),
+            pltpu.VMEM(v.shape, BF16),
+            pltpu.VMEM((4, 4, 8, rows), F32),
+            pltpu.VMEM((2, 1, 4 * third), F32),
+            pltpu.VMEM((4, rows, third), BF16),
+            pltpu.VMEM((4, rows, third), BF16),
+            pltpu.VMEM((4, rows, third), BF16),
+            pltpu.SemaphoreType.DMA((10,)),
+            pltpu.SemaphoreType.DMA((4,)),
+        ],
+        compiler_params=params(),
+        cost_estimate=cost(1.1e10, 1e6),
+    )(where, qk, v, *sums, gains)
+
+
+def out_kernel(where_ref, state_ref, modes_ref, head_ref, *refs):
+    attended, pieces = refs[:4], refs[4:12]
+    out_ref, att_in, group_ref, held_ref, state_in, modes_in, head_in_ref, out_buf, sem = refs[12:]
+    half = pieces[0].shape[0]
+    side, pair, steps, own = (where_ref[j] for j in range(4))
+    third = attended[0].shape[1]
+
+    def window(j):
+        return pl.ds(pl.multiple_of(j * third, third), third)
+
+    loads = load_all(
+        [(attended[j], att_in.at[j]) for j in range(4)]
+        + [(pieces[j], held_ref.at[:half, window(own ^ j)]) for j in range(4)]
+        + [(pieces[4 + j], held_ref.at[half:, window(own ^ j)]) for j in range(4)]
+        + [(state_ref, state_in), (modes_ref, modes_in), (head_ref, head_in_ref)],
+        sem,
+    )
+    for j in range(4):
+        loads[j].wait()
+        part = att_in[j].astype(F32)
+        part = jnp.where(side == 0, part, pltpu.roll(part, third // 2, 1)).astype(BF16)
+        group_ref[:, window(lax.rem((own ^ j) + steps - pair, steps))] = part
+    for copy in loads[4:]:
+        copy.wait()
+    total = times(group_ref[...], held_ref[...])
+    block_out = (state_in[...].astype(F32) + modes_in[2] * total).astype(BF16)
+    head_in = layer_norm(block_out.astype(F32)) * (1.0 + modes_in[4]) + modes_in[3]
+    out_buf[...] = times_turned(head_in_ref[...], head_in.astype(BF16))
+    for copy in load_all([(out_buf, out_ref)], sem):
+        copy.wait()
+
+
+def project(where, state, modes, w_head, attended, pieces):
+    rows, width = state.shape
+    third = width // 4
+    return pl.pallas_call(
+        out_kernel,
+        out_shape=shape_of(w_head.shape[0], rows, dtype=F32),
+        in_specs=[SMEM] + [ANY] * 15,
+        out_specs=ANY,
+        scratch_shapes=[
+            pltpu.VMEM((4, rows, third), BF16),
+            pltpu.VMEM((rows, width), BF16),
+            pltpu.VMEM((width, width), BF16),
+            pltpu.VMEM(state.shape, BF16),
+            pltpu.VMEM(modes.shape, F32),
+            pltpu.VMEM(w_head.shape, BF16),
+            pltpu.VMEM((w_head.shape[0], rows), F32),
+            pltpu.SemaphoreType.DMA((15,)),
+        ],
+        compiler_params=params(),
+        cost_estimate=cost(8e9, 1e6),
+    )(where, state, modes, w_head, *attended, *pieces)
+
+
+def updated_latent(velocity, latent, guidance, step_size, length, position):
+    rows = velocity.shape[1]
+    branch = lax.axis_index("cfg")
+    scale = guidance[0]
+    channels = velocity.shape[0] // 2
+    own = lax.dynamic_slice_in_dim(velocity, branch * channels, channels, 0)
+    outgoing = lax.dynamic_slice_in_dim(velocity, (1 - branch) * channels, channels, 0)
+    other = lax.ppermute(outgoing.astype(BF16), "cfg", SWAP).astype(outgoing.dtype)
+    cond = jnp.where(branch == 0, own, other)
+    uncond = jnp.where(branch == 0, other, own)
+    guided = uncond + scale * (cond - uncond)
+    valid = position * rows + jnp.arange(rows, dtype=jnp.int32) < length
+    current = latent[0].T
+    updated = jnp.where(valid[None, :], current - step_size[0] * guided, current)
+    return updated.T[None]
+
+
+def after(value, *others):
+    return lax.optimization_barrier((value, *others))[0]
+
+
+def team_local(
+    hidden, latent, modulation, w_qkv, w_out, q_gain, k_gain, w_head, lengths, guidance, step_size
+):
+    state = hidden[0, 0]
+    modes = jnp.transpose(modulation, (1, 0, 2))
+    rows, width = state.shape
+    third = width // 4
+    core = lax.axis_index("cfg")
+    position = lax.axis_index("seq")
+    place = lax.axis_index("req")
+    parts = lax.axis_size("req")
+    side, pair = place % 2, place // 2
+    steps = parts // 2
+    group = 2 * position + core
+    up = [(i, (i - 2) % parts) for i in range(parts)]
+    down = [(i, (i + 2) % parts) for i in range(parts)]
+    beside = [(i, i ^ 1) for i in range(parts)]
+
+    def along(piece):
+        return lax.ppermute(piece, "req", up)
+
+    def back(piece):
+        return lax.ppermute(piece, "req", down)
+
+    def across(piece):
+        return lax.ppermute(piece, "req", beside)
+
+    def ints(*values):
+        return jnp.stack([jnp.asarray(value, jnp.int32) for value in values])
+
+    columns = cut_columns(ints(group), w_qkv, w_out)
+    length = lengths[0]
+    places = ints(side, pair, steps, group, length - position * rows, length - (1 - position) * rows)
+    gains = jnp.stack([q_gain, k_gain])[:, None]
+
+    normed = normalise(places, state, modes)
+
+    def step(mine, theirs, gates):
+        now = after(mine[-1], *gates)
+        mine.append(along(now))
+        theirs.append(across(now))
+
+    mine, theirs = [columns], []
+    step(mine, theirs, [])
+    cut, split = columns.shape[0] // 2, 3 * third
+    low = theirs[0][cut:, :split]
+    out_last = theirs[0][:, split:]
+    gates = [mine[1], theirs[0], low, out_last, normed, gains]
+    normed_y = lax.ppermute(after(normed, *gates), "seq", SWAP)
+    normed_c = lax.ppermute(after(normed, *gates), "cfg", SWAP)
+    step(mine, theirs, gates)
+    gates = [mine[2], theirs[1]]
+    step(mine, theirs, gates)
+    out_last = back(after(out_last, *gates))
+    normed_yc = lax.ppermute(normed_y, "cfg", SWAP)
+    norms = [normed, normed_y, normed_c, normed_yc]
+    early = [mine[0], theirs[0], mine[1], theirs[1]]
+    packed = [pack(early, third)]
+    packed_y = [lax.ppermute(packed[0], "seq", SWAP)]
+    acc_qk, acc_v = first_part(norms, early)
+    gates = [mine[3], theirs[2], out_last, packed_y[0], acc_v]
+    upper = across(after(mine[3][:cut, :split], *gates))
+    lower = back(after(low, *gates))
+    late = [mine[2], theirs[2], mine[3], upper, lower]
+    packed.append(pack([mine[2], theirs[2], mine[3], out_last], third))
+    packed_y.append(lax.ppermute(packed[1], "seq", SWAP))
+    packed_c = [lax.ppermute(part, "cfg", SWAP) for part in packed]
+    packed_yc = [lax.ppermute(part, "cfg", SWAP) for part in packed_y]
+
+    qk_full, sums = last_scores(norms, acc_qk, late)
+    v_full = last_values(norms, acc_v, late)
+    diagonal = [(i, 3 - i) for i in range(4)]
+    all_sums = [
+        sums,
+        lax.ppermute(sums, "seq", SWAP),
+        lax.ppermute(sums, "cfg", SWAP),
+        lax.ppermute(sums, ("cfg", "seq"), diagonal),
+    ]
+    v_full = after(v_full, packed_y[1], *packed_c, packed_yc[0])
+    heads = team_attention(places, qk_full, v_full, all_sums, gains)
+    attended = [
+        heads[0],
+        lax.ppermute(heads[2], "cfg", SWAP),
+        lax.ppermute(heads[1], "seq", SWAP),
+        lax.ppermute(heads[3], ("cfg", "seq"), diagonal),
+    ]
+    quarters = [part[j] for j in range(2) for part in (packed, packed_c, packed_y, packed_yc)]
+    velocity = project(places, state, modes, w_head.T, attended, quarters)
+    return updated_latent(velocity, latent, guidance, step_size, length, position)
+
+
+def by_team(mesh, arguments):
+    hidden, w_qkv = arguments[0], arguments[3]
+    sizes = mesh.shape
+    width = hidden.shape[3]
+    depth = w_qkv.shape[0] // sizes["req"]
+    return (
+        sizes["cfg"] == 2
+        and sizes["seq"] == 2
+        and sizes["req"] == 8
+        and width % (4 * DH) == 0
+        and 8 * depth == width
+        and depth % 32 == 0
+        and hidden.shape[2] // sizes["seq"] % 16 == 0
+    )
+
+
 def solution(mesh):
-    return jax.shard_map(
-        local,
-        mesh=mesh,
-        in_specs=(
-            P("cfg", "req", "seq", None),
-            P("req", "seq", "cfg"),
-            P("req", None, None),
-            P("req", None),
-            P("req", None),
-            P(),
-            P(),
-            P(),
-            P("req"),
-            P("req"),
-            P("req"),
-        ),
-        out_specs=P("req", "seq", "cfg"),
-        check_vma=False,
-    )
+    def whole(*arguments):
+        body = team_local if by_team(mesh, arguments) else ring_local
+        return jax.shard_map(
+            body,
+            mesh=mesh,
+            in_specs=(
+                P("cfg", "req", "seq", None),
+                P("req", "seq", "cfg"),
+                P("req", None, None),
+                P("req", None),
+                P("req", None),
+                P(),
+                P(),
+                P(),
+                P("req"),
+                P("req"),
+                P("req"),
+            ),
+            out_specs=P("req", "seq", "cfg"),
+            check_vma=False,
+        )(*arguments)
+
+    return whole

time: 302 us -> 128 us (0.42)
  waiting for transfers between devices: 246 us -> 49.6 us
  Pallas kernels: 0 us -> 42.2 us
  matrix products: 24.5 us -> 0 us
  starting transfers between devices: 1.59 us -> 25.7 us
  between operations: 15.6 us -> 2.33 us
  other arithmetic: 8.06 us -> 1.47 us
    all_gather x2 -> x0, waiting for transfers between devices: 209 us -> none  [the longest x1 199 us: local(): qkv = add_rows(normed, lax.all_gather(w_qkv, 'req', axis=0, tiled=True))]
    pallas_call x0 -> x9, Pallas kernels: none -> 42.2 us  [the longest x1 9.51 us: team_attention(): pl.pallas_call(heads_kernel, out_shape=[shape_of(rows, third)] * 4, in_sp...]
    dot_general x7 -> x0, matrix products: 24.5 us -> none  [the longest x2 11.9 us: add_rows(): return jnp.dot(left, piece, preferred_element_type=jnp.float32)]
    ppermute x2 -> x25, starting transfers between devices: 1.54 us -> 25.7 us  [the longest x3 9.31 us: along(): return lax.ppermute(piece, 'req', up)]
    ppermute x2 -> x25, waiting for transfers between devices: 35.9 us -> 49.6 us  [the longest x1 15.4 us: team_local(): normed_y = lax.ppermute(after(normed, *gates), 'seq', SWAP)]
    reduce_sum x6 -> x0, other arithmetic: 4.2 us -> none  [the longest x2 2.94 us: attend(): total = total * factor + jnp.sum(probs, axis=-1)]
  transfers between devices with their start and end apart: 4 -> 25, of which waited for: 3 -> 9; matrix products, arithmetic and copies ran while one was open for 10% -> 1% of each run, Pallas kernels for 0% -> 26%
where the time goes in v2:
time: 128 us
  waiting for transfers between devices  49.6 us (39%)
  Pallas kernels  42.2 us (33%)
  starting transfers between devices  25.7 us (20%)
  local copies, waits for them, and re-layouts  6.32 us (5%)
  between operations  2.33 us (2%)
  other arithmetic  1.47 us (1%)
    ppermute x1, waiting for transfers between devices, team_local(): normed_y = lax.ppermute(after(normed, *gates), 'seq', SWAP)  15.4 us
    ppermute x4, waiting for transfers between devices, across(): return lax.ppermute(piece, 'req', beside)  9.79 us
    pallas_call x1, Pallas kernels, team_attention(): pl.pallas_call(heads_kernel, out_shape=[shape_of(rows, third)] * 4, in_sp...  9.51 us
    ppermute x3, starting transfers between devices, along(): return lax.ppermute(piece, 'req', up)  9.31 us
    ppermute x3, waiting for transfers between devices, along(): return lax.ppermute(piece, 'req', up)  8.52 us
    pallas_call x1, Pallas kernels, project(): pl.pallas_call(out_kernel, out_shape=shape_of(w_head.shape[0], rows, dtyp...  7.03 us
    ppermute x1, waiting for transfers between devices, team_local(): lax.ppermute(heads[1], 'seq', SWAP)  6.66 us
    ppermute x4, starting transfers between devices, across(): return lax.ppermute(piece, 'req', beside)  6.03 us
  transfers between devices with their start and end apart: 25, of which 9 were waited for; matrix products, arithmetic and copies ran while one was open for 1% of the time, Pallas kernels for 26%

profile of v2, /device:TPU:0, one launch (start us, length us, event | category | flops | bytes accessed | tf_op | source)
XLA Modules:
  0.0 127.6 jit_solution(1880926457879064252)
XLA Ops:
  0.0 2.0 %shard_map.110.refs_4_.refs_0_ = bf16[192,1536]{1,0:T(8,128)(2,1)} custom-call(s32[1]{0:T(128)} %bitcast.6.where_ref, bf16[192,4608]{1,0:T(8,128)(2,1)} %qkv_ref.1, bf16[192,1536]{1,0:T(8,128)(2,1)} %out_ref.1), custom_call_target="tpu_custom_call" | custom-call | flops 2000000000 | bytes 1000000 | tf_op jit(solution)/shard_map/pallas_call | solution.py:197
  2.0 5.1 %collective-permute-start = (bf16[192,1536]{1,0:T(8,128)(2,1)}, bf16[192,1536]{1,0:T(8,128)(2,1)S(1)}, u32[]{:S(2)}, u32[]{:S(2)}) collective-permute-start(bf16[192,1536]{1,0:T(8,128)(2,1)} %shard_map.110.refs_4_.refs_0_), channel_id=1, source_target_pairs={{0,12},{2,14},{4,0},{6,2},{8,4},{10,6},{12,8},{14,10},{1,13},{3,15... | collective-permute-start | bytes 1769480 | tf_op jit(solution)/shard_map/ppermute | solution.py:582
  7.1 1.5 %collective-permute-start.1 = (bf16[192,1536]{1,0:T(8,128)(2,1)}, bf16[192,1536]{1,0:T(8,128)(2,1)S(1)}, u32[]{:S(2)}, u32[]{:S(2)}) collective-permute-start(bf16[192,1536]{1,0:T(8,128)(2,1)} %shard_map.110.refs_4_.refs_0_), channel_id=1, source_target_pairs={{0,2},{2,0},{4,6},{6,4},{8,10},{10,8},{12,14},{14,12},{1,3},{3,1},... | collective-permute-start | bytes 1769480 | tf_op jit(solution)/shard_map/ppermute | solution.py:588
  9.3 0.6 broadcast_in_dim.16.gains_ref
  10.0 0.7 stack.33.where_ref
  10.6 3.9 %shard_map.109.refs_0_ = bf16[288,1536]{1,0:T(8,128)(2,1)} custom-call(s32[6]{0:T(128)} %stack.33.where_ref, bf16[288,1536]{1,0:T(8,128)(2,1)} %bitcast.24, f32[5,1,1536]{2,1,0:T(1,128)} %bitcast.27), custom_call_target="tpu_custom_call" | custom-call | flops 4000000000 | bytes 1000000 | tf_op jit(solution)/shard_map/pallas_call | solution.py:163
  14.5 7.6 %collective-permute-done.1.refs_5_.refs_1_ = bf16[192,1536]{1,0:T(8,128)(2,1)S(1)} collective-permute-done((bf16[192,1536]{1,0:T(8,128)(2,1)}, bf16[192,1536]{1,0:T(8,128)(2,1)S(1)}, u32[]{:S(2)}, u32[]{:S(2)}) %collective-permute-start.1) | collective-permute-done | bytes 589856 | tf_op jit(solution)/shard_map/ppermute | solution.py:588
  22.2 0.0 collective-permute-done.refs_6_.refs_2_
  22.2 1.6 %collective-permute-start.2 = (bf16[288,1536]{1,0:T(8,128)(2,1)}, bf16[288,1536]{1,0:T(8,128)(2,1)S(1)}, u32[]{:S(2)}, u32[]{:S(2)}) collective-permute-start(bf16[288,1536]{1,0:T(8,128)(2,1)} %shard_map.109.refs_0_), channel_id=1, source_target_pairs={{0,1},{1,0},{2,3},{3,2},{4,5},{5,4},{6,7},{7,6},{8,9},{9,8},{10,11... | collective-permute-start | bytes 2654216 | tf_op jit(solution)/shard_map/ppermute | solution.py:611
  23.8 1.5 %collective-permute-start.5 = (bf16[192,1536]{1,0:T(8,128)(2,1)S(1)}, bf16[192,1536]{1,0:T(8,128)(2,1)S(1)}, u32[]{:S(2)}, u32[]{:S(2)}) collective-permute-start(bf16[192,1536]{1,0:T(8,128)(2,1)S(1)} %collective-permute-done.refs_6_.refs_2_), channel_id=1, source_target_pairs={{0,2},{2,0},{4,6},{6,4},{8,10},{10,8},{12,14},{14,12},{1,3},{3,1},... | collective-permute-start | bytes 1769480 | tf_op jit(solution)/shard_map/ppermute | solution.py:588
  25.3 1.9 %collective-permute-start.6 = (bf16[192,1536]{1,0:T(8,128)(2,1)S(1)}, bf16[192,1536]{1,0:T(8,128)(2,1)}, u32[]{:S(2)}, u32[]{:S(2)}) collective-permute-start(bf16[192,1536]{1,0:T(8,128)(2,1)S(1)} %collective-permute-done.refs_6_.refs_2_), channel_id=1, source_target_pairs={{0,12},{2,14},{4,0},{6,2},{8,4},{10,6},{12,8},{14,10},{1,13},{3,15... | collective-permute-start | bytes 1769480 | tf_op jit(solution)/shard_map/ppermute | solution.py:582
  27.2 0.0 collective-permute-start.3
  27.2 15.4 %collective-permute-done.2.refs_1_ = bf16[288,1536]{1,0:T(8,128)(2,1)S(1)} collective-permute-done((bf16[288,1536]{1,0:T(8,128)(2,1)}, bf16[288,1536]{1,0:T(8,128)(2,1)S(1)}, u32[]{:S(2)}, u32[]{:S(2)}) %collective-permute-start.2) | collective-permute-done | bytes 884768 | tf_op jit(solution)/shard_map/ppermute | solution.py:611
  42.7 0.0 collective-permute-start.4
  42.7 0.0 collective-permute-done.5.refs_7_.refs_3_
  42.7 0.0 collective-permute-done.6.refs_5_.refs_0_
  42.7 0.9 copy-done.13
  43.6 2.3 %collective-permute-start.8 = (bf16[192,1536]{1,0:T(8,128)(2,1)}, bf16[192,1536]{1,0:T(8,128)(2,1)S(1)}, u32[]{:S(2)}, u32[]{:S(2)}) collective-permute-start(bf16[192,1536]{1,0:T(8,128)(2,1)} %collective-permute-done.6.refs_5_.refs_0_), channel_id=1, source_target_pairs={{0,12},{2,14},{4,0},{6,2},{8,4},{10,6},{12,8},{14,10},{1,13},{3,15... | collective-permute-start | bytes 1769480 | tf_op jit(solution)/shard_map/ppermute | solution.py:582
  45.9 1.5 %collective-permute-start.7 = (bf16[192,1536]{1,0:T(8,128)(2,1)}, bf16[192,1536]{1,0:T(8,128)(2,1)}, u32[]{:S(2)}, u32[]{:S(2)}) collective-permute-start(bf16[192,1536]{1,0:T(8,128)(2,1)} %collective-permute-done.6.refs_5_.refs_0_), channel_id=1, source_target_pairs={{0,2},{2,0},{4,6},{6,4},{8,10},{10,8},{12,14},{14,12},{1,3},{3,1},... | collective-permute-start | bytes 1769480 | tf_op jit(solution)/shard_map/ppermute | solution.py:588
  47.3 2.0 %shard_map.112.refs_4_ = bf16[768,384]{1,0:T(8,128)(2,1)} custom-call(bf16[192,1536]{1,0:T(8,128)(2,1)} %shard_map.110.refs_4_.refs_0_, bf16[192,1536]{1,0:T(8,128)(2,1)} %copy-done, bf16[192,1536]{1,0:T(8,128)(2,1)} %copy-done.8, bf16[192,1536]{1,0:T(8,128)(2,1)} %copy-done.13), custom_call_target="tpu_custom_call" | custom-call | flops 3000000000 | bytes 1000000 | tf_op jit(solution)/shard_map/pallas_call | solution.py:224
  49.4 1.6 %collective-permute-start.10 = (bf16[768,384]{1,0:T(8,128)(2,1)}, bf16[768,384]{1,0:T(8,128)(2,1)S(1)}, u32[]{:S(2)}, u32[]{:S(2)}) collective-permute-start(bf16[768,384]{1,0:T(8,128)(2,1)} %shard_map.112.refs_4_), channel_id=1, source_target_pairs={{0,1},{1,0},{2,3},{3,2},{4,5},{5,4},{6,7},{7,6},{8,9},{9,8},{10,11... | collective-permute-start | bytes 1769480 | tf_op jit(solution)/shard_map/ppermute | solution.py:621
  51.0 8.5 %collective-permute-done.8.refs_7_.refs_2_ = bf16[192,1536]{1,0:T(8,128)(2,1)S(1)} collective-permute-done((bf16[192,1536]{1,0:T(8,128)(2,1)}, bf16[192,1536]{1,0:T(8,128)(2,1)S(1)}, u32[]{:S(2)}, u32[]{:S(2)}) %collective-permute-start.8) | collective-permute-done | bytes 589856 | tf_op jit(solution)/shard_map/ppermute | solution.py:582
  59.5 0.0 collective-permute-start.14
  59.5 0.0 collective-permute-done.3.refs_2_
  59.5 0.1 collective-permute-start.9
  59.6 0.9 copy-done.6
  60.5 5.4 %shard_map.111 = (f32[4,288,768]{2,1,0:T(8,128)}, f32[4,288,384]{2,1,0:T(8,128)}) custom-call(bf16[288,1536]{1,0:T(8,128)(2,1)} %shard_map.109.refs_0_, bf16[288,1536]{1,0:T(8,128)(2,1)} %copy-done.5, bf16[288,1536]{1,0:T(8,128)(2,1)} %copy-done.6, bf16[288,1536]{1,0:T(8,128)(2,1)} %collective-permute-done.4.refs_3_, ...), custom_call_target="tpu_custom_call" | custom-call | flops 6000000000 | bytes 1000000 | tf_op jit(solution)/shard_map/pallas_call | solution.py:274
  66.0 2.2 %collective-permute-done.9.refs_3_ = bf16[192,384]{1,0:T(8,128)(2,1)S(1)} collective-permute-done((bf16[192,384]{1,0:T(8,128)(2,1)S(1)}, bf16[192,384]{1,0:T(8,128)(2,1)S(1)}, u32[]{:S(2)}, u32[]{:S(2)}) %collective-permute-start.9) | collective-permute-done | bytes 147488 | tf_op jit(solution)/shard_map/ppermute | solution.py:585
  68.2 0.0 collective-permute-done.7.refs_6_.refs_1_
  68.2 0.0 collective-permute-done.10.refs_6_
  68.2 1.6 %collective-permute-start.11 = (bf16[96,1152]{1,0:T(8,128)(2,1)S(1)}, bf16[96,1152]{1,0:T(8,128)(2,1)S(1)}, u32[]{:S(2)}, u32[]{:S(2)}) collective-permute-start(bf16[96,1152]{1,0:T(8,128)(2,1)S(1)} %slice.14), channel_id=1, source_target_pairs={{0,2},{2,0},{4,6},{6,4},{8,10},{10,8},{12,14},{14,12},{1,3},{3,1},... | collective-permute-start | bytes 663560 | tf_op jit(solution)/shard_map/ppermute | solution.py:588
  69.7 0.0 collective-permute-start.12
  69.7 2.0 %shard_map.115.refs_8_ = bf16[768,384]{1,0:T(8,128)(2,1)} custom-call(bf16[192,1536]{1,0:T(8,128)(2,1)} %collective-permute-done.6.refs_5_.refs_0_, bf16[192,1536]{1,0:T(8,128)(2,1)} %collective-permute-done.7.refs_6_.refs_1_, bf16[192,1536]{1,0:T(8,128)(2,1)} %copy-done.1, bf16[192,384]{1,0:T(8,128)(2,1)} %copy-done.19), custom_call_target="tpu_custom_call" | custom-call | flops 3000000000 | bytes 1000000 | tf_op jit(solution)/shard_map/pallas_call | solution.py:224
  71.7 1.6 %collective-permute-start.13 = (bf16[768,384]{1,0:T(8,128)(2,1)}, bf16[768,384]{1,0:T(8,128)(2,1)S(1)}, u32[]{:S(2)}, u32[]{:S(2)}) collective-permute-start(bf16[768,384]{1,0:T(8,128)(2,1)} %shard_map.115.refs_8_), channel_id=1, source_target_pairs={{0,1},{1,0},{2,3},{3,2},{4,5},{5,4},{6,7},{7,6},{8,9},{9,8},{10,11... | collective-permute-start | bytes 1769480 | tf_op jit(solution)/shard_map/ppermute | solution.py:628
  73.3 2.2 %collective-permute-done.11.refs_8_ = bf16[96,1152]{1,0:T(8,128)(2,1)S(1)} collective-permute-done((bf16[96,1152]{1,0:T(8,128)(2,1)S(1)}, bf16[96,1152]{1,0:T(8,128)(2,1)S(1)}, u32[]{:S(2)}, u32[]{:S(2)}) %collective-permute-start.11) | collective-permute-done | bytes 221216 | tf_op jit(solution)/shard_map/ppermute | solution.py:588
  75.5 0.0 collective-permute-start.16
  75.5 3.0 %collective-permute-done.12.refs_9_ = bf16[96,1152]{1,0:T(8,128)(2,1)S(1)} collective-permute-done((bf16[96,1152]{1,0:T(8,128)(2,1)S(1)}, bf16[96,1152]{1,0:T(8,128)(2,1)S(1)}, u32[]{:S(2)}, u32[]{:S(2)}) %collective-permute-start.12) | collective-permute-done | bytes 221216 | tf_op jit(solution)/shard_map/ppermute | solution.py:585
  78.5 0.7 copy-done.15
  79.2 5.9 %shard_map.113 = (f32[4,288,768]{2,1,0:T(8,128)}, f32[4,8,288]{2,1,0:T(8,128)}) custom-call(bf16[288,1536]{1,0:T(8,128)(2,1)} %shard_map.109.refs_0_, bf16[288,1536]{1,0:T(8,128)(2,1)} %copy-done.5, bf16[288,1536]{1,0:T(8,128)(2,1)} %copy-done.6, bf16[288,1536]{1,0:T(8,128)(2,1)} %collective-permute-done.4.refs_3_, ...), custom_call_target="tpu_custom_call" | custom-call | flops 6000000000 | bytes 1000000 | tf_op jit(solution)/shard_map/pallas_call | solution.py:336
  85.2 1.6 %collective-permute-start.17 = (f32[4,8,288]{2,1,0:T(8,128)}, f32[4,8,288]{2,1,0:T(8,128)S(1)}, u32[]{:S(2)}, u32[]{:S(2)}) collective-permute-start(f32[4,8,288]{2,1,0:T(8,128)} %get-tuple-element.30.s0_ref), channel_id=1, source_target_pairs={{0,1},{1,0},{2,3},{3,2},{4,5},{5,4},{6,7},{7,6},{8,9},{9,8},{10,11... | collective-permute-start | bytes 110600 | tf_op jit(solution)/shard_map/ppermute | solution.py:637
  86.8 0.0 collective-permute-done.14.refs_5_
  86.8 0.0 collective-permute-start.18
  86.8 0.2 collective-permute-done.13.refs_10_
  86.9 0.5 collective-permute-start.19
  87.4 4.4 %shard_map.114.v_ref = bf16[4,288,384]{2,1,0:T(8,128)(2,1)} custom-call(bf16[288,1536]{1,0:T(8,128)(2,1)} %shard_map.109.refs_0_, bf16[288,1536]{1,0:T(8,128)(2,1)} %copy-done.5, bf16[288,1536]{1,0:T(8,128)(2,1)} %copy-done.6, bf16[288,1536]{1,0:T(8,128)(2,1)} %collective-permute-done.4.refs_3_, f32[4,288,384]{2,1,0:T(8,128)} %get-tuple-element.25.refs_4_, ...), custom_call_target="tpu_custom_call" | custom-call | flops 4000000000 | bytes 1000000 | tf_op jit(solution)/shard_map/pallas_call | solution.py:377
  91.8 1.2 collective-permute-start.23
  93.0 0.0 collective-permute-done.18.s2_ref
  93.1 0.6 copy-done.20
  93.7 0.1 copy-done.21
  93.7 0.0 copy-done.22
  93.8 9.5 %shard_map.116 = (bf16[288,384]{1,0:T(8,128)(2,1)}, bf16[288,384]{1,0:T(8,128)(2,1)}, bf16[288,384]{1,0:T(8,128)(2,1)}, bf16[288,384]{1,0:T(8,128)(2,1)}) custom-call(s32[6]{0:T(128)} %stack.33.where_ref, f32[4,288,768]{2,1,0:T(8,128)} %get-tuple-element.28.qk_ref, bf16[4,288,384]{2,1,0:T(8,128)(2,1)} %shard_map.114.v_ref, ...), custom_call_target="tpu_custom_call" | custom-call | flops 11000000512 | bytes 1000000 | tf_op jit(solution)/shard_map/pallas_call | solution.py:466
  103.3 0.2 collective-permute-start.20
  103.5 0.8 collective-permute-start.21
  104.3 1.0 collective-permute-start.22
  105.3 0.0 collective-permute-done.20.refs_1_
  105.3 6.7 %collective-permute-done.21.refs_2_ = bf16[288,384]{1,0:T(8,128)(2,1)S(1)} collective-permute-done((bf16[288,384]{1,0:T(8,128)(2,1)}, bf16[288,384]{1,0:T(8,128)(2,1)S(1)}, u32[]{:S(2)}, u32[]{:S(2)}) %collective-permute-start.21) | collective-permute-done | bytes 221216 | tf_op jit(solution)/shard_map/ppermute | solution.py:646
  111.9 3.8 %collective-permute-done.22.refs_3_ = bf16[288,384]{1,0:T(8,128)(2,1)S(1)} collective-permute-done((bf16[288,384]{1,0:T(8,128)(2,1)}, bf16[288,384]{1,0:T(8,128)(2,1)S(1)}, u32[]{:S(2)}, u32[]{:S(2)}) %collective-permute-start.22) | collective-permute-done | bytes 221216 | tf_op jit(solution)/shard_map/ppermute | solution.py:647
  115.8 0.7 copy-done.18
  116.4 0.2 copy-done.12
  116.6 7.0 %shard_map.117 = f32[64,288]{1,0:T(8,128)} custom-call(s32[6]{0:T(128)} %stack.33.where_ref, bf16[288,1536]{1,0:T(8,128)(2,1)} %bitcast.25, f32[5,1,1536]{2,1,0:T(1,128)} %bitcast.28, bf16[64,1536]{1,0:T(8,128)(2,1)} %bitcast.26, bf16[288,384]{1,0:T(8,128)(2,1)} %get-tuple-element.31.refs_0_, bf16[288,384]{1,0:T(8,128)(2,1)} %copy-done.16, ...), custom_call_target="tpu_custom_call" | custom-call | flops 8000000000 | bytes 1000000 | tf_op jit(solution)/shard_map/pallas_call | solution.py:522
  123.7 0.8 dynamic-slice_convert_fusion
  124.5 0.3 collective-permute-start.24
  126.1 0.0 collective-permute-done.24
  126.1 1.4 %fusion.4 = f32[1,288,32]{1,2,0:T(8,128)} fusion(bf16[32,288]{1,0:T(8,128)(2,1)S(1)} %collective-permute-done.24, f32[1,288,32]{1,2,0:T(8,128)S(1)} %copy-done.2, f32[64,288]{1,0:T(8,128)} %shard_map.117, s32[]{:T(128)S(6)} %select_n.37, f32[]{:T(128)} %bitcast.22, f32[]{:T(128)} %bitcast.23, pred[]{:T(512)S(6)} %eq.6, pred[288]{0:T(512)(128)(4,1)S(1)} %add_compare_fusion), kind=kLoop, calls=%fused_computation.7 | loop fusion | flops 82944 | bytes 129325 | tf_op jit(solution)/shard_map/broadcast_in_dim | solution.py:556
  (52 shorter events, 0.2 us)
Async XLA Ops:
  0.0 9.3 %copy-start.3 = (f32[1536]{0:T(1024)S(1)}, f32[1536]{0:T(1024)}, u32[]{:S(2)}) copy-start(f32[1536]{0:T(1024)} %param.17) | copy-start | bytes 18436
  0.0 9.3 %copy-start.4 = (f32[1536]{0:T(1024)S(1)}, f32[1536]{0:T(1024)}, u32[]{:S(2)}) copy-start(f32[1536]{0:T(1024)} %param.16) | copy-start | bytes 18436
  2.0 20.2 %collective-permute-start = (bf16[192,1536]{1,0:T(8,128)(2,1)}, bf16[192,1536]{1,0:T(8,128)(2,1)S(1)}, u32[]{:S(2)}, u32[]{:S(2)}) collective-permute-start(bf16[192,1536]{1,0:T(8,128)(2,1)} %shard_map.110.refs_4_.refs_0_), channel_id=1, source_target_pairs={{0,12},{2,14},{4,0},{6,2},{8,4},{10,6},{12,8},{14,10},{1,13},{3,15... | collective-permute-start | bytes 1769480 | tf_op jit(solution)/shard_map/ppermute | solution.py:582
  7.1 15.0 %collective-permute-start.1 = (bf16[192,1536]{1,0:T(8,128)(2,1)}, bf16[192,1536]{1,0:T(8,128)(2,1)S(1)}, u32[]{:S(2)}, u32[]{:S(2)}) collective-permute-start(bf16[192,1536]{1,0:T(8,128)(2,1)} %shard_map.110.refs_4_.refs_0_), channel_id=1, source_target_pairs={{0,2},{2,0},{4,6},{6,4},{8,10},{10,8},{12,14},{14,12},{1,3},{3,1},... | collective-permute-start | bytes 1769480 | tf_op jit(solution)/shard_map/ppermute | solution.py:588
  22.1 25.2 %copy-start = (bf16[192,1536]{1,0:T(8,128)(2,1)}, bf16[192,1536]{1,0:T(8,128)(2,1)S(1)}, u32[]{:S(2)}) copy-start(bf16[192,1536]{1,0:T(8,128)(2,1)S(1)} %collective-permute-done.1.refs_5_.refs_1_) | copy-start | bytes 1769476
  22.2 20.5 %copy-start.8 = (bf16[192,1536]{1,0:T(8,128)(2,1)}, bf16[192,1536]{1,0:T(8,128)(2,1)S(1)}, u32[]{:S(2)}) copy-start(bf16[192,1536]{1,0:T(8,128)(2,1)S(1)} %collective-permute-done.refs_6_.refs_2_) | copy-start | bytes 1769476
  22.2 20.5 %collective-permute-start.2 = (bf16[288,1536]{1,0:T(8,128)(2,1)}, bf16[288,1536]{1,0:T(8,128)(2,1)S(1)}, u32[]{:S(2)}, u32[]{:S(2)}) collective-permute-start(bf16[288,1536]{1,0:T(8,128)(2,1)} %shard_map.109.refs_0_), channel_id=1, source_target_pairs={{0,1},{1,0},{2,3},{3,2},{4,5},{5,4},{6,7},{7,6},{8,9},{9,8},{10,11... | collective-permute-start | bytes 2654216 | tf_op jit(solution)/shard_map/ppermute | solution.py:611
  23.8 18.9 %collective-permute-start.5 = (bf16[192,1536]{1,0:T(8,128)(2,1)S(1)}, bf16[192,1536]{1,0:T(8,128)(2,1)S(1)}, u32[]{:S(2)}, u32[]{:S(2)}) collective-permute-start(bf16[192,1536]{1,0:T(8,128)(2,1)S(1)} %collective-permute-done.refs_6_.refs_2_), channel_id=1, source_target_pairs={{0,2},{2,0},{4,6},{6,4},{8,10},{10,8},{12,14},{14,12},{1,3},{3,1},... | collective-permute-start | bytes 1769480 | tf_op jit(solution)/shard_map/ppermute | solution.py:588
  25.3 17.4 %collective-permute-start.6 = (bf16[192,1536]{1,0:T(8,128)(2,1)S(1)}, bf16[192,1536]{1,0:T(8,128)(2,1)}, u32[]{:S(2)}, u32[]{:S(2)}) collective-permute-start(bf16[192,1536]{1,0:T(8,128)(2,1)S(1)} %collective-permute-done.refs_6_.refs_2_), channel_id=1, source_target_pairs={{0,12},{2,14},{4,0},{6,2},{8,4},{10,6},{12,8},{14,10},{1,13},{3,15... | collective-permute-start | bytes 1769480 | tf_op jit(solution)/shard_map/ppermute | solution.py:582
  27.2 32.3 %collective-permute-start.3 = (bf16[288,1536]{1,0:T(8,128)(2,1)}, bf16[288,1536]{1,0:T(8,128)(2,1)S(1)}, u32[]{:S(2)}, u32[]{:S(2)}) collective-permute-start(bf16[288,1536]{1,0:T(8,128)(2,1)} %shard_map.109.refs_0_), channel_id=1, source_target_pairs={{0,16},{16,0},{1,17},{17,1},{2,18},{18,2},{3,19},{19,3},{4,20},{20... | collective-permute-start | bytes 2654216 | tf_op jit(solution)/shard_map/ppermute | solution.py:612
  42.7 6.7 %copy-start.5 = (bf16[288,1536]{1,0:T(8,128)(2,1)}, bf16[288,1536]{1,0:T(8,128)(2,1)S(1)}, u32[]{:S(2)}) copy-start(bf16[288,1536]{1,0:T(8,128)(2,1)S(1)} %collective-permute-done.2.refs_1_) | copy-start | bytes 2654212
  42.7 16.9 %collective-permute-start.4 = (bf16[288,1536]{1,0:T(8,128)(2,1)S(1)}, bf16[288,1536]{1,0:T(8,128)(2,1)}, u32[]{:S(2)}, u32[]{:S(2)}) collective-permute-start(bf16[288,1536]{1,0:T(8,128)(2,1)S(1)} %collective-permute-done.2.refs_1_), channel_id=1, source_target_pairs={{0,16},{16,0},{1,17},{17,1},{2,18},{18,2},{3,19},{19,3},{4,20},{20... | collective-permute-start | bytes 2654216 | tf_op jit(solution)/shard_map/ppermute | solution.py:617
  42.7 0.9 copy-start.13
  43.6 15.9 %collective-permute-start.8 = (bf16[192,1536]{1,0:T(8,128)(2,1)}, bf16[192,1536]{1,0:T(8,128)(2,1)S(1)}, u32[]{:S(2)}, u32[]{:S(2)}) collective-permute-start(bf16[192,1536]{1,0:T(8,128)(2,1)} %collective-permute-done.6.refs_5_.refs_0_), channel_id=1, source_target_pairs={{0,12},{2,14},{4,0},{6,2},{8,4},{10,6},{12,8},{14,10},{1,13},{3,15... | collective-permute-start | bytes 1769480 | tf_op jit(solution)/shard_map/ppermute | solution.py:582
  45.9 22.3 %collective-permute-start.7 = (bf16[192,1536]{1,0:T(8,128)(2,1)}, bf16[192,1536]{1,0:T(8,128)(2,1)}, u32[]{:S(2)}, u32[]{:S(2)}) collective-permute-start(bf16[192,1536]{1,0:T(8,128)(2,1)} %collective-permute-done.6.refs_5_.refs_0_), channel_id=1, source_target_pairs={{0,2},{2,0},{4,6},{6,4},{8,10},{10,8},{12,14},{14,12},{1,3},{3,1},... | collective-permute-start | bytes 1769480 | tf_op jit(solution)/shard_map/ppermute | solution.py:588
  49.4 18.8 %collective-permute-start.10 = (bf16[768,384]{1,0:T(8,128)(2,1)}, bf16[768,384]{1,0:T(8,128)(2,1)S(1)}, u32[]{:S(2)}, u32[]{:S(2)}) collective-permute-start(bf16[768,384]{1,0:T(8,128)(2,1)} %shard_map.112.refs_4_), channel_id=1, source_target_pairs={{0,1},{1,0},{2,3},{3,2},{4,5},{5,4},{6,7},{7,6},{8,9},{9,8},{10,11... | collective-permute-start | bytes 1769480 | tf_op jit(solution)/shard_map/ppermute | solution.py:621
  59.5 6.5 %copy-start.1 = (bf16[192,1536]{1,0:T(8,128)(2,1)}, bf16[192,1536]{1,0:T(8,128)(2,1)S(1)}, u32[]{:S(2)}) copy-start(bf16[192,1536]{1,0:T(8,128)(2,1)S(1)} %collective-permute-done.8.refs_7_.refs_2_) | copy-start | bytes 1769476
  59.5 27.3 %collective-permute-start.14 = (bf16[768,384]{1,0:T(8,128)(2,1)}, bf16[768,384]{1,0:T(8,128)(2,1)}, u32[]{:S(2)}, u32[]{:S(2)}) collective-permute-start(bf16[768,384]{1,0:T(8,128)(2,1)} %shard_map.112.refs_4_), channel_id=1, source_target_pairs={{0,16},{16,0},{1,17},{17,1},{2,18},{18,2},{3,19},{19,3},{4,20},{20... | collective-permute-start | bytes 1769480 | tf_op jit(solution)/shard_map/ppermute | solution.py:629
  59.5 1.0 copy-start.6
  59.5 8.6 %collective-permute-start.9 = (bf16[192,384]{1,0:T(8,128)(2,1)S(1)}, bf16[192,384]{1,0:T(8,128)(2,1)S(1)}, u32[]{:S(2)}, u32[]{:S(2)}) collective-permute-start(bf16[192,384]{1,0:T(8,128)(2,1)S(1)} %slice.13), channel_id=1, source_target_pairs={{0,4},{2,6},{4,8},{6,10},{8,12},{10,14},{12,0},{14,2},{1,5},{3,7},... | collective-permute-start | bytes 442376 | tf_op jit(solution)/shard_map/ppermute | solution.py:585
  68.2 1.6 %copy-start.19 = (bf16[192,384]{1,0:T(8,128)(2,1)}, bf16[192,384]{1,0:T(8,128)(2,1)S(1)}, u32[]{:S(2)}) copy-start(bf16[192,384]{1,0:T(8,128)(2,1)S(1)} %collective-permute-done.9.refs_3_) | copy-start | bytes 442372
  68.2 7.3 %copy-start.7 = (bf16[768,384]{1,0:T(8,128)(2,1)}, bf16[768,384]{1,0:T(8,128)(2,1)S(1)}, u32[]{:S(2)}) copy-start(bf16[768,384]{1,0:T(8,128)(2,1)S(1)} %collective-permute-done.10.refs_6_) | copy-start | bytes 1769476
  68.2 7.3 %collective-permute-start.11 = (bf16[96,1152]{1,0:T(8,128)(2,1)S(1)}, bf16[96,1152]{1,0:T(8,128)(2,1)S(1)}, u32[]{:S(2)}, u32[]{:S(2)}) collective-permute-start(bf16[96,1152]{1,0:T(8,128)(2,1)S(1)} %slice.14), channel_id=1, source_target_pairs={{0,2},{2,0},{4,6},{6,4},{8,10},{10,8},{12,14},{14,12},{1,3},{3,1},... | collective-permute-start | bytes 663560 | tf_op jit(solution)/shard_map/ppermute | solution.py:588
  69.7 8.8 %collective-permute-start.12 = (bf16[96,1152]{1,0:T(8,128)(2,1)S(1)}, bf16[96,1152]{1,0:T(8,128)(2,1)S(1)}, u32[]{:S(2)}, u32[]{:S(2)}) collective-permute-start(bf16[96,1152]{1,0:T(8,128)(2,1)S(1)} %slice.12), channel_id=1, source_target_pairs={{0,4},{2,6},{4,8},{6,10},{8,12},{10,14},{12,0},{14,2},{1,5},{3,7},... | collective-permute-start | bytes 663560 | tf_op jit(solution)/shard_map/ppermute | solution.py:585
  71.7 15.2 %collective-permute-start.13 = (bf16[768,384]{1,0:T(8,128)(2,1)}, bf16[768,384]{1,0:T(8,128)(2,1)S(1)}, u32[]{:S(2)}, u32[]{:S(2)}) collective-permute-start(bf16[768,384]{1,0:T(8,128)(2,1)} %shard_map.115.refs_8_), channel_id=1, source_target_pairs={{0,1},{1,0},{2,3},{3,2},{4,5},{5,4},{6,7},{7,6},{8,9},{9,8},{10,11... | collective-permute-start | bytes 1769480 | tf_op jit(solution)/shard_map/ppermute | solution.py:628
  73.3 18.4 %collective-permute-start.15 = (bf16[768,384]{1,0:T(8,128)(2,1)}, bf16[768,384]{1,0:T(8,128)(2,1)S(1)}, u32[]{:S(2)}, u32[]{:S(2)}) collective-permute-start(bf16[768,384]{1,0:T(8,128)(2,1)} %shard_map.115.refs_8_), channel_id=1, source_target_pairs={{0,16},{16,0},{1,17},{17,1},{2,18},{18,2},{3,19},{19,3},{4,20},{20... | collective-permute-start | bytes 1769480 | tf_op jit(solution)/shard_map/ppermute | solution.py:629
  75.5 3.0 %copy-start.14 = (bf16[96,1152]{1,0:T(8,128)(2,1)}, bf16[96,1152]{1,0:T(8,128)(2,1)S(1)}, u32[]{:S(2)}) copy-start(bf16[96,1152]{1,0:T(8,128)(2,1)S(1)} %collective-permute-done.11.refs_8_) | copy-start | bytes 663556
  75.5 17.5 %collective-permute-start.16 = (bf16[768,384]{1,0:T(8,128)(2,1)S(1)}, bf16[768,384]{1,0:T(8,128)(2,1)S(1)}, u32[]{:S(2)}, u32[]{:S(2)}) collective-permute-start(bf16[768,384]{1,0:T(8,128)(2,1)S(1)} %collective-permute-done.10.refs_6_), channel_id=1, source_target_pairs={{0,16},{16,0},{1,17},{17,1},{2,18},{18,2},{3,19},{19,3},{4,20},{20... | collective-permute-start | bytes 1769480 | tf_op jit(solution)/shard_map/ppermute | solution.py:630
  78.5 0.7 copy-start.15
  85.2 7.9 %collective-permute-start.17 = (f32[4,8,288]{2,1,0:T(8,128)}, f32[4,8,288]{2,1,0:T(8,128)S(1)}, u32[]{:S(2)}, u32[]{:S(2)}) collective-permute-start(f32[4,8,288]{2,1,0:T(8,128)} %get-tuple-element.30.s0_ref), channel_id=1, source_target_pairs={{0,1},{1,0},{2,3},{3,2},{4,5},{5,4},{6,7},{7,6},{8,9},{9,8},{10,11... | collective-permute-start | bytes 110600 | tf_op jit(solution)/shard_map/ppermute | solution.py:637
  86.8 6.3 %collective-permute-start.18 = (f32[4,8,288]{2,1,0:T(8,128)}, f32[4,8,288]{2,1,0:T(8,128)S(1)}, u32[]{:S(2)}, u32[]{:S(2)}) collective-permute-start(f32[4,8,288]{2,1,0:T(8,128)} %get-tuple-element.30.s0_ref), channel_id=1, source_target_pairs={{0,16},{16,0},{1,17},{17,1},{2,18},{18,2},{3,19},{19,3},{4,20},{20... | collective-permute-start | bytes 110600 | tf_op jit(solution)/shard_map/ppermute | solution.py:638
  86.9 4.8 %copy-start.9 = (bf16[768,384]{1,0:T(8,128)(2,1)}, bf16[768,384]{1,0:T(8,128)(2,1)S(1)}, u32[]{:S(2)}) copy-start(bf16[768,384]{1,0:T(8,128)(2,1)S(1)} %collective-permute-done.13.refs_10_) | copy-start | bytes 1769476
  86.9 6.1 %collective-permute-start.19 = (f32[4,8,288]{2,1,0:T(8,128)}, f32[4,8,288]{2,1,0:T(8,128)S(1)}, u32[]{:S(2)}, u32[]{:S(2)}) collective-permute-start(f32[4,8,288]{2,1,0:T(8,128)} %get-tuple-element.30.s0_ref), channel_id=1, source_target_pairs={{0,17},{1,16},{16,1},{17,0},{2,19},{3,18},{18,3},{19,2},{4,21},{5,... | collective-permute-start | bytes 110600 | tf_op jit(solution)/shard_map/ppermute | solution.py:639
  91.8 11.5 %copy-start.10 = (bf16[768,384]{1,0:T(8,128)(2,1)}, bf16[768,384]{1,0:T(8,128)(2,1)S(1)}, u32[]{:S(2)}) copy-start(bf16[768,384]{1,0:T(8,128)(2,1)S(1)} %collective-permute-done.15.refs_9_) | copy-start | bytes 1769476
  91.8 23.9 %collective-permute-start.23 = (bf16[768,384]{1,0:T(8,128)(2,1)S(1)}, bf16[768,384]{1,0:T(8,128)(2,1)S(1)}, u32[]{:S(2)}, u32[]{:S(2)}) collective-permute-start(bf16[768,384]{1,0:T(8,128)(2,1)S(1)} %collective-permute-done.13.refs_10_), channel_id=1, source_target_pairs={{0,16},{16,0},{1,17},{17,1},{2,18},{18,2},{3,19},{19,3},{4,20},{20... | collective-permute-start | bytes 1769480 | tf_op jit(solution)/shard_map/ppermute | solution.py:630
  93.0 10.3 %copy-start.11 = (bf16[768,384]{1,0:T(8,128)(2,1)}, bf16[768,384]{1,0:T(8,128)(2,1)S(1)}, u32[]{:S(2)}) copy-start(bf16[768,384]{1,0:T(8,128)(2,1)S(1)} %collective-permute-done.16.refs_7_) | copy-start | bytes 1769476
  93.0 0.7 copy-start.20
  93.1 0.7 copy-start.21
  93.1 0.7 copy-start.22
  103.3 1.9 %collective-permute-start.20 = (bf16[288,384]{1,0:T(8,128)(2,1)}, bf16[288,384]{1,0:T(8,128)(2,1)S(1)}, u32[]{:S(2)}, u32[]{:S(2)}) collective-permute-start(bf16[288,384]{1,0:T(8,128)(2,1)} %get-tuple-element.32), channel_id=1, source_target_pairs={{0,16},{16,0},{1,17},{17,1},{2,18},{18,2},{3,19},{19,3},{4,20},{20... | collective-permute-start | bytes 663560 | tf_op jit(solution)/shard_map/ppermute | solution.py:645
  103.5 8.4 %collective-permute-start.21 = (bf16[288,384]{1,0:T(8,128)(2,1)}, bf16[288,384]{1,0:T(8,128)(2,1)S(1)}, u32[]{:S(2)}, u32[]{:S(2)}) collective-permute-start(bf16[288,384]{1,0:T(8,128)(2,1)} %get-tuple-element.33), channel_id=1, source_target_pairs={{0,1},{1,0},{2,3},{3,2},{4,5},{5,4},{6,7},{7,6},{8,9},{9,8},{10,11... | collective-permute-start | bytes 663560 | tf_op jit(solution)/shard_map/ppermute | solution.py:646
  104.3 11.5 %collective-permute-start.22 = (bf16[288,384]{1,0:T(8,128)(2,1)}, bf16[288,384]{1,0:T(8,128)(2,1)S(1)}, u32[]{:S(2)}, u32[]{:S(2)}) collective-permute-start(bf16[288,384]{1,0:T(8,128)(2,1)} %get-tuple-element.34), channel_id=1, source_target_pairs={{0,17},{1,16},{16,1},{17,0},{2,19},{3,18},{18,3},{19,2},{4,21},{5,... | collective-permute-start | bytes 663560 | tf_op jit(solution)/shard_map/ppermute | solution.py:647
  105.3 10.5 %copy-start.16 = (bf16[288,384]{1,0:T(8,128)(2,1)}, bf16[288,384]{1,0:T(8,128)(2,1)S(1)}, u32[]{:S(2)}) copy-start(bf16[288,384]{1,0:T(8,128)(2,1)S(1)} %collective-permute-done.20.refs_1_) | copy-start | bytes 663556
  111.9 3.8 %copy-start.17 = (bf16[288,384]{1,0:T(8,128)(2,1)}, bf16[288,384]{1,0:T(8,128)(2,1)S(1)}, u32[]{:S(2)}) copy-start(bf16[288,384]{1,0:T(8,128)(2,1)S(1)} %collective-permute-done.21.refs_2_) | copy-start | bytes 663556
  115.7 0.7 copy-start.18
  115.7 0.9 copy-start.12
  116.6 9.5 %copy-start.2 = (f32[1,288,32]{1,2,0:T(8,128)S(1)}, f32[1,288,32]{1,2,0:T(8,128)}, u32[]{:S(2)}) copy-start(f32[1,288,32]{1,2,0:T(8,128)} %param.12) | copy-start | bytes 110596
  124.5 1.6 %collective-permute-start.24 = (bf16[32,288]{1,0:T(8,128)(2,1)S(1)}, bf16[32,288]{1,0:T(8,128)(2,1)S(1)}, u32[]{:S(2)}, u32[]{:S(2)}) collective-permute-start(bf16[32,288]{1,0:T(8,128)(2,1)S(1)} %dynamic-slice_convert_fusion), channel_id=1, source_target_pairs={{0,16},{16,0},{1,17},{17,1},{2,18},{18,2},{3,19},{19,3},{4,20},{20... | collective-permute-start | bytes 55304 | tf_op jit(solution)/shard_map/ppermute | solution.py:549

commit v3 on v2

--- a/solution.py
+++ b/solution.py
@@ -33,13 +33,6 @@
 
 def times_turned(left, right):
     return lax.dot_general(left, right, (((1,), (1,)), ((), ())), preferred_element_type=F32)
-
-
-def load_all(pairs, sem):
-    copies = [pltpu.make_async_copy(source, target, sem.at[j]) for j, (source, target) in enumerate(pairs)]
-    for copy in copies:
-        copy.start()
-    return copies
 
 
 def passed_along(value, axis, steps):
@@ -142,67 +135,58 @@
     return updated[None]
 
 
-def norm_kernel(where_ref, state_ref, modes_ref, out_ref, state_in, modes_in, full_ref, out_buf, sem):
-    side, pair, steps = where_ref[0], where_ref[1], where_ref[2]
-    for copy in load_all([(state_ref, state_in), (modes_ref, modes_in)], sem):
-        copy.wait()
-    wide = state_in[...].astype(F32)
-    full_ref[...] = layer_norm(wide) * (1.0 + modes_in[1]) + modes_in[0]
+def load_all(pairs, sem):
+    copies = [pltpu.make_async_copy(source, target, sem.at[j]) for j, (source, target) in enumerate(pairs)]
+    for copy in copies:
+        copy.start()
+    return copies
+
+
+def entry_kernel(where_ref, qkv_ref, w_out_ref, state_ref, modes_ref, cut_ref, norm_ref, *scratch):
+    cut_buf, state_in, modes_in, full_ref, norm_buf, sem = scratch
+    side, pair, steps, group = (where_ref[j] for j in range(4))
+    third = cut_ref.shape[1] // 4
+    width = 4 * third
+    pairs = []
+    for j in range(4):
+        source_ref, base = (qkv_ref, j * width) if j < 3 else (w_out_ref, 0)
+        source = source_ref.at[:, pl.ds(pl.multiple_of(base + group * third, third), third)]
+        pairs.append((source, cut_buf.at[:, j * third : (j + 1) * third]))
+    loads = load_all([(state_ref, state_in), (modes_ref, modes_in)] + pairs, sem)
+    for copy in loads[:2]:
+        copy.wait()
+    full_ref[...] = layer_norm(state_in[...].astype(F32)) * (1.0 + modes_in[1]) + modes_in[0]
+    for copy in loads[2:]:
+        copy.wait()
+    store = load_all([(cut_buf, cut_ref)], sem)
     count = 4
-    depth = out_ref.shape[1] // count
     for k in range(count):
         owner = lax.rem(pair + k, steps)
-        part = full_ref[:, pl.ds(pl.multiple_of(owner * depth, depth), depth)]
-        part = jnp.where(side == 0, part, pltpu.roll(part, depth // 2, 1))
-        out_buf[:, k * depth : (k + 1) * depth] = part.astype(BF16)
-    for copy in load_all([(out_buf, out_ref)], sem):
-        copy.wait()
-
-
-def normalise(where, state, modes):
+        part = full_ref[:, pl.ds(pl.multiple_of(owner * third, third), third)]
+        part = jnp.where(side == 0, part, pltpu.roll(part, third // 2, 1))
+        norm_buf[:, k * third : (k + 1) * third] = part.astype(BF16)
+    store[0].wait()
+    for copy in load_all([(norm_buf, norm_ref)], sem):
+        copy.wait()
+
+
+def entry(where, w_qkv, w_out, state, modes):
     return pl.pallas_call(
-        norm_kernel,
-        out_shape=shape_of(*state.shape),
-        in_specs=[SMEM, ANY, ANY],
-        out_specs=ANY,
+        entry_kernel,
+        out_shape=[shape_of(*w_out.shape), shape_of(*state.shape)],
+        in_specs=[SMEM, ANY, ANY, ANY, ANY],
+        out_specs=[ANY, ANY],
         scratch_shapes=[
+            pltpu.VMEM(w_out.shape, BF16),
             pltpu.VMEM(state.shape, BF16),
             pltpu.VMEM(modes.shape, F32),
             pltpu.VMEM(state.shape, F32),
             pltpu.VMEM(state.shape, BF16),
-            pltpu.SemaphoreType.DMA((2,)),
+            pltpu.SemaphoreType.DMA((6,)),
         ],
         compiler_params=params(),
         cost_estimate=cost(4e9, 1e6),
-    )(where, state, modes)
-
-
-def cut_kernel(where_ref, qkv_ref, out_ref, cut_ref, buf, sem):
-    group = where_ref[0]
-    third = cut_ref.shape[1] // 4
-    width = qkv_ref.shape[1] // 3
-    pairs = []
-    for j in range(4):
-        source_ref, base = (qkv_ref, j * width) if j < 3 else (out_ref, 0)
-        source = source_ref.at[:, pl.ds(pl.multiple_of(base + group * third, third), third)]
-        pairs.append((source, buf.at[:, j * third : (j + 1) * third]))
-    for copy in load_all(pairs, sem):
-        copy.wait()
-    for copy in load_all([(buf, cut_ref)], sem):
-        copy.wait()
-
-
-def cut_columns(group, w_qkv, w_out):
-    depth, width = w_out.shape
-    return pl.pallas_call(
-        cut_kernel,
-        out_shape=shape_of(depth, width),
-        in_specs=[SMEM, ANY, ANY],
-        out_specs=ANY,
-        scratch_shapes=[pltpu.VMEM((depth, width), BF16), pltpu.SemaphoreType.DMA((4,))],
-        compiler_params=params(),
-        cost_estimate=cost(2e9, 1e6),
-    )(group, w_qkv, w_out)
+    )(where, w_qkv, w_out, state, modes)
 
 
 def pack_kernel(count, *refs):
@@ -255,8 +239,8 @@
         copy.wait()
     stores = []
     for block in range(4):
-        qk_out[block] = times(left_ref[block], held_ref[:, :split])
-        v_out[block] = times(left_ref[block], held_ref[:, split:])
+        qk_out[block] = times(left_ref[block], held_ref[:, :split]).astype(BF16)
+        v_out[block] = times(left_ref[block], held_ref[:, split:]).astype(BF16)
         for j, (source, target) in enumerate(((qk_out, qk_ref), (v_out, v_ref))):
             copy = pltpu.make_async_copy(source.at[block], target.at[block], out_sem.at[2 * block + j])
             copy.start()
@@ -269,8 +253,8 @@
     rows = norms[0].shape[0]
     columns = 3 * norms[0].shape[1] // 4
     deep = sum(piece.shape[0] for piece in pieces)
-    qk = shape_of(4, rows, 2 * columns // 3, dtype=F32)
-    v = shape_of(4, rows, columns // 3, dtype=F32)
+    qk = shape_of(4, rows, 2 * columns // 3)
+    v = shape_of(4, rows, columns // 3)
     return pl.pallas_call(
         functools.partial(first_kernel, len(pieces)),
         out_shape=[qk, v],
@@ -279,8 +263,8 @@
         scratch_shapes=[
             pltpu.VMEM((4, rows, deep), BF16),
             pltpu.VMEM((deep, columns), BF16),
-            pltpu.VMEM(qk.shape, F32),
-            pltpu.VMEM(v.shape, F32),
+            pltpu.VMEM(qk.shape, BF16),
+            pltpu.VMEM(v.shape, BF16),
             pltpu.SemaphoreType.DMA((4 + len(pieces),)),
             pltpu.SemaphoreType.DMA((8,)),
         ],
@@ -289,39 +273,43 @@
     )(*norms, *pieces)
 
 
-def scores_kernel(count, *refs):
-    norms, acc_ref, pieces = refs[:4], refs[4], refs[5 : 5 + count]
-    out_ref, sums_ref, left_ref, held_ref, acc_in, sums_buf, sem, out_sem = refs[5 + count :]
+def scores_kernel(count, where_ref, *refs):
+    norms, acc_ref, gains_ref, pieces = refs[:4], refs[4], refs[5], refs[6 : 6 + count]
+    out_ref, sums_ref, left_ref, held_ref, acc_in, gains_in, out_buf, sums_buf, sem, out_sem = refs[6 + count :]
     deep = held_ref.shape[0]
     third = out_ref.shape[2] // 2
     width = norms[0].shape[1]
     loads = load_all(
         rows_of(pieces, held_ref)
+        + [(gains_ref, gains_in)]
         + [(norms[b].at[:, width - deep :], left_ref.at[b]) for b in range(4)]
         + [(acc_ref.at[b], acc_in.at[b]) for b in range(4)],
         sem,
     )
-    for copy in loads[: count + 4]:
-        copy.wait()
+    mine = pl.ds(pl.multiple_of(where_ref[3] * third, third), third)
     row = lax.broadcasted_iota(jnp.int32, (8, 4 * DH), 0)
     lane = lax.broadcasted_iota(jnp.int32, (8, 4 * DH), 1)
     pick = (row == lane // (2 * DH)).astype(BF16)
+    for copy in loads[: count + 1]:
+        copy.wait()
+    gains = [gains_in[0, :, mine] * (1.4426950408889634 / DH**0.5), gains_in[1, :, mine]]
     stores = []
     for block in range(4):
+        loads[count + 1 + block].wait()
         product = times(left_ref[block], held_ref[...])
-        loads[count + 4 + block].wait()
-        total = acc_in[block] + product
-        acc_in[block] = total
-        stores.append(pltpu.make_async_copy(acc_in.at[block], out_ref.at[block], out_sem.at[block]))
-        stores[-1].start()
+        loads[count + 5 + block].wait()
         squares = []
         for j in range(2):
             square = 0.0
             for h in range(third // DH):
-                part = total[:, j * third + h * DH : j * third + (h + 1) * DH]
+                at = slice(j * third + h * DH, j * third + (h + 1) * DH)
+                part = acc_in[block, :, at].astype(F32) + product[:, at]
                 square += part * part
+                out_buf[block, :, at] = (part * gains[j][:, h * DH : (h + 1) * DH]).astype(BF16)
             high = square.astype(BF16)
             squares += [high, (square - high.astype(F32)).astype(BF16)]
+        stores.append(pltpu.make_async_copy(out_buf.at[block], out_ref.at[block], out_sem.at[block]))
+        stores[-1].start()
         sums_buf[block] = times_turned(pick, jnp.concatenate(squares, axis=1))
     stores.append(pltpu.make_async_copy(sums_buf, sums_ref, out_sem.at[4]))
     stores[-1].start()
@@ -329,26 +317,28 @@
         copy.wait()
 
 
-def last_scores(norms, acc, pieces):
+def last_scores(where, norms, acc, gains, pieces):
     rows = norms[0].shape[0]
     columns = acc.shape[2]
     deep = sum(piece.shape[0] for piece in pieces)
     return pl.pallas_call(
         functools.partial(scores_kernel, len(pieces)),
-        out_shape=[shape_of(4, rows, columns, dtype=F32), shape_of(4, 8, rows, dtype=F32)],
-        in_specs=[ANY] * 5 + [ANY] * len(pieces),
+        out_shape=[shape_of(4, rows, columns), shape_of(4, 8, rows, dtype=F32)],
+        in_specs=[SMEM] + [ANY] * (6 + len(pieces)),
         out_specs=[ANY, ANY],
         scratch_shapes=[
             pltpu.VMEM((4, rows, deep), BF16),
             pltpu.VMEM((deep, columns), BF16),
-            pltpu.VMEM(acc.shape, F32),
+            pltpu.VMEM(acc.shape, BF16),
+            pltpu.VMEM(gains.shape, F32),
+            pltpu.VMEM(acc.shape, BF16),
             pltpu.VMEM((4, 8, rows), F32),
-            pltpu.SemaphoreType.DMA((8 + len(pieces),)),
+            pltpu.SemaphoreType.DMA((9 + len(pieces),)),
             pltpu.SemaphoreType.DMA((5,)),
         ],
         compiler_params=params(),
         cost_estimate=cost(6e9, 1e6),
-    )(*norms, acc, *pieces)
+    )(where, *norms, acc, gains, *pieces)
 
 
 def values_kernel(count, *refs):
@@ -362,11 +352,17 @@
         + [(acc_ref.at[b], acc_in.at[b]) for b in range(4)],
         sem,
     )
-    for copy in loads:
-        copy.wait()
+    for copy in loads[:count]:
+        copy.wait()
+    stores = []
     for block in range(4):
-        out_buf[block] = (acc_in[block] + times(left_ref[block], held_ref[...])).astype(BF16)
-    for copy in load_all([(out_buf, out_ref)], sem):
+        loads[count + block].wait()
+        product = times(left_ref[block], held_ref[...])
+        loads[count + 4 + block].wait()
+        out_buf[block] = (acc_in[block].astype(F32) + product).astype(BF16)
+        stores.append(pltpu.make_async_copy(out_buf.at[block], out_ref.at[block], sem.at[block]))
+        stores[-1].start()
+    for copy in stores:
         copy.wait()
 
 
@@ -382,7 +378,7 @@
         scratch_shapes=[
             pltpu.VMEM((4, rows, deep), BF16),
             pltpu.VMEM((deep, columns), BF16),
-            pltpu.VMEM(acc.shape, F32),
+            pltpu.VMEM(acc.shape, BF16),
             pltpu.VMEM(acc.shape, BF16),
             pltpu.SemaphoreType.DMA((8 + len(pieces),)),
         ],
@@ -391,105 +387,109 @@
     )(*norms, acc, *pieces)
 
 
-def heads_kernel(where_ref, qk_ref, v_ref, s0_ref, s1_ref, s2_ref, s3_ref, gains_ref, *refs):
+def heads_kernel(where_ref, qk_ref, v_ref, s0_ref, s1_ref, s2_ref, s3_ref, *refs):
     outs = refs[:4]
-    qk_in, v_in, sums_in, gains_in, out_buf, q_buf, k_buf, sem, out_sem = refs[4:]
+    qk_in, v_in, sums_in, out_buf, sem, out_sem = refs[4:]
+    rows = qk_ref.shape[1]
     third = qk_ref.shape[2] // 2
+    count = third // DH
     width = 4 * third
-    factor = 1.4426950408889634 / DH**0.5
     sum_refs = (s0_ref, s1_ref, s2_ref, s3_ref)
     loads = load_all(
         [(sum_refs[j], sums_in.at[j]) for j in range(4)]
-        + [(gains_ref, gains_in)]
         + [(qk_ref.at[b], qk_in.at[b]) for b in range(4)]
-        + [(v_ref, v_in)],
+        + [
+            (v_ref.at[b, :, h * DH : (h + 1) * DH], v_in.at[h, b // 2, b % 2 * rows : (b % 2 + 1) * rows, :DH])
+            for b in range(4)
+            for h in range(count)
+        ],
         sem,
     )
-    row = lax.broadcasted_iota(jnp.int32, (24, 2 * DH), 0)
-    lane = lax.broadcasted_iota(jnp.int32, (24, 2 * DH), 1)
-    pick = (row % 8 == lane // DH).astype(BF16)
-    mine = pl.ds(pl.multiple_of(where_ref[3] * third, third), third)
-    for copy in loads[:5]:
-        copy.wait()
-    gains = [gains_in[0, :, mine] * factor, gains_in[1, :, mine]]
-    stores = []
+    for h in range(count):
+        for b in range(2):
+            v_in[h, b, :, DH:] = jnp.ones((2 * rows, DH), BF16)
+    row = lax.broadcasted_iota(jnp.int32, (24, DH), 0)
+    pick = (row % 8 == 0).astype(BF16)
+    place = lax.broadcasted_iota(jnp.int32, (1, rows), 1)
+    masks = [place < where_ref[4 + j] for j in range(2)]
+    for copy in loads[:4]:
+        copy.wait()
+    scale_q, scale_k = [], []
     for block in range(4):
         sums = sums_in[0, block] + sums_in[1, block ^ 1] + sums_in[2, block ^ 2] + sums_in[3, block ^ 3]
         inverse = lax.rsqrt(sums * (1.0 / width) + 1e-06)
         high = inverse.astype(BF16).astype(F32)
         middle = (inverse - high).astype(BF16).astype(F32)
         stacked = jnp.concatenate([high, middle, inverse - high - middle], axis=0).astype(BF16)
-        scales = lax.dot_general(stacked, pick, (((0,), (0,)), ((), ())), preferred_element_type=F32)
-        loads[5 + block].wait()
-        for j, buf in enumerate((q_buf, k_buf)):
-            scale = scales[:, j * DH : (j + 1) * DH]
-            for h in range(third // DH):
-                at = slice(h * DH, (h + 1) * DH)
-                raw = qk_in[block, :, j * third + h * DH : j * third + (h + 1) * DH]
-                buf[block, :, at] = (raw * scale * gains[j][:, at]).astype(BF16)
-    loads[9].wait()
-    for block in (1, 3, 2, 0):
-        attend_heads(where_ref, q_buf, k_buf, v_in, block, out_buf.at[block])
-        stores.append(pltpu.make_async_copy(out_buf.at[block], outs[block], out_sem.at[block]))
-        stores[-1].start()
-    for copy in stores:
-        copy.wait()
-
-
-def attend_heads(where_ref, q_ref, k_ref, v_ref, block, out_ref):
-    rows = q_ref.shape[1]
-    first = block - block % 2
-    place = lax.broadcasted_iota(jnp.int32, (1, rows), 1)
-    masks = [place < where_ref[4 + j] for j in range(2)]
-    for h in range(q_ref.shape[2] // DH):
-        at = slice(h * DH, (h + 1) * DH)
-        query = q_ref[block, :, at]
-        scores = []
+        turned = lax.dot_general(stacked, pick, (((0,), (0,)), ((), ())), preferred_element_type=F32)
+        scale_q.append(turned[:, :1])
+        scale_k.append(inverse[1:2, :])
+    for copy in loads[4:8]:
+        copy.wait()
+    items = [(block, h) for block in (1, 3, 2, 0) for h in range(count)]
+
+    def scores_of(block, h):
+        first = block - block % 2
+        query = qk_in[block, :, h * DH : (h + 1) * DH]
+        found = []
         for j in range(2):
-            part = times_turned(query, k_ref[first + j, :, at])
-            scores.append(jnp.where(masks[j], part, -1e30))
+            keys = qk_in[first + j, :, third + h * DH : third + (h + 1) * DH]
+            part = times_turned(query, keys) * scale_k[first + j]
+            found.append(jnp.where(masks[j], part, -1e30))
+        return found
+
+    stores = []
+    ahead = scores_of(*items[0])
+    for at, (block, h) in enumerate(items):
+        scores = ahead
+        if at + 1 < len(items):
+            ahead = scores_of(*items[at + 1])
+        if at == 0:
+            for copy in loads[8:]:
+                copy.wait()
         top = jnp.maximum(
             jnp.max(scores[0], axis=-1, keepdims=True), jnp.max(scores[1], axis=-1, keepdims=True)
         )
-        total = 0.0
         weighted = 0.0
         for j in range(2):
-            probs = jnp.exp2(scores[j] - top)
-            total += jnp.sum(probs, axis=-1, keepdims=True)
-            weighted += times(probs.astype(BF16), v_ref[first + j, :, at])
-        out_ref[:, at] = (weighted / total).astype(BF16)
-
-
-def team_attention(where, qk, v, sums, gains):
+            probs = jnp.exp2((scores[j] - top) * scale_q[block]).astype(BF16)
+            weighted += times(probs, v_in[h, block // 2, j * rows : (j + 1) * rows, :])
+        out_buf[block, :, h * DH : (h + 1) * DH] = (weighted[:, :DH] / weighted[:, DH:]).astype(BF16)
+        if h == count - 1:
+            stores.append(pltpu.make_async_copy(out_buf.at[block], outs[block], out_sem.at[block]))
+            stores[-1].start()
+    for copy in stores:
+        copy.wait()
+
+
+def team_attention(where, qk, v, sums):
     rows = qk.shape[1]
     third = qk.shape[2] // 2
     return pl.pallas_call(
         heads_kernel,
         out_shape=[shape_of(rows, third)] * 4,
-        in_specs=[SMEM] + [ANY] * 7,
+        in_specs=[SMEM] + [ANY] * 6,
         out_specs=[ANY] * 4,
         scratch_shapes=[
-            pltpu.VMEM(qk.shape, F32),
-            pltpu.VMEM(v.shape, BF16),
+            pltpu.VMEM(qk.shape, BF16),
+            pltpu.VMEM((third // DH, 2, 2 * rows, 2 * DH), BF16),
             pltpu.VMEM((4, 4, 8, rows), F32),
-            pltpu.VMEM((2, 1, 4 * third), F32),
             pltpu.VMEM((4, rows, third), BF16),
-            pltpu.VMEM((4, rows, third), BF16),
-            pltpu.VMEM((4, rows, third), BF16),
-            pltpu.SemaphoreType.DMA((10,)),
+            pltpu.SemaphoreType.DMA((8 + 4 * third // DH,)),
             pltpu.SemaphoreType.DMA((4,)),
         ],
         compiler_params=params(),
         cost_estimate=cost(1.1e10, 1e6),
-    )(where, qk, v, *sums, gains)
+    )(where, qk, v, *sums)
 
 
 def out_kernel(where_ref, state_ref, modes_ref, head_ref, *refs):
     attended, pieces = refs[:4], refs[4:12]
-    out_ref, att_in, group_ref, held_ref, state_in, modes_in, head_in_ref, out_buf, sem = refs[12:]
-    half = pieces[0].shape[0]
+    own_ref, sent_ref = refs[12:14]
+    att_in, group_ref, held_ref, state_in, modes_in, head_in_ref, own_buf, sent_buf, sem = refs[14:]
     side, pair, steps, own = (where_ref[j] for j in range(4))
     third = attended[0].shape[1]
+    half = pieces[0].shape[0]
 
     def window(j):
         return pl.ds(pl.multiple_of(j * third, third), third)
@@ -506,24 +506,32 @@
         part = att_in[j].astype(F32)
         part = jnp.where(side == 0, part, pltpu.roll(part, third // 2, 1)).astype(BF16)
         group_ref[:, window(lax.rem((own ^ j) + steps - pair, steps))] = part
-    for copy in loads[4:]:
-        copy.wait()
-    total = times(group_ref[...], held_ref[...])
+    for copy in loads[4:8]:
+        copy.wait()
+    total = times(group_ref[:, :half], held_ref[:half, :])
+    for copy in loads[8:]:
+        copy.wait()
+    total += times(group_ref[:, half:], held_ref[half:, :])
     block_out = (state_in[...].astype(F32) + modes_in[2] * total).astype(BF16)
     head_in = layer_norm(block_out.astype(F32)) * (1.0 + modes_in[4]) + modes_in[3]
-    out_buf[...] = times_turned(head_in_ref[...], head_in.astype(BF16))
-    for copy in load_all([(out_buf, out_ref)], sem):
+    velocity = times_turned(head_in_ref[...], head_in.astype(BF16))
+    channels = own_buf.shape[0]
+    core = lax.rem(own, 2)
+    own_buf[...] = jnp.where(core == 0, velocity[:channels], velocity[channels:])
+    sent_buf[...] = jnp.where(core == 0, velocity[channels:], velocity[:channels]).astype(BF16)
+    for copy in load_all([(own_buf, own_ref), (sent_buf, sent_ref)], sem):
         copy.wait()
 
 
 def project(where, state, modes, w_head, attended, pieces):
     rows, width = state.shape
     third = width // 4
+    channels = w_head.shape[0] // 2
     return pl.pallas_call(
         out_kernel,
-        out_shape=shape_of(w_head.shape[0], rows, dtype=F32),
+        out_shape=[shape_of(channels, rows, dtype=F32), shape_of(channels, rows)],
         in_specs=[SMEM] + [ANY] * 15,
-        out_specs=ANY,
+        out_specs=[ANY, ANY],
         scratch_shapes=[
             pltpu.VMEM((4, rows, third), BF16),
             pltpu.VMEM((rows, width), BF16),
@@ -531,7 +539,8 @@
             pltpu.VMEM(state.shape, BF16),
             pltpu.VMEM(modes.shape, F32),
             pltpu.VMEM(w_head.shape, BF16),
-            pltpu.VMEM((w_head.shape[0], rows), F32),
+            pltpu.VMEM((channels, rows), F32),
+            pltpu.VMEM((channels, rows), BF16),
             pltpu.SemaphoreType.DMA((15,)),
         ],
         compiler_params=params(),
@@ -539,14 +548,11 @@
     )(where, state, modes, w_head, *attended, *pieces)
 
 
-def updated_latent(velocity, latent, guidance, step_size, length, position):
-    rows = velocity.shape[1]
+def updated_latent(own, outgoing, latent, guidance, step_size, length, position):
+    rows = own.shape[1]
     branch = lax.axis_index("cfg")
     scale = guidance[0]
-    channels = velocity.shape[0] // 2
-    own = lax.dynamic_slice_in_dim(velocity, branch * channels, channels, 0)
-    outgoing = lax.dynamic_slice_in_dim(velocity, (1 - branch) * channels, channels, 0)
-    other = lax.ppermute(outgoing.astype(BF16), "cfg", SWAP).astype(outgoing.dtype)
+    other = lax.ppermute(outgoing, "cfg", SWAP).astype(own.dtype)
     cond = jnp.where(branch == 0, own, other)
     uncond = jnp.where(branch == 0, other, own)
     guided = uncond + scale * (cond - uncond)
@@ -590,12 +596,13 @@
     def ints(*values):
         return jnp.stack([jnp.asarray(value, jnp.int32) for value in values])
 
-    columns = cut_columns(ints(group), w_qkv, w_out)
     length = lengths[0]
     places = ints(side, pair, steps, group, length - position * rows, length - (1 - position) * rows)
     gains = jnp.stack([q_gain, k_gain])[:, None]
 
-    normed = normalise(places, state, modes)
+    columns, normed = entry(places, w_qkv, w_out, state, modes)
+    normed_y = lax.ppermute(normed, "seq", SWAP)
+    normed_c = lax.ppermute(normed, "cfg", SWAP)
 
     def step(mine, theirs, gates):
         now = after(mine[-1], *gates)
@@ -607,9 +614,7 @@
     cut, split = columns.shape[0] // 2, 3 * third
     low = theirs[0][cut:, :split]
     out_last = theirs[0][:, split:]
-    gates = [mine[1], theirs[0], low, out_last, normed, gains]
-    normed_y = lax.ppermute(after(normed, *gates), "seq", SWAP)
-    normed_c = lax.ppermute(after(normed, *gates), "cfg", SWAP)
+    gates = [mine[1], theirs[0], low, out_last, gains]
     step(mine, theirs, gates)
     gates = [mine[2], theirs[1]]
     step(mine, theirs, gates)
@@ -629,7 +634,7 @@
     packed_c = [lax.ppermute(part, "cfg", SWAP) for part in packed]
     packed_yc = [lax.ppermute(part, "cfg", SWAP) for part in packed_y]
 
-    qk_full, sums = last_scores(norms, acc_qk, late)
+    qk_full, sums = last_scores(places, norms, acc_qk, gains, late)
     v_full = last_values(norms, acc_v, late)
     diagonal = [(i, 3 - i) for i in range(4)]
     all_sums = [
@@ -639,7 +644,7 @@
         lax.ppermute(sums, ("cfg", "seq"), diagonal),
     ]
     v_full = after(v_full, packed_y[1], *packed_c, packed_yc[0])
-    heads = team_attention(places, qk_full, v_full, all_sums, gains)
+    heads = team_attention(places, qk_full, v_full, all_sums)
     attended = [
         heads[0],
         lax.ppermute(heads[2], "cfg", SWAP),
@@ -647,8 +652,8 @@
         lax.ppermute(heads[3], ("cfg", "seq"), diagonal),
     ]
     quarters = [part[j] for j in range(2) for part in (packed, packed_c, packed_y, packed_yc)]
-    velocity = project(places, state, modes, w_head.T, attended, quarters)
-    return updated_latent(velocity, latent, guidance, step_size, length, position)
+    own, outgoing = project(places, state, modes, w_head.T, attended, quarters)
+    return updated_latent(own, outgoing, latent, guidance, step_size, length, position)
 
 
 def by_team(mesh, arguments):

time: 128 us -> 117 us (0.914)
  waiting for transfers between devices: 49.6 us -> 43 us
  Pallas kernels: 42.2 us -> 38.5 us
  local copies, waits for them, and re-layouts: 6.32 us -> 4.55 us
    ppermute x3, waiting for transfers between devices: 15.5 us -> 0.01 us  [the longest x1 0.01 us: team_local(): normed_c = lax.ppermute(normed, 'cfg', SWAP)]
    ppermute x4, waiting for transfers between devices: 9.79 us -> 19 us  [across(): return lax.ppermute(piece, 'req', beside)]
    ppermute x3, starting transfers between devices: 9.31 us -> 12.2 us  [along(): return lax.ppermute(piece, 'req', up)]
    pallas_call x1, Pallas kernels: 9.51 us -> 7.35 us  [team_attention(): pl.pallas_call(heads_kernel, out_shape=[shape_of(rows, third)] * 4, in_sp...]
    ppermute x4, starting transfers between devices: 6.03 us -> 4.05 us  [across(): return lax.ppermute(piece, 'req', beside)]
    ppermute x3, starting transfers between devices: 1.89 us -> 3.59 us  [the longest x1 3.03 us: team_local(): normed_y = lax.ppermute(normed, 'seq', SWAP)]
    pallas_call x3 -> x2, Pallas kernels: 12.9 us -> 11.3 us  [the longest x1 7 us: project(): pl.pallas_call(out_kernel, out_shape=[shape_of(channels, rows, dtype=F32)...]
    ppermute x2, starting transfers between devices: 0.06 us -> 1.52 us  [back(): return lax.ppermute(piece, 'req', down)]
  transfers between devices with their start and end apart: 25 -> 25, of which waited for: 9 -> 12; matrix products, arithmetic and copies ran while one was open for 1% -> 1% of each run, Pallas kernels for 26% -> 23%
where the time goes in v3:
time: 117 us; the launch traced here: 116 us
  waiting for transfers between devices  43 us (37%)
  Pallas kernels  38.5 us (33%)
  starting transfers between devices  26.4 us (23%)
  local copies, waits for them, and re-layouts  4.55 us (4%)
  between operations  2.25 us (2%)
  other arithmetic  1.47 us (1%)
    ppermute x4, waiting for transfers between devices, across(): return lax.ppermute(piece, 'req', beside)  19 us
    ppermute x3, starting transfers between devices, along(): return lax.ppermute(piece, 'req', up)  12.2 us
    pallas_call x1, Pallas kernels, team_attention(): pl.pallas_call(heads_kernel, out_shape=[shape_of(rows, third)] * 4, in_sp...  7.35 us
    ppermute x3, waiting for transfers between devices, along(): return lax.ppermute(piece, 'req', up)  7.12 us
    pallas_call x1, Pallas kernels, project(): pl.pallas_call(out_kernel, out_shape=[shape_of(channels, rows, dtype=F32)...  7 us
    ppermute x1, waiting for transfers between devices, team_local(): lax.ppermute(heads[1], 'seq', SWAP)  6.85 us
    pallas_call x1, Pallas kernels, last_scores(): pl.pallas_call(functools.partial(scores_kernel, len(pieces)), out_shape=[...  6.63 us
    ppermute x2, waiting for transfers between devices, back(): return lax.ppermute(piece, 'req', down)  5.37 us
  transfers between devices with their start and end apart: 25, of which 12 were waited for; matrix products, arithmetic and copies ran while one was open for 1% of the time, Pallas kernels for 23%

profile of v3, /device:TPU:0, one launch (start us, length us, event | category | flops | bytes accessed | tf_op | source)
XLA Modules:
  0.0 116.2 jit_solution(13140473087716108371)
XLA Ops:
  0.7 0.6 stack.32.where_ref
  1.3 4.3 %shard_map.109 = (bf16[192,1536]{1,0:T(8,128)(2,1)}, bf16[288,1536]{1,0:T(8,128)(2,1)}) custom-call(s32[6]{0:T(128)} %stack.32.where_ref, bf16[192,4608]{1,0:T(8,128)(2,1)} %qkv_ref.1, bf16[192,1536]{1,0:T(8,128)(2,1)} %w_out_ref.1, bf16[288,1536]{1,0:T(8,128)(2,1)} %bitcast.24, f32[5,1,1536]{2,1,0:T(1,128)} %bitcast.27), custom_call_target="tpu_custom_call" | custom-call | flops 4000000000 | bytes 1000000 | tf_op jit(solution)/shard_map/pallas_call | solution.py:174
  5.6 3.0 %collective-permute-start = (bf16[288,1536]{1,0:T(8,128)(2,1)}, bf16[288,1536]{1,0:T(8,128)(2,1)S(1)}, u32[]{:S(2)}, u32[]{:S(2)}) collective-permute-start(bf16[288,1536]{1,0:T(8,128)(2,1)} %get-tuple-element.23.refs_0_), channel_id=1, source_target_pairs={{0,1},{1,0},{2,3},{3,2},{4,5},{5,4},{6,7},{7,6},{8,9},{9,8},{10,11... | collective-permute-start | bytes 2654216 | tf_op jit(solution)/shard_map/ppermute | solution.py:604
  8.7 1.5 %collective-permute-start.3 = (bf16[192,1536]{1,0:T(8,128)(2,1)}, bf16[192,1536]{1,0:T(8,128)(2,1)S(1)}, u32[]{:S(2)}, u32[]{:S(2)}) collective-permute-start(bf16[192,1536]{1,0:T(8,128)(2,1)} %get-tuple-element.24.refs_4_.refs_0_), channel_id=1, source_target_pairs={{0,2},{2,0},{4,6},{6,4},{8,10},{10,8},{12,14},{14,12},{1,3},{3,1},... | collective-permute-start | bytes 1769480 | tf_op jit(solution)/shard_map/ppermute | solution.py:594
  10.1 3.6 %collective-permute-start.4 = (bf16[192,1536]{1,0:T(8,128)(2,1)}, bf16[192,1536]{1,0:T(8,128)(2,1)S(1)}, u32[]{:S(2)}, u32[]{:S(2)}) collective-permute-start(bf16[192,1536]{1,0:T(8,128)(2,1)} %get-tuple-element.24.refs_4_.refs_0_), channel_id=1, source_target_pairs={{0,12},{2,14},{4,0},{6,2},{8,4},{10,6},{12,8},{14,10},{1,13},{3,15... | collective-permute-start | bytes 1769480 | tf_op jit(solution)/shard_map/ppermute | solution.py:588
  13.8 0.6 broadcast_in_dim.16.refs_5_
  14.4 9.2 %collective-permute-done.3.refs_5_.refs_1_ = bf16[192,1536]{1,0:T(8,128)(2,1)S(1)} collective-permute-done((bf16[192,1536]{1,0:T(8,128)(2,1)}, bf16[192,1536]{1,0:T(8,128)(2,1)S(1)}, u32[]{:S(2)}, u32[]{:S(2)}) %collective-permute-start.3) | collective-permute-done | bytes 589856 | tf_op jit(solution)/shard_map/ppermute | solution.py:594
  23.7 2.4 %collective-permute-done.4.refs_6_.refs_2_ = bf16[192,1536]{1,0:T(8,128)(2,1)S(1)} collective-permute-done((bf16[192,1536]{1,0:T(8,128)(2,1)}, bf16[192,1536]{1,0:T(8,128)(2,1)S(1)}, u32[]{:S(2)}, u32[]{:S(2)}) %collective-permute-start.4) | collective-permute-done | bytes 589856 | tf_op jit(solution)/shard_map/ppermute | solution.py:588
  26.1 0.5 collective-permute-start.5
  26.6 4.2 %collective-permute-start.6 = (bf16[192,1536]{1,0:T(8,128)(2,1)S(1)}, bf16[192,1536]{1,0:T(8,128)(2,1)}, u32[]{:S(2)}, u32[]{:S(2)}) collective-permute-start(bf16[192,1536]{1,0:T(8,128)(2,1)S(1)} %collective-permute-done.4.refs_6_.refs_2_), channel_id=1, source_target_pairs={{0,12},{2,14},{4,0},{6,2},{8,4},{10,6},{12,8},{14,10},{1,13},{3,15... | collective-permute-start | bytes 1769480 | tf_op jit(solution)/shard_map/ppermute | solution.py:588
  30.8 0.0 collective-permute-start.1
  30.8 0.0 collective-permute-done.refs_1_
  30.8 0.5 collective-permute-start.2
  31.3 8.4 %collective-permute-done.5.refs_7_.refs_3_ = bf16[192,1536]{1,0:T(8,128)(2,1)S(1)} collective-permute-done((bf16[192,1536]{1,0:T(8,128)(2,1)S(1)}, bf16[192,1536]{1,0:T(8,128)(2,1)S(1)}, u32[]{:S(2)}, u32[]{:S(2)}) %collective-permute-start.5) | collective-permute-done | bytes 589856 | tf_op jit(solution)/shard_map/ppermute | solution.py:594
  39.7 1.9 %collective-permute-done.6.refs_6_.refs_5_.refs_0_ = bf16[192,1536]{1,0:T(8,128)(2,1)} collective-permute-done((bf16[192,1536]{1,0:T(8,128)(2,1)S(1)}, bf16[192,1536]{1,0:T(8,128)(2,1)}, u32[]{:S(2)}, u32[]{:S(2)}) %collective-permute-start.6) | collective-permute-done | bytes 589856 | tf_op jit(solution)/shard_map/ppermute | solution.py:588
  41.6 1.5 %collective-permute-start.7 = (bf16[192,1536]{1,0:T(8,128)(2,1)}, bf16[192,1536]{1,0:T(8,128)(2,1)S(1)}, u32[]{:S(2)}, u32[]{:S(2)}) collective-permute-start(bf16[192,1536]{1,0:T(8,128)(2,1)} %collective-permute-done.6.refs_6_.refs_5_.refs_0_), channel_id=1, source_target_pairs={{0,2},{2,0},{4,6},{6,4},{8,10},{10,8},{12,14},{14,12},{1,3},{3,1},... | collective-permute-start | bytes 1769480 | tf_op jit(solution)/shard_map/ppermute | solution.py:594
  43.1 4.4 %collective-permute-start.8 = (bf16[192,1536]{1,0:T(8,128)(2,1)}, bf16[192,1536]{1,0:T(8,128)(2,1)S(1)}, u32[]{:S(2)}, u32[]{:S(2)}) collective-permute-start(bf16[192,1536]{1,0:T(8,128)(2,1)} %collective-permute-done.6.refs_6_.refs_5_.refs_0_), channel_id=1, source_target_pairs={{0,12},{2,14},{4,0},{6,2},{8,4},{10,6},{12,8},{14,10},{1,13},{3,15... | collective-permute-start | bytes 1769480 | tf_op jit(solution)/shard_map/ppermute | solution.py:588
  47.5 2.1 %shard_map.111.refs_4_ = bf16[768,384]{1,0:T(8,128)(2,1)} custom-call(bf16[192,1536]{1,0:T(8,128)(2,1)} %get-tuple-element.24.refs_4_.refs_0_, bf16[192,1536]{1,0:T(8,128)(2,1)} %copy-done, bf16[192,1536]{1,0:T(8,128)(2,1)} %copy-done.12, bf16[192,1536]{1,0:T(8,128)(2,1)} %copy-done.14), custom_call_target="tpu_custom_call" | custom-call | flops 3000000000 | bytes 1000000 | tf_op jit(solution)/shard_map/pallas_call | solution.py:208
  49.6 0.6 collective-permute-start.10
  50.2 0.0 collective-permute-done.1.refs_2_
  50.2 0.0 collective-permute-start.14
  50.2 0.0 collective-permute-done.2.refs_3_
  50.2 0.1 collective-permute-start.9
  50.2 0.8 copy-done.6
  51.1 5.2 %shard_map.110 = (bf16[4,288,768]{2,1,0:T(8,128)(2,1)}, bf16[4,288,384]{2,1,0:T(8,128)(2,1)}) custom-call(bf16[288,1536]{1,0:T(8,128)(2,1)} %get-tuple-element.23.refs_0_, bf16[288,1536]{1,0:T(8,128)(2,1)} %copy-done.5, bf16[288,1536]{1,0:T(8,128)(2,1)} %copy-done.6, bf16[288,1536]{1,0:T(8,128)(2,1)} %collective-permute-done.2.refs_3_, ...), custom_call_target="tpu_custom_call" | custom-call | flops 6000000000 | bytes 1000000 | tf_op jit(solution)/shard_map/pallas_call | solution.py:258
  56.3 2.8 %collective-permute-done.8.refs_8_.refs_7_.refs_2_ = bf16[192,1536]{1,0:T(8,128)(2,1)S(1)} collective-permute-done((bf16[192,1536]{1,0:T(8,128)(2,1)}, bf16[192,1536]{1,0:T(8,128)(2,1)S(1)}, u32[]{:S(2)}, u32[]{:S(2)}) %collective-permute-start.8) | collective-permute-done | bytes 589856 | tf_op jit(solution)/shard_map/ppermute | solution.py:588
  59.1 2.1 %collective-permute-done.9.refs_3_ = bf16[192,384]{1,0:T(8,128)(2,1)S(1)} collective-permute-done((bf16[192,384]{1,0:T(8,128)(2,1)S(1)}, bf16[192,384]{1,0:T(8,128)(2,1)S(1)}, u32[]{:S(2)}, u32[]{:S(2)}) %collective-permute-start.9) | collective-permute-done | bytes 147488 | tf_op jit(solution)/shard_map/ppermute | solution.py:591
  61.3 0.0 collective-permute-done.7.refs_7_.refs_6_.refs_1_
  61.3 0.4 collective-permute-done.10.refs_6_
  61.7 0.5 collective-permute-start.11
  62.2 1.5 %collective-permute-start.12 = (bf16[96,1152]{1,0:T(8,128)(2,1)S(1)}, bf16[96,1152]{1,0:T(8,128)(2,1)S(1)}, u32[]{:S(2)}, u32[]{:S(2)}) collective-permute-start(bf16[96,1152]{1,0:T(8,128)(2,1)S(1)} %slice.12), channel_id=1, source_target_pairs={{0,4},{2,6},{4,8},{6,10},{8,12},{10,14},{12,0},{14,2},{1,5},{3,7},... | collective-permute-start | bytes 663560 | tf_op jit(solution)/shard_map/ppermute | solution.py:591
  63.7 2.0 %shard_map.114.refs_8_ = bf16[768,384]{1,0:T(8,128)(2,1)} custom-call(bf16[192,1536]{1,0:T(8,128)(2,1)} %collective-permute-done.6.refs_6_.refs_5_.refs_0_, bf16[192,1536]{1,0:T(8,128)(2,1)} %copy-done.11, bf16[192,1536]{1,0:T(8,128)(2,1)} %copy-done.1, bf16[192,384]{1,0:T(8,128)(2,1)} %copy-done.20), custom_call_target="tpu_custom_call" | custom-call | flops 3000000000 | bytes 1000000 | tf_op jit(solution)/shard_map/pallas_call | solution.py:208
  65.7 0.6 collective-permute-start.13
  66.3 0.0 collective-permute-start.15
  66.3 1.4 %collective-permute-done.11.refs_9_.refs_8_ = bf16[96,1152]{1,0:T(8,128)(2,1)S(1)} collective-permute-done((bf16[96,1152]{1,0:T(8,128)(2,1)S(1)}, bf16[96,1152]{1,0:T(8,128)(2,1)S(1)}, u32[]{:S(2)}, u32[]{:S(2)}) %collective-permute-start.11) | collective-permute-done | bytes 221216 | tf_op jit(solution)/shard_map/ppermute | solution.py:594
  67.6 0.0 collective-permute-start.16
  67.6 3.2 %collective-permute-done.12.refs_10_.refs_9_ = bf16[96,1152]{1,0:T(8,128)(2,1)S(1)} collective-permute-done((bf16[96,1152]{1,0:T(8,128)(2,1)S(1)}, bf16[96,1152]{1,0:T(8,128)(2,1)S(1)}, u32[]{:S(2)}, u32[]{:S(2)}) %collective-permute-start.12) | collective-permute-done | bytes 221216 | tf_op jit(solution)/shard_map/ppermute | solution.py:591
  70.9 0.7 copy-done.16
  71.6 6.6 %shard_map.112 = (bf16[4,288,768]{2,1,0:T(8,128)(2,1)}, f32[4,8,288]{2,1,0:T(8,128)}) custom-call(s32[6]{0:T(128)} %stack.32.where_ref, bf16[288,1536]{1,0:T(8,128)(2,1)} %get-tuple-element.23.refs_0_, bf16[288,1536]{1,0:T(8,128)(2,1)} %copy-done.5, bf16[288,1536]{1,0:T(8,128)(2,1)} %copy-done.6, bf16[288,1536]{1,0:T(8,128)(2,1)} %collective-permute-done.2.refs_3_, ...), custom_call_target="tpu_custom_call" | custom-call | flops 6000000000 | bytes 1000000 | tf_op jit(solution)/shard_map/pallas_call | solution.py:324
  78.2 0.6 collective-permute-start.17
  78.8 0.0 collective-permute-done.14.refs_5_
  78.8 0.0 collective-permute-start.18
  78.8 0.8 collective-permute-done.13.refs_10_
  79.6 0.8 collective-permute-start.19
  80.4 3.9 %shard_map.113.v_ref = bf16[4,288,384]{2,1,0:T(8,128)(2,1)} custom-call(bf16[288,1536]{1,0:T(8,128)(2,1)} %get-tuple-element.23.refs_0_, bf16[288,1536]{1,0:T(8,128)(2,1)} %copy-done.5, bf16[288,1536]{1,0:T(8,128)(2,1)} %copy-done.6, bf16[288,1536]{1,0:T(8,128)(2,1)} %collective-permute-done.2.refs_3_, bf16[4,288,384]{2,1,0:T(8,128)(2,1)} %get-tuple-element.29.refs_4_, ...), custom_call_target="tpu_custom_call" | custom-call | flops 4000000000 | bytes 1000000 | tf_op jit(solution)/shard_map/pallas_call | solution.py:373
  84.4 0.0 collective-permute-done.15.refs_9_
  84.4 0.0 collective-permute-done.16.refs_7_
  84.4 0.1 collective-permute-start.23
  84.5 0.0 collective-permute-done.17.s1_ref
  84.6 0.0 collective-permute-done.19.s3_ref
  84.6 0.8 copy-done.21
  85.4 0.0 copy-done.23
  85.4 7.4 %shard_map.115 = (bf16[288,384]{1,0:T(8,128)(2,1)}, bf16[288,384]{1,0:T(8,128)(2,1)}, bf16[288,384]{1,0:T(8,128)(2,1)}, bf16[288,384]{1,0:T(8,128)(2,1)}) custom-call(s32[6]{0:T(128)} %stack.32.where_ref, bf16[4,288,768]{2,1,0:T(8,128)(2,1)} %get-tuple-element.32.qk_ref, bf16[4,288,384]{2,1,0:T(8,128)(2,1)} %shard_map.113.v_ref, ...), custom_call_target="tpu_custom_call" | custom-call | flops 11000000512 | bytes 1000000 | tf_op jit(solution)/shard_map/pallas_call | solution.py:468
  92.8 0.3 collective-permute-start.20
  93.1 1.0 collective-permute-start.21
  94.1 0.6 collective-permute-start.22
  94.7 6.9 %collective-permute-done.21.refs_2_ = bf16[288,384]{1,0:T(8,128)(2,1)S(1)} collective-permute-done((bf16[288,384]{1,0:T(8,128)(2,1)}, bf16[288,384]{1,0:T(8,128)(2,1)S(1)}, u32[]{:S(2)}, u32[]{:S(2)}) %collective-permute-start.21) | collective-permute-done | bytes 221216 | tf_op jit(solution)/shard_map/ppermute | solution.py:651
  101.6 3.4 %collective-permute-done.22.refs_3_ = bf16[288,384]{1,0:T(8,128)(2,1)S(1)} collective-permute-done((bf16[288,384]{1,0:T(8,128)(2,1)}, bf16[288,384]{1,0:T(8,128)(2,1)S(1)}, u32[]{:S(2)}, u32[]{:S(2)}) %collective-permute-start.22) | collective-permute-done | bytes 221216 | tf_op jit(solution)/shard_map/ppermute | solution.py:652
  105.0 0.0 collective-permute-done.23.refs_11_
  105.0 0.6 copy-done.19
  105.6 0.2 copy-done.13
  105.9 7.0 %shard_map.116 = (f32[32,288]{1,0:T(8,128)}, bf16[32,288]{1,0:T(8,128)(2,1)}) custom-call(s32[6]{0:T(128)} %stack.32.where_ref, bf16[288,1536]{1,0:T(8,128)(2,1)} %bitcast.25, f32[5,1,1536]{2,1,0:T(1,128)} %bitcast.28, bf16[64,1536]{1,0:T(8,128)(2,1)} %bitcast.26, bf16[288,384]{1,0:T(8,128)(2,1)} %get-tuple-element.35.refs_0_, bf16[288,384]{1,0:T(8,128)(2,1)} %copy-done.17, ...), custom_call_target="tpu_custom_call" | custom-call | flops 8000000000 | bytes 1000000 | tf_op jit(solution)/shard_map/pallas_call | solution.py:530
  112.9 0.6 collective-permute-start.24
  114.7 1.4 %fusion.4 = f32[1,288,32]{1,2,0:T(8,128)} fusion(f32[32,288]{1,0:T(8,128)} %get-tuple-element.40, bf16[32,288]{1,0:T(8,128)(2,1)S(1)} %collective-permute-done.24, f32[1,288,32]{1,2,0:T(8,128)S(1)} %copy-done.2, f32[]{:T(128)} %bitcast.22, f32[]{:T(128)} %bitcast.23, pred[]{:T(512)S(6)} %eq.6, pred[288]{0:T(512)(128)(4,1)S(1)} %add_compare_fusion), kind=kLoop, calls=%fused_computation.7 | loop fusion | flops 82944 | bytes 129321 | tf_op jit(solution)/shard_map/broadcast_in_dim | solution.py:562
  (52 shorter events, 0.2 us)
Async XLA Ops:
  1.3 12.5 %copy-start.3 = (f32[1536]{0:T(1024)S(1)}, f32[1536]{0:T(1024)}, u32[]{:S(2)}) copy-start(f32[1536]{0:T(1024)} %param.17) | copy-start | bytes 18436
  1.3 12.5 %copy-start.4 = (f32[1536]{0:T(1024)S(1)}, f32[1536]{0:T(1024)}, u32[]{:S(2)}) copy-start(f32[1536]{0:T(1024)} %param.16) | copy-start | bytes 18436
  5.6 25.2 %collective-permute-start = (bf16[288,1536]{1,0:T(8,128)(2,1)}, bf16[288,1536]{1,0:T(8,128)(2,1)S(1)}, u32[]{:S(2)}, u32[]{:S(2)}) collective-permute-start(bf16[288,1536]{1,0:T(8,128)(2,1)} %get-tuple-element.23.refs_0_), channel_id=1, source_target_pairs={{0,1},{1,0},{2,3},{3,2},{4,5},{5,4},{6,7},{7,6},{8,9},{9,8},{10,11... | collective-permute-start | bytes 2654216 | tf_op jit(solution)/shard_map/ppermute | solution.py:604
  8.7 15.0 %collective-permute-start.3 = (bf16[192,1536]{1,0:T(8,128)(2,1)}, bf16[192,1536]{1,0:T(8,128)(2,1)S(1)}, u32[]{:S(2)}, u32[]{:S(2)}) collective-permute-start(bf16[192,1536]{1,0:T(8,128)(2,1)} %get-tuple-element.24.refs_4_.refs_0_), channel_id=1, source_target_pairs={{0,2},{2,0},{4,6},{6,4},{8,10},{10,8},{12,14},{14,12},{1,3},{3,1},... | collective-permute-start | bytes 1769480 | tf_op jit(solution)/shard_map/ppermute | solution.py:594
  10.1 15.9 %collective-permute-start.4 = (bf16[192,1536]{1,0:T(8,128)(2,1)}, bf16[192,1536]{1,0:T(8,128)(2,1)S(1)}, u32[]{:S(2)}, u32[]{:S(2)}) collective-permute-start(bf16[192,1536]{1,0:T(8,128)(2,1)} %get-tuple-element.24.refs_4_.refs_0_), channel_id=1, source_target_pairs={{0,12},{2,14},{4,0},{6,2},{8,4},{10,6},{12,8},{14,10},{1,13},{3,15... | collective-permute-start | bytes 1769480 | tf_op jit(solution)/shard_map/ppermute | solution.py:588
  23.7 23.9 %copy-start = (bf16[192,1536]{1,0:T(8,128)(2,1)}, bf16[192,1536]{1,0:T(8,128)(2,1)S(1)}, u32[]{:S(2)}) copy-start(bf16[192,1536]{1,0:T(8,128)(2,1)S(1)} %collective-permute-done.3.refs_5_.refs_1_) | copy-start | bytes 1769476
  26.1 15.5 %copy-start.12 = (bf16[192,1536]{1,0:T(8,128)(2,1)}, bf16[192,1536]{1,0:T(8,128)(2,1)S(1)}, u32[]{:S(2)}) copy-start(bf16[192,1536]{1,0:T(8,128)(2,1)S(1)} %collective-permute-done.4.refs_6_.refs_2_) | copy-start | bytes 1769476
  26.1 13.6 %collective-permute-start.5 = (bf16[192,1536]{1,0:T(8,128)(2,1)S(1)}, bf16[192,1536]{1,0:T(8,128)(2,1)S(1)}, u32[]{:S(2)}, u32[]{:S(2)}) collective-permute-start(bf16[192,1536]{1,0:T(8,128)(2,1)S(1)} %collective-permute-done.4.refs_6_.refs_2_), channel_id=1, source_target_pairs={{0,2},{2,0},{4,6},{6,4},{8,10},{10,8},{12,14},{14,12},{1,3},{3,1},... | collective-permute-start | bytes 1769480 | tf_op jit(solution)/shard_map/ppermute | solution.py:594
  26.6 15.0 %collective-permute-start.6 = (bf16[192,1536]{1,0:T(8,128)(2,1)S(1)}, bf16[192,1536]{1,0:T(8,128)(2,1)}, u32[]{:S(2)}, u32[]{:S(2)}) collective-permute-start(bf16[192,1536]{1,0:T(8,128)(2,1)S(1)} %collective-permute-done.4.refs_6_.refs_2_), channel_id=1, source_target_pairs={{0,12},{2,14},{4,0},{6,2},{8,4},{10,6},{12,8},{14,10},{1,13},{3,15... | collective-permute-start | bytes 1769480 | tf_op jit(solution)/shard_map/ppermute | solution.py:588
  30.8 19.4 %collective-permute-start.1 = (bf16[288,1536]{1,0:T(8,128)(2,1)}, bf16[288,1536]{1,0:T(8,128)(2,1)S(1)}, u32[]{:S(2)}, u32[]{:S(2)}) collective-permute-start(bf16[288,1536]{1,0:T(8,128)(2,1)} %get-tuple-element.23.refs_0_), channel_id=1, source_target_pairs={{0,16},{16,0},{1,17},{17,1},{2,18},{18,2},{3,19},{19,3},{4,20},{20... | collective-permute-start | bytes 2654216 | tf_op jit(solution)/shard_map/ppermute | solution.py:605
  30.8 18.8 %copy-start.5 = (bf16[288,1536]{1,0:T(8,128)(2,1)}, bf16[288,1536]{1,0:T(8,128)(2,1)S(1)}, u32[]{:S(2)}) copy-start(bf16[288,1536]{1,0:T(8,128)(2,1)S(1)} %collective-permute-done.refs_1_) | copy-start | bytes 2654212
  30.8 19.4 %collective-permute-start.2 = (bf16[288,1536]{1,0:T(8,128)(2,1)S(1)}, bf16[288,1536]{1,0:T(8,128)(2,1)}, u32[]{:S(2)}, u32[]{:S(2)}) collective-permute-start(bf16[288,1536]{1,0:T(8,128)(2,1)S(1)} %collective-permute-done.refs_1_), channel_id=1, source_target_pairs={{0,16},{16,0},{1,17},{17,1},{2,18},{18,2},{3,19},{19,3},{4,20},{20... | collective-permute-start | bytes 2654216 | tf_op jit(solution)/shard_map/ppermute | solution.py:622
  39.7 3.4 %copy-start.14 = (bf16[192,1536]{1,0:T(8,128)(2,1)}, bf16[192,1536]{1,0:T(8,128)(2,1)S(1)}, u32[]{:S(2)}) copy-start(bf16[192,1536]{1,0:T(8,128)(2,1)S(1)} %collective-permute-done.5.refs_7_.refs_3_) | copy-start | bytes 1769476
  41.6 19.6 %collective-permute-start.7 = (bf16[192,1536]{1,0:T(8,128)(2,1)}, bf16[192,1536]{1,0:T(8,128)(2,1)S(1)}, u32[]{:S(2)}, u32[]{:S(2)}) collective-permute-start(bf16[192,1536]{1,0:T(8,128)(2,1)} %collective-permute-done.6.refs_6_.refs_5_.refs_0_), channel_id=1, source_target_pairs={{0,2},{2,0},{4,6},{6,4},{8,10},{10,8},{12,14},{14,12},{1,3},{3,1},... | collective-permute-start | bytes 1769480 | tf_op jit(solution)/shard_map/ppermute | solution.py:594
  43.1 16.0 %collective-permute-start.8 = (bf16[192,1536]{1,0:T(8,128)(2,1)}, bf16[192,1536]{1,0:T(8,128)(2,1)S(1)}, u32[]{:S(2)}, u32[]{:S(2)}) collective-permute-start(bf16[192,1536]{1,0:T(8,128)(2,1)} %collective-permute-done.6.refs_6_.refs_5_.refs_0_), channel_id=1, source_target_pairs={{0,12},{2,14},{4,0},{6,2},{8,4},{10,6},{12,8},{14,10},{1,13},{3,15... | collective-permute-start | bytes 1769480 | tf_op jit(solution)/shard_map/ppermute | solution.py:588
  49.6 12.1 %collective-permute-start.10 = (bf16[768,384]{1,0:T(8,128)(2,1)}, bf16[768,384]{1,0:T(8,128)(2,1)S(1)}, u32[]{:S(2)}, u32[]{:S(2)}) collective-permute-start(bf16[768,384]{1,0:T(8,128)(2,1)} %shard_map.111.refs_4_), channel_id=1, source_target_pairs={{0,1},{1,0},{2,3},{3,2},{4,5},{5,4},{6,7},{7,6},{8,9},{9,8},{10,11... | collective-permute-start | bytes 1769480 | tf_op jit(solution)/shard_map/ppermute | solution.py:626
  50.2 0.9 copy-start.6
  50.2 28.6 %collective-permute-start.14 = (bf16[768,384]{1,0:T(8,128)(2,1)}, bf16[768,384]{1,0:T(8,128)(2,1)}, u32[]{:S(2)}, u32[]{:S(2)}) collective-permute-start(bf16[768,384]{1,0:T(8,128)(2,1)} %shard_map.111.refs_4_), channel_id=1, source_target_pairs={{0,16},{16,0},{1,17},{17,1},{2,18},{18,2},{3,19},{19,3},{4,20},{20... | collective-permute-start | bytes 1769480 | tf_op jit(solution)/shard_map/ppermute | solution.py:634
  50.2 11.1 %collective-permute-start.9 = (bf16[192,384]{1,0:T(8,128)(2,1)S(1)}, bf16[192,384]{1,0:T(8,128)(2,1)S(1)}, u32[]{:S(2)}, u32[]{:S(2)}) collective-permute-start(bf16[192,384]{1,0:T(8,128)(2,1)S(1)} %slice.13), channel_id=1, source_target_pairs={{0,4},{2,6},{4,8},{6,10},{8,12},{10,14},{12,0},{14,2},{1,5},{3,7},... | collective-permute-start | bytes 442376 | tf_op jit(solution)/shard_map/ppermute | solution.py:591
  59.1 4.6 %copy-start.1 = (bf16[192,1536]{1,0:T(8,128)(2,1)}, bf16[192,1536]{1,0:T(8,128)(2,1)S(1)}, u32[]{:S(2)}) copy-start(bf16[192,1536]{1,0:T(8,128)(2,1)S(1)} %collective-permute-done.8.refs_8_.refs_7_.refs_2_) | copy-start | bytes 1769476
  61.3 2.4 %copy-start.20 = (bf16[192,384]{1,0:T(8,128)(2,1)}, bf16[192,384]{1,0:T(8,128)(2,1)S(1)}, u32[]{:S(2)}) copy-start(bf16[192,384]{1,0:T(8,128)(2,1)S(1)} %collective-permute-done.9.refs_3_) | copy-start | bytes 442372
  61.3 2.4 %copy-start.11 = (bf16[192,1536]{1,0:T(8,128)(2,1)}, bf16[192,1536]{1,0:T(8,128)(2,1)S(1)}, u32[]{:S(2)}) copy-start(bf16[192,1536]{1,0:T(8,128)(2,1)S(1)} %collective-permute-done.7.refs_7_.refs_6_.refs_1_) | copy-start | bytes 1769476
  61.7 5.9 %copy-start.7 = (bf16[768,384]{1,0:T(8,128)(2,1)}, bf16[768,384]{1,0:T(8,128)(2,1)S(1)}, u32[]{:S(2)}) copy-start(bf16[768,384]{1,0:T(8,128)(2,1)S(1)} %collective-permute-done.10.refs_6_) | copy-start | bytes 1769476
  61.7 5.9 %collective-permute-start.11 = (bf16[96,1152]{1,0:T(8,128)(2,1)S(1)}, bf16[96,1152]{1,0:T(8,128)(2,1)S(1)}, u32[]{:S(2)}, u32[]{:S(2)}) collective-permute-start(bf16[96,1152]{1,0:T(8,128)(2,1)S(1)} %slice.14), channel_id=1, source_target_pairs={{0,2},{2,0},{4,6},{6,4},{8,10},{10,8},{12,14},{14,12},{1,3},{3,1},... | collective-permute-start | bytes 663560 | tf_op jit(solution)/shard_map/ppermute | solution.py:594
  62.2 8.6 %collective-permute-start.12 = (bf16[96,1152]{1,0:T(8,128)(2,1)S(1)}, bf16[96,1152]{1,0:T(8,128)(2,1)S(1)}, u32[]{:S(2)}, u32[]{:S(2)}) collective-permute-start(bf16[96,1152]{1,0:T(8,128)(2,1)S(1)} %slice.12), channel_id=1, source_target_pairs={{0,4},{2,6},{4,8},{6,10},{8,12},{10,14},{12,0},{14,2},{1,5},{3,7},... | collective-permute-start | bytes 663560 | tf_op jit(solution)/shard_map/ppermute | solution.py:591
  65.7 13.9 %collective-permute-start.13 = (bf16[768,384]{1,0:T(8,128)(2,1)}, bf16[768,384]{1,0:T(8,128)(2,1)S(1)}, u32[]{:S(2)}, u32[]{:S(2)}) collective-permute-start(bf16[768,384]{1,0:T(8,128)(2,1)} %shard_map.114.refs_8_), channel_id=1, source_target_pairs={{0,1},{1,0},{2,3},{3,2},{4,5},{5,4},{6,7},{7,6},{8,9},{9,8},{10,11... | collective-permute-start | bytes 1769480 | tf_op jit(solution)/shard_map/ppermute | solution.py:633
  66.3 18.1 %collective-permute-start.15 = (bf16[768,384]{1,0:T(8,128)(2,1)}, bf16[768,384]{1,0:T(8,128)(2,1)S(1)}, u32[]{:S(2)}, u32[]{:S(2)}) collective-permute-start(bf16[768,384]{1,0:T(8,128)(2,1)} %shard_map.114.refs_8_), channel_id=1, source_target_pairs={{0,16},{16,0},{1,17},{17,1},{2,18},{18,2},{3,19},{19,3},{4,20},{20... | collective-permute-start | bytes 1769480 | tf_op jit(solution)/shard_map/ppermute | solution.py:634
  67.6 3.3 %copy-start.15 = (bf16[96,1152]{1,0:T(8,128)(2,1)}, bf16[96,1152]{1,0:T(8,128)(2,1)S(1)}, u32[]{:S(2)}) copy-start(bf16[96,1152]{1,0:T(8,128)(2,1)S(1)} %collective-permute-done.11.refs_9_.refs_8_) | copy-start | bytes 663556
  67.6 16.8 %collective-permute-start.16 = (bf16[768,384]{1,0:T(8,128)(2,1)S(1)}, bf16[768,384]{1,0:T(8,128)(2,1)S(1)}, u32[]{:S(2)}, u32[]{:S(2)}) collective-permute-start(bf16[768,384]{1,0:T(8,128)(2,1)S(1)} %collective-permute-done.10.refs_6_), channel_id=1, source_target_pairs={{0,16},{16,0},{1,17},{17,1},{2,18},{18,2},{3,19},{19,3},{4,20},{20... | collective-permute-start | bytes 1769480 | tf_op jit(solution)/shard_map/ppermute | solution.py:635
  70.9 0.7 copy-start.16
  78.2 6.3 %collective-permute-start.17 = (f32[4,8,288]{2,1,0:T(8,128)}, f32[4,8,288]{2,1,0:T(8,128)S(1)}, u32[]{:S(2)}, u32[]{:S(2)}) collective-permute-start(f32[4,8,288]{2,1,0:T(8,128)} %get-tuple-element.34.s0_ref), channel_id=1, source_target_pairs={{0,1},{1,0},{2,3},{3,2},{4,5},{5,4},{6,7},{7,6},{8,9},{9,8},{10,11... | collective-permute-start | bytes 110600 | tf_op jit(solution)/shard_map/ppermute | solution.py:642
  78.8 5.8 %collective-permute-start.18 = (f32[4,8,288]{2,1,0:T(8,128)}, f32[4,8,288]{2,1,0:T(8,128)S(1)}, u32[]{:S(2)}, u32[]{:S(2)}) collective-permute-start(f32[4,8,288]{2,1,0:T(8,128)} %get-tuple-element.34.s0_ref), channel_id=1, source_target_pairs={{0,16},{16,0},{1,17},{17,1},{2,18},{18,2},{3,19},{19,3},{4,20},{20... | collective-permute-start | bytes 110600 | tf_op jit(solution)/shard_map/ppermute | solution.py:643
  79.6 4.8 %copy-start.8 = (bf16[768,384]{1,0:T(8,128)(2,1)}, bf16[768,384]{1,0:T(8,128)(2,1)S(1)}, u32[]{:S(2)}) copy-start(bf16[768,384]{1,0:T(8,128)(2,1)S(1)} %collective-permute-done.13.refs_10_) | copy-start | bytes 1769476
  79.6 4.9 %collective-permute-start.19 = (f32[4,8,288]{2,1,0:T(8,128)}, f32[4,8,288]{2,1,0:T(8,128)S(1)}, u32[]{:S(2)}, u32[]{:S(2)}) collective-permute-start(f32[4,8,288]{2,1,0:T(8,128)} %get-tuple-element.34.s0_ref), channel_id=1, source_target_pairs={{0,17},{1,16},{16,1},{17,0},{2,19},{3,18},{18,3},{19,2},{4,21},{5,... | collective-permute-start | bytes 110600 | tf_op jit(solution)/shard_map/ppermute | solution.py:644
  84.4 8.4 %copy-start.9 = (bf16[768,384]{1,0:T(8,128)(2,1)}, bf16[768,384]{1,0:T(8,128)(2,1)S(1)}, u32[]{:S(2)}) copy-start(bf16[768,384]{1,0:T(8,128)(2,1)S(1)} %collective-permute-done.15.refs_9_) | copy-start | bytes 1769476
  84.4 8.4 %copy-start.10 = (bf16[768,384]{1,0:T(8,128)(2,1)}, bf16[768,384]{1,0:T(8,128)(2,1)S(1)}, u32[]{:S(2)}) copy-start(bf16[768,384]{1,0:T(8,128)(2,1)S(1)} %collective-permute-done.16.refs_7_) | copy-start | bytes 1769476
  84.4 20.6 %collective-permute-start.23 = (bf16[768,384]{1,0:T(8,128)(2,1)S(1)}, bf16[768,384]{1,0:T(8,128)(2,1)S(1)}, u32[]{:S(2)}, u32[]{:S(2)}) collective-permute-start(bf16[768,384]{1,0:T(8,128)(2,1)S(1)} %collective-permute-done.13.refs_10_), channel_id=1, source_target_pairs={{0,16},{16,0},{1,17},{17,1},{2,18},{18,2},{3,19},{19,3},{4,20},{20... | collective-permute-start | bytes 1769480 | tf_op jit(solution)/shard_map/ppermute | solution.py:635
  84.6 0.8 copy-start.21
  84.6 0.8 copy-start.22
  84.6 0.8 copy-start.23
  92.8 1.9 %collective-permute-start.20 = (bf16[288,384]{1,0:T(8,128)(2,1)}, bf16[288,384]{1,0:T(8,128)(2,1)S(1)}, u32[]{:S(2)}, u32[]{:S(2)}) collective-permute-start(bf16[288,384]{1,0:T(8,128)(2,1)} %get-tuple-element.36), channel_id=1, source_target_pairs={{0,16},{16,0},{1,17},{17,1},{2,18},{18,2},{3,19},{19,3},{4,20},{20... | collective-permute-start | bytes 663560 | tf_op jit(solution)/shard_map/ppermute | solution.py:650
  93.1 8.5 %collective-permute-start.21 = (bf16[288,384]{1,0:T(8,128)(2,1)}, bf16[288,384]{1,0:T(8,128)(2,1)S(1)}, u32[]{:S(2)}, u32[]{:S(2)}) collective-permute-start(bf16[288,384]{1,0:T(8,128)(2,1)} %get-tuple-element.37), channel_id=1, source_target_pairs={{0,1},{1,0},{2,3},{3,2},{4,5},{5,4},{6,7},{7,6},{8,9},{9,8},{10,11... | collective-permute-start | bytes 663560 | tf_op jit(solution)/shard_map/ppermute | solution.py:651
  94.1 10.8 %collective-permute-start.22 = (bf16[288,384]{1,0:T(8,128)(2,1)}, bf16[288,384]{1,0:T(8,128)(2,1)S(1)}, u32[]{:S(2)}, u32[]{:S(2)}) collective-permute-start(bf16[288,384]{1,0:T(8,128)(2,1)} %get-tuple-element.38), channel_id=1, source_target_pairs={{0,17},{1,16},{16,1},{17,0},{2,19},{3,18},{18,3},{19,2},{4,21},{5,... | collective-permute-start | bytes 663560 | tf_op jit(solution)/shard_map/ppermute | solution.py:652
  94.7 10.3 %copy-start.17 = (bf16[288,384]{1,0:T(8,128)(2,1)}, bf16[288,384]{1,0:T(8,128)(2,1)S(1)}, u32[]{:S(2)}) copy-start(bf16[288,384]{1,0:T(8,128)(2,1)S(1)} %collective-permute-done.20.refs_1_) | copy-start | bytes 663556
  101.6 3.4 %copy-start.18 = (bf16[288,384]{1,0:T(8,128)(2,1)}, bf16[288,384]{1,0:T(8,128)(2,1)S(1)}, u32[]{:S(2)}) copy-start(bf16[288,384]{1,0:T(8,128)(2,1)S(1)} %collective-permute-done.21.refs_2_) | copy-start | bytes 663556
  105.0 0.7 copy-start.19
  105.0 0.9 copy-start.13
  105.9 8.9 %copy-start.2 = (f32[1,288,32]{1,2,0:T(8,128)S(1)}, f32[1,288,32]{1,2,0:T(8,128)}, u32[]{:S(2)}) copy-start(f32[1,288,32]{1,2,0:T(8,128)} %param.12) | copy-start | bytes 110596
  112.9 1.9 %collective-permute-start.24 = (bf16[32,288]{1,0:T(8,128)(2,1)}, bf16[32,288]{1,0:T(8,128)(2,1)S(1)}, u32[]{:S(2)}, u32[]{:S(2)}) collective-permute-start(bf16[32,288]{1,0:T(8,128)(2,1)} %get-tuple-element.39), channel_id=1, source_target_pairs={{0,16},{16,0},{1,17},{17,1},{2,18},{18,2},{3,19},{19,3},{4,20},{20... | collective-permute-start | bytes 55304 | tf_op jit(solution)/shard_map/ppermute | solution.py:555

commit v4 on v3

--- a/solution.py
+++ b/solution.py
@@ -142,39 +142,54 @@
     return copies
 
 
-def entry_kernel(where_ref, qkv_ref, w_out_ref, state_ref, modes_ref, cut_ref, norm_ref, *scratch):
-    cut_buf, state_in, modes_in, full_ref, norm_buf, sem = scratch
-    side, pair, steps, group = (where_ref[j] for j in range(4))
+def places():
+    place = lax.axis_index("req")
+    group = 2 * lax.axis_index("seq") + lax.axis_index("cfg")
+    return lax.rem(place, 2), place // 2, lax.axis_size("req") // 2, group
+
+
+def window(j, size):
+    return pl.ds(pl.multiple_of(j * size, size), size)
+
+
+def scaled_norm(values, shift, scale):
+    centered = values - jnp.mean(values, axis=-1, keepdims=True)
+    inverse = lax.rsqrt(jnp.mean(centered * centered, axis=-1, keepdims=True) + 1e-06)
+    return centered * inverse * (1.0 + scale) + shift
+
+
+def entry_kernel(qkv_ref, w_out_ref, state_ref, modes_ref, cut_ref, norm_ref, *scratch):
+    cut_buf, state_in, modes_in, full_ref, norm_buf, sem, out_sem = scratch
+    side, pair, steps, group = places()
     third = cut_ref.shape[1] // 4
-    width = 4 * third
-    pairs = []
-    for j in range(4):
-        source_ref, base = (qkv_ref, j * width) if j < 3 else (w_out_ref, 0)
-        source = source_ref.at[:, pl.ds(pl.multiple_of(base + group * third, third), third)]
-        pairs.append((source, cut_buf.at[:, j * third : (j + 1) * third]))
-    loads = load_all([(state_ref, state_in), (modes_ref, modes_in)] + pairs, sem)
+    loads = [(state_ref, state_in), (modes_ref, modes_in)]
+    for j in range(3):
+        loads.append((qkv_ref.at[:, window(4 * j + group, third)], cut_buf.at[:, j * third : (j + 1) * third]))
+    loads.append((w_out_ref.at[:, window(group, third)], cut_buf.at[:, 3 * third :]))
+    loads = load_all(loads, sem)
     for copy in loads[:2]:
         copy.wait()
-    full_ref[...] = layer_norm(state_in[...].astype(F32)) * (1.0 + modes_in[1]) + modes_in[0]
+    full_ref[...] = scaled_norm(state_in[...].astype(F32), modes_in[0], modes_in[1])
     for copy in loads[2:]:
         copy.wait()
-    store = load_all([(cut_buf, cut_ref)], sem)
+    stores = [pltpu.make_async_copy(cut_buf, cut_ref, out_sem.at[0])]
+    stores[0].start()
     count = 4
     for k in range(count):
-        owner = lax.rem(pair + k, steps)
-        part = full_ref[:, pl.ds(pl.multiple_of(owner * third, third), third)]
+        part = full_ref[:, window(lax.rem(pair + k, steps), third)]
         part = jnp.where(side == 0, part, pltpu.roll(part, third // 2, 1))
         norm_buf[:, k * third : (k + 1) * third] = part.astype(BF16)
-    store[0].wait()
-    for copy in load_all([(norm_buf, norm_ref)], sem):
-        copy.wait()
-
-
-def entry(where, w_qkv, w_out, state, modes):
+    stores.append(pltpu.make_async_copy(norm_buf, norm_ref, out_sem.at[1]))
+    stores[1].start()
+    for copy in stores:
+        copy.wait()
+
+
+def entry(w_qkv, w_out, state, modes):
     return pl.pallas_call(
         entry_kernel,
         out_shape=[shape_of(*w_out.shape), shape_of(*state.shape)],
-        in_specs=[SMEM, ANY, ANY, ANY, ANY],
+        in_specs=[ANY] * 4,
         out_specs=[ANY, ANY],
         scratch_shapes=[
             pltpu.VMEM(w_out.shape, BF16),
@@ -183,10 +198,11 @@
             pltpu.VMEM(state.shape, F32),
             pltpu.VMEM(state.shape, BF16),
             pltpu.SemaphoreType.DMA((6,)),
+            pltpu.SemaphoreType.DMA((2,)),
         ],
         compiler_params=params(),
         cost_estimate=cost(4e9, 1e6),
-    )(where, w_qkv, w_out, state, modes)
+    )(w_qkv, w_out, state, modes)
 
 
 def pack_kernel(count, *refs):
@@ -273,31 +289,31 @@
     )(*norms, *pieces)
 
 
-def scores_kernel(count, where_ref, *refs):
+def scores_kernel(count, *refs):
     norms, acc_ref, gains_ref, pieces = refs[:4], refs[4], refs[5], refs[6 : 6 + count]
-    out_ref, sums_ref, left_ref, held_ref, acc_in, gains_in, out_buf, sums_buf, sem, out_sem = refs[6 + count :]
+    out_ref, sums_ref, left_ref, held_ref, acc_in, gains_in, out_buf, sums_buf, sem, rest_sem, out_sem = refs[6 + count :]
     deep = held_ref.shape[0]
     third = out_ref.shape[2] // 2
     width = norms[0].shape[1]
-    loads = load_all(
-        rows_of(pieces, held_ref)
-        + [(gains_ref, gains_in)]
-        + [(norms[b].at[:, width - deep :], left_ref.at[b]) for b in range(4)]
-        + [(acc_ref.at[b], acc_in.at[b]) for b in range(4)],
-        sem,
-    )
-    mine = pl.ds(pl.multiple_of(where_ref[3] * third, third), third)
+    first = [(norms[0].at[:, width - deep :], left_ref.at[0]), (acc_ref.at[0], acc_in.at[0])]
+    loads = load_all(rows_of(pieces, held_ref) + [(gains_ref, gains_in)] + first, sem)
+    mine = window(places()[3], third)
     row = lax.broadcasted_iota(jnp.int32, (8, 4 * DH), 0)
     lane = lax.broadcasted_iota(jnp.int32, (8, 4 * DH), 1)
     pick = (row == lane // (2 * DH)).astype(BF16)
-    for copy in loads[: count + 1]:
-        copy.wait()
+    for copy in loads:
+        copy.wait()
+    rest = []
+    for b in range(1, 4):
+        rest += [(norms[b].at[:, width - deep :], left_ref.at[b]), (acc_ref.at[b], acc_in.at[b])]
+    loads = load_all(rest, rest_sem)
     gains = [gains_in[0, :, mine] * (1.4426950408889634 / DH**0.5), gains_in[1, :, mine]]
     stores = []
     for block in range(4):
-        loads[count + 1 + block].wait()
+        if block:
+            loads[2 * block - 2].wait()
+            loads[2 * block - 1].wait()
         product = times(left_ref[block], held_ref[...])
-        loads[count + 5 + block].wait()
         squares = []
         for j in range(2):
             square = 0.0
@@ -317,14 +333,14 @@
         copy.wait()
 
 
-def last_scores(where, norms, acc, gains, pieces):
+def last_scores(norms, acc, gains, pieces):
     rows = norms[0].shape[0]
     columns = acc.shape[2]
     deep = sum(piece.shape[0] for piece in pieces)
     return pl.pallas_call(
         functools.partial(scores_kernel, len(pieces)),
         out_shape=[shape_of(4, rows, columns), shape_of(4, 8, rows, dtype=F32)],
-        in_specs=[SMEM] + [ANY] * (6 + len(pieces)),
+        in_specs=[ANY] * (6 + len(pieces)),
         out_specs=[ANY, ANY],
         scratch_shapes=[
             pltpu.VMEM((4, rows, deep), BF16),
@@ -333,12 +349,13 @@
             pltpu.VMEM(gains.shape, F32),
             pltpu.VMEM(acc.shape, BF16),
             pltpu.VMEM((4, 8, rows), F32),
-            pltpu.SemaphoreType.DMA((9 + len(pieces),)),
+            pltpu.SemaphoreType.DMA((3 + len(pieces),)),
+            pltpu.SemaphoreType.DMA((6,)),
             pltpu.SemaphoreType.DMA((5,)),
         ],
         compiler_params=params(),
         cost_estimate=cost(6e9, 1e6),
-    )(where, *norms, acc, gains, *pieces)
+    )(*norms, acc, gains, *pieces)
 
 
 def values_kernel(count, *refs):
@@ -387,7 +404,7 @@
     )(*norms, acc, *pieces)
 
 
-def heads_kernel(where_ref, qk_ref, v_ref, s0_ref, s1_ref, s2_ref, s3_ref, *refs):
+def heads_kernel(length_ref, qk_ref, v_ref, s0_ref, s1_ref, s2_ref, s3_ref, *refs):
     outs = refs[:4]
     qk_in, v_in, sums_in, out_buf, sem, out_sem = refs[4:]
     rows = qk_ref.shape[1]
@@ -411,7 +428,8 @@
     row = lax.broadcasted_iota(jnp.int32, (24, DH), 0)
     pick = (row % 8 == 0).astype(BF16)
     place = lax.broadcasted_iota(jnp.int32, (1, rows), 1)
-    masks = [place < where_ref[4 + j] for j in range(2)]
+    position = lax.axis_index("seq")
+    masks = [place < length_ref[0] - (j + position - 2 * j * position) * rows for j in range(2)]
     for copy in loads[:4]:
         copy.wait()
     scale_q, scale_k = [], []
@@ -462,7 +480,7 @@
         copy.wait()
 
 
-def team_attention(where, qk, v, sums):
+def team_attention(length, qk, v, sums):
     rows = qk.shape[1]
     third = qk.shape[2] // 2
     return pl.pallas_call(
@@ -480,24 +498,20 @@
         ],
         compiler_params=params(),
         cost_estimate=cost(1.1e10, 1e6),
-    )(where, qk, v, *sums)
-
-
-def out_kernel(where_ref, state_ref, modes_ref, head_ref, *refs):
+    )(length, qk, v, *sums)
+
+
+def out_kernel(state_ref, modes_ref, head_ref, *refs):
     attended, pieces = refs[:4], refs[4:12]
     own_ref, sent_ref = refs[12:14]
     att_in, group_ref, held_ref, state_in, modes_in, head_in_ref, own_buf, sent_buf, sem = refs[14:]
-    side, pair, steps, own = (where_ref[j] for j in range(4))
+    side, pair, steps, own = places()
     third = attended[0].shape[1]
     half = pieces[0].shape[0]
-
-    def window(j):
-        return pl.ds(pl.multiple_of(j * third, third), third)
-
     loads = load_all(
         [(attended[j], att_in.at[j]) for j in range(4)]
-        + [(pieces[j], held_ref.at[:half, window(own ^ j)]) for j in range(4)]
-        + [(pieces[4 + j], held_ref.at[half:, window(own ^ j)]) for j in range(4)]
+        + [(pieces[j], held_ref.at[:half, window(own ^ j, third)]) for j in range(4)]
+        + [(pieces[4 + j], held_ref.at[half:, window(own ^ j, third)]) for j in range(4)]
         + [(state_ref, state_in), (modes_ref, modes_in), (head_ref, head_in_ref)],
         sem,
     )
@@ -505,7 +519,7 @@
         loads[j].wait()
         part = att_in[j].astype(F32)
         part = jnp.where(side == 0, part, pltpu.roll(part, third // 2, 1)).astype(BF16)
-        group_ref[:, window(lax.rem((own ^ j) + steps - pair, steps))] = part
+        group_ref[:, window(lax.rem((own ^ j) + steps - pair, steps), third)] = part
     for copy in loads[4:8]:
         copy.wait()
     total = times(group_ref[:, :half], held_ref[:half, :])
@@ -513,24 +527,24 @@
         copy.wait()
     total += times(group_ref[:, half:], held_ref[half:, :])
     block_out = (state_in[...].astype(F32) + modes_in[2] * total).astype(BF16)
-    head_in = layer_norm(block_out.astype(F32)) * (1.0 + modes_in[4]) + modes_in[3]
+    head_in = scaled_norm(block_out.astype(F32), modes_in[3], modes_in[4])
     velocity = times_turned(head_in_ref[...], head_in.astype(BF16))
     channels = own_buf.shape[0]
-    core = lax.rem(own, 2)
+    core = lax.axis_index("cfg")
     own_buf[...] = jnp.where(core == 0, velocity[:channels], velocity[channels:])
     sent_buf[...] = jnp.where(core == 0, velocity[channels:], velocity[:channels]).astype(BF16)
     for copy in load_all([(own_buf, own_ref), (sent_buf, sent_ref)], sem):
         copy.wait()
 
 
-def project(where, state, modes, w_head, attended, pieces):
+def project(state, modes, w_head, attended, pieces):
     rows, width = state.shape
     third = width // 4
     channels = w_head.shape[0] // 2
     return pl.pallas_call(
         out_kernel,
         out_shape=[shape_of(channels, rows, dtype=F32), shape_of(channels, rows)],
-        in_specs=[SMEM] + [ANY] * 15,
+        in_specs=[ANY] * 15,
         out_specs=[ANY, ANY],
         scratch_shapes=[
             pltpu.VMEM((4, rows, third), BF16),
@@ -545,7 +559,7 @@
         ],
         compiler_params=params(),
         cost_estimate=cost(8e9, 1e6),
-    )(where, state, modes, w_head, *attended, *pieces)
+    )(state, modes, w_head, *attended, *pieces)
 
 
 def updated_latent(own, outgoing, latent, guidance, step_size, length, position):
@@ -573,13 +587,7 @@
     modes = jnp.transpose(modulation, (1, 0, 2))
     rows, width = state.shape
     third = width // 4
-    core = lax.axis_index("cfg")
-    position = lax.axis_index("seq")
-    place = lax.axis_index("req")
     parts = lax.axis_size("req")
-    side, pair = place % 2, place // 2
-    steps = parts // 2
-    group = 2 * position + core
     up = [(i, (i - 2) % parts) for i in range(parts)]
     down = [(i, (i + 2) % parts) for i in range(parts)]
     beside = [(i, i ^ 1) for i in range(parts)]
@@ -593,14 +601,8 @@
     def across(piece):
         return lax.ppermute(piece, "req", beside)
 
-    def ints(*values):
-        return jnp.stack([jnp.asarray(value, jnp.int32) for value in values])
-
-    length = lengths[0]
-    places = ints(side, pair, steps, group, length - position * rows, length - (1 - position) * rows)
     gains = jnp.stack([q_gain, k_gain])[:, None]
-
-    columns, normed = entry(places, w_qkv, w_out, state, modes)
+    columns, normed = entry(w_qkv, w_out, state, modes)
     normed_y = lax.ppermute(normed, "seq", SWAP)
     normed_c = lax.ppermute(normed, "cfg", SWAP)
 
@@ -619,10 +621,10 @@
     gates = [mine[2], theirs[1]]
     step(mine, theirs, gates)
     out_last = back(after(out_last, *gates))
+    early = [mine[0], theirs[0], mine[1], theirs[1]]
+    packed = [pack(early, third)]
     normed_yc = lax.ppermute(normed_y, "cfg", SWAP)
     norms = [normed, normed_y, normed_c, normed_yc]
-    early = [mine[0], theirs[0], mine[1], theirs[1]]
-    packed = [pack(early, third)]
     packed_y = [lax.ppermute(packed[0], "seq", SWAP)]
     acc_qk, acc_v = first_part(norms, early)
     gates = [mine[3], theirs[2], out_last, packed_y[0], acc_v]
@@ -634,7 +636,7 @@
     packed_c = [lax.ppermute(part, "cfg", SWAP) for part in packed]
     packed_yc = [lax.ppermute(part, "cfg", SWAP) for part in packed_y]
 
-    qk_full, sums = last_scores(places, norms, acc_qk, gains, late)
+    qk_full, sums = last_scores(norms, acc_qk, gains, late)
     v_full = last_values(norms, acc_v, late)
     diagonal = [(i, 3 - i) for i in range(4)]
     all_sums = [
@@ -644,7 +646,7 @@
         lax.ppermute(sums, ("cfg", "seq"), diagonal),
     ]
     v_full = after(v_full, packed_y[1], *packed_c, packed_yc[0])
-    heads = team_attention(places, qk_full, v_full, all_sums)
+    heads = team_attention(lengths, qk_full, v_full, all_sums)
     attended = [
         heads[0],
         lax.ppermute(heads[2], "cfg", SWAP),
@@ -652,8 +654,8 @@
         lax.ppermute(heads[3], ("cfg", "seq"), diagonal),
     ]
     quarters = [part[j] for j in range(2) for part in (packed, packed_c, packed_y, packed_yc)]
-    own, outgoing = project(places, state, modes, w_head.T, attended, quarters)
-    return updated_latent(own, outgoing, latent, guidance, step_size, length, position)
+    own, outgoing = project(state, modes, w_head.T, attended, quarters)
+    return updated_latent(own, outgoing, latent, guidance, step_size, lengths[0], lax.axis_index("seq"))
 
 
 def by_team(mesh, arguments):

time: 117 us -> 112 us (0.957)
  Pallas kernels: 38.5 us -> 35.2 us
    ppermute x1, waiting for transfers between devices: 0.84 us -> 2.21 us  [team_local(): packed_y.append(lax.ppermute(packed[1], 'seq', SWAP))]
    pallas_call x1, Pallas kernels: 4.33 us -> 3.15 us  [entry(): pl.pallas_call(entry_kernel, out_shape=[shape_of(*w_out.shape), shape_of(...]
where the time goes in v4:
time: 112 us
  waiting for transfers between devices  43.6 us (39%)
  Pallas kernels  35.2 us (31%)
  starting transfers between devices  25.8 us (23%)
  local copies, waits for them, and re-layouts  3.74 us (3%)
  between operations  2.26 us (2%)
  other arithmetic  1.47 us (1%)
    ppermute x4, waiting for transfers between devices, across(): return lax.ppermute(piece, 'req', beside)  18.5 us
    ppermute x3, starting transfers between devices, along(): return lax.ppermute(piece, 'req', up)  12.1 us
    ppermute x1, waiting for transfers between devices, team_local(): lax.ppermute(heads[1], 'seq', SWAP)  6.91 us
    ppermute x3, waiting for transfers between devices, along(): return lax.ppermute(piece, 'req', up)  6.79 us
    pallas_call x1, Pallas kernels, team_attention(): pl.pallas_call(heads_kernel, out_shape=[shape_of(rows, third)] * 4, in_sp...  6.69 us
    pallas_call x1, Pallas kernels, project(): pl.pallas_call(out_kernel, out_shape=[shape_of(channels, rows, dtype=F32)...  6.18 us
    pallas_call x1, Pallas kernels, last_scores(): pl.pallas_call(functools.partial(scores_kernel, len(pieces)), out_shape=[...  5.77 us
    pallas_call x1, Pallas kernels, first_part(): pl.pallas_call(functools.partial(first_kernel, len(pieces)), out_shape=[q...  5.24 us
  transfers between devices with their start and end apart: 25, of which 12 were waited for; matrix products, arithmetic and copies ran while one was open for 1% of the time, Pallas kernels for 23%

profile of v4, /device:TPU:0, one launch (start us, length us, event | category | flops | bytes accessed | tf_op | source)
XLA Modules:
  0.0 112.0 jit_solution(2849340968007219726)
XLA Ops:
  0.0 3.1 %shard_map.109 = (bf16[192,1536]{1,0:T(8,128)(2,1)}, bf16[288,1536]{1,0:T(8,128)(2,1)}) custom-call(bf16[192,4608]{1,0:T(8,128)(2,1)} %qkv_ref.1, bf16[192,1536]{1,0:T(8,128)(2,1)} %w_out_ref.1, bf16[288,1536]{1,0:T(8,128)(2,1)} %bitcast.17, f32[5,1,1536]{2,1,0:T(1,128)} %bitcast.20), custom_call_target="tpu_custom_call" | custom-call | flops 4000000000 | bytes 1000000 | tf_op jit(solution)/shard_map/pallas_call | solution.py:189
  3.2 3.0 %collective-permute-start = (bf16[288,1536]{1,0:T(8,128)(2,1)}, bf16[288,1536]{1,0:T(8,128)(2,1)S(1)}, u32[]{:S(2)}, u32[]{:S(2)}) collective-permute-start(bf16[288,1536]{1,0:T(8,128)(2,1)} %get-tuple-element.23.refs_0_), channel_id=1, source_target_pairs={{0,1},{1,0},{2,3},{3,2},{4,5},{5,4},{6,7},{7,6},{8,9},{9,8},{10,11... | collective-permute-start | bytes 2654216 | tf_op jit(solution)/shard_map/ppermute | solution.py:606
  6.2 1.5 %collective-permute-start.3 = (bf16[192,1536]{1,0:T(8,128)(2,1)}, bf16[192,1536]{1,0:T(8,128)(2,1)S(1)}, u32[]{:S(2)}, u32[]{:S(2)}) collective-permute-start(bf16[192,1536]{1,0:T(8,128)(2,1)} %get-tuple-element.24.refs_4_.refs_0_), channel_id=1, source_target_pairs={{0,2},{2,0},{4,6},{6,4},{8,10},{10,8},{12,14},{14,12},{1,3},{3,1},... | collective-permute-start | bytes 1769480 | tf_op jit(solution)/shard_map/ppermute | solution.py:602
  7.7 3.6 %collective-permute-start.4 = (bf16[192,1536]{1,0:T(8,128)(2,1)}, bf16[192,1536]{1,0:T(8,128)(2,1)S(1)}, u32[]{:S(2)}, u32[]{:S(2)}) collective-permute-start(bf16[192,1536]{1,0:T(8,128)(2,1)} %get-tuple-element.24.refs_4_.refs_0_), channel_id=1, source_target_pairs={{0,12},{2,14},{4,0},{6,2},{8,4},{10,6},{12,8},{14,10},{1,13},{3,15... | collective-permute-start | bytes 1769480 | tf_op jit(solution)/shard_map/ppermute | solution.py:596
  11.3 0.6 broadcast_in_dim.16.refs_5_
  11.9 9.2 %collective-permute-done.3.refs_5_.refs_1_ = bf16[192,1536]{1,0:T(8,128)(2,1)S(1)} collective-permute-done((bf16[192,1536]{1,0:T(8,128)(2,1)}, bf16[192,1536]{1,0:T(8,128)(2,1)S(1)}, u32[]{:S(2)}, u32[]{:S(2)}) %collective-permute-start.3) | collective-permute-done | bytes 589856 | tf_op jit(solution)/shard_map/ppermute | solution.py:602
  21.2 2.4 %collective-permute-done.4.refs_6_.refs_2_ = bf16[192,1536]{1,0:T(8,128)(2,1)S(1)} collective-permute-done((bf16[192,1536]{1,0:T(8,128)(2,1)}, bf16[192,1536]{1,0:T(8,128)(2,1)S(1)}, u32[]{:S(2)}, u32[]{:S(2)}) %collective-permute-start.4) | collective-permute-done | bytes 589856 | tf_op jit(solution)/shard_map/ppermute | solution.py:596
  23.6 0.5 collective-permute-start.5
  24.2 4.2 %collective-permute-start.6 = (bf16[192,1536]{1,0:T(8,128)(2,1)S(1)}, bf16[192,1536]{1,0:T(8,128)(2,1)S(1)}, u32[]{:S(2)}, u32[]{:S(2)}) collective-permute-start(bf16[192,1536]{1,0:T(8,128)(2,1)S(1)} %collective-permute-done.4.refs_6_.refs_2_), channel_id=1, source_target_pairs={{0,12},{2,14},{4,0},{6,2},{8,4},{10,6},{12,8},{14,10},{1,13},{3,15... | collective-permute-start | bytes 1769480 | tf_op jit(solution)/shard_map/ppermute | solution.py:596
  28.3 0.0 collective-permute-start.1
  28.3 0.0 collective-permute-done.refs_1_
  28.4 0.5 collective-permute-start.2
  28.9 8.4 %collective-permute-done.5.refs_7_.refs_3_ = bf16[192,1536]{1,0:T(8,128)(2,1)S(1)} collective-permute-done((bf16[192,1536]{1,0:T(8,128)(2,1)S(1)}, bf16[192,1536]{1,0:T(8,128)(2,1)S(1)}, u32[]{:S(2)}, u32[]{:S(2)}) %collective-permute-start.5) | collective-permute-done | bytes 589856 | tf_op jit(solution)/shard_map/ppermute | solution.py:602
  37.2 1.9 %collective-permute-done.6.refs_6_.refs_5_.refs_0_ = bf16[192,1536]{1,0:T(8,128)(2,1)S(1)} collective-permute-done((bf16[192,1536]{1,0:T(8,128)(2,1)S(1)}, bf16[192,1536]{1,0:T(8,128)(2,1)S(1)}, u32[]{:S(2)}, u32[]{:S(2)}) %collective-permute-start.6) | collective-permute-done | bytes 589856 | tf_op jit(solution)/shard_map/ppermute | solution.py:596
  39.2 1.5 %collective-permute-start.7 = (bf16[192,1536]{1,0:T(8,128)(2,1)S(1)}, bf16[192,1536]{1,0:T(8,128)(2,1)}, u32[]{:S(2)}, u32[]{:S(2)}) collective-permute-start(bf16[192,1536]{1,0:T(8,128)(2,1)S(1)} %collective-permute-done.6.refs_6_.refs_5_.refs_0_), channel_id=1, source_target_pairs={{0,2},{2,0},{4,6},{6,4},{8,10},{10,8},{12,14},{14,12},{1,3},{3,1},... | collective-permute-start | bytes 1769480 | tf_op jit(solution)/shard_map/ppermute | solution.py:602
  40.7 4.3 %collective-permute-start.8 = (bf16[192,1536]{1,0:T(8,128)(2,1)S(1)}, bf16[192,1536]{1,0:T(8,128)(2,1)S(1)}, u32[]{:S(2)}, u32[]{:S(2)}) collective-permute-start(bf16[192,1536]{1,0:T(8,128)(2,1)S(1)} %collective-permute-done.6.refs_6_.refs_5_.refs_0_), channel_id=1, source_target_pairs={{0,12},{2,14},{4,0},{6,2},{8,4},{10,6},{12,8},{14,10},{1,13},{3,15... | collective-permute-start | bytes 1769480 | tf_op jit(solution)/shard_map/ppermute | solution.py:596
  44.9 2.1 %shard_map.111.refs_4_ = bf16[768,384]{1,0:T(8,128)(2,1)} custom-call(bf16[192,1536]{1,0:T(8,128)(2,1)} %get-tuple-element.24.refs_4_.refs_0_, bf16[192,1536]{1,0:T(8,128)(2,1)} %copy-done, bf16[192,1536]{1,0:T(8,128)(2,1)} %copy-done.12, bf16[192,1536]{1,0:T(8,128)(2,1)} %copy-done.14), custom_call_target="tpu_custom_call" | custom-call | flops 3000000000 | bytes 1000000 | tf_op jit(solution)/shard_map/pallas_call | solution.py:224
  47.0 0.6 collective-permute-start.10
  47.6 0.0 collective-permute-done.1.refs_2_
  47.6 0.0 collective-permute-start.14
  47.6 0.0 collective-permute-done.2.refs_3_
  47.6 0.1 collective-permute-start.9
  47.7 0.8 copy-done.6
  48.5 5.2 %shard_map.110 = (bf16[4,288,768]{2,1,0:T(8,128)(2,1)}, bf16[4,288,384]{2,1,0:T(8,128)(2,1)}) custom-call(bf16[288,1536]{1,0:T(8,128)(2,1)} %get-tuple-element.23.refs_0_, bf16[288,1536]{1,0:T(8,128)(2,1)} %copy-done.5, bf16[288,1536]{1,0:T(8,128)(2,1)} %copy-done.6, bf16[288,1536]{1,0:T(8,128)(2,1)} %collective-permute-done.2.refs_3_, ...), custom_call_target="tpu_custom_call" | custom-call | flops 6000000000 | bytes 1000000 | tf_op jit(solution)/shard_map/pallas_call | solution.py:274
  53.8 2.5 %collective-permute-done.8.refs_8_.refs_7_.refs_2_ = bf16[192,1536]{1,0:T(8,128)(2,1)S(1)} collective-permute-done((bf16[192,1536]{1,0:T(8,128)(2,1)S(1)}, bf16[192,1536]{1,0:T(8,128)(2,1)S(1)}, u32[]{:S(2)}, u32[]{:S(2)}) %collective-permute-start.8) | collective-permute-done | bytes 589856 | tf_op jit(solution)/shard_map/ppermute | solution.py:596
  56.2 2.2 %collective-permute-done.9.refs_3_ = bf16[192,384]{1,0:T(8,128)(2,1)S(1)} collective-permute-done((bf16[192,384]{1,0:T(8,128)(2,1)S(1)}, bf16[192,384]{1,0:T(8,128)(2,1)S(1)}, u32[]{:S(2)}, u32[]{:S(2)}) %collective-permute-start.9) | collective-permute-done | bytes 147488 | tf_op jit(solution)/shard_map/ppermute | solution.py:599
  58.5 0.0 collective-permute-done.7.refs_7_.refs_6_.refs_1_
  58.5 0.7 collective-permute-done.10.refs_6_
  59.1 0.5 collective-permute-start.11
  59.7 1.2 %collective-permute-start.12 = (bf16[96,1152]{1,0:T(8,128)(2,1)S(1)}, bf16[96,1152]{1,0:T(8,128)(2,1)S(1)}, u32[]{:S(2)}, u32[]{:S(2)}) collective-permute-start(bf16[96,1152]{1,0:T(8,128)(2,1)S(1)} %slice.12), channel_id=1, source_target_pairs={{0,4},{2,6},{4,8},{6,10},{8,12},{10,14},{12,0},{14,2},{1,5},{3,7},... | collective-permute-start | bytes 663560 | tf_op jit(solution)/shard_map/ppermute | solution.py:599
  60.9 2.0 %shard_map.114.refs_8_ = bf16[768,384]{1,0:T(8,128)(2,1)} custom-call(bf16[192,1536]{1,0:T(8,128)(2,1)} %copy-done.9, bf16[192,1536]{1,0:T(8,128)(2,1)} %collective-permute-done.7.refs_7_.refs_6_.refs_1_, bf16[192,1536]{1,0:T(8,128)(2,1)} %copy-done.1, bf16[192,384]{1,0:T(8,128)(2,1)} %copy-done.20), custom_call_target="tpu_custom_call" | custom-call | flops 3000000000 | bytes 1000000 | tf_op jit(solution)/shard_map/pallas_call | solution.py:224
  62.9 0.6 collective-permute-start.13
  64.1 0.1 collective-permute-start.15
  64.2 0.9 collective-permute-done.11.refs_9_.refs_8_
  65.1 0.0 collective-permute-start.16
  65.1 3.0 %collective-permute-done.12.refs_10_.refs_9_ = bf16[96,1152]{1,0:T(8,128)(2,1)S(1)} collective-permute-done((bf16[96,1152]{1,0:T(8,128)(2,1)S(1)}, bf16[96,1152]{1,0:T(8,128)(2,1)S(1)}, u32[]{:S(2)}, u32[]{:S(2)}) %collective-permute-start.12) | collective-permute-done | bytes 221216 | tf_op jit(solution)/shard_map/ppermute | solution.py:599
  68.1 0.7 copy-done.16
  68.8 5.8 %shard_map.112 = (bf16[4,288,768]{2,1,0:T(8,128)(2,1)}, f32[4,8,288]{2,1,0:T(8,128)}) custom-call(bf16[288,1536]{1,0:T(8,128)(2,1)} %get-tuple-element.23.refs_0_, bf16[288,1536]{1,0:T(8,128)(2,1)} %copy-done.5, bf16[288,1536]{1,0:T(8,128)(2,1)} %copy-done.6, bf16[288,1536]{1,0:T(8,128)(2,1)} %collective-permute-done.2.refs_3_, ...), custom_call_target="tpu_custom_call" | custom-call | flops 6000000000 | bytes 1000000 | tf_op jit(solution)/shard_map/pallas_call | solution.py:340
  74.6 0.6 collective-permute-start.17
  75.2 0.0 collective-permute-done.14.refs_5_
  75.2 0.0 collective-permute-start.18
  75.2 2.2 %collective-permute-done.13.refs_10_ = bf16[768,384]{1,0:T(8,128)(2,1)S(1)} collective-permute-done((bf16[768,384]{1,0:T(8,128)(2,1)}, bf16[768,384]{1,0:T(8,128)(2,1)S(1)}, u32[]{:S(2)}, u32[]{:S(2)}) %collective-permute-start.13) | collective-permute-done | bytes 589856 | tf_op jit(solution)/shard_map/ppermute | solution.py:635
  77.4 4.1 %shard_map.113.v_ref = bf16[4,288,384]{2,1,0:T(8,128)(2,1)} custom-call(bf16[288,1536]{1,0:T(8,128)(2,1)} %get-tuple-element.23.refs_0_, bf16[288,1536]{1,0:T(8,128)(2,1)} %copy-done.5, bf16[288,1536]{1,0:T(8,128)(2,1)} %copy-done.6, bf16[288,1536]{1,0:T(8,128)(2,1)} %collective-permute-done.2.refs_3_, bf16[4,288,384]{2,1,0:T(8,128)(2,1)} %get-tuple-element.29.refs_4_, ...), custom_call_target="tpu_custom_call" | custom-call | flops 4000000000 | bytes 1000000 | tf_op jit(solution)/shard_map/pallas_call | solution.py:390
  81.5 0.0 collective-permute-done.15.refs_9_
  81.5 0.0 collective-permute-done.16.refs_7_
  81.6 0.5 collective-permute-start.23
  82.0 0.0 collective-permute-done.17.s1_ref
  82.0 0.0 collective-permute-done.18.s2_ref
  82.1 0.6 copy-done.21
  82.7 0.0 copy-done.22
  82.7 0.0 copy-done.23
  82.7 6.7 %shard_map.115 = (bf16[288,384]{1,0:T(8,128)(2,1)}, bf16[288,384]{1,0:T(8,128)(2,1)}, bf16[288,384]{1,0:T(8,128)(2,1)}, bf16[288,384]{1,0:T(8,128)(2,1)}) custom-call(s32[1]{0:T(128)} %copy.12.length_ref, bf16[4,288,768]{2,1,0:T(8,128)(2,1)} %get-tuple-element.32.qk_ref, bf16[4,288,384]{2,1,0:T(8,128)(2,1)} %shard_map.113.v_ref, ...), custom_call_target="tpu_custom_call" | custom-call | flops 11000000512 | bytes 1000000 | tf_op jit(solution)/shard_map/pallas_call | solution.py:486
  89.4 0.4 collective-permute-start.20
  89.8 1.4 %collective-permute-start.21 = (bf16[288,384]{1,0:T(8,128)(2,1)}, bf16[288,384]{1,0:T(8,128)(2,1)S(1)}, u32[]{:S(2)}, u32[]{:S(2)}) collective-permute-start(bf16[288,384]{1,0:T(8,128)(2,1)} %get-tuple-element.37), channel_id=1, source_target_pairs={{0,1},{1,0},{2,3},{3,2},{4,5},{5,4},{6,7},{7,6},{8,9},{9,8},{10,11... | collective-permute-start | bytes 663560 | tf_op jit(solution)/shard_map/ppermute | solution.py:653
  91.2 0.1 collective-permute-start.22
  91.3 0.0 collective-permute-done.20.refs_1_
  91.3 6.9 %collective-permute-done.21.refs_2_ = bf16[288,384]{1,0:T(8,128)(2,1)S(1)} collective-permute-done((bf16[288,384]{1,0:T(8,128)(2,1)}, bf16[288,384]{1,0:T(8,128)(2,1)S(1)}, u32[]{:S(2)}, u32[]{:S(2)}) %collective-permute-start.21) | collective-permute-done | bytes 221216 | tf_op jit(solution)/shard_map/ppermute | solution.py:653
  98.2 3.3 %collective-permute-done.22.refs_3_ = bf16[288,384]{1,0:T(8,128)(2,1)S(1)} collective-permute-done((bf16[288,384]{1,0:T(8,128)(2,1)}, bf16[288,384]{1,0:T(8,128)(2,1)S(1)}, u32[]{:S(2)}, u32[]{:S(2)}) %collective-permute-start.22) | collective-permute-done | bytes 221216 | tf_op jit(solution)/shard_map/ppermute | solution.py:654
  101.5 0.0 collective-permute-done.23.refs_11_
  101.6 0.6 copy-done.19
  102.2 0.2 copy-done.13
  102.4 6.2 %shard_map.116 = (f32[32,288]{1,0:T(8,128)}, bf16[32,288]{1,0:T(8,128)(2,1)}) custom-call(bf16[288,1536]{1,0:T(8,128)(2,1)} %bitcast.18, f32[5,1,1536]{2,1,0:T(1,128)} %bitcast.21, bf16[64,1536]{1,0:T(8,128)(2,1)} %bitcast.19, bf16[288,384]{1,0:T(8,128)(2,1)} %get-tuple-element.35.refs_0_, bf16[288,384]{1,0:T(8,128)(2,1)} %copy-done.17, ...), custom_call_target="tpu_custom_call" | custom-call | flops 8000000000 | bytes 1000000 | tf_op jit(solution)/shard_map/pallas_call | solution.py:544
  108.6 0.6 collective-permute-start.24
  110.6 1.4 %fusion.4 = f32[1,288,32]{1,2,0:T(8,128)} fusion(f32[32,288]{1,0:T(8,128)} %get-tuple-element.40, bf16[32,288]{1,0:T(8,128)(2,1)S(1)} %collective-permute-done.24, f32[1,288,32]{1,2,0:T(8,128)S(1)} %copy-done.2, f32[]{:T(128)} %bitcast.15, f32[]{:T(128)} %bitcast.16, pred[]{:T(512)S(6)} %eq.4, pred[288]{0:T(512)(128)(4,1)S(1)} %add_compare_fusion), kind=kLoop, calls=%fused_computation.7 | loop fusion | flops 82944 | bytes 129321 | tf_op jit(solution)/shard_map/broadcast_in_dim | solution.py:576
  (51 shorter events, 0.2 us)
Async XLA Ops:
  0.0 11.3 %copy-start.3 = (f32[1536]{0:T(1024)S(1)}, f32[1536]{0:T(1024)}, u32[]{:S(2)}) copy-start(f32[1536]{0:T(1024)} %param.17) | copy-start | bytes 18436
  0.0 11.3 %copy-start.4 = (f32[1536]{0:T(1024)S(1)}, f32[1536]{0:T(1024)}, u32[]{:S(2)}) copy-start(f32[1536]{0:T(1024)} %param.16) | copy-start | bytes 18436
  3.2 25.2 %collective-permute-start = (bf16[288,1536]{1,0:T(8,128)(2,1)}, bf16[288,1536]{1,0:T(8,128)(2,1)S(1)}, u32[]{:S(2)}, u32[]{:S(2)}) collective-permute-start(bf16[288,1536]{1,0:T(8,128)(2,1)} %get-tuple-element.23.refs_0_), channel_id=1, source_target_pairs={{0,1},{1,0},{2,3},{3,2},{4,5},{5,4},{6,7},{7,6},{8,9},{9,8},{10,11... | collective-permute-start | bytes 2654216 | tf_op jit(solution)/shard_map/ppermute | solution.py:606
  6.2 15.0 %collective-permute-start.3 = (bf16[192,1536]{1,0:T(8,128)(2,1)}, bf16[192,1536]{1,0:T(8,128)(2,1)S(1)}, u32[]{:S(2)}, u32[]{:S(2)}) collective-permute-start(bf16[192,1536]{1,0:T(8,128)(2,1)} %get-tuple-element.24.refs_4_.refs_0_), channel_id=1, source_target_pairs={{0,2},{2,0},{4,6},{6,4},{8,10},{10,8},{12,14},{14,12},{1,3},{3,1},... | collective-permute-start | bytes 1769480 | tf_op jit(solution)/shard_map/ppermute | solution.py:602
  7.7 15.9 %collective-permute-start.4 = (bf16[192,1536]{1,0:T(8,128)(2,1)}, bf16[192,1536]{1,0:T(8,128)(2,1)S(1)}, u32[]{:S(2)}, u32[]{:S(2)}) collective-permute-start(bf16[192,1536]{1,0:T(8,128)(2,1)} %get-tuple-element.24.refs_4_.refs_0_), channel_id=1, source_target_pairs={{0,12},{2,14},{4,0},{6,2},{8,4},{10,6},{12,8},{14,10},{1,13},{3,15... | collective-permute-start | bytes 1769480 | tf_op jit(solution)/shard_map/ppermute | solution.py:596
  21.2 23.7 %copy-start = (bf16[192,1536]{1,0:T(8,128)(2,1)}, bf16[192,1536]{1,0:T(8,128)(2,1)S(1)}, u32[]{:S(2)}) copy-start(bf16[192,1536]{1,0:T(8,128)(2,1)S(1)} %collective-permute-done.3.refs_5_.refs_1_) | copy-start | bytes 1769476
  23.6 15.5 %copy-start.12 = (bf16[192,1536]{1,0:T(8,128)(2,1)}, bf16[192,1536]{1,0:T(8,128)(2,1)S(1)}, u32[]{:S(2)}) copy-start(bf16[192,1536]{1,0:T(8,128)(2,1)S(1)} %collective-permute-done.4.refs_6_.refs_2_) | copy-start | bytes 1769476
  23.6 13.6 %collective-permute-start.5 = (bf16[192,1536]{1,0:T(8,128)(2,1)S(1)}, bf16[192,1536]{1,0:T(8,128)(2,1)S(1)}, u32[]{:S(2)}, u32[]{:S(2)}) collective-permute-start(bf16[192,1536]{1,0:T(8,128)(2,1)S(1)} %collective-permute-done.4.refs_6_.refs_2_), channel_id=1, source_target_pairs={{0,2},{2,0},{4,6},{6,4},{8,10},{10,8},{12,14},{14,12},{1,3},{3,1},... | collective-permute-start | bytes 1769480 | tf_op jit(solution)/shard_map/ppermute | solution.py:602
  24.2 15.0 %collective-permute-start.6 = (bf16[192,1536]{1,0:T(8,128)(2,1)S(1)}, bf16[192,1536]{1,0:T(8,128)(2,1)S(1)}, u32[]{:S(2)}, u32[]{:S(2)}) collective-permute-start(bf16[192,1536]{1,0:T(8,128)(2,1)S(1)} %collective-permute-done.4.refs_6_.refs_2_), channel_id=1, source_target_pairs={{0,12},{2,14},{4,0},{6,2},{8,4},{10,6},{12,8},{14,10},{1,13},{3,15... | collective-permute-start | bytes 1769480 | tf_op jit(solution)/shard_map/ppermute | solution.py:596
  28.3 19.3 %collective-permute-start.1 = (bf16[288,1536]{1,0:T(8,128)(2,1)}, bf16[288,1536]{1,0:T(8,128)(2,1)S(1)}, u32[]{:S(2)}, u32[]{:S(2)}) collective-permute-start(bf16[288,1536]{1,0:T(8,128)(2,1)} %get-tuple-element.23.refs_0_), channel_id=1, source_target_pairs={{0,16},{16,0},{1,17},{17,1},{2,18},{18,2},{3,19},{19,3},{4,20},{20... | collective-permute-start | bytes 2654216 | tf_op jit(solution)/shard_map/ppermute | solution.py:607
  28.3 18.7 %copy-start.5 = (bf16[288,1536]{1,0:T(8,128)(2,1)}, bf16[288,1536]{1,0:T(8,128)(2,1)S(1)}, u32[]{:S(2)}) copy-start(bf16[288,1536]{1,0:T(8,128)(2,1)S(1)} %collective-permute-done.refs_1_) | copy-start | bytes 2654212
  28.4 19.3 %collective-permute-start.2 = (bf16[288,1536]{1,0:T(8,128)(2,1)S(1)}, bf16[288,1536]{1,0:T(8,128)(2,1)}, u32[]{:S(2)}, u32[]{:S(2)}) collective-permute-start(bf16[288,1536]{1,0:T(8,128)(2,1)S(1)} %collective-permute-done.refs_1_), channel_id=1, source_target_pairs={{0,16},{16,0},{1,17},{17,1},{2,18},{18,2},{3,19},{19,3},{4,20},{20... | collective-permute-start | bytes 2654216 | tf_op jit(solution)/shard_map/ppermute | solution.py:626
  37.2 3.4 %copy-start.14 = (bf16[192,1536]{1,0:T(8,128)(2,1)}, bf16[192,1536]{1,0:T(8,128)(2,1)S(1)}, u32[]{:S(2)}) copy-start(bf16[192,1536]{1,0:T(8,128)(2,1)S(1)} %collective-permute-done.5.refs_7_.refs_3_) | copy-start | bytes 1769476
  39.2 7.9 %copy-start.9 = (bf16[192,1536]{1,0:T(8,128)(2,1)}, bf16[192,1536]{1,0:T(8,128)(2,1)S(1)}, u32[]{:S(2)}) copy-start(bf16[192,1536]{1,0:T(8,128)(2,1)S(1)} %collective-permute-done.6.refs_6_.refs_5_.refs_0_) | copy-start | bytes 1769476
  39.2 19.3 %collective-permute-start.7 = (bf16[192,1536]{1,0:T(8,128)(2,1)S(1)}, bf16[192,1536]{1,0:T(8,128)(2,1)}, u32[]{:S(2)}, u32[]{:S(2)}) collective-permute-start(bf16[192,1536]{1,0:T(8,128)(2,1)S(1)} %collective-permute-done.6.refs_6_.refs_5_.refs_0_), channel_id=1, source_target_pairs={{0,2},{2,0},{4,6},{6,4},{8,10},{10,8},{12,14},{14,12},{1,3},{3,1},... | collective-permute-start | bytes 1769480 | tf_op jit(solution)/shard_map/ppermute | solution.py:602
  40.7 15.6 %collective-permute-start.8 = (bf16[192,1536]{1,0:T(8,128)(2,1)S(1)}, bf16[192,1536]{1,0:T(8,128)(2,1)S(1)}, u32[]{:S(2)}, u32[]{:S(2)}) collective-permute-start(bf16[192,1536]{1,0:T(8,128)(2,1)S(1)} %collective-permute-done.6.refs_6_.refs_5_.refs_0_), channel_id=1, source_target_pairs={{0,12},{2,14},{4,0},{6,2},{8,4},{10,6},{12,8},{14,10},{1,13},{3,15... | collective-permute-start | bytes 1769480 | tf_op jit(solution)/shard_map/ppermute | solution.py:596
  47.0 12.1 %collective-permute-start.10 = (bf16[768,384]{1,0:T(8,128)(2,1)}, bf16[768,384]{1,0:T(8,128)(2,1)S(1)}, u32[]{:S(2)}, u32[]{:S(2)}) collective-permute-start(bf16[768,384]{1,0:T(8,128)(2,1)} %shard_map.111.refs_4_), channel_id=1, source_target_pairs={{0,1},{1,0},{2,3},{3,2},{4,5},{5,4},{6,7},{7,6},{8,9},{9,8},{10,11... | collective-permute-start | bytes 1769480 | tf_op jit(solution)/shard_map/ppermute | solution.py:628
  47.6 0.9 copy-start.6
  47.6 27.5 %collective-permute-start.14 = (bf16[768,384]{1,0:T(8,128)(2,1)}, bf16[768,384]{1,0:T(8,128)(2,1)}, u32[]{:S(2)}, u32[]{:S(2)}) collective-permute-start(bf16[768,384]{1,0:T(8,128)(2,1)} %shard_map.111.refs_4_), channel_id=1, source_target_pairs={{0,16},{16,0},{1,17},{17,1},{2,18},{18,2},{3,19},{19,3},{4,20},{20... | collective-permute-start | bytes 1769480 | tf_op jit(solution)/shard_map/ppermute | solution.py:636
  47.6 10.8 %collective-permute-start.9 = (bf16[192,384]{1,0:T(8,128)(2,1)S(1)}, bf16[192,384]{1,0:T(8,128)(2,1)S(1)}, u32[]{:S(2)}, u32[]{:S(2)}) collective-permute-start(bf16[192,384]{1,0:T(8,128)(2,1)S(1)} %slice.13), channel_id=1, source_target_pairs={{0,4},{2,6},{4,8},{6,10},{8,12},{10,14},{12,0},{14,2},{1,5},{3,7},... | collective-permute-start | bytes 442376 | tf_op jit(solution)/shard_map/ppermute | solution.py:599
  56.2 4.7 %copy-start.1 = (bf16[192,1536]{1,0:T(8,128)(2,1)}, bf16[192,1536]{1,0:T(8,128)(2,1)S(1)}, u32[]{:S(2)}) copy-start(bf16[192,1536]{1,0:T(8,128)(2,1)S(1)} %collective-permute-done.8.refs_8_.refs_7_.refs_2_) | copy-start | bytes 1769476
  58.5 2.5 %copy-start.20 = (bf16[192,384]{1,0:T(8,128)(2,1)}, bf16[192,384]{1,0:T(8,128)(2,1)S(1)}, u32[]{:S(2)}) copy-start(bf16[192,384]{1,0:T(8,128)(2,1)S(1)} %collective-permute-done.9.refs_3_) | copy-start | bytes 442372
  59.1 5.9 %copy-start.7 = (bf16[768,384]{1,0:T(8,128)(2,1)}, bf16[768,384]{1,0:T(8,128)(2,1)S(1)}, u32[]{:S(2)}) copy-start(bf16[768,384]{1,0:T(8,128)(2,1)S(1)} %collective-permute-done.10.refs_6_) | copy-start | bytes 1769476
  59.1 5.9 %collective-permute-start.11 = (bf16[96,1152]{1,0:T(8,128)(2,1)S(1)}, bf16[96,1152]{1,0:T(8,128)(2,1)S(1)}, u32[]{:S(2)}, u32[]{:S(2)}) collective-permute-start(bf16[96,1152]{1,0:T(8,128)(2,1)S(1)} %slice.14), channel_id=1, source_target_pairs={{0,2},{2,0},{4,6},{6,4},{8,10},{10,8},{12,14},{14,12},{1,3},{3,1},... | collective-permute-start | bytes 663560 | tf_op jit(solution)/shard_map/ppermute | solution.py:602
  59.7 8.4 %collective-permute-start.12 = (bf16[96,1152]{1,0:T(8,128)(2,1)S(1)}, bf16[96,1152]{1,0:T(8,128)(2,1)S(1)}, u32[]{:S(2)}, u32[]{:S(2)}) collective-permute-start(bf16[96,1152]{1,0:T(8,128)(2,1)S(1)} %slice.12), channel_id=1, source_target_pairs={{0,4},{2,6},{4,8},{6,10},{8,12},{10,14},{12,0},{14,2},{1,5},{3,7},... | collective-permute-start | bytes 663560 | tf_op jit(solution)/shard_map/ppermute | solution.py:599
  62.9 14.5 %collective-permute-start.13 = (bf16[768,384]{1,0:T(8,128)(2,1)}, bf16[768,384]{1,0:T(8,128)(2,1)S(1)}, u32[]{:S(2)}, u32[]{:S(2)}) collective-permute-start(bf16[768,384]{1,0:T(8,128)(2,1)} %shard_map.114.refs_8_), channel_id=1, source_target_pairs={{0,1},{1,0},{2,3},{3,2},{4,5},{5,4},{6,7},{7,6},{8,9},{9,8},{10,11... | collective-permute-start | bytes 1769480 | tf_op jit(solution)/shard_map/ppermute | solution.py:635
  64.1 17.4 %collective-permute-start.15 = (bf16[768,384]{1,0:T(8,128)(2,1)}, bf16[768,384]{1,0:T(8,128)(2,1)S(1)}, u32[]{:S(2)}, u32[]{:S(2)}) collective-permute-start(bf16[768,384]{1,0:T(8,128)(2,1)} %shard_map.114.refs_8_), channel_id=1, source_target_pairs={{0,16},{16,0},{1,17},{17,1},{2,18},{18,2},{3,19},{19,3},{4,20},{20... | collective-permute-start | bytes 1769480 | tf_op jit(solution)/shard_map/ppermute | solution.py:636
  65.1 3.0 %copy-start.15 = (bf16[96,1152]{1,0:T(8,128)(2,1)}, bf16[96,1152]{1,0:T(8,128)(2,1)S(1)}, u32[]{:S(2)}) copy-start(bf16[96,1152]{1,0:T(8,128)(2,1)S(1)} %collective-permute-done.11.refs_9_.refs_8_) | copy-start | bytes 663556
  65.1 16.5 %collective-permute-start.16 = (bf16[768,384]{1,0:T(8,128)(2,1)S(1)}, bf16[768,384]{1,0:T(8,128)(2,1)S(1)}, u32[]{:S(2)}, u32[]{:S(2)}) collective-permute-start(bf16[768,384]{1,0:T(8,128)(2,1)S(1)} %collective-permute-done.10.refs_6_), channel_id=1, source_target_pairs={{0,16},{16,0},{1,17},{17,1},{2,18},{18,2},{3,19},{19,3},{4,20},{20... | collective-permute-start | bytes 1769480 | tf_op jit(solution)/shard_map/ppermute | solution.py:637
  68.1 0.7 copy-start.16
  74.6 7.5 %collective-permute-start.17 = (f32[4,8,288]{2,1,0:T(8,128)}, f32[4,8,288]{2,1,0:T(8,128)S(1)}, u32[]{:S(2)}, u32[]{:S(2)}) collective-permute-start(f32[4,8,288]{2,1,0:T(8,128)} %get-tuple-element.34.s0_ref), channel_id=1, source_target_pairs={{0,1},{1,0},{2,3},{3,2},{4,5},{5,4},{6,7},{7,6},{8,9},{9,8},{10,11... | collective-permute-start | bytes 110600 | tf_op jit(solution)/shard_map/ppermute | solution.py:644
  75.2 6.9 %collective-permute-start.18 = (f32[4,8,288]{2,1,0:T(8,128)}, f32[4,8,288]{2,1,0:T(8,128)S(1)}, u32[]{:S(2)}, u32[]{:S(2)}) collective-permute-start(f32[4,8,288]{2,1,0:T(8,128)} %get-tuple-element.34.s0_ref), channel_id=1, source_target_pairs={{0,16},{16,0},{1,17},{17,1},{2,18},{18,2},{3,19},{19,3},{4,20},{20... | collective-permute-start | bytes 110600 | tf_op jit(solution)/shard_map/ppermute | solution.py:645
  77.4 4.2 %copy-start.8 = (bf16[768,384]{1,0:T(8,128)(2,1)}, bf16[768,384]{1,0:T(8,128)(2,1)S(1)}, u32[]{:S(2)}) copy-start(bf16[768,384]{1,0:T(8,128)(2,1)S(1)} %collective-permute-done.13.refs_10_) | copy-start | bytes 1769476
  77.4 4.7 %collective-permute-start.19 = (f32[4,8,288]{2,1,0:T(8,128)}, f32[4,8,288]{2,1,0:T(8,128)S(1)}, u32[]{:S(2)}, u32[]{:S(2)}) collective-permute-start(f32[4,8,288]{2,1,0:T(8,128)} %get-tuple-element.34.s0_ref), channel_id=1, source_target_pairs={{0,17},{1,16},{16,1},{17,0},{2,19},{3,18},{18,3},{19,2},{4,21},{5,... | collective-permute-start | bytes 110600 | tf_op jit(solution)/shard_map/ppermute | solution.py:646
  81.5 7.9 %copy-start.10 = (bf16[768,384]{1,0:T(8,128)(2,1)}, bf16[768,384]{1,0:T(8,128)(2,1)S(1)}, u32[]{:S(2)}) copy-start(bf16[768,384]{1,0:T(8,128)(2,1)S(1)} %collective-permute-done.15.refs_9_) | copy-start | bytes 1769476
  81.5 7.9 %copy-start.11 = (bf16[768,384]{1,0:T(8,128)(2,1)}, bf16[768,384]{1,0:T(8,128)(2,1)S(1)}, u32[]{:S(2)}) copy-start(bf16[768,384]{1,0:T(8,128)(2,1)S(1)} %collective-permute-done.16.refs_7_) | copy-start | bytes 1769476
  81.6 20.0 %collective-permute-start.23 = (bf16[768,384]{1,0:T(8,128)(2,1)S(1)}, bf16[768,384]{1,0:T(8,128)(2,1)S(1)}, u32[]{:S(2)}, u32[]{:S(2)}) collective-permute-start(bf16[768,384]{1,0:T(8,128)(2,1)S(1)} %collective-permute-done.13.refs_10_), channel_id=1, source_target_pairs={{0,16},{16,0},{1,17},{17,1},{2,18},{18,2},{3,19},{19,3},{4,20},{20... | collective-permute-start | bytes 1769480 | tf_op jit(solution)/shard_map/ppermute | solution.py:637
  82.0 0.6 copy-start.21
  82.0 0.6 copy-start.22
  82.1 0.6 copy-start.23
  89.4 1.9 %collective-permute-start.20 = (bf16[288,384]{1,0:T(8,128)(2,1)}, bf16[288,384]{1,0:T(8,128)(2,1)S(1)}, u32[]{:S(2)}, u32[]{:S(2)}) collective-permute-start(bf16[288,384]{1,0:T(8,128)(2,1)} %get-tuple-element.36), channel_id=1, source_target_pairs={{0,16},{16,0},{1,17},{17,1},{2,18},{18,2},{3,19},{19,3},{4,20},{20... | collective-permute-start | bytes 663560 | tf_op jit(solution)/shard_map/ppermute | solution.py:652
  89.8 8.5 %collective-permute-start.21 = (bf16[288,384]{1,0:T(8,128)(2,1)}, bf16[288,384]{1,0:T(8,128)(2,1)S(1)}, u32[]{:S(2)}, u32[]{:S(2)}) collective-permute-start(bf16[288,384]{1,0:T(8,128)(2,1)} %get-tuple-element.37), channel_id=1, source_target_pairs={{0,1},{1,0},{2,3},{3,2},{4,5},{5,4},{6,7},{7,6},{8,9},{9,8},{10,11... | collective-permute-start | bytes 663560 | tf_op jit(solution)/shard_map/ppermute | solution.py:653
  91.2 10.3 %collective-permute-start.22 = (bf16[288,384]{1,0:T(8,128)(2,1)}, bf16[288,384]{1,0:T(8,128)(2,1)S(1)}, u32[]{:S(2)}, u32[]{:S(2)}) collective-permute-start(bf16[288,384]{1,0:T(8,128)(2,1)} %get-tuple-element.38), channel_id=1, source_target_pairs={{0,17},{1,16},{16,1},{17,0},{2,19},{3,18},{18,3},{19,2},{4,21},{5,... | collective-permute-start | bytes 663560 | tf_op jit(solution)/shard_map/ppermute | solution.py:654
  91.3 10.2 %copy-start.17 = (bf16[288,384]{1,0:T(8,128)(2,1)}, bf16[288,384]{1,0:T(8,128)(2,1)S(1)}, u32[]{:S(2)}) copy-start(bf16[288,384]{1,0:T(8,128)(2,1)S(1)} %collective-permute-done.20.refs_1_) | copy-start | bytes 663556
  98.2 3.3 %copy-start.18 = (bf16[288,384]{1,0:T(8,128)(2,1)}, bf16[288,384]{1,0:T(8,128)(2,1)S(1)}, u32[]{:S(2)}) copy-start(bf16[288,384]{1,0:T(8,128)(2,1)S(1)} %collective-permute-done.21.refs_2_) | copy-start | bytes 663556
  101.5 0.7 copy-start.19
  101.5 0.9 copy-start.13
  102.4 8.1 %copy-start.2 = (f32[1,288,32]{1,2,0:T(8,128)S(1)}, f32[1,288,32]{1,2,0:T(8,128)}, u32[]{:S(2)}) copy-start(f32[1,288,32]{1,2,0:T(8,128)} %param.12) | copy-start | bytes 110596
  108.6 1.9 %collective-permute-start.24 = (bf16[32,288]{1,0:T(8,128)(2,1)}, bf16[32,288]{1,0:T(8,128)(2,1)S(1)}, u32[]{:S(2)}, u32[]{:S(2)}) collective-permute-start(bf16[32,288]{1,0:T(8,128)(2,1)} %get-tuple-element.39), channel_id=1, source_target_pairs={{0,16},{16,0},{1,17},{17,1},{2,18},{18,2},{3,19},{19,3},{4,20},{20... | collective-permute-start | bytes 55304 | tf_op jit(solution)/shard_map/ppermute | solution.py:569

commit v5 on v4

--- a/solution.py
+++ b/solution.py
@@ -142,10 +142,14 @@
     return copies
 
 
+def fold(pair):
+    return pair ^ (pair // 2)
+
+
 def places():
     place = lax.axis_index("req")
     group = 2 * lax.axis_index("seq") + lax.axis_index("cfg")
-    return lax.rem(place, 2), place // 2, lax.axis_size("req") // 2, group
+    return lax.rem(place, 2), fold(place // 2), lax.axis_size("req") // 2, group
 
 
 def window(j, size):
@@ -176,7 +180,7 @@
     stores[0].start()
     count = 4
     for k in range(count):
-        part = full_ref[:, window(lax.rem(pair + k, steps), third)]
+        part = full_ref[:, window(fold(lax.rem(pair + k, steps)), third)]
         part = jnp.where(side == 0, part, pltpu.roll(part, third // 2, 1))
         norm_buf[:, k * third : (k + 1) * third] = part.astype(BF16)
     stores.append(pltpu.make_async_copy(norm_buf, norm_ref, out_sem.at[1]))
@@ -404,27 +408,26 @@
     )(*norms, acc, *pieces)
 
 
-def heads_kernel(length_ref, qk_ref, v_ref, s0_ref, s1_ref, s2_ref, s3_ref, *refs):
-    outs = refs[:4]
-    qk_in, v_in, sums_in, out_buf, sem, out_sem = refs[4:]
+def heads_kernel(blocks, length_ref, qk_ref, v_ref, s0_ref, s1_ref, s2_ref, s3_ref, *refs):
+    outs = refs[:2]
+    qk_in, v_in, sums_in, out_buf, sem, out_sem = refs[2:]
     rows = qk_ref.shape[1]
     third = qk_ref.shape[2] // 2
     count = third // DH
     width = 4 * third
     sum_refs = (s0_ref, s1_ref, s2_ref, s3_ref)
-    loads = load_all(
-        [(sum_refs[j], sums_in.at[j]) for j in range(4)]
-        + [(qk_ref.at[b], qk_in.at[b]) for b in range(4)]
-        + [
-            (v_ref.at[b, :, h * DH : (h + 1) * DH], v_in.at[h, b // 2, b % 2 * rows : (b % 2 + 1) * rows, :DH])
-            for b in range(4)
-            for h in range(count)
-        ],
-        sem,
-    )
-    for h in range(count):
-        for b in range(2):
-            v_in[h, b, :, DH:] = jnp.ones((2 * rows, DH), BF16)
+    loads = [(sum_refs[j], sums_in.at[j]) for j in range(4)]
+    order = [b for block in blocks for b in (block - block % 2, block - block % 2 + 1)]
+    for b in order:
+        loads.append((qk_ref.at[b], qk_in.at[b]))
+    for b in order:
+        held = v_in.at[b // 2, b % 2 * rows : (b % 2 + 1) * rows]
+        for h in range(count):
+            loads.append((v_ref.at[b, :, h * DH : (h + 1) * DH], held.at[:, 2 * h * DH : (2 * h + 1) * DH]))
+    loads = load_all(loads, sem)
+    for b in range(2):
+        for h in range(count):
+            v_in[b, :, (2 * h + 1) * DH : (2 * h + 2) * DH] = jnp.ones((2 * rows, DH), BF16)
     row = lax.broadcasted_iota(jnp.int32, (24, DH), 0)
     pick = (row % 8 == 0).astype(BF16)
     place = lax.broadcasted_iota(jnp.int32, (1, rows), 1)
@@ -432,21 +435,23 @@
     masks = [place < length_ref[0] - (j + position - 2 * j * position) * rows for j in range(2)]
     for copy in loads[:4]:
         copy.wait()
-    scale_q, scale_k = [], []
+    scale_q, scale_k = {}, {}
     for block in range(4):
         sums = sums_in[0, block] + sums_in[1, block ^ 1] + sums_in[2, block ^ 2] + sums_in[3, block ^ 3]
         inverse = lax.rsqrt(sums * (1.0 / width) + 1e-06)
-        high = inverse.astype(BF16).astype(F32)
-        middle = (inverse - high).astype(BF16).astype(F32)
-        stacked = jnp.concatenate([high, middle, inverse - high - middle], axis=0).astype(BF16)
-        turned = lax.dot_general(stacked, pick, (((0,), (0,)), ((), ())), preferred_element_type=F32)
-        scale_q.append(turned[:, :1])
-        scale_k.append(inverse[1:2, :])
-    for copy in loads[4:8]:
-        copy.wait()
-    items = [(block, h) for block in (1, 3, 2, 0) for h in range(count)]
-
-    def scores_of(block, h):
+        scale_k[block] = inverse[1:2, :]
+        if block in blocks:
+            high = inverse.astype(BF16).astype(F32)
+            middle = (inverse - high).astype(BF16).astype(F32)
+            stacked = jnp.concatenate([high, middle, inverse - high - middle], axis=0).astype(BF16)
+            turned = lax.dot_general(stacked, pick, (((0,), (0,)), ((), ())), preferred_element_type=F32)
+            scale_q[block] = turned[:, :1]
+    items = [(at, block, h) for at, block in enumerate(blocks) for h in range(count)]
+
+    def scores_of(at, block, h):
+        if h == 0:
+            for copy in loads[4 + 2 * at : 6 + 2 * at]:
+                copy.wait()
         first = block - block % 2
         query = qk_in[block, :, h * DH : (h + 1) * DH]
         found = []
@@ -458,12 +463,12 @@
 
     stores = []
     ahead = scores_of(*items[0])
-    for at, (block, h) in enumerate(items):
+    for turn, (at, block, h) in enumerate(items):
         scores = ahead
-        if at + 1 < len(items):
-            ahead = scores_of(*items[at + 1])
-        if at == 0:
-            for copy in loads[8:]:
+        if turn + 1 < len(items):
+            ahead = scores_of(*items[turn + 1])
+        if h == 0:
+            for copy in loads[8 + 2 * count * at : 8 + 2 * count * (at + 1)]:
                 copy.wait()
         top = jnp.maximum(
             jnp.max(scores[0], axis=-1, keepdims=True), jnp.max(scores[1], axis=-1, keepdims=True)
@@ -471,33 +476,35 @@
         weighted = 0.0
         for j in range(2):
             probs = jnp.exp2((scores[j] - top) * scale_q[block]).astype(BF16)
-            weighted += times(probs, v_in[h, block // 2, j * rows : (j + 1) * rows, :])
-        out_buf[block, :, h * DH : (h + 1) * DH] = (weighted[:, :DH] / weighted[:, DH:]).astype(BF16)
+            values = v_in[block // 2, j * rows : (j + 1) * rows, 2 * h * DH : (2 * h + 2) * DH]
+            weighted += times(probs, values)
+        out_buf[at, :, h * DH : (h + 1) * DH] = (weighted[:, :DH] / weighted[:, DH:]).astype(BF16)
         if h == count - 1:
-            stores.append(pltpu.make_async_copy(out_buf.at[block], outs[block], out_sem.at[block]))
+            stores.append(pltpu.make_async_copy(out_buf.at[at], outs[at], out_sem.at[at]))
             stores[-1].start()
     for copy in stores:
         copy.wait()
 
 
-def team_attention(length, qk, v, sums):
+def team_attention(blocks, effort, length, qk, v, sums):
     rows = qk.shape[1]
     third = qk.shape[2] // 2
+    count = third // DH
     return pl.pallas_call(
-        heads_kernel,
-        out_shape=[shape_of(rows, third)] * 4,
+        functools.partial(heads_kernel, blocks),
+        out_shape=[shape_of(rows, third)] * 2,
         in_specs=[SMEM] + [ANY] * 6,
-        out_specs=[ANY] * 4,
+        out_specs=[ANY] * 2,
         scratch_shapes=[
             pltpu.VMEM(qk.shape, BF16),
-            pltpu.VMEM((third // DH, 2, 2 * rows, 2 * DH), BF16),
+            pltpu.VMEM((2, 2 * rows, 2 * third), BF16),
             pltpu.VMEM((4, 4, 8, rows), F32),
-            pltpu.VMEM((4, rows, third), BF16),
-            pltpu.SemaphoreType.DMA((8 + 4 * third // DH,)),
-            pltpu.SemaphoreType.DMA((4,)),
+            pltpu.VMEM((2, rows, third), BF16),
+            pltpu.SemaphoreType.DMA((8 + 4 * count,)),
+            pltpu.SemaphoreType.DMA((2,)),
         ],
         compiler_params=params(),
-        cost_estimate=cost(1.1e10, 1e6),
+        cost_estimate=cost(effort, 1e6),
     )(length, qk, v, *sums)
 
 
@@ -519,7 +526,7 @@
         loads[j].wait()
         part = att_in[j].astype(F32)
         part = jnp.where(side == 0, part, pltpu.roll(part, third // 2, 1)).astype(BF16)
-        group_ref[:, window(lax.rem((own ^ j) + steps - pair, steps), third)] = part
+        group_ref[:, window(lax.rem(fold(own ^ j) + steps - pair, steps), third)] = part
     for copy in loads[4:8]:
         copy.wait()
     total = times(group_ref[:, :half], held_ref[:half, :])
@@ -588,8 +595,8 @@
     rows, width = state.shape
     third = width // 4
     parts = lax.axis_size("req")
-    up = [(i, (i - 2) % parts) for i in range(parts)]
-    down = [(i, (i + 2) % parts) for i in range(parts)]
+    up = [(2 * fold(i) + side, 2 * fold((i - 1) % 4) + side) for i in range(4) for side in range(2)]
+    down = [(target, source) for source, target in up]
     beside = [(i, i ^ 1) for i in range(parts)]
 
     def along(piece):
@@ -645,13 +652,15 @@
         lax.ppermute(sums, "cfg", SWAP),
         lax.ppermute(sums, ("cfg", "seq"), diagonal),
     ]
-    v_full = after(v_full, packed_y[1], *packed_c, packed_yc[0])
-    heads = team_attention(lengths, qk_full, v_full, all_sums)
+    v_full = after(v_full, packed_c[0], packed_yc[0])
+    far = team_attention((1, 3), 6e9, lengths, qk_full, v_full, all_sums)
+    far = lax.optimization_barrier((*far, packed_y[1], packed_c[1]))[:2]
+    near = team_attention((2, 0), 1e6, lengths, after(qk_full, far[0]), v_full, all_sums)
     attended = [
-        heads[0],
-        lax.ppermute(heads[2], "cfg", SWAP),
-        lax.ppermute(heads[1], "seq", SWAP),
-        lax.ppermute(heads[3], ("cfg", "seq"), diagonal),
+        near[1],
+        lax.ppermute(near[0], "cfg", SWAP),
+        lax.ppermute(far[0], "seq", SWAP),
+        lax.ppermute(far[1], ("cfg", "seq"), diagonal),
     ]
     quarters = [part[j] for j in range(2) for part in (packed, packed_c, packed_y, packed_yc)]
     own, outgoing = project(state, modes, w_head.T, attended, quarters)

time: 112 us -> 108 us (0.964)
  waiting for transfers between devices: 43.6 us -> 37.8 us
  Pallas kernels: 35.2 us -> 38.2 us
  starting transfers between devices: 25.8 us -> 23.9 us
    ppermute x4, waiting for transfers between devices: 18.5 us -> 22.9 us  [across(): return lax.ppermute(piece, 'req', beside)]
    ppermute x3, waiting for transfers between devices: 10.2 us -> 6.11 us  [the longest x1 5.4 us: team_local(): lax.ppermute(far[1], ('cfg', 'seq'), diagonal)]
    pallas_call x1 -> x2, Pallas kernels: 6.69 us -> 9.92 us  [team_attention(): pl.pallas_call(functools.partial(heads_kernel, blocks), out_shape=[shape_...]
    ppermute x3, starting transfers between devices: 12.1 us -> 9.25 us  [along(): return lax.ppermute(piece, 'req', up)]
    ppermute x3, waiting for transfers between devices: 6.79 us -> 4.18 us  [along(): return lax.ppermute(piece, 'req', up)]
    ppermute x1, waiting for transfers between devices: 2.21 us -> 0.01 us  [team_local(): packed_y.append(lax.ppermute(packed[1], 'seq', SWAP))]
    ppermute x1, starting transfers between devices: 0.01 us -> 1.13 us  [team_local(): lax.ppermute(sums, ('cfg', 'seq'), diagonal)]
    unnamed x48 -> x50, local copies, waits for them, and re-layouts: 3.07 us -> 3.08 us
  transfers between devices with their start and end apart: 25 -> 25, of which waited for: 12 -> 11; matrix products, arithmetic and copies ran while one was open for 1% -> 1% of each run, Pallas kernels for 23% -> 27%
where the time goes in v5:
time: 108 us; the launch traced here: 107 us
  Pallas kernels  38.2 us (35%)
  waiting for transfers between devices  37.8 us (35%)
  starting transfers between devices  23.9 us (22%)
  local copies, waits for them, and re-layouts  3.74 us (3%)
  between operations  2.31 us (2%)
  other arithmetic  1.47 us (1%)
    ppermute x4, waiting for transfers between devices, across(): return lax.ppermute(piece, 'req', beside)  22.9 us
    pallas_call x2, Pallas kernels, team_attention(): pl.pallas_call(functools.partial(heads_kernel, blocks), out_shape=[shape_...  9.92 us
    ppermute x3, starting transfers between devices, along(): return lax.ppermute(piece, 'req', up)  9.25 us
    pallas_call x1, Pallas kernels, project(): pl.pallas_call(out_kernel, out_shape=[shape_of(channels, rows, dtype=F32)...  6.17 us
    pallas_call x1, Pallas kernels, last_scores(): pl.pallas_call(functools.partial(scores_kernel, len(pieces)), out_shape=[...  5.77 us
    ppermute x1, waiting for transfers between devices, team_local(): lax.ppermute(far[1], ('cfg', 'seq'), diagonal)  5.4 us
    pallas_call x1, Pallas kernels, first_part(): pl.pallas_call(functools.partial(first_kernel, len(pieces)), out_shape=[q...  5.22 us
    ppermute x2, waiting for transfers between devices, back(): return lax.ppermute(piece, 'req', down)  4.59 us
  transfers between devices with their start and end apart: 25, of which 11 were waited for; matrix products, arithmetic and copies ran while one was open for 1% of the time, Pallas kernels for 27%

profile of v5, /device:TPU:0, one launch (start us, length us, event | category | flops | bytes accessed | tf_op | source)
XLA Modules:
  0.0 107.5 jit_solution(2814809660774437738)
XLA Ops:
  0.0 3.2 %shard_map.109 = (bf16[192,1536]{1,0:T(8,128)(2,1)}, bf16[288,1536]{1,0:T(8,128)(2,1)}) custom-call(bf16[192,4608]{1,0:T(8,128)(2,1)} %qkv_ref.1, bf16[192,1536]{1,0:T(8,128)(2,1)} %w_out_ref.1, bf16[288,1536]{1,0:T(8,128)(2,1)} %bitcast.17, f32[5,1,1536]{2,1,0:T(1,128)} %bitcast.20), custom_call_target="tpu_custom_call" | custom-call | flops 4000000000 | bytes 1000000 | tf_op jit(solution)/shard_map/pallas_call | solution.py:193
  3.2 3.0 %collective-permute-start = (bf16[288,1536]{1,0:T(8,128)(2,1)}, bf16[288,1536]{1,0:T(8,128)(2,1)S(1)}, u32[]{:S(2)}, u32[]{:S(2)}) collective-permute-start(bf16[288,1536]{1,0:T(8,128)(2,1)} %get-tuple-element.26.refs_0_), channel_id=1, source_target_pairs={{0,1},{1,0},{2,3},{3,2},{4,5},{5,4},{6,7},{7,6},{8,9},{9,8},{10,11... | collective-permute-start | bytes 2654216 | tf_op jit(solution)/shard_map/ppermute | solution.py:613
  6.2 1.5 %collective-permute-start.3 = (bf16[192,1536]{1,0:T(8,128)(2,1)}, bf16[192,1536]{1,0:T(8,128)(2,1)S(1)}, u32[]{:S(2)}, u32[]{:S(2)}) collective-permute-start(bf16[192,1536]{1,0:T(8,128)(2,1)} %get-tuple-element.27.refs_4_.refs_0_), channel_id=1, source_target_pairs={{0,2},{2,0},{4,6},{6,4},{8,10},{10,8},{12,14},{14,12},{1,3},{3,1},... | collective-permute-start | bytes 1769480 | tf_op jit(solution)/shard_map/ppermute | solution.py:609
  7.7 2.6 %collective-permute-start.4 = (bf16[192,1536]{1,0:T(8,128)(2,1)}, bf16[192,1536]{1,0:T(8,128)(2,1)S(1)}, u32[]{:S(2)}, u32[]{:S(2)}) collective-permute-start(bf16[192,1536]{1,0:T(8,128)(2,1)} %get-tuple-element.27.refs_4_.refs_0_), channel_id=1, source_target_pairs={{0,8},{2,10},{4,0},{6,2},{12,4},{14,6},{8,12},{10,14},{1,9},{3,11}... | collective-permute-start | bytes 1769480 | tf_op jit(solution)/shard_map/ppermute | solution.py:603
  10.4 0.6 broadcast_in_dim.16.refs_5_
  11.0 10.2 %collective-permute-done.3.refs_5_.refs_1_ = bf16[192,1536]{1,0:T(8,128)(2,1)S(1)} collective-permute-done((bf16[192,1536]{1,0:T(8,128)(2,1)}, bf16[192,1536]{1,0:T(8,128)(2,1)S(1)}, u32[]{:S(2)}, u32[]{:S(2)}) %collective-permute-start.3) | collective-permute-done | bytes 589856 | tf_op jit(solution)/shard_map/ppermute | solution.py:609
  21.3 1.4 %collective-permute-done.4.refs_6_.refs_2_ = bf16[192,1536]{1,0:T(8,128)(2,1)S(1)} collective-permute-done((bf16[192,1536]{1,0:T(8,128)(2,1)}, bf16[192,1536]{1,0:T(8,128)(2,1)S(1)}, u32[]{:S(2)}, u32[]{:S(2)}) %collective-permute-start.4) | collective-permute-done | bytes 589856 | tf_op jit(solution)/shard_map/ppermute | solution.py:603
  22.6 0.5 collective-permute-start.5
  23.2 3.3 %collective-permute-start.6 = (bf16[192,1536]{1,0:T(8,128)(2,1)S(1)}, bf16[192,1536]{1,0:T(8,128)(2,1)S(1)}, u32[]{:S(2)}, u32[]{:S(2)}) collective-permute-start(bf16[192,1536]{1,0:T(8,128)(2,1)S(1)} %collective-permute-done.4.refs_6_.refs_2_), channel_id=1, source_target_pairs={{0,8},{2,10},{4,0},{6,2},{12,4},{14,6},{8,12},{10,14},{1,9},{3,11}... | collective-permute-start | bytes 1769480 | tf_op jit(solution)/shard_map/ppermute | solution.py:603
  26.4 0.0 collective-permute-start.1
  26.5 0.0 collective-permute-done.refs_1_
  26.5 0.5 collective-permute-start.2
  27.0 9.3 %collective-permute-done.5.refs_7_.refs_3_ = bf16[192,1536]{1,0:T(8,128)(2,1)S(1)} collective-permute-done((bf16[192,1536]{1,0:T(8,128)(2,1)S(1)}, bf16[192,1536]{1,0:T(8,128)(2,1)S(1)}, u32[]{:S(2)}, u32[]{:S(2)}) %collective-permute-start.5) | collective-permute-done | bytes 589856 | tf_op jit(solution)/shard_map/ppermute | solution.py:609
  36.2 1.0 collective-permute-done.6.refs_6_.refs_5_.refs_0_
  37.3 1.5 %collective-permute-start.7 = (bf16[192,1536]{1,0:T(8,128)(2,1)S(1)}, bf16[192,1536]{1,0:T(8,128)(2,1)}, u32[]{:S(2)}, u32[]{:S(2)}) collective-permute-start(bf16[192,1536]{1,0:T(8,128)(2,1)S(1)} %collective-permute-done.6.refs_6_.refs_5_.refs_0_), channel_id=1, source_target_pairs={{0,2},{2,0},{4,6},{6,4},{8,10},{10,8},{12,14},{14,12},{1,3},{3,1},... | collective-permute-start | bytes 1769480 | tf_op jit(solution)/shard_map/ppermute | solution.py:609
  38.8 3.4 %collective-permute-start.8 = (bf16[192,1536]{1,0:T(8,128)(2,1)S(1)}, bf16[192,1536]{1,0:T(8,128)(2,1)S(1)}, u32[]{:S(2)}, u32[]{:S(2)}) collective-permute-start(bf16[192,1536]{1,0:T(8,128)(2,1)S(1)} %collective-permute-done.6.refs_6_.refs_5_.refs_0_), channel_id=1, source_target_pairs={{0,8},{2,10},{4,0},{6,2},{12,4},{14,6},{8,12},{10,14},{1,9},{3,11}... | collective-permute-start | bytes 1769480 | tf_op jit(solution)/shard_map/ppermute | solution.py:603
  42.2 2.0 %shard_map.111.refs_4_ = bf16[768,384]{1,0:T(8,128)(2,1)} custom-call(bf16[192,1536]{1,0:T(8,128)(2,1)} %get-tuple-element.27.refs_4_.refs_0_, bf16[192,1536]{1,0:T(8,128)(2,1)} %copy-done, bf16[192,1536]{1,0:T(8,128)(2,1)} %copy-done.15, bf16[192,1536]{1,0:T(8,128)(2,1)} %copy-done.17), custom_call_target="tpu_custom_call" | custom-call | flops 3000000000 | bytes 1000000 | tf_op jit(solution)/shard_map/pallas_call | solution.py:228
  44.2 0.6 collective-permute-start.10
  45.4 0.0 collective-permute-done.1.refs_2_
  45.5 0.1 collective-permute-start.13
  45.5 0.0 collective-permute-done.2.refs_3_
  45.6 0.1 collective-permute-start.9
  45.6 0.7 copy-done.9
  46.4 5.2 %shard_map.110 = (bf16[4,288,768]{2,1,0:T(8,128)(2,1)}, bf16[4,288,384]{2,1,0:T(8,128)(2,1)}) custom-call(bf16[288,1536]{1,0:T(8,128)(2,1)} %get-tuple-element.26.refs_0_, bf16[288,1536]{1,0:T(8,128)(2,1)} %copy-done.8, bf16[288,1536]{1,0:T(8,128)(2,1)} %copy-done.9, bf16[288,1536]{1,0:T(8,128)(2,1)} %collective-permute-done.2.refs_3_, ...), custom_call_target="tpu_custom_call" | custom-call | flops 6000000000 | bytes 1000000 | tf_op jit(solution)/shard_map/pallas_call | solution.py:278
  51.6 1.7 %collective-permute-done.8.refs_8_.refs_7_.refs_2_ = bf16[192,1536]{1,0:T(8,128)(2,1)S(1)} collective-permute-done((bf16[192,1536]{1,0:T(8,128)(2,1)S(1)}, bf16[192,1536]{1,0:T(8,128)(2,1)S(1)}, u32[]{:S(2)}, u32[]{:S(2)}) %collective-permute-start.8) | collective-permute-done | bytes 589856 | tf_op jit(solution)/shard_map/ppermute | solution.py:603
  53.4 3.4 %collective-permute-done.9.refs_3_ = bf16[192,384]{1,0:T(8,128)(2,1)S(1)} collective-permute-done((bf16[192,384]{1,0:T(8,128)(2,1)S(1)}, bf16[192,384]{1,0:T(8,128)(2,1)S(1)}, u32[]{:S(2)}, u32[]{:S(2)}) %collective-permute-start.9) | collective-permute-done | bytes 147488 | tf_op jit(solution)/shard_map/ppermute | solution.py:606
  56.8 0.0 collective-permute-done.7.refs_7_.refs_6_.refs_1_
  56.8 0.0 collective-permute-done.10.refs_6_
  56.8 0.6 collective-permute-start.11
  57.4 0.6 collective-permute-start.12
  58.0 0.0 collective-permute-start.14
  58.0 2.0 %shard_map.115.refs_8_ = bf16[768,384]{1,0:T(8,128)(2,1)} custom-call(bf16[192,1536]{1,0:T(8,128)(2,1)} %copy-done.12, bf16[192,1536]{1,0:T(8,128)(2,1)} %collective-permute-done.7.refs_7_.refs_6_.refs_1_, bf16[192,1536]{1,0:T(8,128)(2,1)} %copy-done.1, bf16[192,384]{1,0:T(8,128)(2,1)} %copy-done.24), custom_call_target="tpu_custom_call" | custom-call | flops 3000000000 | bytes 1000000 | tf_op jit(solution)/shard_map/pallas_call | solution.py:228
  60.1 0.6 collective-permute-start.18
  60.7 3.4 %collective-permute-done.11.refs_9_.refs_8_ = bf16[96,1152]{1,0:T(8,128)(2,1)S(1)} collective-permute-done((bf16[96,1152]{1,0:T(8,128)(2,1)S(1)}, bf16[96,1152]{1,0:T(8,128)(2,1)S(1)}, u32[]{:S(2)}, u32[]{:S(2)}) %collective-permute-start.11) | collective-permute-done | bytes 221216 | tf_op jit(solution)/shard_map/ppermute | solution.py:609
  64.1 0.0 collective-permute-start.19
  64.1 1.1 %collective-permute-done.12.refs_10_.refs_9_ = bf16[96,1152]{1,0:T(8,128)(2,1)S(1)} collective-permute-done((bf16[96,1152]{1,0:T(8,128)(2,1)S(1)}, bf16[96,1152]{1,0:T(8,128)(2,1)S(1)}, u32[]{:S(2)}, u32[]{:S(2)}) %collective-permute-start.12) | collective-permute-done | bytes 221216 | tf_op jit(solution)/shard_map/ppermute | solution.py:606
  65.2 0.7 copy-done.19
  65.9 5.8 %shard_map.112 = (bf16[4,288,768]{2,1,0:T(8,128)(2,1)}, f32[4,8,288]{2,1,0:T(8,128)}) custom-call(bf16[288,1536]{1,0:T(8,128)(2,1)} %get-tuple-element.26.refs_0_, bf16[288,1536]{1,0:T(8,128)(2,1)} %copy-done.8, bf16[288,1536]{1,0:T(8,128)(2,1)} %copy-done.9, bf16[288,1536]{1,0:T(8,128)(2,1)} %collective-permute-done.2.refs_3_, ...), custom_call_target="tpu_custom_call" | custom-call | flops 6000000000 | bytes 1000000 | tf_op jit(solution)/shard_map/pallas_call | solution.py:344
  71.7 1.1 %collective-permute-start.15 = (f32[4,8,288]{2,1,0:T(8,128)}, f32[4,8,288]{2,1,0:T(8,128)S(1)}, u32[]{:S(2)}, u32[]{:S(2)}) collective-permute-start(f32[4,8,288]{2,1,0:T(8,128)} %get-tuple-element.37.s0_ref), channel_id=1, source_target_pairs={{0,1},{1,0},{2,3},{3,2},{4,5},{5,4},{6,7},{7,6},{8,9},{9,8},{10,11... | collective-permute-start | bytes 110600 | tf_op jit(solution)/shard_map/ppermute | solution.py:651
  72.8 0.0 collective-permute-done.13.refs_5_
  72.8 0.0 collective-permute-done.14.refs_7_
  72.8 1.1 %collective-permute-start.17 = (f32[4,8,288]{2,1,0:T(8,128)}, f32[4,8,288]{2,1,0:T(8,128)S(1)}, u32[]{:S(2)}, u32[]{:S(2)}) collective-permute-start(f32[4,8,288]{2,1,0:T(8,128)} %get-tuple-element.37.s0_ref), channel_id=1, source_target_pairs={{0,17},{1,16},{16,1},{17,0},{2,19},{3,18},{18,3},{19,2},{4,21},{5,... | collective-permute-start | bytes 110600 | tf_op jit(solution)/shard_map/ppermute | solution.py:653
  73.9 3.9 %shard_map.113.v_ref = bf16[4,288,384]{2,1,0:T(8,128)(2,1)} custom-call(bf16[288,1536]{1,0:T(8,128)(2,1)} %get-tuple-element.26.refs_0_, bf16[288,1536]{1,0:T(8,128)(2,1)} %copy-done.8, bf16[288,1536]{1,0:T(8,128)(2,1)} %copy-done.9, bf16[288,1536]{1,0:T(8,128)(2,1)} %collective-permute-done.2.refs_3_, bf16[4,288,384]{2,1,0:T(8,128)(2,1)} %get-tuple-element.32.refs_4_, ...), custom_call_target="tpu_custom_call" | custom-call | flops 4000000000 | bytes 1000000 | tf_op jit(solution)/shard_map/pallas_call | solution.py:394
  77.9 0.0 collective-permute-done.18.refs_10_
  77.9 0.1 collective-permute-start.23
  78.0 0.0 collective-permute-done.15.s1_ref
  78.0 0.0 collective-permute-done.16.s2_ref
  78.1 0.7 copy-done.3
  78.7 0.0 copy-done.4
  78.8 0.0 copy-done.5
  78.8 5.0 %shard_map.114 = (bf16[288,384]{1,0:T(8,128)(2,1)}, bf16[288,384]{1,0:T(8,128)(2,1)}) custom-call(s32[1]{0:T(128)} %copy.12.length_ref, bf16[4,288,768]{2,1,0:T(8,128)(2,1)} %get-tuple-element.41.qk_ref, bf16[4,288,384]{2,1,0:T(8,128)(2,1)} %shard_map.113.v_ref, f32[4,8,288]{2,1,0:T(8,128)} %get-tuple-element.37.s0_ref, f32[4,8,288]{2,1,0:T(8,128)} %copy-done.3, ...), custom_call_target="tpu_custom_call" | custom-call | flops 6000000000 | bytes 1000000 | tf_op jit(solution)/shard_map/pallas_call | solution.py:493
  83.8 1.1 %collective-permute-start.21 = (bf16[288,384]{1,0:T(8,128)(2,1)}, bf16[288,384]{1,0:T(8,128)(2,1)S(1)}, u32[]{:S(2)}, u32[]{:S(2)}) collective-permute-start(bf16[288,384]{1,0:T(8,128)(2,1)} %get-tuple-element.40), channel_id=1, source_target_pairs={{0,1},{1,0},{2,3},{3,2},{4,5},{5,4},{6,7},{7,6},{8,9},{9,8},{10,11... | collective-permute-start | bytes 663560 | tf_op jit(solution)/shard_map/ppermute | solution.py:662
  84.9 5.0 %shard_map.116 = (bf16[288,384]{1,0:T(8,128)(2,1)}, bf16[288,384]{1,0:T(8,128)(2,1)}) custom-call(s32[1]{0:T(128)} %copy.12.length_ref, bf16[4,288,768]{2,1,0:T(8,128)(2,1)} %get-tuple-element.41.qk_ref, bf16[4,288,384]{2,1,0:T(8,128)(2,1)} %shard_map.113.v_ref, f32[4,8,288]{2,1,0:T(8,128)} %get-tuple-element.37.s0_ref, f32[4,8,288]{2,1,0:T(8,128)} %copy-done.3, ...), custom_call_target="tpu_custom_call" | custom-call | flops 1000000 | bytes 1000000 | tf_op jit(solution)/shard_map/pallas_call | solution.py:493
  89.8 0.1 collective-permute-start.20
  90.0 1.1 collective-permute-start.22
  91.1 0.5 collective-permute-done.20.refs_1_
  91.6 0.2 collective-permute-done.21.refs_2_
  91.8 5.4 %collective-permute-done.22.refs_3_ = bf16[288,384]{1,0:T(8,128)(2,1)S(1)} collective-permute-done((bf16[288,384]{1,0:T(8,128)(2,1)S(1)}, bf16[288,384]{1,0:T(8,128)(2,1)S(1)}, u32[]{:S(2)}, u32[]{:S(2)}) %collective-permute-start.22) | collective-permute-done | bytes 221216 | tf_op jit(solution)/shard_map/ppermute | solution.py:663
  97.2 0.6 copy-done.23
  97.8 0.2 copy-done.16
  98.1 6.2 %shard_map.117 = (f32[32,288]{1,0:T(8,128)}, bf16[32,288]{1,0:T(8,128)(2,1)}) custom-call(bf16[288,1536]{1,0:T(8,128)(2,1)} %bitcast.18, f32[5,1,1536]{2,1,0:T(1,128)} %bitcast.21, bf16[64,1536]{1,0:T(8,128)(2,1)} %bitcast.19, bf16[288,384]{1,0:T(8,128)(2,1)} %get-tuple-element.42.refs_0_, bf16[288,384]{1,0:T(8,128)(2,1)} %copy-done.22, ...), custom_call_target="tpu_custom_call" | custom-call | flops 8000000000 | bytes 1000000 | tf_op jit(solution)/shard_map/pallas_call | solution.py:551
  104.2 0.4 collective-permute-start.24
  106.0 0.0 collective-permute-done.24
  106.0 1.4 %fusion.4 = f32[1,288,32]{1,2,0:T(8,128)} fusion(f32[32,288]{1,0:T(8,128)} %get-tuple-element.46, bf16[32,288]{1,0:T(8,128)(2,1)S(1)} %collective-permute-done.24, f32[1,288,32]{1,2,0:T(8,128)S(1)} %copy-done.2, f32[]{:T(128)} %bitcast.15, f32[]{:T(128)} %bitcast.16, pred[]{:T(512)S(6)} %eq.4, pred[288]{0:T(512)(128)(4,1)S(1)} %add_compare_fusion), kind=kLoop, calls=%fused_computation.7 | loop fusion | flops 82944 | bytes 129321 | tf_op jit(solution)/shard_map/broadcast_in_dim | solution.py:583
  (54 shorter events, 0.2 us)
Async XLA Ops:
  0.0 10.3 %copy-start.6 = (f32[1536]{0:T(1024)S(1)}, f32[1536]{0:T(1024)}, u32[]{:S(2)}) copy-start(f32[1536]{0:T(1024)} %param.17) | copy-start | bytes 18436
  0.0 10.3 %copy-start.7 = (f32[1536]{0:T(1024)S(1)}, f32[1536]{0:T(1024)}, u32[]{:S(2)}) copy-start(f32[1536]{0:T(1024)} %param.16) | copy-start | bytes 18436
  3.2 23.3 %collective-permute-start = (bf16[288,1536]{1,0:T(8,128)(2,1)}, bf16[288,1536]{1,0:T(8,128)(2,1)S(1)}, u32[]{:S(2)}, u32[]{:S(2)}) collective-permute-start(bf16[288,1536]{1,0:T(8,128)(2,1)} %get-tuple-element.26.refs_0_), channel_id=1, source_target_pairs={{0,1},{1,0},{2,3},{3,2},{4,5},{5,4},{6,7},{7,6},{8,9},{9,8},{10,11... | collective-permute-start | bytes 2654216 | tf_op jit(solution)/shard_map/ppermute | solution.py:613
  6.2 15.0 %collective-permute-start.3 = (bf16[192,1536]{1,0:T(8,128)(2,1)}, bf16[192,1536]{1,0:T(8,128)(2,1)S(1)}, u32[]{:S(2)}, u32[]{:S(2)}) collective-permute-start(bf16[192,1536]{1,0:T(8,128)(2,1)} %get-tuple-element.27.refs_4_.refs_0_), channel_id=1, source_target_pairs={{0,2},{2,0},{4,6},{6,4},{8,10},{10,8},{12,14},{14,12},{1,3},{3,1},... | collective-permute-start | bytes 1769480 | tf_op jit(solution)/shard_map/ppermute | solution.py:609
  7.7 14.9 %collective-permute-start.4 = (bf16[192,1536]{1,0:T(8,128)(2,1)}, bf16[192,1536]{1,0:T(8,128)(2,1)S(1)}, u32[]{:S(2)}, u32[]{:S(2)}) collective-permute-start(bf16[192,1536]{1,0:T(8,128)(2,1)} %get-tuple-element.27.refs_4_.refs_0_), channel_id=1, source_target_pairs={{0,8},{2,10},{4,0},{6,2},{12,4},{14,6},{8,12},{10,14},{1,9},{3,11}... | collective-permute-start | bytes 1769480 | tf_op jit(solution)/shard_map/ppermute | solution.py:603
  21.2 21.0 %copy-start = (bf16[192,1536]{1,0:T(8,128)(2,1)}, bf16[192,1536]{1,0:T(8,128)(2,1)S(1)}, u32[]{:S(2)}) copy-start(bf16[192,1536]{1,0:T(8,128)(2,1)S(1)} %collective-permute-done.3.refs_5_.refs_1_) | copy-start | bytes 1769476
  22.6 14.6 %copy-start.15 = (bf16[192,1536]{1,0:T(8,128)(2,1)}, bf16[192,1536]{1,0:T(8,128)(2,1)S(1)}, u32[]{:S(2)}) copy-start(bf16[192,1536]{1,0:T(8,128)(2,1)S(1)} %collective-permute-done.4.refs_6_.refs_2_) | copy-start | bytes 1769476
  22.6 13.6 %collective-permute-start.5 = (bf16[192,1536]{1,0:T(8,128)(2,1)S(1)}, bf16[192,1536]{1,0:T(8,128)(2,1)S(1)}, u32[]{:S(2)}, u32[]{:S(2)}) collective-permute-start(bf16[192,1536]{1,0:T(8,128)(2,1)S(1)} %collective-permute-done.4.refs_6_.refs_2_), channel_id=1, source_target_pairs={{0,2},{2,0},{4,6},{6,4},{8,10},{10,8},{12,14},{14,12},{1,3},{3,1},... | collective-permute-start | bytes 1769480 | tf_op jit(solution)/shard_map/ppermute | solution.py:609
  23.2 14.1 %collective-permute-start.6 = (bf16[192,1536]{1,0:T(8,128)(2,1)S(1)}, bf16[192,1536]{1,0:T(8,128)(2,1)S(1)}, u32[]{:S(2)}, u32[]{:S(2)}) collective-permute-start(bf16[192,1536]{1,0:T(8,128)(2,1)S(1)} %collective-permute-done.4.refs_6_.refs_2_), channel_id=1, source_target_pairs={{0,8},{2,10},{4,0},{6,2},{12,4},{14,6},{8,12},{10,14},{1,9},{3,11}... | collective-permute-start | bytes 1769480 | tf_op jit(solution)/shard_map/ppermute | solution.py:603
  26.4 19.0 %collective-permute-start.1 = (bf16[288,1536]{1,0:T(8,128)(2,1)}, bf16[288,1536]{1,0:T(8,128)(2,1)S(1)}, u32[]{:S(2)}, u32[]{:S(2)}) collective-permute-start(bf16[288,1536]{1,0:T(8,128)(2,1)} %get-tuple-element.26.refs_0_), channel_id=1, source_target_pairs={{0,16},{16,0},{1,17},{17,1},{2,18},{18,2},{3,19},{19,3},{4,20},{20... | collective-permute-start | bytes 2654216 | tf_op jit(solution)/shard_map/ppermute | solution.py:614
  26.5 17.8 %copy-start.8 = (bf16[288,1536]{1,0:T(8,128)(2,1)}, bf16[288,1536]{1,0:T(8,128)(2,1)S(1)}, u32[]{:S(2)}) copy-start(bf16[288,1536]{1,0:T(8,128)(2,1)S(1)} %collective-permute-done.refs_1_) | copy-start | bytes 2654212
  26.5 19.1 %collective-permute-start.2 = (bf16[288,1536]{1,0:T(8,128)(2,1)S(1)}, bf16[288,1536]{1,0:T(8,128)(2,1)}, u32[]{:S(2)}, u32[]{:S(2)}) collective-permute-start(bf16[288,1536]{1,0:T(8,128)(2,1)S(1)} %collective-permute-done.refs_1_), channel_id=1, source_target_pairs={{0,16},{16,0},{1,17},{17,1},{2,18},{18,2},{3,19},{19,3},{4,20},{20... | collective-permute-start | bytes 2654216 | tf_op jit(solution)/shard_map/ppermute | solution.py:633
  36.2 2.5 %copy-start.17 = (bf16[192,1536]{1,0:T(8,128)(2,1)}, bf16[192,1536]{1,0:T(8,128)(2,1)S(1)}, u32[]{:S(2)}) copy-start(bf16[192,1536]{1,0:T(8,128)(2,1)S(1)} %collective-permute-done.5.refs_7_.refs_3_) | copy-start | bytes 1769476
  37.3 6.9 %copy-start.12 = (bf16[192,1536]{1,0:T(8,128)(2,1)}, bf16[192,1536]{1,0:T(8,128)(2,1)S(1)}, u32[]{:S(2)}) copy-start(bf16[192,1536]{1,0:T(8,128)(2,1)S(1)} %collective-permute-done.6.refs_6_.refs_5_.refs_0_) | copy-start | bytes 1769476
  37.3 19.5 %collective-permute-start.7 = (bf16[192,1536]{1,0:T(8,128)(2,1)S(1)}, bf16[192,1536]{1,0:T(8,128)(2,1)}, u32[]{:S(2)}, u32[]{:S(2)}) collective-permute-start(bf16[192,1536]{1,0:T(8,128)(2,1)S(1)} %collective-permute-done.6.refs_6_.refs_5_.refs_0_), channel_id=1, source_target_pairs={{0,2},{2,0},{4,6},{6,4},{8,10},{10,8},{12,14},{14,12},{1,3},{3,1},... | collective-permute-start | bytes 1769480 | tf_op jit(solution)/shard_map/ppermute | solution.py:609
  38.8 14.6 %collective-permute-start.8 = (bf16[192,1536]{1,0:T(8,128)(2,1)S(1)}, bf16[192,1536]{1,0:T(8,128)(2,1)S(1)}, u32[]{:S(2)}, u32[]{:S(2)}) collective-permute-start(bf16[192,1536]{1,0:T(8,128)(2,1)S(1)} %collective-permute-done.6.refs_6_.refs_5_.refs_0_), channel_id=1, source_target_pairs={{0,8},{2,10},{4,0},{6,2},{12,4},{14,6},{8,12},{10,14},{1,9},{3,11}... | collective-permute-start | bytes 1769480 | tf_op jit(solution)/shard_map/ppermute | solution.py:603
  44.2 12.6 %collective-permute-start.10 = (bf16[768,384]{1,0:T(8,128)(2,1)}, bf16[768,384]{1,0:T(8,128)(2,1)S(1)}, u32[]{:S(2)}, u32[]{:S(2)}) collective-permute-start(bf16[768,384]{1,0:T(8,128)(2,1)} %shard_map.111.refs_4_), channel_id=1, source_target_pairs={{0,1},{1,0},{2,3},{3,2},{4,5},{5,4},{6,7},{7,6},{8,9},{9,8},{10,11... | collective-permute-start | bytes 1769480 | tf_op jit(solution)/shard_map/ppermute | solution.py:635
  45.5 0.9 copy-start.9
  45.5 27.3 %collective-permute-start.13 = (bf16[768,384]{1,0:T(8,128)(2,1)}, bf16[768,384]{1,0:T(8,128)(2,1)}, u32[]{:S(2)}, u32[]{:S(2)}) collective-permute-start(bf16[768,384]{1,0:T(8,128)(2,1)} %shard_map.111.refs_4_), channel_id=1, source_target_pairs={{0,16},{16,0},{1,17},{17,1},{2,18},{18,2},{3,19},{19,3},{4,20},{20... | collective-permute-start | bytes 1769480 | tf_op jit(solution)/shard_map/ppermute | solution.py:643
  45.6 11.3 %collective-permute-start.9 = (bf16[192,384]{1,0:T(8,128)(2,1)S(1)}, bf16[192,384]{1,0:T(8,128)(2,1)S(1)}, u32[]{:S(2)}, u32[]{:S(2)}) collective-permute-start(bf16[192,384]{1,0:T(8,128)(2,1)S(1)} %slice.13), channel_id=1, source_target_pairs={{8,0},{10,2},{0,4},{2,6},{4,12},{6,14},{12,8},{14,10},{9,1},{11,3}... | collective-permute-start | bytes 442376 | tf_op jit(solution)/shard_map/ppermute | solution.py:606
  53.4 4.7 %copy-start.1 = (bf16[192,1536]{1,0:T(8,128)(2,1)}, bf16[192,1536]{1,0:T(8,128)(2,1)S(1)}, u32[]{:S(2)}) copy-start(bf16[192,1536]{1,0:T(8,128)(2,1)S(1)} %collective-permute-done.8.refs_8_.refs_7_.refs_2_) | copy-start | bytes 1769476
  56.8 1.2 %copy-start.24 = (bf16[192,384]{1,0:T(8,128)(2,1)}, bf16[192,384]{1,0:T(8,128)(2,1)S(1)}, u32[]{:S(2)}) copy-start(bf16[192,384]{1,0:T(8,128)(2,1)S(1)} %collective-permute-done.9.refs_3_) | copy-start | bytes 442372
  56.8 3.2 %copy-start.10 = (bf16[768,384]{1,0:T(8,128)(2,1)}, bf16[768,384]{1,0:T(8,128)(2,1)S(1)}, u32[]{:S(2)}) copy-start(bf16[768,384]{1,0:T(8,128)(2,1)S(1)} %collective-permute-done.10.refs_6_) | copy-start | bytes 1769476
  56.8 7.2 %collective-permute-start.11 = (bf16[96,1152]{1,0:T(8,128)(2,1)S(1)}, bf16[96,1152]{1,0:T(8,128)(2,1)S(1)}, u32[]{:S(2)}, u32[]{:S(2)}) collective-permute-start(bf16[96,1152]{1,0:T(8,128)(2,1)S(1)} %slice.14), channel_id=1, source_target_pairs={{0,2},{2,0},{4,6},{6,4},{8,10},{10,8},{12,14},{14,12},{1,3},{3,1},... | collective-permute-start | bytes 663560 | tf_op jit(solution)/shard_map/ppermute | solution.py:609
  57.4 7.8 %collective-permute-start.12 = (bf16[96,1152]{1,0:T(8,128)(2,1)S(1)}, bf16[96,1152]{1,0:T(8,128)(2,1)S(1)}, u32[]{:S(2)}, u32[]{:S(2)}) collective-permute-start(bf16[96,1152]{1,0:T(8,128)(2,1)S(1)} %slice.12), channel_id=1, source_target_pairs={{8,0},{10,2},{0,4},{2,6},{4,12},{6,14},{12,8},{14,10},{9,1},{11,3}... | collective-permute-start | bytes 663560 | tf_op jit(solution)/shard_map/ppermute | solution.py:606
  58.0 14.8 %collective-permute-start.14 = (bf16[768,384]{1,0:T(8,128)(2,1)S(1)}, bf16[768,384]{1,0:T(8,128)(2,1)S(1)}, u32[]{:S(2)}, u32[]{:S(2)}) collective-permute-start(bf16[768,384]{1,0:T(8,128)(2,1)S(1)} %collective-permute-done.10.refs_6_), channel_id=1, source_target_pairs={{0,16},{16,0},{1,17},{17,1},{2,18},{18,2},{3,19},{19,3},{4,20},{20... | collective-permute-start | bytes 1769480 | tf_op jit(solution)/shard_map/ppermute | solution.py:644
  60.1 17.8 %collective-permute-start.18 = (bf16[768,384]{1,0:T(8,128)(2,1)}, bf16[768,384]{1,0:T(8,128)(2,1)S(1)}, u32[]{:S(2)}, u32[]{:S(2)}) collective-permute-start(bf16[768,384]{1,0:T(8,128)(2,1)} %shard_map.115.refs_8_), channel_id=1, source_target_pairs={{0,1},{1,0},{2,3},{3,2},{4,5},{5,4},{6,7},{7,6},{8,9},{9,8},{10,11... | collective-permute-start | bytes 1769480 | tf_op jit(solution)/shard_map/ppermute | solution.py:642
  64.1 1.2 %copy-start.18 = (bf16[96,1152]{1,0:T(8,128)(2,1)}, bf16[96,1152]{1,0:T(8,128)(2,1)S(1)}, u32[]{:S(2)}) copy-start(bf16[96,1152]{1,0:T(8,128)(2,1)S(1)} %collective-permute-done.11.refs_9_.refs_8_) | copy-start | bytes 663556
  64.1 19.7 %collective-permute-start.19 = (bf16[768,384]{1,0:T(8,128)(2,1)}, bf16[768,384]{1,0:T(8,128)(2,1)S(1)}, u32[]{:S(2)}, u32[]{:S(2)}) collective-permute-start(bf16[768,384]{1,0:T(8,128)(2,1)} %shard_map.115.refs_8_), channel_id=1, source_target_pairs={{0,16},{16,0},{1,17},{17,1},{2,18},{18,2},{3,19},{19,3},{4,20},{20... | collective-permute-start | bytes 1769480 | tf_op jit(solution)/shard_map/ppermute | solution.py:643
  65.2 0.7 copy-start.19
  71.7 6.3 %collective-permute-start.15 = (f32[4,8,288]{2,1,0:T(8,128)}, f32[4,8,288]{2,1,0:T(8,128)S(1)}, u32[]{:S(2)}, u32[]{:S(2)}) collective-permute-start(f32[4,8,288]{2,1,0:T(8,128)} %get-tuple-element.37.s0_ref), channel_id=1, source_target_pairs={{0,1},{1,0},{2,3},{3,2},{4,5},{5,4},{6,7},{7,6},{8,9},{9,8},{10,11... | collective-permute-start | bytes 110600 | tf_op jit(solution)/shard_map/ppermute | solution.py:651
  72.8 5.3 %collective-permute-start.16 = (f32[4,8,288]{2,1,0:T(8,128)}, f32[4,8,288]{2,1,0:T(8,128)S(1)}, u32[]{:S(2)}, u32[]{:S(2)}) collective-permute-start(f32[4,8,288]{2,1,0:T(8,128)} %get-tuple-element.37.s0_ref), channel_id=1, source_target_pairs={{0,16},{16,0},{1,17},{17,1},{2,18},{18,2},{3,19},{19,3},{4,20},{20... | collective-permute-start | bytes 110600 | tf_op jit(solution)/shard_map/ppermute | solution.py:652
  72.8 5.1 %copy-start.11 = (bf16[768,384]{1,0:T(8,128)(2,1)}, bf16[768,384]{1,0:T(8,128)(2,1)S(1)}, u32[]{:S(2)}) copy-start(bf16[768,384]{1,0:T(8,128)(2,1)S(1)} %collective-permute-done.14.refs_7_) | copy-start | bytes 1769476
  72.8 5.2 %collective-permute-start.17 = (f32[4,8,288]{2,1,0:T(8,128)}, f32[4,8,288]{2,1,0:T(8,128)S(1)}, u32[]{:S(2)}, u32[]{:S(2)}) collective-permute-start(f32[4,8,288]{2,1,0:T(8,128)} %get-tuple-element.37.s0_ref), channel_id=1, source_target_pairs={{0,17},{1,16},{16,1},{17,0},{2,19},{3,18},{18,3},{19,2},{4,21},{5,... | collective-permute-start | bytes 110600 | tf_op jit(solution)/shard_map/ppermute | solution.py:653
  77.9 5.8 %copy-start.13 = (bf16[768,384]{1,0:T(8,128)(2,1)}, bf16[768,384]{1,0:T(8,128)(2,1)S(1)}, u32[]{:S(2)}) copy-start(bf16[768,384]{1,0:T(8,128)(2,1)S(1)} %collective-permute-done.18.refs_10_) | copy-start | bytes 1769476
  77.9 19.3 %collective-permute-start.23 = (bf16[768,384]{1,0:T(8,128)(2,1)S(1)}, bf16[768,384]{1,0:T(8,128)(2,1)S(1)}, u32[]{:S(2)}, u32[]{:S(2)}) collective-permute-start(bf16[768,384]{1,0:T(8,128)(2,1)S(1)} %collective-permute-done.18.refs_10_), channel_id=1, source_target_pairs={{0,16},{16,0},{1,17},{17,1},{2,18},{18,2},{3,19},{19,3},{4,20},{20... | collective-permute-start | bytes 1769480 | tf_op jit(solution)/shard_map/ppermute | solution.py:644
  78.0 0.7 copy-start.3
  78.1 0.7 copy-start.4
  78.1 0.7 copy-start.5
  83.8 6.2 %copy-start.21 = (bf16[288,384]{1,0:T(8,128)(2,1)S(1)}, bf16[288,384]{1,0:T(8,128)(2,1)}, u32[]{:S(2)}) copy-start(bf16[288,384]{1,0:T(8,128)(2,1)} %get-tuple-element.44) | copy-start | bytes 663556
  83.8 13.4 %copy-start.14 = (bf16[768,384]{1,0:T(8,128)(2,1)}, bf16[768,384]{1,0:T(8,128)(2,1)S(1)}, u32[]{:S(2)}) copy-start(bf16[768,384]{1,0:T(8,128)(2,1)S(1)} %collective-permute-done.19.refs_9_) | copy-start | bytes 1769476
  83.8 8.0 %collective-permute-start.21 = (bf16[288,384]{1,0:T(8,128)(2,1)}, bf16[288,384]{1,0:T(8,128)(2,1)S(1)}, u32[]{:S(2)}, u32[]{:S(2)}) collective-permute-start(bf16[288,384]{1,0:T(8,128)(2,1)} %get-tuple-element.40), channel_id=1, source_target_pairs={{0,1},{1,0},{2,3},{3,2},{4,5},{5,4},{6,7},{7,6},{8,9},{9,8},{10,11... | collective-permute-start | bytes 663560 | tf_op jit(solution)/shard_map/ppermute | solution.py:662
  89.8 1.8 %collective-permute-start.20 = (bf16[288,384]{1,0:T(8,128)(2,1)}, bf16[288,384]{1,0:T(8,128)(2,1)S(1)}, u32[]{:S(2)}, u32[]{:S(2)}) collective-permute-start(bf16[288,384]{1,0:T(8,128)(2,1)} %get-tuple-element.43), channel_id=1, source_target_pairs={{0,16},{16,0},{1,17},{17,1},{2,18},{18,2},{3,19},{19,3},{4,20},{20... | collective-permute-start | bytes 663560 | tf_op jit(solution)/shard_map/ppermute | solution.py:661
  90.0 7.2 %collective-permute-start.22 = (bf16[288,384]{1,0:T(8,128)(2,1)S(1)}, bf16[288,384]{1,0:T(8,128)(2,1)S(1)}, u32[]{:S(2)}, u32[]{:S(2)}) collective-permute-start(bf16[288,384]{1,0:T(8,128)(2,1)S(1)} %copy-done.21), channel_id=1, source_target_pairs={{0,17},{1,16},{16,1},{17,0},{2,19},{3,18},{18,3},{19,2},{4,21},{5,... | collective-permute-start | bytes 663560 | tf_op jit(solution)/shard_map/ppermute | solution.py:663
  91.6 5.6 %copy-start.22 = (bf16[288,384]{1,0:T(8,128)(2,1)}, bf16[288,384]{1,0:T(8,128)(2,1)S(1)}, u32[]{:S(2)}) copy-start(bf16[288,384]{1,0:T(8,128)(2,1)S(1)} %collective-permute-done.20.refs_1_) | copy-start | bytes 663556
  91.8 5.4 %copy-start.20 = (bf16[288,384]{1,0:T(8,128)(2,1)}, bf16[288,384]{1,0:T(8,128)(2,1)S(1)}, u32[]{:S(2)}) copy-start(bf16[288,384]{1,0:T(8,128)(2,1)S(1)} %collective-permute-done.21.refs_2_) | copy-start | bytes 663556
  97.2 0.7 copy-start.23
  97.2 0.9 copy-start.16
  98.1 8.0 %copy-start.2 = (f32[1,288,32]{1,2,0:T(8,128)S(1)}, f32[1,288,32]{1,2,0:T(8,128)}, u32[]{:S(2)}) copy-start(f32[1,288,32]{1,2,0:T(8,128)} %param.12) | copy-start | bytes 110596
  104.2 1.8 %collective-permute-start.24 = (bf16[32,288]{1,0:T(8,128)(2,1)}, bf16[32,288]{1,0:T(8,128)(2,1)S(1)}, u32[]{:S(2)}, u32[]{:S(2)}) collective-permute-start(bf16[32,288]{1,0:T(8,128)(2,1)} %get-tuple-element.45), channel_id=1, source_target_pairs={{0,16},{16,0},{1,17},{17,1},{2,18},{18,2},{3,19},{19,3},{4,20},{20... | collective-permute-start | bytes 55304 | tf_op jit(solution)/shard_map/ppermute | solution.py:576

commit v6 on v5

--- a/solution.py
+++ b/solution.py
@@ -15,8 +15,8 @@
 F32 = jnp.float32
 
 
-def params():
-    return pltpu.CompilerParams(vmem_limit_bytes=60 * 2**20)
+def params(megabytes):
+    return pltpu.CompilerParams(vmem_limit_bytes=megabytes * 2**20)
 
 
 def cost(flops, moved, exps=0):
@@ -204,7 +204,7 @@
             pltpu.SemaphoreType.DMA((6,)),
             pltpu.SemaphoreType.DMA((2,)),
         ],
-        compiler_params=params(),
+        compiler_params=params(60),
         cost_estimate=cost(4e9, 1e6),
     )(w_qkv, w_out, state, modes)
 
@@ -231,7 +231,7 @@
         in_specs=[ANY] * len(pieces),
         out_specs=ANY,
         scratch_shapes=[pltpu.VMEM(full.shape, BF16), pltpu.SemaphoreType.DMA((len(pieces),))],
-        compiler_params=params(),
+        compiler_params=params(40),
         cost_estimate=cost(3e9, 1e6),
     )(*pieces)
 
@@ -288,7 +288,7 @@
             pltpu.SemaphoreType.DMA((4 + len(pieces),)),
             pltpu.SemaphoreType.DMA((8,)),
         ],
-        compiler_params=params(),
+        compiler_params=params(40),
         cost_estimate=cost(6e9, 1e6),
     )(*norms, *pieces)
 
@@ -357,7 +357,7 @@
             pltpu.SemaphoreType.DMA((6,)),
             pltpu.SemaphoreType.DMA((5,)),
         ],
-        compiler_params=params(),
+        compiler_params=params(48),
         cost_estimate=cost(6e9, 1e6),
     )(*norms, acc, gains, *pieces)
 
@@ -403,7 +403,7 @@
             pltpu.VMEM(acc.shape, BF16),
             pltpu.SemaphoreType.DMA((8 + len(pieces),)),
         ],
-        compiler_params=params(),
+        compiler_params=params(48),
         cost_estimate=cost(4e9, 1e6),
     )(*norms, acc, *pieces)
 
@@ -503,7 +503,7 @@
             pltpu.SemaphoreType.DMA((8 + 4 * count,)),
             pltpu.SemaphoreType.DMA((2,)),
         ],
-        compiler_params=params(),
+        compiler_params=params(50),
         cost_estimate=cost(effort, 1e6),
     )(length, qk, v, *sums)
 
@@ -564,7 +564,7 @@
             pltpu.VMEM((channels, rows), BF16),
             pltpu.SemaphoreType.DMA((15,)),
         ],
-        compiler_params=params(),
+        compiler_params=params(50),
         cost_estimate=cost(8e9, 1e6),
     )(state, modes, w_head, *attended, *pieces)
 

time: 108 us -> 104 us (0.963)
  Pallas kernels: 38.2 us -> 34.7 us
  waiting for transfers between devices: 37.8 us -> 40.6 us
  local copies, waits for them, and re-layouts: 3.74 us -> 2.11 us
    pallas_call x2, Pallas kernels: 4.04 us -> 0.62 us  [pack(): pl.pallas_call(functools.partial(pack_kernel, len(pieces)), out_shape=ful...]
    ppermute x4, waiting for transfers between devices: 22.9 us -> 25.3 us  [across(): return lax.ppermute(piece, 'req', beside)]
    unnamed x50 -> x26, local copies, waits for them, and re-layouts: 3.08 us -> 2.04 us
  transfers between devices with their start and end apart: 25 -> 25, of which waited for: 11 -> 10; matrix products, arithmetic and copies ran while one was open for 1% -> 0% of each run, Pallas kernels for 27% -> 25%
where the time goes in v6:
time: 104 us
  waiting for transfers between devices  40.6 us (39%)
  Pallas kernels  34.7 us (33%)
  starting transfers between devices  23.7 us (23%)
  between operations  2.28 us (2%)
  local copies, waits for them, and re-layouts  2.11 us (2%)
    ppermute x4, waiting for transfers between devices, across(): return lax.ppermute(piece, 'req', beside)  25.3 us
    pallas_call x2, Pallas kernels, team_attention(): pl.pallas_call(functools.partial(heads_kernel, blocks), out_shape=[shape_...  10.1 us
    ppermute x3, starting transfers between devices, along(): return lax.ppermute(piece, 'req', up)  9.25 us
    pallas_call x1, Pallas kernels, first_part(): pl.pallas_call(functools.partial(first_kernel, len(pieces)), out_shape=[q...  5.97 us
    pallas_call x1, Pallas kernels, project(): pl.pallas_call(out_kernel, out_shape=[shape_of(channels, rows, dtype=F32)...  5.66 us
    pallas_call x1, Pallas kernels, last_scores(): pl.pallas_call(functools.partial(scores_kernel, len(pieces)), out_shape=[...  5.32 us
    ppermute x1, waiting for transfers between devices, team_local(): lax.ppermute(far[1], ('cfg', 'seq'), diagonal)  5.11 us
    ppermute x3, waiting for transfers between devices, along(): return lax.ppermute(piece, 'req', up)  4.94 us
  transfers between devices with their start and end apart: 25, of which 10 were waited for; matrix products, arithmetic and copies ran while one was open for 0% of the time, Pallas kernels for 25%

profile of v6, /device:TPU:0, one launch (start us, length us, event | category | flops | bytes accessed | tf_op | source)
XLA Modules:
  0.0 104.1 jit_solution(910370151001611143)
XLA Ops:
  0.0 3.2 %shard_map.109 = (bf16[192,1536]{1,0:T(8,128)(2,1)}, bf16[288,1536]{1,0:T(8,128)(2,1)}) custom-call(bf16[192,4608]{1,0:T(8,128)(2,1)} %qkv_ref.1, bf16[192,1536]{1,0:T(8,128)(2,1)} %w_out_ref.1, bf16[288,1536]{1,0:T(8,128)(2,1)} %bitcast.20, f32[5,1,1536]{2,1,0:T(1,128)} %bitcast.18), custom_call_target="tpu_custom_call" | custom-call | flops 4000000000 | bytes 1000000 | tf_op jit(solution)/shard_map/pallas_call | solution.py:193
  3.2 3.0 %collective-permute-start = (bf16[288,1536]{1,0:T(8,128)(2,1)}, bf16[288,1536]{1,0:T(8,128)(2,1)S(1)}, u32[]{:S(2)}, u32[]{:S(2)}) collective-permute-start(bf16[288,1536]{1,0:T(8,128)(2,1)} %get-tuple-element.26.refs_0_), channel_id=1, source_target_pairs={{0,1},{1,0},{2,3},{3,2},{4,5},{5,4},{6,7},{7,6},{8,9},{9,8},{10,11... | collective-permute-start | bytes 2654216 | tf_op jit(solution)/shard_map/ppermute | solution.py:613
  6.2 1.5 %collective-permute-start.3 = (bf16[192,1536]{1,0:T(8,128)(2,1)}, bf16[192,1536]{1,0:T(8,128)(2,1)S(1)}, u32[]{:S(2)}, u32[]{:S(2)}) collective-permute-start(bf16[192,1536]{1,0:T(8,128)(2,1)} %get-tuple-element.27.refs_4_.refs_0_), channel_id=1, source_target_pairs={{0,2},{2,0},{4,6},{6,4},{8,10},{10,8},{12,14},{14,12},{1,3},{3,1},... | collective-permute-start | bytes 1769480 | tf_op jit(solution)/shard_map/ppermute | solution.py:609
  7.7 2.6 %collective-permute-start.4 = (bf16[192,1536]{1,0:T(8,128)(2,1)}, bf16[192,1536]{1,0:T(8,128)(2,1)S(1)}, u32[]{:S(2)}, u32[]{:S(2)}) collective-permute-start(bf16[192,1536]{1,0:T(8,128)(2,1)} %get-tuple-element.27.refs_4_.refs_0_), channel_id=1, source_target_pairs={{0,8},{2,10},{4,0},{6,2},{12,4},{14,6},{8,12},{10,14},{1,9},{3,11}... | collective-permute-start | bytes 1769480 | tf_op jit(solution)/shard_map/ppermute | solution.py:603
  10.4 10.8 %collective-permute-done.3.refs_5_.refs_1_ = bf16[192,1536]{1,0:T(8,128)(2,1)S(1)} collective-permute-done((bf16[192,1536]{1,0:T(8,128)(2,1)}, bf16[192,1536]{1,0:T(8,128)(2,1)S(1)}, u32[]{:S(2)}, u32[]{:S(2)}) %collective-permute-start.3) | collective-permute-done | bytes 589856 | tf_op jit(solution)/shard_map/ppermute | solution.py:609
  21.3 1.4 %collective-permute-done.4.refs_6_.refs_2_ = bf16[192,1536]{1,0:T(8,128)(2,1)S(1)} collective-permute-done((bf16[192,1536]{1,0:T(8,128)(2,1)}, bf16[192,1536]{1,0:T(8,128)(2,1)S(1)}, u32[]{:S(2)}, u32[]{:S(2)}) %collective-permute-start.4) | collective-permute-done | bytes 589856 | tf_op jit(solution)/shard_map/ppermute | solution.py:603
  22.6 0.5 collective-permute-start.5
  23.2 3.3 %collective-permute-start.6 = (bf16[192,1536]{1,0:T(8,128)(2,1)S(1)}, bf16[192,1536]{1,0:T(8,128)(2,1)S(1)}, u32[]{:S(2)}, u32[]{:S(2)}) collective-permute-start(bf16[192,1536]{1,0:T(8,128)(2,1)S(1)} %collective-permute-done.4.refs_6_.refs_2_), channel_id=1, source_target_pairs={{0,8},{2,10},{4,0},{6,2},{12,4},{14,6},{8,12},{10,14},{1,9},{3,11}... | collective-permute-start | bytes 1769480 | tf_op jit(solution)/shard_map/ppermute | solution.py:603
  26.4 0.0 collective-permute-start.1
  26.5 0.0 collective-permute-done.refs_1_
  26.5 0.5 collective-permute-start.2
  27.0 9.3 %collective-permute-done.5.refs_7_.refs_3_ = bf16[192,1536]{1,0:T(8,128)(2,1)S(1)} collective-permute-done((bf16[192,1536]{1,0:T(8,128)(2,1)S(1)}, bf16[192,1536]{1,0:T(8,128)(2,1)S(1)}, u32[]{:S(2)}, u32[]{:S(2)}) %collective-permute-start.5) | collective-permute-done | bytes 589856 | tf_op jit(solution)/shard_map/ppermute | solution.py:609
  36.2 1.0 %collective-permute-done.6.refs_6_.refs_5_.refs_0_ = bf16[192,1536]{1,0:T(8,128)(2,1)S(1)} collective-permute-done((bf16[192,1536]{1,0:T(8,128)(2,1)S(1)}, bf16[192,1536]{1,0:T(8,128)(2,1)S(1)}, u32[]{:S(2)}, u32[]{:S(2)}) %collective-permute-start.6) | collective-permute-done | bytes 589856 | tf_op jit(solution)/shard_map/ppermute | solution.py:603
  37.3 1.5 %collective-permute-start.7 = (bf16[192,1536]{1,0:T(8,128)(2,1)S(1)}, bf16[192,1536]{1,0:T(8,128)(2,1)S(1)}, u32[]{:S(2)}, u32[]{:S(2)}) collective-permute-start(bf16[192,1536]{1,0:T(8,128)(2,1)S(1)} %collective-permute-done.6.refs_6_.refs_5_.refs_0_), channel_id=1, source_target_pairs={{0,2},{2,0},{4,6},{6,4},{8,10},{10,8},{12,14},{14,12},{1,3},{3,1},... | collective-permute-start | bytes 1769480 | tf_op jit(solution)/shard_map/ppermute | solution.py:609
  38.8 3.4 %collective-permute-start.8 = (bf16[192,1536]{1,0:T(8,128)(2,1)S(1)}, bf16[192,1536]{1,0:T(8,128)(2,1)S(1)}, u32[]{:S(2)}, u32[]{:S(2)}) collective-permute-start(bf16[192,1536]{1,0:T(8,128)(2,1)S(1)} %collective-permute-done.6.refs_6_.refs_5_.refs_0_), channel_id=1, source_target_pairs={{0,8},{2,10},{4,0},{6,2},{12,4},{14,6},{8,12},{10,14},{1,9},{3,11}... | collective-permute-start | bytes 1769480 | tf_op jit(solution)/shard_map/ppermute | solution.py:603
  42.1 1.1 %copy-done.4 = bf16[192,1536]{1,0:T(8,128)(2,1)S(1)} copy-done((bf16[192,1536]{1,0:T(8,128)(2,1)S(1)}, bf16[192,1536]{1,0:T(8,128)(2,1)}, u32[]{:S(2)}) %copy-start.4) | copy-done | bytes 589848
  43.2 0.2 shard_map.111.refs_4_
  43.4 0.6 collective-permute-start.10
  44.7 0.0 collective-permute-done.1.refs_2_
  44.7 0.1 collective-permute-start.13
  44.8 0.0 collective-permute-done.2.refs_3_
  44.8 0.1 collective-permute-start.9
  44.8 0.0 copy-done.1
  44.8 6.0 %shard_map.110 = (bf16[4,288,768]{2,1,0:T(8,128)(2,1)S(1)}, bf16[4,288,384]{2,1,0:T(8,128)(2,1)S(1)}) custom-call(bf16[288,1536]{1,0:T(8,128)(2,1)S(1)} %copy-done.1, bf16[288,1536]{1,0:T(8,128)(2,1)S(1)} %collective-permute-done.refs_1_, bf16[288,1536]{1,0:T(8,128)(2,1)S(1)} %collective-permute-done.1.refs_2_, ...), custom_call_target="tpu_custom_call" | custom-call | flops 6000000000 | bytes 1000000 | tf_op jit(solution)/shard_map/pallas_call | solution.py:278
  50.9 2.5 %collective-permute-done.8.refs_8_.refs_7_.refs_2_ = bf16[192,1536]{1,0:T(8,128)(2,1)S(1)} collective-permute-done((bf16[192,1536]{1,0:T(8,128)(2,1)S(1)}, bf16[192,1536]{1,0:T(8,128)(2,1)S(1)}, u32[]{:S(2)}, u32[]{:S(2)}) %collective-permute-start.8) | collective-permute-done | bytes 589856 | tf_op jit(solution)/shard_map/ppermute | solution.py:603
  53.4 3.4 %collective-permute-done.9.refs_3_ = bf16[192,384]{1,0:T(8,128)(2,1)S(1)} collective-permute-done((bf16[192,384]{1,0:T(8,128)(2,1)S(1)}, bf16[192,384]{1,0:T(8,128)(2,1)S(1)}, u32[]{:S(2)}, u32[]{:S(2)}) %collective-permute-start.9) | collective-permute-done | bytes 147488 | tf_op jit(solution)/shard_map/ppermute | solution.py:606
  56.8 0.0 collective-permute-done.7.refs_7_.refs_6_.refs_1_
  56.8 0.0 collective-permute-done.10.refs_6_
  56.8 0.5 collective-permute-start.11
  57.3 0.7 collective-permute-start.12
  58.0 0.0 collective-permute-start.14
  58.0 0.4 shard_map.115.refs_8_
  58.4 0.5 collective-permute-start.18
  59.0 5.2 %collective-permute-done.11.refs_9_.refs_8_ = bf16[96,1152]{1,0:T(8,128)(2,1)S(1)} collective-permute-done((bf16[96,1152]{1,0:T(8,128)(2,1)S(1)}, bf16[96,1152]{1,0:T(8,128)(2,1)S(1)}, u32[]{:S(2)}, u32[]{:S(2)}) %collective-permute-start.11) | collective-permute-done | bytes 221216 | tf_op jit(solution)/shard_map/ppermute | solution.py:609
  64.2 0.0 collective-permute-start.19
  64.2 1.2 %collective-permute-done.12.refs_10_.refs_9_ = bf16[96,1152]{1,0:T(8,128)(2,1)S(1)} collective-permute-done((bf16[96,1152]{1,0:T(8,128)(2,1)S(1)}, bf16[96,1152]{1,0:T(8,128)(2,1)S(1)}, u32[]{:S(2)}, u32[]{:S(2)}) %collective-permute-start.12) | collective-permute-done | bytes 221216 | tf_op jit(solution)/shard_map/ppermute | solution.py:606
  65.3 5.3 %shard_map.112 = (bf16[4,288,768]{2,1,0:T(8,128)(2,1)}, f32[4,8,288]{2,1,0:T(8,128)S(1)}) custom-call(bf16[288,1536]{1,0:T(8,128)(2,1)S(1)} %copy-done.1, bf16[288,1536]{1,0:T(8,128)(2,1)S(1)} %collective-permute-done.refs_1_, bf16[288,1536]{1,0:T(8,128)(2,1)S(1)} %collective-permute-done.1.refs_2_, bf16[288,1536]{1,0:T(8,128)(2,1)S(1)} %collective-permute-done.2.refs_3_, ...), custom_call_target="tpu_custom_call" | custom-call | flops 6000000000 | bytes 1000000 | tf_op jit(solution)/shard_map/pallas_call | solution.py:344
  70.7 0.5 collective-permute-start.15
  71.2 0.0 collective-permute-done.13.refs_5_
  71.2 0.0 collective-permute-start.16
  71.2 0.0 collective-permute-done.14.refs_7_
  71.2 1.7 %collective-permute-start.17 = (f32[4,8,288]{2,1,0:T(8,128)S(1)}, f32[4,8,288]{2,1,0:T(8,128)S(1)}, u32[]{:S(2)}, u32[]{:S(2)}) collective-permute-start(f32[4,8,288]{2,1,0:T(8,128)S(1)} %get-tuple-element.37.s0_ref), channel_id=1, source_target_pairs={{0,17},{1,16},{16,1},{17,0},{2,19},{3,18},{18,3},{19,2},{4,21},{5,... | collective-permute-start | bytes 110600 | tf_op jit(solution)/shard_map/ppermute | solution.py:653
  72.9 3.8 %shard_map.113.v_ref = bf16[4,288,384]{2,1,0:T(8,128)(2,1)S(1)} custom-call(bf16[288,1536]{1,0:T(8,128)(2,1)S(1)} %copy-done.1, bf16[288,1536]{1,0:T(8,128)(2,1)S(1)} %collective-permute-done.refs_1_, bf16[288,1536]{1,0:T(8,128)(2,1)S(1)} %collective-permute-done.1.refs_2_, bf16[288,1536]{1,0:T(8,128)(2,1)} %copy-done.2, bf16[4,288,384]{2,1,0:T(8,128)(2,1)} %copy-done.7, ...), custom_call_target="tpu_custom_call" | custom-call | flops 4000000000 | bytes 1000000 | tf_op jit(solution)/shard_map/pallas_call | solution.py:394
  76.7 0.0 collective-permute-done.18.refs_10_
  76.7 0.1 collective-permute-start.23
  76.9 0.0 collective-permute-done.15.s1_ref
  76.9 0.0 collective-permute-done.16.s2_ref
  76.9 0.0 collective-permute-done.17.s3_ref
  76.9 5.1 %shard_map.114 = (bf16[288,384]{1,0:T(8,128)(2,1)}, bf16[288,384]{1,0:T(8,128)(2,1)S(1)}) custom-call(s32[1]{0:T(128)} %copy.12.length_ref, bf16[4,288,768]{2,1,0:T(8,128)(2,1)S(1)} %copy-done, bf16[4,288,384]{2,1,0:T(8,128)(2,1)S(1)} %shard_map.113.v_ref, f32[4,8,288]{2,1,0:T(8,128)S(1)} %get-tuple-element.37.s0_ref, ...), custom_call_target="tpu_custom_call" | custom-call | flops 6000000000 | bytes 1000000 | tf_op jit(solution)/shard_map/pallas_call | solution.py:493
  82.0 0.0 copy-start.6
  82.0 0.0 collective-permute-done.19.refs_9_
  82.0 0.5 collective-permute-start.21
  82.5 5.0 %shard_map.116 = (bf16[288,384]{1,0:T(8,128)(2,1)}, bf16[288,384]{1,0:T(8,128)(2,1)S(1)}) custom-call(s32[1]{0:T(128)} %copy.12.length_ref, bf16[4,288,768]{2,1,0:T(8,128)(2,1)S(1)} %copy-done, bf16[4,288,384]{2,1,0:T(8,128)(2,1)S(1)} %shard_map.113.v_ref, f32[4,8,288]{2,1,0:T(8,128)S(1)} %get-tuple-element.37.s0_ref, ...), custom_call_target="tpu_custom_call" | custom-call | flops 1000000 | bytes 1000000 | tf_op jit(solution)/shard_map/pallas_call | solution.py:493
  87.6 0.2 collective-permute-start.20
  87.8 1.5 %collective-permute-start.22 = (bf16[288,384]{1,0:T(8,128)(2,1)S(1)}, bf16[288,384]{1,0:T(8,128)(2,1)}, u32[]{:S(2)}, u32[]{:S(2)}) collective-permute-start(bf16[288,384]{1,0:T(8,128)(2,1)S(1)} %get-tuple-element.44), channel_id=1, source_target_pairs={{0,17},{1,16},{16,1},{17,0},{2,19},{3,18},{18,3},{19,2},{4,21},{5,... | collective-permute-start | bytes 663560 | tf_op jit(solution)/shard_map/ppermute | solution.py:663
  89.3 0.0 collective-permute-done.20.refs_1_
  89.3 0.7 collective-permute-done.21.refs_2_
  90.1 5.1 %collective-permute-done.22.refs_3_ = bf16[288,384]{1,0:T(8,128)(2,1)} collective-permute-done((bf16[288,384]{1,0:T(8,128)(2,1)S(1)}, bf16[288,384]{1,0:T(8,128)(2,1)}, u32[]{:S(2)}, u32[]{:S(2)}) %collective-permute-start.22) | collective-permute-done | bytes 221216 | tf_op jit(solution)/shard_map/ppermute | solution.py:663
  95.2 0.0 collective-permute-done.23.refs_11_
  95.2 0.9 copy-done.5
  96.1 5.7 %shard_map.117 = (f32[32,288]{1,0:T(8,128)S(1)}, bf16[32,288]{1,0:T(8,128)(2,1)S(1)}) custom-call(bf16[288,1536]{1,0:T(8,128)(2,1)} %bitcast.21, f32[5,1,1536]{2,1,0:T(1,128)S(1)} %bitcast.19, bf16[64,1536]{1,0:T(8,128)(2,1)S(1)} %bitcast.17, bf16[288,384]{1,0:T(8,128)(2,1)S(1)} %get-tuple-element.42.refs_0_, ...), custom_call_target="tpu_custom_call" | custom-call | flops 8000000000 | bytes 1000000 | tf_op jit(solution)/shard_map/pallas_call | solution.py:551
  101.8 0.3 collective-permute-start.24
  103.4 0.0 collective-permute-done.24
  103.5 0.6 fusion.4
  (30 shorter events, 0.1 us)
Async XLA Ops:
  0.0 10.3 %copy-start.10 = (f32[1536]{0:T(1024)S(1)}, f32[1536]{0:T(1024)}, u32[]{:S(2)}) copy-start(f32[1536]{0:T(1024)} %param.17) | copy-start | bytes 18436
  0.0 10.3 %copy-start.11 = (f32[1536]{0:T(1024)S(1)}, f32[1536]{0:T(1024)}, u32[]{:S(2)}) copy-start(f32[1536]{0:T(1024)} %param.16) | copy-start | bytes 18436
  3.2 23.3 %collective-permute-start = (bf16[288,1536]{1,0:T(8,128)(2,1)}, bf16[288,1536]{1,0:T(8,128)(2,1)S(1)}, u32[]{:S(2)}, u32[]{:S(2)}) collective-permute-start(bf16[288,1536]{1,0:T(8,128)(2,1)} %get-tuple-element.26.refs_0_), channel_id=1, source_target_pairs={{0,1},{1,0},{2,3},{3,2},{4,5},{5,4},{6,7},{7,6},{8,9},{9,8},{10,11... | collective-permute-start | bytes 2654216 | tf_op jit(solution)/shard_map/ppermute | solution.py:613
  6.2 15.0 %collective-permute-start.3 = (bf16[192,1536]{1,0:T(8,128)(2,1)}, bf16[192,1536]{1,0:T(8,128)(2,1)S(1)}, u32[]{:S(2)}, u32[]{:S(2)}) collective-permute-start(bf16[192,1536]{1,0:T(8,128)(2,1)} %get-tuple-element.27.refs_4_.refs_0_), channel_id=1, source_target_pairs={{0,2},{2,0},{4,6},{6,4},{8,10},{10,8},{12,14},{14,12},{1,3},{3,1},... | collective-permute-start | bytes 1769480 | tf_op jit(solution)/shard_map/ppermute | solution.py:609
  7.7 14.9 %collective-permute-start.4 = (bf16[192,1536]{1,0:T(8,128)(2,1)}, bf16[192,1536]{1,0:T(8,128)(2,1)S(1)}, u32[]{:S(2)}, u32[]{:S(2)}) collective-permute-start(bf16[192,1536]{1,0:T(8,128)(2,1)} %get-tuple-element.27.refs_4_.refs_0_), channel_id=1, source_target_pairs={{0,8},{2,10},{4,0},{6,2},{12,4},{14,6},{8,12},{10,14},{1,9},{3,11}... | collective-permute-start | bytes 1769480 | tf_op jit(solution)/shard_map/ppermute | solution.py:603
  21.2 23.6 %copy-start.1 = (bf16[288,1536]{1,0:T(8,128)(2,1)S(1)}, bf16[288,1536]{1,0:T(8,128)(2,1)}, u32[]{:S(2)}) copy-start(bf16[288,1536]{1,0:T(8,128)(2,1)} %get-tuple-element.26.refs_0_) | copy-start | bytes 2654212
  22.6 13.6 %collective-permute-start.5 = (bf16[192,1536]{1,0:T(8,128)(2,1)S(1)}, bf16[192,1536]{1,0:T(8,128)(2,1)S(1)}, u32[]{:S(2)}, u32[]{:S(2)}) collective-permute-start(bf16[192,1536]{1,0:T(8,128)(2,1)S(1)} %collective-permute-done.4.refs_6_.refs_2_), channel_id=1, source_target_pairs={{0,2},{2,0},{4,6},{6,4},{8,10},{10,8},{12,14},{14,12},{1,3},{3,1},... | collective-permute-start | bytes 1769480 | tf_op jit(solution)/shard_map/ppermute | solution.py:609
  23.2 14.1 %collective-permute-start.6 = (bf16[192,1536]{1,0:T(8,128)(2,1)S(1)}, bf16[192,1536]{1,0:T(8,128)(2,1)S(1)}, u32[]{:S(2)}, u32[]{:S(2)}) collective-permute-start(bf16[192,1536]{1,0:T(8,128)(2,1)S(1)} %collective-permute-done.4.refs_6_.refs_2_), channel_id=1, source_target_pairs={{0,8},{2,10},{4,0},{6,2},{12,4},{14,6},{8,12},{10,14},{1,9},{3,11}... | collective-permute-start | bytes 1769480 | tf_op jit(solution)/shard_map/ppermute | solution.py:603
  26.4 18.2 %collective-permute-start.1 = (bf16[288,1536]{1,0:T(8,128)(2,1)}, bf16[288,1536]{1,0:T(8,128)(2,1)S(1)}, u32[]{:S(2)}, u32[]{:S(2)}) collective-permute-start(bf16[288,1536]{1,0:T(8,128)(2,1)} %get-tuple-element.26.refs_0_), channel_id=1, source_target_pairs={{0,16},{16,0},{1,17},{17,1},{2,18},{18,2},{3,19},{19,3},{4,20},{20... | collective-permute-start | bytes 2654216 | tf_op jit(solution)/shard_map/ppermute | solution.py:614
  26.5 18.3 %collective-permute-start.2 = (bf16[288,1536]{1,0:T(8,128)(2,1)S(1)}, bf16[288,1536]{1,0:T(8,128)(2,1)S(1)}, u32[]{:S(2)}, u32[]{:S(2)}) collective-permute-start(bf16[288,1536]{1,0:T(8,128)(2,1)S(1)} %collective-permute-done.refs_1_), channel_id=1, source_target_pairs={{0,16},{16,0},{1,17},{17,1},{2,18},{18,2},{3,19},{19,3},{4,20},{20... | collective-permute-start | bytes 2654216 | tf_op jit(solution)/shard_map/ppermute | solution.py:633
  37.3 19.5 %collective-permute-start.7 = (bf16[192,1536]{1,0:T(8,128)(2,1)S(1)}, bf16[192,1536]{1,0:T(8,128)(2,1)S(1)}, u32[]{:S(2)}, u32[]{:S(2)}) collective-permute-start(bf16[192,1536]{1,0:T(8,128)(2,1)S(1)} %collective-permute-done.6.refs_6_.refs_5_.refs_0_), channel_id=1, source_target_pairs={{0,2},{2,0},{4,6},{6,4},{8,10},{10,8},{12,14},{14,12},{1,3},{3,1},... | collective-permute-start | bytes 1769480 | tf_op jit(solution)/shard_map/ppermute | solution.py:609
  38.8 14.6 %collective-permute-start.8 = (bf16[192,1536]{1,0:T(8,128)(2,1)S(1)}, bf16[192,1536]{1,0:T(8,128)(2,1)S(1)}, u32[]{:S(2)}, u32[]{:S(2)}) collective-permute-start(bf16[192,1536]{1,0:T(8,128)(2,1)S(1)} %collective-permute-done.6.refs_6_.refs_5_.refs_0_), channel_id=1, source_target_pairs={{0,8},{2,10},{4,0},{6,2},{12,4},{14,6},{8,12},{10,14},{1,9},{3,11}... | collective-permute-start | bytes 1769480 | tf_op jit(solution)/shard_map/ppermute | solution.py:603
  42.1 1.1 %copy-start.4 = (bf16[192,1536]{1,0:T(8,128)(2,1)S(1)}, bf16[192,1536]{1,0:T(8,128)(2,1)}, u32[]{:S(2)}) copy-start(bf16[192,1536]{1,0:T(8,128)(2,1)} %get-tuple-element.27.refs_4_.refs_0_) | copy-start | bytes 1769476
  43.4 13.3 %collective-permute-start.10 = (bf16[768,384]{1,0:T(8,128)(2,1)S(1)}, bf16[768,384]{1,0:T(8,128)(2,1)S(1)}, u32[]{:S(2)}, u32[]{:S(2)}) collective-permute-start(bf16[768,384]{1,0:T(8,128)(2,1)S(1)} %shard_map.111.refs_4_), channel_id=1, source_target_pairs={{0,1},{1,0},{2,3},{3,2},{4,5},{5,4},{6,7},{7,6},{8,9},{9,8},{10,11... | collective-permute-start | bytes 1769480 | tf_op jit(solution)/shard_map/ppermute | solution.py:635
  44.7 26.5 %collective-permute-start.13 = (bf16[768,384]{1,0:T(8,128)(2,1)S(1)}, bf16[768,384]{1,0:T(8,128)(2,1)S(1)}, u32[]{:S(2)}, u32[]{:S(2)}) collective-permute-start(bf16[768,384]{1,0:T(8,128)(2,1)S(1)} %shard_map.111.refs_4_), channel_id=1, source_target_pairs={{0,16},{16,0},{1,17},{17,1},{2,18},{18,2},{3,19},{19,3},{4,20},{20... | collective-permute-start | bytes 1769480 | tf_op jit(solution)/shard_map/ppermute | solution.py:643
  44.8 20.6 %copy-start.2 = (bf16[288,1536]{1,0:T(8,128)(2,1)}, bf16[288,1536]{1,0:T(8,128)(2,1)S(1)}, u32[]{:S(2)}) copy-start(bf16[288,1536]{1,0:T(8,128)(2,1)S(1)} %collective-permute-done.2.refs_3_) | copy-start | bytes 2654212
  44.8 12.0 %collective-permute-start.9 = (bf16[192,384]{1,0:T(8,128)(2,1)S(1)}, bf16[192,384]{1,0:T(8,128)(2,1)S(1)}, u32[]{:S(2)}, u32[]{:S(2)}) collective-permute-start(bf16[192,384]{1,0:T(8,128)(2,1)S(1)} %slice.13), channel_id=1, source_target_pairs={{8,0},{10,2},{0,4},{2,6},{4,12},{6,14},{12,8},{14,10},{9,1},{11,3}... | collective-permute-start | bytes 442376 | tf_op jit(solution)/shard_map/ppermute | solution.py:606
  50.8 7.6 %copy-start.7 = (bf16[4,288,384]{2,1,0:T(8,128)(2,1)}, bf16[4,288,384]{2,1,0:T(8,128)(2,1)S(1)}, u32[]{:S(2)}) copy-start(bf16[4,288,384]{2,1,0:T(8,128)(2,1)S(1)} %get-tuple-element.32.refs_4_) | copy-start | bytes 2654212
  50.8 7.6 %copy-start.8 = (bf16[4,288,768]{2,1,0:T(8,128)(2,1)}, bf16[4,288,768]{2,1,0:T(8,128)(2,1)S(1)}, u32[]{:S(2)}) copy-start(bf16[4,288,768]{2,1,0:T(8,128)(2,1)S(1)} %get-tuple-element.29.refs_4_) | copy-start | bytes 5308420
  56.8 7.4 %collective-permute-start.11 = (bf16[96,1152]{1,0:T(8,128)(2,1)S(1)}, bf16[96,1152]{1,0:T(8,128)(2,1)S(1)}, u32[]{:S(2)}, u32[]{:S(2)}) collective-permute-start(bf16[96,1152]{1,0:T(8,128)(2,1)S(1)} %slice.14), channel_id=1, source_target_pairs={{0,2},{2,0},{4,6},{6,4},{8,10},{10,8},{12,14},{14,12},{1,3},{3,1},... | collective-permute-start | bytes 663560 | tf_op jit(solution)/shard_map/ppermute | solution.py:609
  57.3 8.0 %collective-permute-start.12 = (bf16[96,1152]{1,0:T(8,128)(2,1)S(1)}, bf16[96,1152]{1,0:T(8,128)(2,1)S(1)}, u32[]{:S(2)}, u32[]{:S(2)}) collective-permute-start(bf16[96,1152]{1,0:T(8,128)(2,1)S(1)} %slice.12), channel_id=1, source_target_pairs={{8,0},{10,2},{0,4},{2,6},{4,12},{6,14},{12,8},{14,10},{9,1},{11,3}... | collective-permute-start | bytes 663560 | tf_op jit(solution)/shard_map/ppermute | solution.py:606
  58.0 13.2 %collective-permute-start.14 = (bf16[768,384]{1,0:T(8,128)(2,1)S(1)}, bf16[768,384]{1,0:T(8,128)(2,1)S(1)}, u32[]{:S(2)}, u32[]{:S(2)}) collective-permute-start(bf16[768,384]{1,0:T(8,128)(2,1)S(1)} %collective-permute-done.10.refs_6_), channel_id=1, source_target_pairs={{0,16},{16,0},{1,17},{17,1},{2,18},{18,2},{3,19},{19,3},{4,20},{20... | collective-permute-start | bytes 1769480 | tf_op jit(solution)/shard_map/ppermute | solution.py:644
  58.4 12.3 %copy-start.3 = (bf16[768,384]{1,0:T(8,128)(2,1)}, bf16[768,384]{1,0:T(8,128)(2,1)S(1)}, u32[]{:S(2)}) copy-start(bf16[768,384]{1,0:T(8,128)(2,1)S(1)} %shard_map.115.refs_8_) | copy-start | bytes 1769476
  58.4 18.3 %collective-permute-start.18 = (bf16[768,384]{1,0:T(8,128)(2,1)S(1)}, bf16[768,384]{1,0:T(8,128)(2,1)}, u32[]{:S(2)}, u32[]{:S(2)}) collective-permute-start(bf16[768,384]{1,0:T(8,128)(2,1)S(1)} %shard_map.115.refs_8_), channel_id=1, source_target_pairs={{0,1},{1,0},{2,3},{3,2},{4,5},{5,4},{6,7},{7,6},{8,9},{9,8},{10,11... | collective-permute-start | bytes 1769480 | tf_op jit(solution)/shard_map/ppermute | solution.py:642
  64.2 17.8 %collective-permute-start.19 = (bf16[768,384]{1,0:T(8,128)(2,1)S(1)}, bf16[768,384]{1,0:T(8,128)(2,1)S(1)}, u32[]{:S(2)}, u32[]{:S(2)}) collective-permute-start(bf16[768,384]{1,0:T(8,128)(2,1)S(1)} %shard_map.115.refs_8_), channel_id=1, source_target_pairs={{0,16},{16,0},{1,17},{17,1},{2,18},{18,2},{3,19},{19,3},{4,20},{20... | collective-permute-start | bytes 1769480 | tf_op jit(solution)/shard_map/ppermute | solution.py:643
  70.7 6.2 %copy-start = (bf16[4,288,768]{2,1,0:T(8,128)(2,1)S(1)}, bf16[4,288,768]{2,1,0:T(8,128)(2,1)}, u32[]{:S(2)}) copy-start(bf16[4,288,768]{2,1,0:T(8,128)(2,1)} %get-tuple-element.41.qk_ref) | copy-start | bytes 5308420
  70.7 6.2 %collective-permute-start.15 = (f32[4,8,288]{2,1,0:T(8,128)S(1)}, f32[4,8,288]{2,1,0:T(8,128)S(1)}, u32[]{:S(2)}, u32[]{:S(2)}) collective-permute-start(f32[4,8,288]{2,1,0:T(8,128)S(1)} %get-tuple-element.37.s0_ref), channel_id=1, source_target_pairs={{0,1},{1,0},{2,3},{3,2},{4,5},{5,4},{6,7},{7,6},{8,9},{9,8},{10,11... | collective-permute-start | bytes 110600 | tf_op jit(solution)/shard_map/ppermute | solution.py:651
  71.2 5.7 %collective-permute-start.16 = (f32[4,8,288]{2,1,0:T(8,128)S(1)}, f32[4,8,288]{2,1,0:T(8,128)S(1)}, u32[]{:S(2)}, u32[]{:S(2)}) collective-permute-start(f32[4,8,288]{2,1,0:T(8,128)S(1)} %get-tuple-element.37.s0_ref), channel_id=1, source_target_pairs={{0,16},{16,0},{1,17},{17,1},{2,18},{18,2},{3,19},{19,3},{4,20},{20... | collective-permute-start | bytes 110600 | tf_op jit(solution)/shard_map/ppermute | solution.py:652
  71.2 5.7 %collective-permute-start.17 = (f32[4,8,288]{2,1,0:T(8,128)S(1)}, f32[4,8,288]{2,1,0:T(8,128)S(1)}, u32[]{:S(2)}, u32[]{:S(2)}) collective-permute-start(f32[4,8,288]{2,1,0:T(8,128)S(1)} %get-tuple-element.37.s0_ref), channel_id=1, source_target_pairs={{0,17},{1,16},{16,1},{17,0},{2,19},{3,18},{18,3},{19,2},{4,21},{5,... | collective-permute-start | bytes 110600 | tf_op jit(solution)/shard_map/ppermute | solution.py:653
  76.7 18.4 %collective-permute-start.23 = (bf16[768,384]{1,0:T(8,128)(2,1)}, bf16[768,384]{1,0:T(8,128)(2,1)}, u32[]{:S(2)}, u32[]{:S(2)}) collective-permute-start(bf16[768,384]{1,0:T(8,128)(2,1)} %collective-permute-done.18.refs_10_), channel_id=1, source_target_pairs={{0,16},{16,0},{1,17},{17,1},{2,18},{18,2},{3,19},{19,3},{4,20},{20... | collective-permute-start | bytes 1769480 | tf_op jit(solution)/shard_map/ppermute | solution.py:644
  82.0 13.2 %copy-start.6 = (f32[1,5,1536]{2,0,1:T(1,128)S(1)}, f32[1,5,1536]{2,0,1:T(1,128)}, u32[]{:S(2)}) copy-start(f32[1,5,1536]{2,0,1:T(1,128)} %param.13) | copy-start | bytes 92164
  82.0 7.3 %copy-start.12 = (bf16[768,384]{1,0:T(8,128)(2,1)}, bf16[768,384]{1,0:T(8,128)(2,1)S(1)}, u32[]{:S(2)}) copy-start(bf16[768,384]{1,0:T(8,128)(2,1)S(1)} %collective-permute-done.19.refs_9_) | copy-start | bytes 1769476
  82.0 8.1 %collective-permute-start.21 = (bf16[288,384]{1,0:T(8,128)(2,1)}, bf16[288,384]{1,0:T(8,128)(2,1)S(1)}, u32[]{:S(2)}, u32[]{:S(2)}) collective-permute-start(bf16[288,384]{1,0:T(8,128)(2,1)} %get-tuple-element.40), channel_id=1, source_target_pairs={{0,1},{1,0},{2,3},{3,2},{4,5},{5,4},{6,7},{7,6},{8,9},{9,8},{10,11... | collective-permute-start | bytes 663560 | tf_op jit(solution)/shard_map/ppermute | solution.py:662
  87.6 1.8 %collective-permute-start.20 = (bf16[288,384]{1,0:T(8,128)(2,1)}, bf16[288,384]{1,0:T(8,128)(2,1)S(1)}, u32[]{:S(2)}, u32[]{:S(2)}) collective-permute-start(bf16[288,384]{1,0:T(8,128)(2,1)} %get-tuple-element.43), channel_id=1, source_target_pairs={{0,16},{16,0},{1,17},{17,1},{2,18},{18,2},{3,19},{19,3},{4,20},{20... | collective-permute-start | bytes 663560 | tf_op jit(solution)/shard_map/ppermute | solution.py:661
  87.8 7.4 %collective-permute-start.22 = (bf16[288,384]{1,0:T(8,128)(2,1)S(1)}, bf16[288,384]{1,0:T(8,128)(2,1)}, u32[]{:S(2)}, u32[]{:S(2)}) collective-permute-start(bf16[288,384]{1,0:T(8,128)(2,1)S(1)} %get-tuple-element.44), channel_id=1, source_target_pairs={{0,17},{1,16},{16,1},{17,0},{2,19},{3,18},{18,3},{19,2},{4,21},{5,... | collective-permute-start | bytes 663560 | tf_op jit(solution)/shard_map/ppermute | solution.py:663
  95.2 0.9 copy-start.5
  96.1 7.3 %copy-start.9 = (f32[1,288,32]{1,2,0:T(8,128)S(1)}, f32[1,288,32]{1,2,0:T(8,128)}, u32[]{:S(2)}) copy-start(f32[1,288,32]{1,2,0:T(8,128)} %param.12) | copy-start | bytes 110596
  101.8 1.7 %collective-permute-start.24 = (bf16[32,288]{1,0:T(8,128)(2,1)S(1)}, bf16[32,288]{1,0:T(8,128)(2,1)S(1)}, u32[]{:S(2)}, u32[]{:S(2)}) collective-permute-start(bf16[32,288]{1,0:T(8,128)(2,1)S(1)} %get-tuple-element.45), channel_id=1, source_target_pairs={{0,16},{16,0},{1,17},{17,1},{2,18},{18,2},{3,19},{19,3},{4,20},{20... | collective-permute-start | bytes 55304 | tf_op jit(solution)/shard_map/ppermute | solution.py:576

commit v7 on v6

--- a/solution.py
+++ b/solution.py
@@ -9,6 +9,7 @@
 
 DH = 128
 SWAP = [(0, 1), (1, 0)]
+VMEM = pl.BlockSpec(memory_space=pltpu.VMEM)
 SMEM = pl.BlockSpec(memory_space=pltpu.SMEM)
 ANY = pl.BlockSpec(memory_space=pl.ANY)
 BF16 = jnp.bfloat16
@@ -249,24 +250,15 @@
 def first_kernel(count, *refs):
     norms, pieces = refs[:4], refs[4 : 4 + count]
     qk_ref, v_ref = refs[4 + count : 6 + count]
-    left_ref, held_ref, qk_out, v_out, sem, out_sem = refs[6 + count :]
+    held_ref, sem = refs[6 + count :]
     deep, columns = held_ref.shape
     split = 2 * columns // 3
-    loads = load_all(
-        rows_of(pieces, held_ref) + [(norms[b].at[:, :deep], left_ref.at[b]) for b in range(4)], sem
-    )
+    loads = load_all(rows_of(pieces, held_ref), sem)
     for copy in loads:
         copy.wait()
-    stores = []
     for block in range(4):
-        qk_out[block] = times(left_ref[block], held_ref[:, :split]).astype(BF16)
-        v_out[block] = times(left_ref[block], held_ref[:, split:]).astype(BF16)
-        for j, (source, target) in enumerate(((qk_out, qk_ref), (v_out, v_ref))):
-            copy = pltpu.make_async_copy(source.at[block], target.at[block], out_sem.at[2 * block + j])
-            copy.start()
-            stores.append(copy)
-    for copy in stores:
-        copy.wait()
+        qk_ref[block] = times(norms[block][:, :deep], held_ref[:, :split]).astype(BF16)
+        v_ref[block] = times(norms[block][:, :deep], held_ref[:, split:]).astype(BF16)
 
 
 def first_part(norms, pieces):
@@ -278,15 +270,11 @@
     return pl.pallas_call(
         functools.partial(first_kernel, len(pieces)),
         out_shape=[qk, v],
-        in_specs=[ANY] * (4 + len(pieces)),
-        out_specs=[ANY] * 2,
+        in_specs=[VMEM] * 4 + [ANY] * len(pieces),
+        out_specs=[VMEM] * 2,
         scratch_shapes=[
-            pltpu.VMEM((4, rows, deep), BF16),
             pltpu.VMEM((deep, columns), BF16),
-            pltpu.VMEM(qk.shape, BF16),
-            pltpu.VMEM(v.shape, BF16),
-            pltpu.SemaphoreType.DMA((4 + len(pieces),)),
-            pltpu.SemaphoreType.DMA((8,)),
+            pltpu.SemaphoreType.DMA((len(pieces),)),
         ],
         compiler_params=params(40),
         cost_estimate=cost(6e9, 1e6),
@@ -295,46 +283,31 @@
 
 def scores_kernel(count, *refs):
     norms, acc_ref, gains_ref, pieces = refs[:4], refs[4], refs[5], refs[6 : 6 + count]
-    out_ref, sums_ref, left_ref, held_ref, acc_in, gains_in, out_buf, sums_buf, sem, rest_sem, out_sem = refs[6 + count :]
+    out_ref, sums_ref, held_ref, gains_in, sem = refs[6 + count :]
     deep = held_ref.shape[0]
     third = out_ref.shape[2] // 2
     width = norms[0].shape[1]
-    first = [(norms[0].at[:, width - deep :], left_ref.at[0]), (acc_ref.at[0], acc_in.at[0])]
-    loads = load_all(rows_of(pieces, held_ref) + [(gains_ref, gains_in)] + first, sem)
+    loads = load_all(rows_of(pieces, held_ref) + [(gains_ref, gains_in)], sem)
     mine = window(places()[3], third)
     row = lax.broadcasted_iota(jnp.int32, (8, 4 * DH), 0)
     lane = lax.broadcasted_iota(jnp.int32, (8, 4 * DH), 1)
     pick = (row == lane // (2 * DH)).astype(BF16)
     for copy in loads:
         copy.wait()
-    rest = []
-    for b in range(1, 4):
-        rest += [(norms[b].at[:, width - deep :], left_ref.at[b]), (acc_ref.at[b], acc_in.at[b])]
-    loads = load_all(rest, rest_sem)
     gains = [gains_in[0, :, mine] * (1.4426950408889634 / DH**0.5), gains_in[1, :, mine]]
-    stores = []
     for block in range(4):
-        if block:
-            loads[2 * block - 2].wait()
-            loads[2 * block - 1].wait()
-        product = times(left_ref[block], held_ref[...])
+        product = times(norms[block][:, width - deep :], held_ref[...])
         squares = []
         for j in range(2):
             square = 0.0
             for h in range(third // DH):
                 at = slice(j * third + h * DH, j * third + (h + 1) * DH)
-                part = acc_in[block, :, at].astype(F32) + product[:, at]
+                part = acc_ref[block, :, at].astype(F32) + product[:, at]
                 square += part * part
-                out_buf[block, :, at] = (part * gains[j][:, h * DH : (h + 1) * DH]).astype(BF16)
+                out_ref[block, :, at] = (part * gains[j][:, h * DH : (h + 1) * DH]).astype(BF16)
             high = square.astype(BF16)
             squares += [high, (square - high.astype(F32)).astype(BF16)]
-        stores.append(pltpu.make_async_copy(out_buf.at[block], out_ref.at[block], out_sem.at[block]))
-        stores[-1].start()
-        sums_buf[block] = times_turned(pick, jnp.concatenate(squares, axis=1))
-    stores.append(pltpu.make_async_copy(sums_buf, sums_ref, out_sem.at[4]))
-    stores[-1].start()
-    for copy in stores:
-        copy.wait()
+        sums_ref[block] = times_turned(pick, jnp.concatenate(squares, axis=1))
 
 
 def last_scores(norms, acc, gains, pieces):
@@ -344,47 +317,29 @@
     return pl.pallas_call(
         functools.partial(scores_kernel, len(pieces)),
         out_shape=[shape_of(4, rows, columns), shape_of(4, 8, rows, dtype=F32)],
-        in_specs=[ANY] * (6 + len(pieces)),
-        out_specs=[ANY, ANY],
+        in_specs=[VMEM] * 5 + [ANY] * (1 + len(pieces)),
+        out_specs=[VMEM, VMEM],
         scratch_shapes=[
-            pltpu.VMEM((4, rows, deep), BF16),
             pltpu.VMEM((deep, columns), BF16),
-            pltpu.VMEM(acc.shape, BF16),
             pltpu.VMEM(gains.shape, F32),
-            pltpu.VMEM(acc.shape, BF16),
-            pltpu.VMEM((4, 8, rows), F32),
-            pltpu.SemaphoreType.DMA((3 + len(pieces),)),
-            pltpu.SemaphoreType.DMA((6,)),
-            pltpu.SemaphoreType.DMA((5,)),
+            pltpu.SemaphoreType.DMA((1 + len(pieces),)),
         ],
-        compiler_params=params(48),
+        compiler_params=params(40),
         cost_estimate=cost(6e9, 1e6),
     )(*norms, acc, gains, *pieces)
 
 
 def values_kernel(count, *refs):
     norms, acc_ref, pieces = refs[:4], refs[4], refs[5 : 5 + count]
-    out_ref, left_ref, held_ref, acc_in, out_buf, sem = refs[5 + count :]
+    out_ref, held_ref, sem = refs[5 + count :]
     deep, columns = held_ref.shape
     width = norms[0].shape[1]
-    loads = load_all(
-        rows_of(pieces, held_ref, 2 * columns)
-        + [(norms[b].at[:, width - deep :], left_ref.at[b]) for b in range(4)]
-        + [(acc_ref.at[b], acc_in.at[b]) for b in range(4)],
-        sem,
-    )
-    for copy in loads[:count]:
-        copy.wait()
-    stores = []
+    loads = load_all(rows_of(pieces, held_ref, 2 * columns), sem)
+    for copy in loads:
+        copy.wait()
     for block in range(4):
-        loads[count + block].wait()
-        product = times(left_ref[block], held_ref[...])
-        loads[count + 4 + block].wait()
-        out_buf[block] = (acc_in[block].astype(F32) + product).astype(BF16)
-        stores.append(pltpu.make_async_copy(out_buf.at[block], out_ref.at[block], sem.at[block]))
-        stores[-1].start()
-    for copy in stores:
-        copy.wait()
+        product = times(norms[block][:, width - deep :], held_ref[...])
+        out_ref[block] = (acc_ref[block].astype(F32) + product).astype(BF16)
 
 
 def last_values(norms, acc, pieces):
@@ -394,23 +349,21 @@
     return pl.pallas_call(
         functools.partial(values_kernel, len(pieces)),
         out_shape=shape_of(4, rows, columns),
-        in_specs=[ANY] * 5 + [ANY] * len(pieces),
-        out_specs=ANY,
+        in_specs=[VMEM] * 5 + [ANY] * len(pieces),
+        out_specs=VMEM,
         scratch_shapes=[
-            pltpu.VMEM((4, rows, deep), BF16),
             pltpu.VMEM((deep, columns), BF16),
-            pltpu.VMEM(acc.shape, BF16),
-            pltpu.VMEM(acc.shape, BF16),
-            pltpu.SemaphoreType.DMA((8 + len(pieces),)),
+            pltpu.SemaphoreType.DMA((len(pieces),)),
         ],
-        compiler_params=params(48),
+        compiler_params=params(40),
         cost_estimate=cost(4e9, 1e6),
     )(*norms, acc, *pieces)
 
 
 def heads_kernel(blocks, length_ref, qk_ref, v_ref, s0_ref, s1_ref, s2_ref, s3_ref, *refs):
     outs = refs[:2]
-    qk_in, v_in, sums_in, out_buf, sem, out_sem = refs[2:]
+    v_in, sums_in, out_buf, sem, out_sem = refs[2:]
+    qk_in = qk_ref
     rows = qk_ref.shape[1]
     third = qk_ref.shape[2] // 2
     count = third // DH
@@ -418,8 +371,6 @@
     sum_refs = (s0_ref, s1_ref, s2_ref, s3_ref)
     loads = [(sum_refs[j], sums_in.at[j]) for j in range(4)]
     order = [b for block in blocks for b in (block - block % 2, block - block % 2 + 1)]
-    for b in order:
-        loads.append((qk_ref.at[b], qk_in.at[b]))
     for b in order:
         held = v_in.at[b // 2, b % 2 * rows : (b % 2 + 1) * rows]
         for h in range(count):
@@ -449,9 +400,6 @@
     items = [(at, block, h) for at, block in enumerate(blocks) for h in range(count)]
 
     def scores_of(at, block, h):
-        if h == 0:
-            for copy in loads[4 + 2 * at : 6 + 2 * at]:
-                copy.wait()
         first = block - block % 2
         query = qk_in[block, :, h * DH : (h + 1) * DH]
         found = []
@@ -468,7 +416,7 @@
         if turn + 1 < len(items):
             ahead = scores_of(*items[turn + 1])
         if h == 0:
-            for copy in loads[8 + 2 * count * at : 8 + 2 * count * (at + 1)]:
+            for copy in loads[4 + 2 * count * at : 4 + 2 * count * (at + 1)]:
                 copy.wait()
         top = jnp.maximum(
             jnp.max(scores[0], axis=-1, keepdims=True), jnp.max(scores[1], axis=-1, keepdims=True)
@@ -493,17 +441,16 @@
     return pl.pallas_call(
         functools.partial(heads_kernel, blocks),
         out_shape=[shape_of(rows, third)] * 2,
-        in_specs=[SMEM] + [ANY] * 6,
+        in_specs=[SMEM, VMEM] + [ANY] * 5,
         out_specs=[ANY] * 2,
         scratch_shapes=[
-            pltpu.VMEM(qk.shape, BF16),
             pltpu.VMEM((2, 2 * rows, 2 * third), BF16),
             pltpu.VMEM((4, 4, 8, rows), F32),
             pltpu.VMEM((2, rows, third), BF16),
-            pltpu.SemaphoreType.DMA((8 + 4 * count,)),
+            pltpu.SemaphoreType.DMA((4 + 4 * count,)),
             pltpu.SemaphoreType.DMA((2,)),
         ],
-        compiler_params=params(50),
+        compiler_params=params(40),
         cost_estimate=cost(effort, 1e6),
     )(length, qk, v, *sums)
 

time: 104 us -> 101 us (0.971)
  Pallas kernels: 34.7 us -> 23.6 us
  waiting for transfers between devices: 40.6 us -> 48.7 us
    ppermute x3, waiting for transfers between devices: 4.94 us -> 8.31 us  [along(): return lax.ppermute(piece, 'req', up)]
    pallas_call x1, Pallas kernels: 5.97 us -> 2.65 us  [first_part(): pl.pallas_call(functools.partial(first_kernel, len(pieces)), out_shape=[q...]
    ppermute x1, waiting for transfers between devices: 0.01 us -> 3.04 us  [team_local(): packed_y.append(lax.ppermute(packed[1], 'seq', SWAP))]
    pallas_call x2, Pallas kernels: 10.1 us -> 7.45 us  [team_attention(): pl.pallas_call(functools.partial(heads_kernel, blocks), out_shape=[shape_...]
    pallas_call x1, Pallas kernels: 3.82 us -> 1.21 us  [last_values(): pl.pallas_call(functools.partial(values_kernel, len(pieces)), out_shape=s...]
    pallas_call x1, Pallas kernels: 5.32 us -> 2.87 us  [last_scores(): pl.pallas_call(functools.partial(scores_kernel, len(pieces)), out_shape=[...]
    ppermute x1, waiting for transfers between devices: 0.73 us -> 2.14 us  [team_local(): lax.ppermute(far[0], 'seq', SWAP)]
  transfers between devices with their start and end apart: 25 -> 25, of which waited for: 10 -> 13; matrix products, arithmetic and copies ran while one was open for 0% -> 0% of each run, Pallas kernels for 25% -> 15%
where the time goes in v7:
time: 101 us
  waiting for transfers between devices  48.7 us (48%)
  Pallas kernels  23.6 us (23%)
  starting transfers between devices  23.5 us (23%)
  between operations  2.22 us (2%)
  local copies, waits for them, and re-layouts  2.09 us (2%)
    ppermute x4, waiting for transfers between devices, across(): return lax.ppermute(piece, 'req', beside)  25.3 us
    ppermute x3, starting transfers between devices, along(): return lax.ppermute(piece, 'req', up)  9.25 us
    ppermute x3, waiting for transfers between devices, along(): return lax.ppermute(piece, 'req', up)  8.31 us
    pallas_call x2, Pallas kernels, team_attention(): pl.pallas_call(functools.partial(heads_kernel, blocks), out_shape=[shape_...  7.45 us
    pallas_call x1, Pallas kernels, project(): pl.pallas_call(out_kernel, out_shape=[shape_of(channels, rows, dtype=F32)...  5.66 us
    ppermute x2, waiting for transfers between devices, back(): return lax.ppermute(piece, 'req', down)  4.52 us
    ppermute x1, waiting for transfers between devices, team_local(): lax.ppermute(far[1], ('cfg', 'seq'), diagonal)  4.15 us
    ppermute x4, starting transfers between devices, across(): return lax.ppermute(piece, 'req', beside)  4.05 us
  transfers between devices with their start and end apart: 25, of which 13 were waited for; matrix products, arithmetic and copies ran while one was open for 0% of the time, Pallas kernels for 15%

profile of v7, /device:TPU:0, one launch (start us, length us, event | category | flops | bytes accessed | tf_op | source)
XLA Modules:
  0.0 100.8 jit_solution(11497221141620996550)
XLA Ops:
  0.0 3.2 %shard_map.109 = (bf16[192,1536]{1,0:T(8,128)(2,1)}, bf16[288,1536]{1,0:T(8,128)(2,1)}) custom-call(bf16[192,4608]{1,0:T(8,128)(2,1)} %qkv_ref.1, bf16[192,1536]{1,0:T(8,128)(2,1)} %w_out_ref.1, bf16[288,1536]{1,0:T(8,128)(2,1)} %bitcast.20, f32[5,1,1536]{2,1,0:T(1,128)} %bitcast.18), custom_call_target="tpu_custom_call" | custom-call | flops 4000000000 | bytes 1000000 | tf_op jit(solution)/shard_map/pallas_call | solution.py:194
  3.2 3.0 %collective-permute-start = (bf16[288,1536]{1,0:T(8,128)(2,1)}, bf16[288,1536]{1,0:T(8,128)(2,1)S(1)}, u32[]{:S(2)}, u32[]{:S(2)}) collective-permute-start(bf16[288,1536]{1,0:T(8,128)(2,1)} %get-tuple-element.26.refs_0_), channel_id=1, source_target_pairs={{0,1},{1,0},{2,3},{3,2},{4,5},{5,4},{6,7},{7,6},{8,9},{9,8},{10,11... | collective-permute-start | bytes 2654216 | tf_op jit(solution)/shard_map/ppermute | solution.py:560
  6.2 1.5 %collective-permute-start.3 = (bf16[192,1536]{1,0:T(8,128)(2,1)}, bf16[192,1536]{1,0:T(8,128)(2,1)S(1)}, u32[]{:S(2)}, u32[]{:S(2)}) collective-permute-start(bf16[192,1536]{1,0:T(8,128)(2,1)} %get-tuple-element.27.refs_4_.refs_0_), channel_id=1, source_target_pairs={{0,2},{2,0},{4,6},{6,4},{8,10},{10,8},{12,14},{14,12},{1,3},{3,1},... | collective-permute-start | bytes 1769480 | tf_op jit(solution)/shard_map/ppermute | solution.py:556
  7.7 2.6 %collective-permute-start.4 = (bf16[192,1536]{1,0:T(8,128)(2,1)}, bf16[192,1536]{1,0:T(8,128)(2,1)S(1)}, u32[]{:S(2)}, u32[]{:S(2)}) collective-permute-start(bf16[192,1536]{1,0:T(8,128)(2,1)} %get-tuple-element.27.refs_4_.refs_0_), channel_id=1, source_target_pairs={{0,8},{2,10},{4,0},{6,2},{12,4},{14,6},{8,12},{10,14},{1,9},{3,11}... | collective-permute-start | bytes 1769480 | tf_op jit(solution)/shard_map/ppermute | solution.py:550
  10.3 0.0 copy-done.7
  10.4 10.8 %collective-permute-done.3.refs_5_.refs_1_ = bf16[192,1536]{1,0:T(8,128)(2,1)S(1)} collective-permute-done((bf16[192,1536]{1,0:T(8,128)(2,1)}, bf16[192,1536]{1,0:T(8,128)(2,1)S(1)}, u32[]{:S(2)}, u32[]{:S(2)}) %collective-permute-start.3) | collective-permute-done | bytes 589856 | tf_op jit(solution)/shard_map/ppermute | solution.py:556
  21.3 1.4 %collective-permute-done.4.refs_6_.refs_2_ = bf16[192,1536]{1,0:T(8,128)(2,1)S(1)} collective-permute-done((bf16[192,1536]{1,0:T(8,128)(2,1)}, bf16[192,1536]{1,0:T(8,128)(2,1)S(1)}, u32[]{:S(2)}, u32[]{:S(2)}) %collective-permute-start.4) | collective-permute-done | bytes 589856 | tf_op jit(solution)/shard_map/ppermute | solution.py:550
  22.6 0.5 collective-permute-start.5
  23.2 3.3 %collective-permute-start.6 = (bf16[192,1536]{1,0:T(8,128)(2,1)S(1)}, bf16[192,1536]{1,0:T(8,128)(2,1)S(1)}, u32[]{:S(2)}, u32[]{:S(2)}) collective-permute-start(bf16[192,1536]{1,0:T(8,128)(2,1)S(1)} %collective-permute-done.4.refs_6_.refs_2_), channel_id=1, source_target_pairs={{0,8},{2,10},{4,0},{6,2},{12,4},{14,6},{8,12},{10,14},{1,9},{3,11}... | collective-permute-start | bytes 1769480 | tf_op jit(solution)/shard_map/ppermute | solution.py:550
  26.5 0.0 collective-permute-start.1
  26.5 0.0 collective-permute-done.refs_1_
  26.5 0.5 collective-permute-start.2
  27.0 9.3 %collective-permute-done.5.refs_7_.refs_3_ = bf16[192,1536]{1,0:T(8,128)(2,1)S(1)} collective-permute-done((bf16[192,1536]{1,0:T(8,128)(2,1)S(1)}, bf16[192,1536]{1,0:T(8,128)(2,1)S(1)}, u32[]{:S(2)}, u32[]{:S(2)}) %collective-permute-start.5) | collective-permute-done | bytes 589856 | tf_op jit(solution)/shard_map/ppermute | solution.py:556
  36.2 1.0 %collective-permute-done.6.refs_6_.refs_5_.refs_0_ = bf16[192,1536]{1,0:T(8,128)(2,1)S(1)} collective-permute-done((bf16[192,1536]{1,0:T(8,128)(2,1)S(1)}, bf16[192,1536]{1,0:T(8,128)(2,1)S(1)}, u32[]{:S(2)}, u32[]{:S(2)}) %collective-permute-start.6) | collective-permute-done | bytes 589856 | tf_op jit(solution)/shard_map/ppermute | solution.py:550
  37.3 1.5 %collective-permute-start.7 = (bf16[192,1536]{1,0:T(8,128)(2,1)S(1)}, bf16[192,1536]{1,0:T(8,128)(2,1)S(1)}, u32[]{:S(2)}, u32[]{:S(2)}) collective-permute-start(bf16[192,1536]{1,0:T(8,128)(2,1)S(1)} %collective-permute-done.6.refs_6_.refs_5_.refs_0_), channel_id=1, source_target_pairs={{0,2},{2,0},{4,6},{6,4},{8,10},{10,8},{12,14},{14,12},{1,3},{3,1},... | collective-permute-start | bytes 1769480 | tf_op jit(solution)/shard_map/ppermute | solution.py:556
  38.8 3.4 %collective-permute-start.8 = (bf16[192,1536]{1,0:T(8,128)(2,1)S(1)}, bf16[192,1536]{1,0:T(8,128)(2,1)S(1)}, u32[]{:S(2)}, u32[]{:S(2)}) collective-permute-start(bf16[192,1536]{1,0:T(8,128)(2,1)S(1)} %collective-permute-done.6.refs_6_.refs_5_.refs_0_), channel_id=1, source_target_pairs={{0,8},{2,10},{4,0},{6,2},{12,4},{14,6},{8,12},{10,14},{1,9},{3,11}... | collective-permute-start | bytes 1769480 | tf_op jit(solution)/shard_map/ppermute | solution.py:550
  42.1 1.1 %copy-done.2 = bf16[192,1536]{1,0:T(8,128)(2,1)S(1)} copy-done((bf16[192,1536]{1,0:T(8,128)(2,1)S(1)}, bf16[192,1536]{1,0:T(8,128)(2,1)}, u32[]{:S(2)}) %copy-start.2) | copy-done | bytes 589848
  43.2 0.2 shard_map.111.refs_4_
  43.4 0.6 collective-permute-start.10
  44.7 0.0 collective-permute-done.1.refs_2_
  44.7 0.1 collective-permute-start.13
  44.8 0.0 collective-permute-done.2.refs_3_
  44.8 0.1 collective-permute-start.9
  44.8 2.6 %shard_map.110 = (bf16[4,288,768]{2,1,0:T(8,128)(2,1)S(1)}, bf16[4,288,384]{2,1,0:T(8,128)(2,1)S(1)}) custom-call(bf16[288,1536]{1,0:T(8,128)(2,1)S(1)} %copy-done, bf16[288,1536]{1,0:T(8,128)(2,1)S(1)} %collective-permute-done.refs_1_, bf16[288,1536]{1,0:T(8,128)(2,1)S(1)} %collective-permute-done.1.refs_2_, ...), custom_call_target="tpu_custom_call" | custom-call | flops 6000000000 | bytes 1000000 | tf_op jit(solution)/shard_map/pallas_call | solution.py:270
  47.5 5.9 %collective-permute-done.8.refs_8_.refs_7_.refs_2_ = bf16[192,1536]{1,0:T(8,128)(2,1)S(1)} collective-permute-done((bf16[192,1536]{1,0:T(8,128)(2,1)S(1)}, bf16[192,1536]{1,0:T(8,128)(2,1)S(1)}, u32[]{:S(2)}, u32[]{:S(2)}) %collective-permute-start.8) | collective-permute-done | bytes 589856 | tf_op jit(solution)/shard_map/ppermute | solution.py:550
  53.4 3.4 %collective-permute-done.9.refs_3_ = bf16[192,384]{1,0:T(8,128)(2,1)S(1)} collective-permute-done((bf16[192,384]{1,0:T(8,128)(2,1)S(1)}, bf16[192,384]{1,0:T(8,128)(2,1)S(1)}, u32[]{:S(2)}, u32[]{:S(2)}) %collective-permute-start.9) | collective-permute-done | bytes 147488 | tf_op jit(solution)/shard_map/ppermute | solution.py:553
  56.8 0.0 collective-permute-done.7.refs_7_.refs_6_.refs_1_
  56.8 0.0 collective-permute-done.10.refs_6_
  56.8 0.5 collective-permute-start.11
  57.3 0.7 collective-permute-start.12
  58.0 0.0 collective-permute-start.14
  58.0 0.4 shard_map.115.refs_8_
  58.4 0.5 collective-permute-start.18
  58.9 5.2 %collective-permute-done.11.refs_9_.refs_8_ = bf16[96,1152]{1,0:T(8,128)(2,1)S(1)} collective-permute-done((bf16[96,1152]{1,0:T(8,128)(2,1)S(1)}, bf16[96,1152]{1,0:T(8,128)(2,1)S(1)}, u32[]{:S(2)}, u32[]{:S(2)}) %collective-permute-start.11) | collective-permute-done | bytes 221216 | tf_op jit(solution)/shard_map/ppermute | solution.py:556
  64.2 0.0 collective-permute-start.19
  64.2 1.2 %collective-permute-done.12.refs_10_.refs_9_ = bf16[96,1152]{1,0:T(8,128)(2,1)S(1)} collective-permute-done((bf16[96,1152]{1,0:T(8,128)(2,1)S(1)}, bf16[96,1152]{1,0:T(8,128)(2,1)S(1)}, u32[]{:S(2)}, u32[]{:S(2)}) %collective-permute-start.12) | collective-permute-done | bytes 221216 | tf_op jit(solution)/shard_map/ppermute | solution.py:553
  65.3 2.9 %shard_map.112 = (bf16[4,288,768]{2,1,0:T(8,128)(2,1)S(1)}, f32[4,8,288]{2,1,0:T(8,128)S(1)}) custom-call(bf16[288,1536]{1,0:T(8,128)(2,1)S(1)} %copy-done, bf16[288,1536]{1,0:T(8,128)(2,1)S(1)} %collective-permute-done.refs_1_, bf16[288,1536]{1,0:T(8,128)(2,1)S(1)} %collective-permute-done.1.refs_2_, bf16[288,1536]{1,0:T(8,128)(2,1)S(1)} %collective-permute-done.2.refs_3_, ...), custom_call_target="tpu_custom_call" | custom-call | flops 6000000000 | bytes 1000000 | tf_op jit(solution)/shard_map/pallas_call | solution.py:317
  68.2 0.5 collective-permute-start.15
  68.7 0.0 collective-permute-done.13.refs_5_
  68.7 0.0 collective-permute-start.16
  68.7 0.0 collective-permute-done.14.refs_7_
  68.7 1.7 %collective-permute-start.17 = (f32[4,8,288]{2,1,0:T(8,128)S(1)}, f32[4,8,288]{2,1,0:T(8,128)S(1)}, u32[]{:S(2)}, u32[]{:S(2)}) collective-permute-start(f32[4,8,288]{2,1,0:T(8,128)S(1)} %get-tuple-element.37.s0_ref), channel_id=1, source_target_pairs={{0,17},{1,16},{16,1},{17,0},{2,19},{3,18},{18,3},{19,2},{4,21},{5,... | collective-permute-start | bytes 110600 | tf_op jit(solution)/shard_map/ppermute | solution.py:600
  70.4 1.2 %shard_map.113.v_ref = bf16[4,288,384]{2,1,0:T(8,128)(2,1)S(1)} custom-call(bf16[288,1536]{1,0:T(8,128)(2,1)S(1)} %copy-done, bf16[288,1536]{1,0:T(8,128)(2,1)S(1)} %collective-permute-done.refs_1_, bf16[288,1536]{1,0:T(8,128)(2,1)S(1)} %collective-permute-done.1.refs_2_, bf16[288,1536]{1,0:T(8,128)(2,1)S(1)} %collective-permute-done.2.refs_3_, ...), custom_call_target="tpu_custom_call" | custom-call | flops 4000000000 | bytes 1000000 | tf_op jit(solution)/shard_map/pallas_call | solution.py:349
  71.7 3.0 %collective-permute-done.18.refs_10_ = bf16[768,384]{1,0:T(8,128)(2,1)} collective-permute-done((bf16[768,384]{1,0:T(8,128)(2,1)S(1)}, bf16[768,384]{1,0:T(8,128)(2,1)}, u32[]{:S(2)}, u32[]{:S(2)}) %collective-permute-start.18) | collective-permute-done | bytes 589856 | tf_op jit(solution)/shard_map/ppermute | solution.py:589
  74.7 0.0 collective-permute-start.23
  74.7 0.9 collective-permute-done.15.s1_ref
  75.6 0.0 collective-permute-done.16.s2_ref
  75.6 0.3 collective-permute-done.17.s3_ref
  75.9 3.7 %shard_map.114 = (bf16[288,384]{1,0:T(8,128)(2,1)}, bf16[288,384]{1,0:T(8,128)(2,1)S(1)}) custom-call(s32[1]{0:T(128)} %copy.12.length_ref, bf16[4,288,768]{2,1,0:T(8,128)(2,1)S(1)} %get-tuple-element.41.qk_ref, bf16[4,288,384]{2,1,0:T(8,128)(2,1)S(1)} %shard_map.113.v_ref, f32[4,8,288]{2,1,0:T(8,128)S(1)} %get-tuple-element.37.s0_ref, ...), custom_call_target="tpu_custom_call" | custom-call | flops 6000000000 | bytes 1000000 | tf_op jit(solution)/shard_map/pallas_call | solution.py:441
  79.7 0.0 copy-start.4
  79.7 0.0 collective-permute-done.19.refs_9_
  79.7 0.5 collective-permute-start.21
  80.2 3.7 %shard_map.116 = (bf16[288,384]{1,0:T(8,128)(2,1)}, bf16[288,384]{1,0:T(8,128)(2,1)S(1)}) custom-call(s32[1]{0:T(128)} %copy.12.length_ref, bf16[4,288,768]{2,1,0:T(8,128)(2,1)S(1)} %get-tuple-element.41.qk_ref, bf16[4,288,384]{2,1,0:T(8,128)(2,1)S(1)} %shard_map.113.v_ref, f32[4,8,288]{2,1,0:T(8,128)S(1)} %get-tuple-element.37.s0_ref, ...), custom_call_target="tpu_custom_call" | custom-call | flops 1000000 | bytes 1000000 | tf_op jit(solution)/shard_map/pallas_call | solution.py:441
  84.0 0.1 collective-permute-start.20
  84.0 1.7 %collective-permute-start.22 = (bf16[288,384]{1,0:T(8,128)(2,1)S(1)}, bf16[288,384]{1,0:T(8,128)(2,1)}, u32[]{:S(2)}, u32[]{:S(2)}) collective-permute-start(bf16[288,384]{1,0:T(8,128)(2,1)S(1)} %get-tuple-element.44), channel_id=1, source_target_pairs={{0,17},{1,16},{16,1},{17,0},{2,19},{3,18},{18,3},{19,2},{4,21},{5,... | collective-permute-start | bytes 663560 | tf_op jit(solution)/shard_map/ppermute | solution.py:610
  85.7 0.0 collective-permute-done.20.refs_1_
  85.7 2.1 %collective-permute-done.21.refs_2_ = bf16[288,384]{1,0:T(8,128)(2,1)S(1)} collective-permute-done((bf16[288,384]{1,0:T(8,128)(2,1)}, bf16[288,384]{1,0:T(8,128)(2,1)S(1)}, u32[]{:S(2)}, u32[]{:S(2)}) %collective-permute-start.21) | collective-permute-done | bytes 221216 | tf_op jit(solution)/shard_map/ppermute | solution.py:609
  87.9 4.1 %collective-permute-done.22.refs_3_ = bf16[288,384]{1,0:T(8,128)(2,1)} collective-permute-done((bf16[288,384]{1,0:T(8,128)(2,1)S(1)}, bf16[288,384]{1,0:T(8,128)(2,1)}, u32[]{:S(2)}, u32[]{:S(2)}) %collective-permute-start.22) | collective-permute-done | bytes 221216 | tf_op jit(solution)/shard_map/ppermute | solution.py:610
  92.0 0.0 collective-permute-done.23.refs_11_
  92.0 0.9 copy-done.3
  92.9 5.7 %shard_map.117 = (f32[32,288]{1,0:T(8,128)S(1)}, bf16[32,288]{1,0:T(8,128)(2,1)S(1)}) custom-call(bf16[288,1536]{1,0:T(8,128)(2,1)} %bitcast.21, f32[5,1,1536]{2,1,0:T(1,128)S(1)} %bitcast.19, bf16[64,1536]{1,0:T(8,128)(2,1)S(1)} %bitcast.17, bf16[288,384]{1,0:T(8,128)(2,1)S(1)} %get-tuple-element.42.refs_0_, ...), custom_call_target="tpu_custom_call" | custom-call | flops 8000000000 | bytes 1000000 | tf_op jit(solution)/shard_map/pallas_call | solution.py:498
  98.6 0.2 collective-permute-start.24
  100.1 0.0 collective-permute-done.24
  100.2 0.6 fusion.4
  (22 shorter events, 0.1 us)
Async XLA Ops:
  0.0 10.3 %copy-start.6 = (f32[1536]{0:T(1024)S(1)}, f32[1536]{0:T(1024)}, u32[]{:S(2)}) copy-start(f32[1536]{0:T(1024)} %param.17) | copy-start | bytes 18436
  0.0 10.3 %copy-start.7 = (f32[1536]{0:T(1024)S(1)}, f32[1536]{0:T(1024)}, u32[]{:S(2)}) copy-start(f32[1536]{0:T(1024)} %param.16) | copy-start | bytes 18436
  3.2 23.3 %collective-permute-start = (bf16[288,1536]{1,0:T(8,128)(2,1)}, bf16[288,1536]{1,0:T(8,128)(2,1)S(1)}, u32[]{:S(2)}, u32[]{:S(2)}) collective-permute-start(bf16[288,1536]{1,0:T(8,128)(2,1)} %get-tuple-element.26.refs_0_), channel_id=1, source_target_pairs={{0,1},{1,0},{2,3},{3,2},{4,5},{5,4},{6,7},{7,6},{8,9},{9,8},{10,11... | collective-permute-start | bytes 2654216 | tf_op jit(solution)/shard_map/ppermute | solution.py:560
  6.2 15.0 %collective-permute-start.3 = (bf16[192,1536]{1,0:T(8,128)(2,1)}, bf16[192,1536]{1,0:T(8,128)(2,1)S(1)}, u32[]{:S(2)}, u32[]{:S(2)}) collective-permute-start(bf16[192,1536]{1,0:T(8,128)(2,1)} %get-tuple-element.27.refs_4_.refs_0_), channel_id=1, source_target_pairs={{0,2},{2,0},{4,6},{6,4},{8,10},{10,8},{12,14},{14,12},{1,3},{3,1},... | collective-permute-start | bytes 1769480 | tf_op jit(solution)/shard_map/ppermute | solution.py:556
  7.7 14.9 %collective-permute-start.4 = (bf16[192,1536]{1,0:T(8,128)(2,1)}, bf16[192,1536]{1,0:T(8,128)(2,1)S(1)}, u32[]{:S(2)}, u32[]{:S(2)}) collective-permute-start(bf16[192,1536]{1,0:T(8,128)(2,1)} %get-tuple-element.27.refs_4_.refs_0_), channel_id=1, source_target_pairs={{0,8},{2,10},{4,0},{6,2},{12,4},{14,6},{8,12},{10,14},{1,9},{3,11}... | collective-permute-start | bytes 1769480 | tf_op jit(solution)/shard_map/ppermute | solution.py:550
  21.3 23.6 %copy-start = (bf16[288,1536]{1,0:T(8,128)(2,1)S(1)}, bf16[288,1536]{1,0:T(8,128)(2,1)}, u32[]{:S(2)}) copy-start(bf16[288,1536]{1,0:T(8,128)(2,1)} %get-tuple-element.26.refs_0_) | copy-start | bytes 2654212
  22.6 13.6 %collective-permute-start.5 = (bf16[192,1536]{1,0:T(8,128)(2,1)S(1)}, bf16[192,1536]{1,0:T(8,128)(2,1)S(1)}, u32[]{:S(2)}, u32[]{:S(2)}) collective-permute-start(bf16[192,1536]{1,0:T(8,128)(2,1)S(1)} %collective-permute-done.4.refs_6_.refs_2_), channel_id=1, source_target_pairs={{0,2},{2,0},{4,6},{6,4},{8,10},{10,8},{12,14},{14,12},{1,3},{3,1},... | collective-permute-start | bytes 1769480 | tf_op jit(solution)/shard_map/ppermute | solution.py:556
  23.2 14.1 %collective-permute-start.6 = (bf16[192,1536]{1,0:T(8,128)(2,1)S(1)}, bf16[192,1536]{1,0:T(8,128)(2,1)S(1)}, u32[]{:S(2)}, u32[]{:S(2)}) collective-permute-start(bf16[192,1536]{1,0:T(8,128)(2,1)S(1)} %collective-permute-done.4.refs_6_.refs_2_), channel_id=1, source_target_pairs={{0,8},{2,10},{4,0},{6,2},{12,4},{14,6},{8,12},{10,14},{1,9},{3,11}... | collective-permute-start | bytes 1769480 | tf_op jit(solution)/shard_map/ppermute | solution.py:550
  26.5 18.2 %collective-permute-start.1 = (bf16[288,1536]{1,0:T(8,128)(2,1)}, bf16[288,1536]{1,0:T(8,128)(2,1)S(1)}, u32[]{:S(2)}, u32[]{:S(2)}) collective-permute-start(bf16[288,1536]{1,0:T(8,128)(2,1)} %get-tuple-element.26.refs_0_), channel_id=1, source_target_pairs={{0,16},{16,0},{1,17},{17,1},{2,18},{18,2},{3,19},{19,3},{4,20},{20... | collective-permute-start | bytes 2654216 | tf_op jit(solution)/shard_map/ppermute | solution.py:561
  26.5 18.3 %collective-permute-start.2 = (bf16[288,1536]{1,0:T(8,128)(2,1)S(1)}, bf16[288,1536]{1,0:T(8,128)(2,1)S(1)}, u32[]{:S(2)}, u32[]{:S(2)}) collective-permute-start(bf16[288,1536]{1,0:T(8,128)(2,1)S(1)} %collective-permute-done.refs_1_), channel_id=1, source_target_pairs={{0,16},{16,0},{1,17},{17,1},{2,18},{18,2},{3,19},{19,3},{4,20},{20... | collective-permute-start | bytes 2654216 | tf_op jit(solution)/shard_map/ppermute | solution.py:580
  37.3 19.5 %collective-permute-start.7 = (bf16[192,1536]{1,0:T(8,128)(2,1)S(1)}, bf16[192,1536]{1,0:T(8,128)(2,1)S(1)}, u32[]{:S(2)}, u32[]{:S(2)}) collective-permute-start(bf16[192,1536]{1,0:T(8,128)(2,1)S(1)} %collective-permute-done.6.refs_6_.refs_5_.refs_0_), channel_id=1, source_target_pairs={{0,2},{2,0},{4,6},{6,4},{8,10},{10,8},{12,14},{14,12},{1,3},{3,1},... | collective-permute-start | bytes 1769480 | tf_op jit(solution)/shard_map/ppermute | solution.py:556
  38.8 14.6 %collective-permute-start.8 = (bf16[192,1536]{1,0:T(8,128)(2,1)S(1)}, bf16[192,1536]{1,0:T(8,128)(2,1)S(1)}, u32[]{:S(2)}, u32[]{:S(2)}) collective-permute-start(bf16[192,1536]{1,0:T(8,128)(2,1)S(1)} %collective-permute-done.6.refs_6_.refs_5_.refs_0_), channel_id=1, source_target_pairs={{0,8},{2,10},{4,0},{6,2},{12,4},{14,6},{8,12},{10,14},{1,9},{3,11}... | collective-permute-start | bytes 1769480 | tf_op jit(solution)/shard_map/ppermute | solution.py:550
  42.1 1.1 %copy-start.2 = (bf16[192,1536]{1,0:T(8,128)(2,1)S(1)}, bf16[192,1536]{1,0:T(8,128)(2,1)}, u32[]{:S(2)}) copy-start(bf16[192,1536]{1,0:T(8,128)(2,1)} %get-tuple-element.27.refs_4_.refs_0_) | copy-start | bytes 1769476
  43.4 13.3 %collective-permute-start.10 = (bf16[768,384]{1,0:T(8,128)(2,1)S(1)}, bf16[768,384]{1,0:T(8,128)(2,1)S(1)}, u32[]{:S(2)}, u32[]{:S(2)}) collective-permute-start(bf16[768,384]{1,0:T(8,128)(2,1)S(1)} %shard_map.111.refs_4_), channel_id=1, source_target_pairs={{0,1},{1,0},{2,3},{3,2},{4,5},{5,4},{6,7},{7,6},{8,9},{9,8},{10,11... | collective-permute-start | bytes 1769480 | tf_op jit(solution)/shard_map/ppermute | solution.py:582
  44.7 24.1 %collective-permute-start.13 = (bf16[768,384]{1,0:T(8,128)(2,1)S(1)}, bf16[768,384]{1,0:T(8,128)(2,1)S(1)}, u32[]{:S(2)}, u32[]{:S(2)}) collective-permute-start(bf16[768,384]{1,0:T(8,128)(2,1)S(1)} %shard_map.111.refs_4_), channel_id=1, source_target_pairs={{0,16},{16,0},{1,17},{17,1},{2,18},{18,2},{3,19},{19,3},{4,20},{20... | collective-permute-start | bytes 1769480 | tf_op jit(solution)/shard_map/ppermute | solution.py:590
  44.8 12.0 %collective-permute-start.9 = (bf16[192,384]{1,0:T(8,128)(2,1)S(1)}, bf16[192,384]{1,0:T(8,128)(2,1)S(1)}, u32[]{:S(2)}, u32[]{:S(2)}) collective-permute-start(bf16[192,384]{1,0:T(8,128)(2,1)S(1)} %slice.13), channel_id=1, source_target_pairs={{8,0},{10,2},{0,4},{2,6},{4,12},{6,14},{12,8},{14,10},{9,1},{11,3}... | collective-permute-start | bytes 442376 | tf_op jit(solution)/shard_map/ppermute | solution.py:553
  56.8 7.4 %collective-permute-start.11 = (bf16[96,1152]{1,0:T(8,128)(2,1)S(1)}, bf16[96,1152]{1,0:T(8,128)(2,1)S(1)}, u32[]{:S(2)}, u32[]{:S(2)}) collective-permute-start(bf16[96,1152]{1,0:T(8,128)(2,1)S(1)} %slice.14), channel_id=1, source_target_pairs={{0,2},{2,0},{4,6},{6,4},{8,10},{10,8},{12,14},{14,12},{1,3},{3,1},... | collective-permute-start | bytes 663560 | tf_op jit(solution)/shard_map/ppermute | solution.py:556
  57.3 8.0 %collective-permute-start.12 = (bf16[96,1152]{1,0:T(8,128)(2,1)S(1)}, bf16[96,1152]{1,0:T(8,128)(2,1)S(1)}, u32[]{:S(2)}, u32[]{:S(2)}) collective-permute-start(bf16[96,1152]{1,0:T(8,128)(2,1)S(1)} %slice.12), channel_id=1, source_target_pairs={{8,0},{10,2},{0,4},{2,6},{4,12},{6,14},{12,8},{14,10},{9,1},{11,3}... | collective-permute-start | bytes 663560 | tf_op jit(solution)/shard_map/ppermute | solution.py:553
  58.0 10.8 %collective-permute-start.14 = (bf16[768,384]{1,0:T(8,128)(2,1)S(1)}, bf16[768,384]{1,0:T(8,128)(2,1)S(1)}, u32[]{:S(2)}, u32[]{:S(2)}) collective-permute-start(bf16[768,384]{1,0:T(8,128)(2,1)S(1)} %collective-permute-done.10.refs_6_), channel_id=1, source_target_pairs={{0,16},{16,0},{1,17},{17,1},{2,18},{18,2},{3,19},{19,3},{4,20},{20... | collective-permute-start | bytes 1769480 | tf_op jit(solution)/shard_map/ppermute | solution.py:591
  58.4 9.8 %copy-start.1 = (bf16[768,384]{1,0:T(8,128)(2,1)}, bf16[768,384]{1,0:T(8,128)(2,1)S(1)}, u32[]{:S(2)}) copy-start(bf16[768,384]{1,0:T(8,128)(2,1)S(1)} %shard_map.115.refs_8_) | copy-start | bytes 1769476
  58.4 16.3 %collective-permute-start.18 = (bf16[768,384]{1,0:T(8,128)(2,1)S(1)}, bf16[768,384]{1,0:T(8,128)(2,1)}, u32[]{:S(2)}, u32[]{:S(2)}) collective-permute-start(bf16[768,384]{1,0:T(8,128)(2,1)S(1)} %shard_map.115.refs_8_), channel_id=1, source_target_pairs={{0,1},{1,0},{2,3},{3,2},{4,5},{5,4},{6,7},{7,6},{8,9},{9,8},{10,11... | collective-permute-start | bytes 1769480 | tf_op jit(solution)/shard_map/ppermute | solution.py:589
  64.2 15.5 %collective-permute-start.19 = (bf16[768,384]{1,0:T(8,128)(2,1)S(1)}, bf16[768,384]{1,0:T(8,128)(2,1)S(1)}, u32[]{:S(2)}, u32[]{:S(2)}) collective-permute-start(bf16[768,384]{1,0:T(8,128)(2,1)S(1)} %shard_map.115.refs_8_), channel_id=1, source_target_pairs={{0,16},{16,0},{1,17},{17,1},{2,18},{18,2},{3,19},{19,3},{4,20},{20... | collective-permute-start | bytes 1769480 | tf_op jit(solution)/shard_map/ppermute | solution.py:590
  68.2 7.4 %collective-permute-start.15 = (f32[4,8,288]{2,1,0:T(8,128)S(1)}, f32[4,8,288]{2,1,0:T(8,128)S(1)}, u32[]{:S(2)}, u32[]{:S(2)}) collective-permute-start(f32[4,8,288]{2,1,0:T(8,128)S(1)} %get-tuple-element.37.s0_ref), channel_id=1, source_target_pairs={{0,1},{1,0},{2,3},{3,2},{4,5},{5,4},{6,7},{7,6},{8,9},{9,8},{10,11... | collective-permute-start | bytes 110600 | tf_op jit(solution)/shard_map/ppermute | solution.py:598
  68.7 6.9 %collective-permute-start.16 = (f32[4,8,288]{2,1,0:T(8,128)S(1)}, f32[4,8,288]{2,1,0:T(8,128)S(1)}, u32[]{:S(2)}, u32[]{:S(2)}) collective-permute-start(f32[4,8,288]{2,1,0:T(8,128)S(1)} %get-tuple-element.37.s0_ref), channel_id=1, source_target_pairs={{0,16},{16,0},{1,17},{17,1},{2,18},{18,2},{3,19},{19,3},{4,20},{20... | collective-permute-start | bytes 110600 | tf_op jit(solution)/shard_map/ppermute | solution.py:599
  68.7 7.2 %collective-permute-start.17 = (f32[4,8,288]{2,1,0:T(8,128)S(1)}, f32[4,8,288]{2,1,0:T(8,128)S(1)}, u32[]{:S(2)}, u32[]{:S(2)}) collective-permute-start(f32[4,8,288]{2,1,0:T(8,128)S(1)} %get-tuple-element.37.s0_ref), channel_id=1, source_target_pairs={{0,17},{1,16},{16,1},{17,0},{2,19},{3,18},{18,3},{19,2},{4,21},{5,... | collective-permute-start | bytes 110600 | tf_op jit(solution)/shard_map/ppermute | solution.py:600
  74.7 17.3 %collective-permute-start.23 = (bf16[768,384]{1,0:T(8,128)(2,1)}, bf16[768,384]{1,0:T(8,128)(2,1)}, u32[]{:S(2)}, u32[]{:S(2)}) collective-permute-start(bf16[768,384]{1,0:T(8,128)(2,1)} %collective-permute-done.18.refs_10_), channel_id=1, source_target_pairs={{0,16},{16,0},{1,17},{17,1},{2,18},{18,2},{3,19},{19,3},{4,20},{20... | collective-permute-start | bytes 1769480 | tf_op jit(solution)/shard_map/ppermute | solution.py:591
  79.7 12.3 %copy-start.4 = (f32[1,5,1536]{2,0,1:T(1,128)S(1)}, f32[1,5,1536]{2,0,1:T(1,128)}, u32[]{:S(2)}) copy-start(f32[1,5,1536]{2,0,1:T(1,128)} %param.13) | copy-start | bytes 92164
  79.7 6.0 %copy-start.8 = (bf16[768,384]{1,0:T(8,128)(2,1)}, bf16[768,384]{1,0:T(8,128)(2,1)S(1)}, u32[]{:S(2)}) copy-start(bf16[768,384]{1,0:T(8,128)(2,1)S(1)} %collective-permute-done.19.refs_9_) | copy-start | bytes 1769476
  79.7 8.2 %collective-permute-start.21 = (bf16[288,384]{1,0:T(8,128)(2,1)}, bf16[288,384]{1,0:T(8,128)(2,1)S(1)}, u32[]{:S(2)}, u32[]{:S(2)}) collective-permute-start(bf16[288,384]{1,0:T(8,128)(2,1)} %get-tuple-element.40), channel_id=1, source_target_pairs={{0,1},{1,0},{2,3},{3,2},{4,5},{5,4},{6,7},{7,6},{8,9},{9,8},{10,11... | collective-permute-start | bytes 663560 | tf_op jit(solution)/shard_map/ppermute | solution.py:609
  84.0 1.8 %collective-permute-start.20 = (bf16[288,384]{1,0:T(8,128)(2,1)}, bf16[288,384]{1,0:T(8,128)(2,1)S(1)}, u32[]{:S(2)}, u32[]{:S(2)}) collective-permute-start(bf16[288,384]{1,0:T(8,128)(2,1)} %get-tuple-element.43), channel_id=1, source_target_pairs={{0,16},{16,0},{1,17},{17,1},{2,18},{18,2},{3,19},{19,3},{4,20},{20... | collective-permute-start | bytes 663560 | tf_op jit(solution)/shard_map/ppermute | solution.py:608
  84.0 8.0 %collective-permute-start.22 = (bf16[288,384]{1,0:T(8,128)(2,1)S(1)}, bf16[288,384]{1,0:T(8,128)(2,1)}, u32[]{:S(2)}, u32[]{:S(2)}) collective-permute-start(bf16[288,384]{1,0:T(8,128)(2,1)S(1)} %get-tuple-element.44), channel_id=1, source_target_pairs={{0,17},{1,16},{16,1},{17,0},{2,19},{3,18},{18,3},{19,2},{4,21},{5,... | collective-permute-start | bytes 663560 | tf_op jit(solution)/shard_map/ppermute | solution.py:610
  92.0 0.9 copy-start.3
  92.9 7.2 %copy-start.5 = (f32[1,288,32]{1,2,0:T(8,128)S(1)}, f32[1,288,32]{1,2,0:T(8,128)}, u32[]{:S(2)}) copy-start(f32[1,288,32]{1,2,0:T(8,128)} %param.12) | copy-start | bytes 110596
  98.6 1.6 %collective-permute-start.24 = (bf16[32,288]{1,0:T(8,128)(2,1)S(1)}, bf16[32,288]{1,0:T(8,128)(2,1)S(1)}, u32[]{:S(2)}, u32[]{:S(2)}) collective-permute-start(bf16[32,288]{1,0:T(8,128)(2,1)S(1)} %get-tuple-element.45), channel_id=1, source_target_pairs={{0,16},{16,0},{1,17},{17,1},{2,18},{18,2},{3,19},{19,3},{4,20},{20... | collective-permute-start | bytes 55304 | tf_op jit(solution)/shard_map/ppermute | solution.py:523

commit v8 on v7

--- a/solution.py
+++ b/solution.py
@@ -474,12 +474,9 @@
         part = att_in[j].astype(F32)
         part = jnp.where(side == 0, part, pltpu.roll(part, third // 2, 1)).astype(BF16)
         group_ref[:, window(lax.rem(fold(own ^ j) + steps - pair, steps), third)] = part
-    for copy in loads[4:8]:
-        copy.wait()
-    total = times(group_ref[:, :half], held_ref[:half, :])
-    for copy in loads[8:]:
-        copy.wait()
-    total += times(group_ref[:, half:], held_ref[half:, :])
+    for copy in loads[4:]:
+        copy.wait()
+    total = times(group_ref[...], held_ref[...])
     block_out = (state_in[...].astype(F32) + modes_in[2] * total).astype(BF16)
     head_in = scaled_norm(block_out.astype(F32), modes_in[3], modes_in[4])
     velocity = times_turned(head_in_ref[...], head_in.astype(BF16))
@@ -567,7 +564,7 @@
 
     mine, theirs = [columns], []
     step(mine, theirs, [])
-    cut, split = columns.shape[0] // 2, 3 * third
+    cut, split = columns.shape[0] // 2 + 16, 3 * third
     low = theirs[0][cut:, :split]
     out_last = theirs[0][:, split:]
     gates = [mine[1], theirs[0], low, out_last, gains]
@@ -576,16 +573,16 @@
     step(mine, theirs, gates)
     out_last = back(after(out_last, *gates))
     early = [mine[0], theirs[0], mine[1], theirs[1]]
-    packed = [pack(early, third)]
+    packed = [pack([*early, mine[2]], third)]
     normed_yc = lax.ppermute(normed_y, "cfg", SWAP)
     norms = [normed, normed_y, normed_c, normed_yc]
     packed_y = [lax.ppermute(packed[0], "seq", SWAP)]
     acc_qk, acc_v = first_part(norms, early)
-    gates = [mine[3], theirs[2], out_last, packed_y[0], acc_v]
+    gates = [mine[3], theirs[2], out_last, acc_v]
     upper = across(after(mine[3][:cut, :split], *gates))
     lower = back(after(low, *gates))
     late = [mine[2], theirs[2], mine[3], upper, lower]
-    packed.append(pack([mine[2], theirs[2], mine[3], out_last], third))
+    packed.append(pack([after(theirs[2], packed_y[0]), mine[3], out_last], third))
     packed_y.append(lax.ppermute(packed[1], "seq", SWAP))
     packed_c = [lax.ppermute(part, "cfg", SWAP) for part in packed]
     packed_yc = [lax.ppermute(part, "cfg", SWAP) for part in packed_y]

time: 101 us -> 99.6 us (0.986)
  waiting for transfers between devices: 48.7 us -> 44 us
  starting transfers between devices: 23.5 us -> 26.3 us
    ppermute x4, waiting for transfers between devices: 25.3 us -> 20.1 us  [across(): return lax.ppermute(piece, 'req', beside)]
    ppermute x2, waiting for transfers between devices: 4.52 us -> 7.79 us  [back(): return lax.ppermute(piece, 'req', down)]
    ppermute x1, waiting for transfers between devices: 3.04 us -> 0.01 us  [team_local(): packed_y.append(lax.ppermute(packed[1], 'seq', SWAP))]
    ppermute x1, starting transfers between devices: 1.69 us -> 0.62 us  [team_local(): lax.ppermute(sums, ('cfg', 'seq'), diagonal)]
    ppermute x1, starting transfers between devices: 0.51 us -> 1.58 us  [team_local(): lax.ppermute(sums, 'seq', SWAP)]
    ppermute x1, starting transfers between devices: 0.54 us -> 1.58 us  [team_local(): packed_y.append(lax.ppermute(packed[1], 'seq', SWAP))]
    ppermute x1, waiting for transfers between devices: 2.14 us -> 1.11 us  [team_local(): lax.ppermute(far[0], 'seq', SWAP)]
    unnamed x18 -> x20, local copies, waits for them, and re-layouts: 2.02 us -> 2.02 us
  transfers between devices with their start and end apart: 25 -> 25, of which waited for: 13 -> 12; matrix products, arithmetic and copies ran while one was open for 0% -> 0% of each run, Pallas kernels for 15% -> 16%
where the time goes in v8:
time: 99.6 us; the launch traced here: 99.4 us
  waiting for transfers between devices  44 us (44%)
  starting transfers between devices  26.3 us (26%)
  Pallas kernels  24.1 us (24%)
  between operations  2.21 us (2%)
  local copies, waits for them, and re-layouts  2.1 us (2%)
    ppermute x4, waiting for transfers between devices, across(): return lax.ppermute(piece, 'req', beside)  20.1 us
    ppermute x3, starting transfers between devices, along(): return lax.ppermute(piece, 'req', up)  9.25 us
    ppermute x3, waiting for transfers between devices, along(): return lax.ppermute(piece, 'req', up)  8.7 us
    pallas_call x2, Pallas kernels, team_attention(): pl.pallas_call(functools.partial(heads_kernel, blocks), out_shape=[shape_...  8.02 us
    ppermute x2, waiting for transfers between devices, back(): return lax.ppermute(piece, 'req', down)  7.79 us
    pallas_call x1, Pallas kernels, project(): pl.pallas_call(out_kernel, out_shape=[shape_of(channels, rows, dtype=F32)...  5.24 us
    ppermute x4, starting transfers between devices, across(): return lax.ppermute(piece, 'req', beside)  5.01 us
    ppermute x1, waiting for transfers between devices, team_local(): lax.ppermute(far[1], ('cfg', 'seq'), diagonal)  4.42 us
  transfers between devices with their start and end apart: 25, of which 12 were waited for; matrix products, arithmetic and copies ran while one was open for 0% of the time, Pallas kernels for 16%

profile of v8, /device:TPU:0, one launch (start us, length us, event | category | flops | bytes accessed | tf_op | source)
XLA Modules:
  0.0 99.4 jit_solution(11818007290829107887)
XLA Ops:
  0.0 3.2 %shard_map.109 = (bf16[192,1536]{1,0:T(8,128)(2,1)}, bf16[288,1536]{1,0:T(8,128)(2,1)}) custom-call(bf16[192,4608]{1,0:T(8,128)(2,1)} %qkv_ref.1, bf16[192,1536]{1,0:T(8,128)(2,1)} %w_out_ref.1, bf16[288,1536]{1,0:T(8,128)(2,1)} %bitcast.20, f32[5,1,1536]{2,1,0:T(1,128)} %bitcast.18), custom_call_target="tpu_custom_call" | custom-call | flops 4000000000 | bytes 1000000 | tf_op jit(solution)/shard_map/pallas_call | solution.py:194
  3.2 3.0 %collective-permute-start = (bf16[288,1536]{1,0:T(8,128)(2,1)}, bf16[288,1536]{1,0:T(8,128)(2,1)S(1)}, u32[]{:S(2)}, u32[]{:S(2)}) collective-permute-start(bf16[288,1536]{1,0:T(8,128)(2,1)} %get-tuple-element.27.refs_0_), channel_id=1, source_target_pairs={{0,1},{1,0},{2,3},{3,2},{4,5},{5,4},{6,7},{7,6},{8,9},{9,8},{10,11... | collective-permute-start | bytes 2654216 | tf_op jit(solution)/shard_map/ppermute | solution.py:557
  6.2 1.5 %collective-permute-start.3 = (bf16[192,1536]{1,0:T(8,128)(2,1)}, bf16[192,1536]{1,0:T(8,128)(2,1)S(1)}, u32[]{:S(2)}, u32[]{:S(2)}) collective-permute-start(bf16[192,1536]{1,0:T(8,128)(2,1)} %get-tuple-element.28.refs_4_.refs_0_), channel_id=1, source_target_pairs={{0,2},{2,0},{4,6},{6,4},{8,10},{10,8},{12,14},{14,12},{1,3},{3,1},... | collective-permute-start | bytes 1769480 | tf_op jit(solution)/shard_map/ppermute | solution.py:553
  7.7 2.6 %collective-permute-start.4 = (bf16[192,1536]{1,0:T(8,128)(2,1)}, bf16[192,1536]{1,0:T(8,128)(2,1)S(1)}, u32[]{:S(2)}, u32[]{:S(2)}) collective-permute-start(bf16[192,1536]{1,0:T(8,128)(2,1)} %get-tuple-element.28.refs_4_.refs_0_), channel_id=1, source_target_pairs={{0,8},{2,10},{4,0},{6,2},{12,4},{14,6},{8,12},{10,14},{1,9},{3,11}... | collective-permute-start | bytes 1769480 | tf_op jit(solution)/shard_map/ppermute | solution.py:547
  10.4 10.8 %collective-permute-done.3.refs_5_.refs_1_ = bf16[192,1536]{1,0:T(8,128)(2,1)S(1)} collective-permute-done((bf16[192,1536]{1,0:T(8,128)(2,1)}, bf16[192,1536]{1,0:T(8,128)(2,1)S(1)}, u32[]{:S(2)}, u32[]{:S(2)}) %collective-permute-start.3) | collective-permute-done | bytes 589856 | tf_op jit(solution)/shard_map/ppermute | solution.py:553
  21.3 1.4 %collective-permute-done.4.refs_6_.refs_2_ = bf16[192,1536]{1,0:T(8,128)(2,1)S(1)} collective-permute-done((bf16[192,1536]{1,0:T(8,128)(2,1)}, bf16[192,1536]{1,0:T(8,128)(2,1)S(1)}, u32[]{:S(2)}, u32[]{:S(2)}) %collective-permute-start.4) | collective-permute-done | bytes 589856 | tf_op jit(solution)/shard_map/ppermute | solution.py:547
  22.6 0.5 collective-permute-start.5
  23.2 3.3 %collective-permute-start.6 = (bf16[192,1536]{1,0:T(8,128)(2,1)S(1)}, bf16[192,1536]{1,0:T(8,128)(2,1)S(1)}, u32[]{:S(2)}, u32[]{:S(2)}) collective-permute-start(bf16[192,1536]{1,0:T(8,128)(2,1)S(1)} %collective-permute-done.4.refs_6_.refs_2_), channel_id=1, source_target_pairs={{0,8},{2,10},{4,0},{6,2},{12,4},{14,6},{8,12},{10,14},{1,9},{3,11}... | collective-permute-start | bytes 1769480 | tf_op jit(solution)/shard_map/ppermute | solution.py:547
  26.4 0.0 collective-permute-start.1
  26.4 0.0 collective-permute-done.refs_1_
  26.5 0.5 collective-permute-start.2
  27.0 9.3 %collective-permute-done.5.refs_7_.refs_3_ = bf16[192,1536]{1,0:T(8,128)(2,1)S(1)} collective-permute-done((bf16[192,1536]{1,0:T(8,128)(2,1)S(1)}, bf16[192,1536]{1,0:T(8,128)(2,1)S(1)}, u32[]{:S(2)}, u32[]{:S(2)}) %collective-permute-start.5) | collective-permute-done | bytes 589856 | tf_op jit(solution)/shard_map/ppermute | solution.py:553
  36.2 1.0 %collective-permute-done.6.refs_6_.refs_5_.refs_4_ = bf16[192,1536]{1,0:T(8,128)(2,1)S(1)} collective-permute-done((bf16[192,1536]{1,0:T(8,128)(2,1)S(1)}, bf16[192,1536]{1,0:T(8,128)(2,1)S(1)}, u32[]{:S(2)}, u32[]{:S(2)}) %collective-permute-start.6) | collective-permute-done | bytes 589856 | tf_op jit(solution)/shard_map/ppermute | solution.py:547
  37.3 1.1 %copy-done.1 = bf16[192,1536]{1,0:T(8,128)(2,1)S(1)} copy-done((bf16[192,1536]{1,0:T(8,128)(2,1)S(1)}, bf16[192,1536]{1,0:T(8,128)(2,1)}, u32[]{:S(2)}) %copy-start.1) | copy-done | bytes 589848
  38.3 0.4 shard_map.113.refs_4_
  38.8 0.6 collective-permute-start.13
  39.3 3.4 %collective-permute-start.8 = (bf16[192,1536]{1,0:T(8,128)(2,1)S(1)}, bf16[192,1536]{1,0:T(8,128)(2,1)S(1)}, u32[]{:S(2)}, u32[]{:S(2)}) collective-permute-start(bf16[192,1536]{1,0:T(8,128)(2,1)S(1)} %collective-permute-done.6.refs_6_.refs_5_.refs_4_), channel_id=1, source_target_pairs={{0,8},{2,10},{4,0},{6,2},{12,4},{14,6},{8,12},{10,14},{1,9},{3,11}... | collective-permute-start | bytes 1769480 | tf_op jit(solution)/shard_map/ppermute | solution.py:547
  42.7 1.5 %collective-permute-start.7 = (bf16[192,1536]{1,0:T(8,128)(2,1)S(1)}, bf16[192,1536]{1,0:T(8,128)(2,1)S(1)}, u32[]{:S(2)}, u32[]{:S(2)}) collective-permute-start(bf16[192,1536]{1,0:T(8,128)(2,1)S(1)} %collective-permute-done.6.refs_6_.refs_5_.refs_4_), channel_id=1, source_target_pairs={{0,2},{2,0},{4,6},{6,4},{8,10},{10,8},{12,14},{14,12},{1,3},{3,1},... | collective-permute-start | bytes 1769480 | tf_op jit(solution)/shard_map/ppermute | solution.py:553
  44.9 0.0 collective-permute-done.1.refs_2_
  44.9 0.1 collective-permute-start.12
  45.0 0.0 collective-permute-done.2.refs_3_
  45.0 0.1 collective-permute-start.9
  45.0 2.6 %shard_map.110 = (bf16[4,288,768]{2,1,0:T(8,128)(2,1)S(1)}, bf16[4,288,384]{2,1,0:T(8,128)(2,1)S(1)}) custom-call(bf16[288,1536]{1,0:T(8,128)(2,1)S(1)} %copy-done, bf16[288,1536]{1,0:T(8,128)(2,1)S(1)} %collective-permute-done.refs_1_, bf16[288,1536]{1,0:T(8,128)(2,1)S(1)} %collective-permute-done.1.refs_2_, ...), custom_call_target="tpu_custom_call" | custom-call | flops 6000000000 | bytes 1000000 | tf_op jit(solution)/shard_map/pallas_call | solution.py:270
  47.7 6.3 %collective-permute-done.8.refs_8_.refs_7_.refs_1_ = bf16[192,1536]{1,0:T(8,128)(2,1)S(1)} collective-permute-done((bf16[192,1536]{1,0:T(8,128)(2,1)S(1)}, bf16[192,1536]{1,0:T(8,128)(2,1)S(1)}, u32[]{:S(2)}, u32[]{:S(2)}) %collective-permute-start.8) | collective-permute-done | bytes 589856 | tf_op jit(solution)/shard_map/ppermute | solution.py:547
  54.0 3.4 %collective-permute-done.9.refs_2_ = bf16[192,384]{1,0:T(8,128)(2,1)S(1)} collective-permute-done((bf16[192,384]{1,0:T(8,128)(2,1)S(1)}, bf16[192,384]{1,0:T(8,128)(2,1)S(1)}, u32[]{:S(2)}, u32[]{:S(2)}) %collective-permute-start.9) | collective-permute-done | bytes 147488 | tf_op jit(solution)/shard_map/ppermute | solution.py:550
  57.3 0.0 collective-permute-done.7.refs_7_.refs_6_.refs_0_
  57.4 1.5 %collective-permute-start.10 = (bf16[112,1152]{1,0:T(8,128)(2,1)S(1)}, bf16[112,1152]{1,0:T(8,128)(2,1)S(1)}, u32[]{:S(2)}, u32[]{:S(2)}) collective-permute-start(bf16[112,1152]{1,0:T(8,128)(2,1)S(1)} %slice.14), channel_id=1, source_target_pairs={{0,2},{2,0},{4,6},{6,4},{8,10},{10,8},{12,14},{14,12},{1,3},{3,1},... | collective-permute-start | bytes 774152 | tf_op jit(solution)/shard_map/ppermute | solution.py:553
  58.8 0.7 collective-permute-start.11
  59.5 0.0 collective-permute-done.13.refs_6_
  59.5 0.5 shard_map.115.refs_8_
  60.0 1.6 %collective-permute-start.18 = (bf16[576,384]{1,0:T(8,128)(2,1)S(1)}, bf16[576,384]{1,0:T(8,128)(2,1)S(1)}, u32[]{:S(2)}, u32[]{:S(2)}) collective-permute-start(bf16[576,384]{1,0:T(8,128)(2,1)S(1)} %shard_map.115.refs_8_), channel_id=1, source_target_pairs={{0,1},{1,0},{2,3},{3,2},{4,5},{5,4},{6,7},{7,6},{8,9},{9,8},{10,11... | collective-permute-start | bytes 1327112 | tf_op jit(solution)/shard_map/ppermute | solution.py:586
  61.6 0.0 collective-permute-start.14
  61.6 4.4 %collective-permute-done.11.refs_10_.refs_9_ = bf16[80,1152]{1,0:T(8,128)(2,1)S(1)} collective-permute-done((bf16[80,1152]{1,0:T(8,128)(2,1)S(1)}, bf16[80,1152]{1,0:T(8,128)(2,1)S(1)}, u32[]{:S(2)}, u32[]{:S(2)}) %collective-permute-start.11) | collective-permute-done | bytes 184352 | tf_op jit(solution)/shard_map/ppermute | solution.py:550
  66.1 0.0 collective-permute-done.10.refs_9_.refs_8_
  66.1 2.9 %shard_map.111 = (bf16[4,288,768]{2,1,0:T(8,128)(2,1)S(1)}, f32[4,8,288]{2,1,0:T(8,128)S(1)}) custom-call(bf16[288,1536]{1,0:T(8,128)(2,1)S(1)} %copy-done, bf16[288,1536]{1,0:T(8,128)(2,1)S(1)} %collective-permute-done.refs_1_, bf16[288,1536]{1,0:T(8,128)(2,1)S(1)} %collective-permute-done.1.refs_2_, bf16[288,1536]{1,0:T(8,128)(2,1)S(1)} %collective-permute-done.2.refs_3_, ...), custom_call_target="tpu_custom_call" | custom-call | flops 6000000000 | bytes 1000000 | tf_op jit(solution)/shard_map/pallas_call | solution.py:317
  69.0 1.6 %collective-permute-start.15 = (f32[4,8,288]{2,1,0:T(8,128)S(1)}, f32[4,8,288]{2,1,0:T(8,128)S(1)}, u32[]{:S(2)}, u32[]{:S(2)}) collective-permute-start(f32[4,8,288]{2,1,0:T(8,128)S(1)} %get-tuple-element.38.s0_ref), channel_id=1, source_target_pairs={{0,1},{1,0},{2,3},{3,2},{4,5},{5,4},{6,7},{7,6},{8,9},{9,8},{10,11... | collective-permute-start | bytes 110600 | tf_op jit(solution)/shard_map/ppermute | solution.py:595
  70.6 0.0 collective-permute-start.16
  70.6 0.0 collective-permute-done.12.refs_5_
  70.6 0.6 collective-permute-start.17
  71.2 1.2 %shard_map.112.v_ref = bf16[4,288,384]{2,1,0:T(8,128)(2,1)S(1)} custom-call(bf16[288,1536]{1,0:T(8,128)(2,1)S(1)} %copy-done, bf16[288,1536]{1,0:T(8,128)(2,1)S(1)} %collective-permute-done.refs_1_, bf16[288,1536]{1,0:T(8,128)(2,1)S(1)} %collective-permute-done.1.refs_2_, bf16[288,1536]{1,0:T(8,128)(2,1)S(1)} %collective-permute-done.2.refs_3_, ...), custom_call_target="tpu_custom_call" | custom-call | flops 4000000000 | bytes 1000000 | tf_op jit(solution)/shard_map/pallas_call | solution.py:349
  72.4 0.0 collective-permute-done.18.refs_10_
  72.4 0.1 collective-permute-start.19
  72.6 0.0 collective-permute-done.14.refs_7_
  72.6 0.4 collective-permute-start.23
  73.0 0.1 collective-permute-done.15.s1_ref
  73.1 0.0 collective-permute-done.16.s2_ref
  73.1 1.0 %collective-permute-done.17.s3_ref = f32[4,8,288]{2,1,0:T(8,128)S(1)} collective-permute-done((f32[4,8,288]{2,1,0:T(8,128)S(1)}, f32[4,8,288]{2,1,0:T(8,128)S(1)}, u32[]{:S(2)}, u32[]{:S(2)}) %collective-permute-start.17) | collective-permute-done | bytes 36896 | tf_op jit(solution)/shard_map/ppermute | solution.py:597
  74.2 4.3 %shard_map.114 = (bf16[288,384]{1,0:T(8,128)(2,1)S(1)}, bf16[288,384]{1,0:T(8,128)(2,1)S(1)}) custom-call(s32[1]{0:T(128)} %copy.12.length_ref, bf16[4,288,768]{2,1,0:T(8,128)(2,1)S(1)} %get-tuple-element.43.qk_ref, bf16[4,288,384]{2,1,0:T(8,128)(2,1)S(1)} %shard_map.112.v_ref, f32[4,8,288]{2,1,0:T(8,128)S(1)} %get-tuple-element.38.s0_ref, ...), custom_call_target="tpu_custom_call" | custom-call | flops 6000000000 | bytes 1000000 | tf_op jit(solution)/shard_map/pallas_call | solution.py:441
  78.5 0.0 copy-start.3
  78.5 0.0 collective-permute-done.19.refs_9_
  78.5 1.1 %collective-permute-start.21 = (bf16[288,384]{1,0:T(8,128)(2,1)S(1)}, bf16[288,384]{1,0:T(8,128)(2,1)S(1)}, u32[]{:S(2)}, u32[]{:S(2)}) collective-permute-start(bf16[288,384]{1,0:T(8,128)(2,1)S(1)} %get-tuple-element.42), channel_id=1, source_target_pairs={{0,1},{1,0},{2,3},{3,2},{4,5},{5,4},{6,7},{7,6},{8,9},{9,8},{10,11... | collective-permute-start | bytes 663560 | tf_op jit(solution)/shard_map/ppermute | solution.py:606
  79.6 3.7 %shard_map.116 = (bf16[288,384]{1,0:T(8,128)(2,1)}, bf16[288,384]{1,0:T(8,128)(2,1)S(1)}) custom-call(s32[1]{0:T(128)} %copy.12.length_ref, bf16[4,288,768]{2,1,0:T(8,128)(2,1)S(1)} %get-tuple-element.43.qk_ref, bf16[4,288,384]{2,1,0:T(8,128)(2,1)S(1)} %shard_map.112.v_ref, f32[4,8,288]{2,1,0:T(8,128)S(1)} %get-tuple-element.38.s0_ref, ...), custom_call_target="tpu_custom_call" | custom-call | flops 1000000 | bytes 1000000 | tf_op jit(solution)/shard_map/pallas_call | solution.py:441
  83.3 0.1 collective-permute-start.20
  83.5 1.0 %collective-permute-start.22 = (bf16[288,384]{1,0:T(8,128)(2,1)S(1)}, bf16[288,384]{1,0:T(8,128)(2,1)}, u32[]{:S(2)}, u32[]{:S(2)}) collective-permute-start(bf16[288,384]{1,0:T(8,128)(2,1)S(1)} %get-tuple-element.46), channel_id=1, source_target_pairs={{0,17},{1,16},{16,1},{17,0},{2,19},{3,18},{18,3},{19,2},{4,21},{5,... | collective-permute-start | bytes 663560 | tf_op jit(solution)/shard_map/ppermute | solution.py:607
  84.5 0.0 collective-permute-done.23.refs_11_
  84.5 0.7 collective-permute-done.20.refs_1_
  85.2 1.1 %collective-permute-done.21.refs_2_ = bf16[288,384]{1,0:T(8,128)(2,1)S(1)} collective-permute-done((bf16[288,384]{1,0:T(8,128)(2,1)S(1)}, bf16[288,384]{1,0:T(8,128)(2,1)S(1)}, u32[]{:S(2)}, u32[]{:S(2)}) %collective-permute-start.21) | collective-permute-done | bytes 221216 | tf_op jit(solution)/shard_map/ppermute | solution.py:606
  86.3 4.4 %collective-permute-done.22.refs_3_ = bf16[288,384]{1,0:T(8,128)(2,1)} collective-permute-done((bf16[288,384]{1,0:T(8,128)(2,1)S(1)}, bf16[288,384]{1,0:T(8,128)(2,1)}, u32[]{:S(2)}, u32[]{:S(2)}) %collective-permute-start.22) | collective-permute-done | bytes 221216 | tf_op jit(solution)/shard_map/ppermute | solution.py:607
  90.8 0.9 copy-done.2
  91.7 5.2 %shard_map.117 = (f32[32,288]{1,0:T(8,128)S(1)}, bf16[32,288]{1,0:T(8,128)(2,1)S(1)}) custom-call(bf16[288,1536]{1,0:T(8,128)(2,1)} %bitcast.21, f32[5,1,1536]{2,1,0:T(1,128)S(1)} %bitcast.19, bf16[64,1536]{1,0:T(8,128)(2,1)S(1)} %bitcast.17, bf16[288,384]{1,0:T(8,128)(2,1)S(1)} %get-tuple-element.44.refs_0_, ...), custom_call_target="tpu_custom_call" | custom-call | flops 8000000000 | bytes 1000000 | tf_op jit(solution)/shard_map/pallas_call | solution.py:495
  96.9 0.5 collective-permute-start.24
  98.7 0.0 collective-permute-done.24
  98.7 0.0 copy-done.4
  98.7 0.6 fusion.4
  (24 shorter events, 0.1 us)
Async XLA Ops:
  0.0 10.3 %copy-start.5 = (f32[1536]{0:T(1024)S(1)}, f32[1536]{0:T(1024)}, u32[]{:S(2)}) copy-start(f32[1536]{0:T(1024)} %param.17) | copy-start | bytes 18436
  0.0 10.3 %copy-start.6 = (f32[1536]{0:T(1024)S(1)}, f32[1536]{0:T(1024)}, u32[]{:S(2)}) copy-start(f32[1536]{0:T(1024)} %param.16) | copy-start | bytes 18436
  3.2 23.3 %collective-permute-start = (bf16[288,1536]{1,0:T(8,128)(2,1)}, bf16[288,1536]{1,0:T(8,128)(2,1)S(1)}, u32[]{:S(2)}, u32[]{:S(2)}) collective-permute-start(bf16[288,1536]{1,0:T(8,128)(2,1)} %get-tuple-element.27.refs_0_), channel_id=1, source_target_pairs={{0,1},{1,0},{2,3},{3,2},{4,5},{5,4},{6,7},{7,6},{8,9},{9,8},{10,11... | collective-permute-start | bytes 2654216 | tf_op jit(solution)/shard_map/ppermute | solution.py:557
  6.2 15.0 %collective-permute-start.3 = (bf16[192,1536]{1,0:T(8,128)(2,1)}, bf16[192,1536]{1,0:T(8,128)(2,1)S(1)}, u32[]{:S(2)}, u32[]{:S(2)}) collective-permute-start(bf16[192,1536]{1,0:T(8,128)(2,1)} %get-tuple-element.28.refs_4_.refs_0_), channel_id=1, source_target_pairs={{0,2},{2,0},{4,6},{6,4},{8,10},{10,8},{12,14},{14,12},{1,3},{3,1},... | collective-permute-start | bytes 1769480 | tf_op jit(solution)/shard_map/ppermute | solution.py:553
  7.7 14.9 %collective-permute-start.4 = (bf16[192,1536]{1,0:T(8,128)(2,1)}, bf16[192,1536]{1,0:T(8,128)(2,1)S(1)}, u32[]{:S(2)}, u32[]{:S(2)}) collective-permute-start(bf16[192,1536]{1,0:T(8,128)(2,1)} %get-tuple-element.28.refs_4_.refs_0_), channel_id=1, source_target_pairs={{0,8},{2,10},{4,0},{6,2},{12,4},{14,6},{8,12},{10,14},{1,9},{3,11}... | collective-permute-start | bytes 1769480 | tf_op jit(solution)/shard_map/ppermute | solution.py:547
  21.2 23.8 %copy-start = (bf16[288,1536]{1,0:T(8,128)(2,1)S(1)}, bf16[288,1536]{1,0:T(8,128)(2,1)}, u32[]{:S(2)}) copy-start(bf16[288,1536]{1,0:T(8,128)(2,1)} %get-tuple-element.27.refs_0_) | copy-start | bytes 2654212
  22.6 13.6 %collective-permute-start.5 = (bf16[192,1536]{1,0:T(8,128)(2,1)S(1)}, bf16[192,1536]{1,0:T(8,128)(2,1)S(1)}, u32[]{:S(2)}, u32[]{:S(2)}) collective-permute-start(bf16[192,1536]{1,0:T(8,128)(2,1)S(1)} %collective-permute-done.4.refs_6_.refs_2_), channel_id=1, source_target_pairs={{0,2},{2,0},{4,6},{6,4},{8,10},{10,8},{12,14},{14,12},{1,3},{3,1},... | collective-permute-start | bytes 1769480 | tf_op jit(solution)/shard_map/ppermute | solution.py:553
  23.2 14.1 %collective-permute-start.6 = (bf16[192,1536]{1,0:T(8,128)(2,1)S(1)}, bf16[192,1536]{1,0:T(8,128)(2,1)S(1)}, u32[]{:S(2)}, u32[]{:S(2)}) collective-permute-start(bf16[192,1536]{1,0:T(8,128)(2,1)S(1)} %collective-permute-done.4.refs_6_.refs_2_), channel_id=1, source_target_pairs={{0,8},{2,10},{4,0},{6,2},{12,4},{14,6},{8,12},{10,14},{1,9},{3,11}... | collective-permute-start | bytes 1769480 | tf_op jit(solution)/shard_map/ppermute | solution.py:547
  26.4 18.4 %collective-permute-start.1 = (bf16[288,1536]{1,0:T(8,128)(2,1)}, bf16[288,1536]{1,0:T(8,128)(2,1)S(1)}, u32[]{:S(2)}, u32[]{:S(2)}) collective-permute-start(bf16[288,1536]{1,0:T(8,128)(2,1)} %get-tuple-element.27.refs_0_), channel_id=1, source_target_pairs={{0,16},{16,0},{1,17},{17,1},{2,18},{18,2},{3,19},{19,3},{4,20},{20... | collective-permute-start | bytes 2654216 | tf_op jit(solution)/shard_map/ppermute | solution.py:558
  26.5 18.5 %collective-permute-start.2 = (bf16[288,1536]{1,0:T(8,128)(2,1)S(1)}, bf16[288,1536]{1,0:T(8,128)(2,1)S(1)}, u32[]{:S(2)}, u32[]{:S(2)}) collective-permute-start(bf16[288,1536]{1,0:T(8,128)(2,1)S(1)} %collective-permute-done.refs_1_), channel_id=1, source_target_pairs={{0,16},{16,0},{1,17},{17,1},{2,18},{18,2},{3,19},{19,3},{4,20},{20... | collective-permute-start | bytes 2654216 | tf_op jit(solution)/shard_map/ppermute | solution.py:577
  37.3 1.1 %copy-start.1 = (bf16[192,1536]{1,0:T(8,128)(2,1)S(1)}, bf16[192,1536]{1,0:T(8,128)(2,1)}, u32[]{:S(2)}) copy-start(bf16[192,1536]{1,0:T(8,128)(2,1)} %get-tuple-element.28.refs_4_.refs_0_) | copy-start | bytes 1769476
  38.8 20.8 %collective-permute-start.13 = (bf16[960,384]{1,0:T(8,128)(2,1)S(1)}, bf16[960,384]{1,0:T(8,128)(2,1)S(1)}, u32[]{:S(2)}, u32[]{:S(2)}) collective-permute-start(bf16[960,384]{1,0:T(8,128)(2,1)S(1)} %shard_map.113.refs_4_), channel_id=1, source_target_pairs={{0,1},{1,0},{2,3},{3,2},{4,5},{5,4},{6,7},{7,6},{8,9},{9,8},{10,11... | collective-permute-start | bytes 2211848 | tf_op jit(solution)/shard_map/ppermute | solution.py:579
  39.3 14.6 %collective-permute-start.8 = (bf16[192,1536]{1,0:T(8,128)(2,1)S(1)}, bf16[192,1536]{1,0:T(8,128)(2,1)S(1)}, u32[]{:S(2)}, u32[]{:S(2)}) collective-permute-start(bf16[192,1536]{1,0:T(8,128)(2,1)S(1)} %collective-permute-done.6.refs_6_.refs_5_.refs_4_), channel_id=1, source_target_pairs={{0,8},{2,10},{4,0},{6,2},{12,4},{14,6},{8,12},{10,14},{1,9},{3,11}... | collective-permute-start | bytes 1769480 | tf_op jit(solution)/shard_map/ppermute | solution.py:547
  42.7 14.6 %collective-permute-start.7 = (bf16[192,1536]{1,0:T(8,128)(2,1)S(1)}, bf16[192,1536]{1,0:T(8,128)(2,1)S(1)}, u32[]{:S(2)}, u32[]{:S(2)}) collective-permute-start(bf16[192,1536]{1,0:T(8,128)(2,1)S(1)} %collective-permute-done.6.refs_6_.refs_5_.refs_4_), channel_id=1, source_target_pairs={{0,2},{2,0},{4,6},{6,4},{8,10},{10,8},{12,14},{14,12},{1,3},{3,1},... | collective-permute-start | bytes 1769480 | tf_op jit(solution)/shard_map/ppermute | solution.py:553
  44.9 25.7 %collective-permute-start.12 = (bf16[960,384]{1,0:T(8,128)(2,1)S(1)}, bf16[960,384]{1,0:T(8,128)(2,1)S(1)}, u32[]{:S(2)}, u32[]{:S(2)}) collective-permute-start(bf16[960,384]{1,0:T(8,128)(2,1)S(1)} %shard_map.113.refs_4_), channel_id=1, source_target_pairs={{0,16},{16,0},{1,17},{17,1},{2,18},{18,2},{3,19},{19,3},{4,20},{20... | collective-permute-start | bytes 2211848 | tf_op jit(solution)/shard_map/ppermute | solution.py:587
  45.0 12.4 %collective-permute-start.9 = (bf16[192,384]{1,0:T(8,128)(2,1)S(1)}, bf16[192,384]{1,0:T(8,128)(2,1)S(1)}, u32[]{:S(2)}, u32[]{:S(2)}) collective-permute-start(bf16[192,384]{1,0:T(8,128)(2,1)S(1)} %slice.13), channel_id=1, source_target_pairs={{8,0},{10,2},{0,4},{2,6},{4,12},{6,14},{12,8},{14,10},{9,1},{11,3}... | collective-permute-start | bytes 442376 | tf_op jit(solution)/shard_map/ppermute | solution.py:550
  57.4 8.7 %collective-permute-start.10 = (bf16[112,1152]{1,0:T(8,128)(2,1)S(1)}, bf16[112,1152]{1,0:T(8,128)(2,1)S(1)}, u32[]{:S(2)}, u32[]{:S(2)}) collective-permute-start(bf16[112,1152]{1,0:T(8,128)(2,1)S(1)} %slice.14), channel_id=1, source_target_pairs={{0,2},{2,0},{4,6},{6,4},{8,10},{10,8},{12,14},{14,12},{1,3},{3,1},... | collective-permute-start | bytes 774152 | tf_op jit(solution)/shard_map/ppermute | solution.py:553
  58.8 7.2 %collective-permute-start.11 = (bf16[80,1152]{1,0:T(8,128)(2,1)S(1)}, bf16[80,1152]{1,0:T(8,128)(2,1)S(1)}, u32[]{:S(2)}, u32[]{:S(2)}) collective-permute-start(bf16[80,1152]{1,0:T(8,128)(2,1)S(1)} %slice.12), channel_id=1, source_target_pairs={{8,0},{10,2},{0,4},{2,6},{4,12},{6,14},{12,8},{14,10},{9,1},{11,3}... | collective-permute-start | bytes 552968 | tf_op jit(solution)/shard_map/ppermute | solution.py:550
  59.5 2.1 %copy-start.7 = (bf16[960,384]{1,0:T(8,128)(2,1)}, bf16[960,384]{1,0:T(8,128)(2,1)S(1)}, u32[]{:S(2)}) copy-start(bf16[960,384]{1,0:T(8,128)(2,1)S(1)} %collective-permute-done.13.refs_6_) | copy-start | bytes 2211844
  60.0 12.4 %collective-permute-start.18 = (bf16[576,384]{1,0:T(8,128)(2,1)S(1)}, bf16[576,384]{1,0:T(8,128)(2,1)S(1)}, u32[]{:S(2)}, u32[]{:S(2)}) collective-permute-start(bf16[576,384]{1,0:T(8,128)(2,1)S(1)} %shard_map.115.refs_8_), channel_id=1, source_target_pairs={{0,1},{1,0},{2,3},{3,2},{4,5},{5,4},{6,7},{7,6},{8,9},{9,8},{10,11... | collective-permute-start | bytes 1327112 | tf_op jit(solution)/shard_map/ppermute | solution.py:586
  61.6 10.9 %collective-permute-start.14 = (bf16[960,384]{1,0:T(8,128)(2,1)S(1)}, bf16[960,384]{1,0:T(8,128)(2,1)S(1)}, u32[]{:S(2)}, u32[]{:S(2)}) collective-permute-start(bf16[960,384]{1,0:T(8,128)(2,1)S(1)} %collective-permute-done.13.refs_6_), channel_id=1, source_target_pairs={{0,16},{16,0},{1,17},{17,1},{2,18},{18,2},{3,19},{19,3},{4,20},{20... | collective-permute-start | bytes 2211848 | tf_op jit(solution)/shard_map/ppermute | solution.py:588
  69.0 4.2 %collective-permute-start.15 = (f32[4,8,288]{2,1,0:T(8,128)S(1)}, f32[4,8,288]{2,1,0:T(8,128)S(1)}, u32[]{:S(2)}, u32[]{:S(2)}) collective-permute-start(f32[4,8,288]{2,1,0:T(8,128)S(1)} %get-tuple-element.38.s0_ref), channel_id=1, source_target_pairs={{0,1},{1,0},{2,3},{3,2},{4,5},{5,4},{6,7},{7,6},{8,9},{9,8},{10,11... | collective-permute-start | bytes 110600 | tf_op jit(solution)/shard_map/ppermute | solution.py:595
  70.6 2.6 %collective-permute-start.16 = (f32[4,8,288]{2,1,0:T(8,128)S(1)}, f32[4,8,288]{2,1,0:T(8,128)S(1)}, u32[]{:S(2)}, u32[]{:S(2)}) collective-permute-start(f32[4,8,288]{2,1,0:T(8,128)S(1)} %get-tuple-element.38.s0_ref), channel_id=1, source_target_pairs={{0,16},{16,0},{1,17},{17,1},{2,18},{18,2},{3,19},{19,3},{4,20},{20... | collective-permute-start | bytes 110600 | tf_op jit(solution)/shard_map/ppermute | solution.py:596
  70.6 1.8 %copy-start.8 = (bf16[960,384]{1,0:T(8,128)(2,1)}, bf16[960,384]{1,0:T(8,128)(2,1)S(1)}, u32[]{:S(2)}) copy-start(bf16[960,384]{1,0:T(8,128)(2,1)S(1)} %collective-permute-done.12.refs_5_) | copy-start | bytes 2211844
  70.6 3.6 %collective-permute-start.17 = (f32[4,8,288]{2,1,0:T(8,128)S(1)}, f32[4,8,288]{2,1,0:T(8,128)S(1)}, u32[]{:S(2)}, u32[]{:S(2)}) collective-permute-start(f32[4,8,288]{2,1,0:T(8,128)S(1)} %get-tuple-element.38.s0_ref), channel_id=1, source_target_pairs={{0,17},{1,16},{16,1},{17,0},{2,19},{3,18},{18,3},{19,2},{4,21},{5,... | collective-permute-start | bytes 110600 | tf_op jit(solution)/shard_map/ppermute | solution.py:597
  72.4 6.0 %collective-permute-start.19 = (bf16[576,384]{1,0:T(8,128)(2,1)S(1)}, bf16[576,384]{1,0:T(8,128)(2,1)S(1)}, u32[]{:S(2)}, u32[]{:S(2)}) collective-permute-start(bf16[576,384]{1,0:T(8,128)(2,1)S(1)} %shard_map.115.refs_8_), channel_id=1, source_target_pairs={{0,16},{16,0},{1,17},{17,1},{2,18},{18,2},{3,19},{19,3},{4,20},{20... | collective-permute-start | bytes 1327112 | tf_op jit(solution)/shard_map/ppermute | solution.py:587
  72.6 5.9 %copy-start.9 = (bf16[960,384]{1,0:T(8,128)(2,1)}, bf16[960,384]{1,0:T(8,128)(2,1)S(1)}, u32[]{:S(2)}) copy-start(bf16[960,384]{1,0:T(8,128)(2,1)S(1)} %collective-permute-done.14.refs_7_) | copy-start | bytes 2211844
  72.6 11.9 %collective-permute-start.23 = (bf16[576,384]{1,0:T(8,128)(2,1)S(1)}, bf16[576,384]{1,0:T(8,128)(2,1)S(1)}, u32[]{:S(2)}, u32[]{:S(2)}) collective-permute-start(bf16[576,384]{1,0:T(8,128)(2,1)S(1)} %collective-permute-done.18.refs_10_), channel_id=1, source_target_pairs={{0,16},{16,0},{1,17},{17,1},{2,18},{18,2},{3,19},{19,3},{4,20},{20... | collective-permute-start | bytes 1327112 | tf_op jit(solution)/shard_map/ppermute | solution.py:588
  78.5 12.3 %copy-start.3 = (f32[1,5,1536]{2,0,1:T(1,128)S(1)}, f32[1,5,1536]{2,0,1:T(1,128)}, u32[]{:S(2)}) copy-start(f32[1,5,1536]{2,0,1:T(1,128)} %param.13) | copy-start | bytes 92164
  78.5 7.8 %collective-permute-start.21 = (bf16[288,384]{1,0:T(8,128)(2,1)S(1)}, bf16[288,384]{1,0:T(8,128)(2,1)S(1)}, u32[]{:S(2)}, u32[]{:S(2)}) collective-permute-start(bf16[288,384]{1,0:T(8,128)(2,1)S(1)} %get-tuple-element.42), channel_id=1, source_target_pairs={{0,1},{1,0},{2,3},{3,2},{4,5},{5,4},{6,7},{7,6},{8,9},{9,8},{10,11... | collective-permute-start | bytes 663560 | tf_op jit(solution)/shard_map/ppermute | solution.py:606
  83.3 1.9 %collective-permute-start.20 = (bf16[288,384]{1,0:T(8,128)(2,1)}, bf16[288,384]{1,0:T(8,128)(2,1)}, u32[]{:S(2)}, u32[]{:S(2)}) collective-permute-start(bf16[288,384]{1,0:T(8,128)(2,1)} %get-tuple-element.45), channel_id=1, source_target_pairs={{0,16},{16,0},{1,17},{17,1},{2,18},{18,2},{3,19},{19,3},{4,20},{20... | collective-permute-start | bytes 663560 | tf_op jit(solution)/shard_map/ppermute | solution.py:605
  83.5 7.3 %collective-permute-start.22 = (bf16[288,384]{1,0:T(8,128)(2,1)S(1)}, bf16[288,384]{1,0:T(8,128)(2,1)}, u32[]{:S(2)}, u32[]{:S(2)}) collective-permute-start(bf16[288,384]{1,0:T(8,128)(2,1)S(1)} %get-tuple-element.46), channel_id=1, source_target_pairs={{0,17},{1,16},{16,1},{17,0},{2,19},{3,18},{18,3},{19,2},{4,21},{5,... | collective-permute-start | bytes 663560 | tf_op jit(solution)/shard_map/ppermute | solution.py:607
  90.7 0.9 copy-start.2
  91.7 7.0 %copy-start.4 = (f32[1,288,32]{1,2,0:T(8,128)S(1)}, f32[1,288,32]{1,2,0:T(8,128)}, u32[]{:S(2)}) copy-start(f32[1,288,32]{1,2,0:T(8,128)} %param.12) | copy-start | bytes 110596
  96.9 1.8 %collective-permute-start.24 = (bf16[32,288]{1,0:T(8,128)(2,1)S(1)}, bf16[32,288]{1,0:T(8,128)(2,1)S(1)}, u32[]{:S(2)}, u32[]{:S(2)}) collective-permute-start(bf16[32,288]{1,0:T(8,128)(2,1)S(1)} %get-tuple-element.47), channel_id=1, source_target_pairs={{0,16},{16,0},{1,17},{17,1},{2,18},{18,2},{3,19},{19,3},{4,20},{20... | collective-permute-start | bytes 55304 | tf_op jit(solution)/shard_map/ppermute | solution.py:520
